TPU v7x, 32 devices: a whole 2x2x4 slice. The times are simulated.
32 devices in a mesh: section: 4 (over x, core), ctx: 8 (over z, y).
Axes of the slice: x: 2, y: 2, z: 4, core: 2. Of those that a mesh axis runs over, the one named last changes fastest.
Arguments:
- handoff: bfloat16 [4, 2, 768, 4096], P('section', None, 'ctx'), may hold values from -500 to 500
- norm_gain: bfloat16 [4, 4096], P('section'), may hold values from 0.099609375 to 1.8984375
- kv_weight: bfloat16 [4, 4096, 1024], P('section', 'ctx'), may hold values from -0.09375 to 0.09375
- queries: bfloat16 [4, 2, 768, 4096], P('section', None, 'ctx'), may hold values from -120 to 120
- span_order: int32 [2, 16], replicated, may hold values from 0 to 15, each once within a row
Outputs:
- partial_out: bfloat16 [4, 2, 768, 4096], P('section', None, 'ctx')
- log_sum: float32 [4, 2, 32, 768], P('section', None, None, 'ctx')
Inputs may be any that keep to these rules, and one draw needn't show every extreme that they name: Each row of span_order names every span of 0 to 15 once.
All inputs are finite; a program needn't handle non-finite values.
Results may differ from a plain program's by a relative error of at most 0.012.
The roundings to bfloat16 on the way count: a program that leaves them out, or rounds other values in their place, can miss the bound.
Values may be sent and summed in bfloat16 or wider, within the bound.
No kernel may reach another device: no remote copies, remote signals or barrier semaphores. Data moves between devices by JAX's collectives and lax.ppermute only.
A program may use at most 64 MiB of HBM per device.

v0:
```python
import jax
import jax.numpy as jnp
from jax import lax
from jax.sharding import PartitionSpec as P

QH = 32
KVH = 4
HD = 128
WINDOW = 4


rope_base = 500000.0


def passed_along(block, axis, distance):
    devices = range(lax.axis_size(axis))
    route = [((i - distance) % len(devices), i) for i in devices]
    return lax.ppermute(block, axis, route)


def rotate(key_vecs, positions):
    half_dim = key_vecs.shape[-1] // 2
    frequency = rope_base ** (-2.0 * jnp.arange(half_dim, dtype=jnp.float32) / key_vecs.shape[-1])
    angles = positions.astype(jnp.float32)[..., None, None] * frequency
    cosine = jnp.cos(angles)
    sine_part = jnp.sin(angles)
    first_half = key_vecs[..., :half_dim]
    second = key_vecs[..., half_dim:]
    return jnp.concatenate(
        [first_half * cosine - second * sine_part, second * cosine + first_half * sine_part],
        axis=-1,
    )


def on_device(handoff, norm_gain, kv_weight, queries, span_order):
    layer_in = passed_along(handoff, "section", 1)
    micro_count, tok_rows, model_width = (layer_in.shape[1], layer_in.shape[2], layer_in.shape[3])
    activations = layer_in[0].astype(jnp.float32)
    scale = lax.rsqrt(jnp.mean(activations * activations, axis=-1, keepdims=True) + 1e-05)
    normed = (activations * scale * norm_gain[0].astype(jnp.float32)).astype(jnp.bfloat16)
    flat_rows = normed.reshape(micro_count * tok_rows, model_width)
    weight = kv_weight[0]
    kv_width = weight.shape[1] // 2

    def add_rows(shard_rows):
        return jnp.dot(flat_rows, shard_rows, preferred_element_type=jnp.float32)

    key_part = add_rows(lax.all_gather(weight[:, :kv_width], "ctx", axis=0, tiled=True))
    value_part = add_rows(lax.all_gather(weight[:, kv_width:], "ctx", axis=0, tiled=True))
    cycle_size = lax.axis_size("ctx")
    own_index = lax.axis_index("ctx")
    span_len = tok_rows // 2

    def device_positions(device):
        span_ids = lax.dynamic_slice_in_dim(span_order, 2 * device, 2, 1)
        spread = (
            span_ids[:, :, None] * span_len + jnp.arange(span_len, dtype=jnp.int32)[None, None, :]
        )
        return spread.reshape(micro_count, tok_rows)

    own_pos = device_positions(own_index)
    key_vecs = rotate(key_part.reshape(micro_count, tok_rows, KVH, HD), own_pos)
    kv_block = jnp.concatenate(
        [
            key_vecs.reshape(micro_count, tok_rows, kv_width),
            value_part.reshape(micro_count, tok_rows, kv_width),
        ],
        axis=-1,
    ).astype(jnp.bfloat16)
    blocks = [kv_block]
    current = kv_block
    for step_num in range(1, WINDOW):
        current = passed_along(current, "ctx", 1)
        blocks.append(current)
    window_kv = jnp.concatenate(blocks, axis=1)
    window_pos = jnp.concatenate(
        [device_positions((own_index - step_num) % cycle_size) for step_num in range(WINDOW)],
        axis=1,
    )
    group_size = QH // KVH
    query_block = queries[0].reshape(micro_count, tok_rows, KVH, group_size, HD)
    results = []
    log_sums = []
    for micro_idx in range(micro_count):
        key_rows = window_kv[micro_idx, :, :kv_width].reshape(-1, KVH, HD)
        value_rows = window_kv[micro_idx, :, kv_width:].reshape(-1, KVH, HD)
        scores = jnp.einsum(
            "tkgd,ukd->kgtu", query_block[micro_idx], key_rows, preferred_element_type=jnp.float32
        ) * HD ** (-0.5)
        visible = (
            window_pos[micro_idx][None, None, None, :] <= own_pos[micro_idx][None, None, :, None]
        )
        scores = jnp.where(visible, scores, -jnp.inf)
        row_max = jnp.max(scores, axis=-1, keepdims=True)
        exps = jnp.exp(scores - row_max)
        running = jnp.sum(exps, axis=-1, keepdims=True)
        weights_bf = exps.astype(jnp.bfloat16)
        mixed = jnp.einsum(
            "kgtu,ukd->tkgd", weights_bf, value_rows, preferred_element_type=jnp.float32
        )
        denominator = jnp.moveaxis(running[..., 0], 2, 0)[..., None]
        results.append((mixed / denominator).astype(jnp.bfloat16).reshape(tok_rows, QH * HD))
        log_sums.append((row_max + jnp.log(running))[..., 0].reshape(QH, tok_rows))
    return (jnp.stack(results)[None], jnp.stack(log_sums)[None])


def solution(mesh):
    placed = (
        P("section", None, "ctx", None),
        P("section", None),
        P("section", "ctx", None),
        P("section", None, "ctx", None),
        P(),
    )
    return jax.shard_map(
        on_device,
        mesh=mesh,
        in_specs=placed,
        out_specs=(P("section", None, "ctx", None), P("section", None, None, "ctx")),
        check_vma=False,
    )
```

profile of v0, /device:TPU:0, one launch (start us, length us, event | category | flops | bytes accessed | tf_op | source)
XLA Modules:
  0.0 228.6 jit_solution(5074069389822792288)
XLA Ops:
  7.2 2.3 fusion.64
  9.6 0.7 all-gather.5.cloned.1.call-update
  10.3 0.5 collective-permute-start
  11.8 0.4 multiply_cosine_fusion
  12.2 18.8 %collective-permute-done = bf16[1,2,96,4096]{3,2,1,0:T(8,128)(2,1)S(1)} collective-permute-done((bf16[1,2,96,4096]{3,2,1,0:T(8,128)(2,1)}, bf16[1,2,96,4096]{3,2,1,0:T(8,128)(2,1)S(1)}, u32[]{:S(2)}, u32[]{:S(2)}) %collective-permute-start) | collective-permute-done | bytes 1572896 | tf_op jit(solution)/shard_map/ppermute | solution.py:18
  31.0 0.4 fusion.10
  31.4 55.4 %all-gather.3.cloned.1.call-done = bf16[4096,512]{1,0:T(8,128)(2,1)} async-done(((bf16[512,512]{1,0:T(8,128)(2,1)}), bf16[4096,512]{1,0:T(8,128)(2,1)}) %all-gather.3.cloned.1.call-update) | async-done | bytes 4194320 | tf_op jit(solution)/shard_map/all_gather | solution.py:48
  86.9 6.4 %copy.12 = bf16[512,4096]{1,0:T(8,128)(2,1)} copy(bf16[512,4096]{0,1:T(8,128)(2,1)} %bitcast.98) | data formatting | bytes 8388608 | tf_op jit(solution)/shard_map/dot_general | solution.py:46
  93.2 4.0 %fusion.28 = f32[2,96,4,128]{3,1,2,0:T(8,128)S(1)} fusion(bf16[4,128,4096,1]{2,1,0,3:T(8,128)(2,1)} %bitcast.99, bf16[1,2,96,4096]{3,2,1,0:T(8,128)(2,1)S(1)} %collective-permute-done, f32[4096]{0:T(1024)S(1)} %bitcast.109, f32[2,96]{1,0:T(2,128)S(1)} %add_rsqrt_fusion), kind=kOutput, calls=%fused_computation.32 | convolution fusion | flops 808452096 | bytes 6177536 | tf_op jit(solution)/shard_map/dot_general | solution.py:46
  97.3 0.2 subtract_convert_fusion
  97.6 63.0 %all-gather.5.cloned.1.call-done = bf16[4096,512]{1,0:T(8,128)(2,1)} async-done(((bf16[512,512]{1,0:T(8,128)(2,1)}), bf16[4096,512]{1,0:T(8,128)(2,1)}) %all-gather.5.cloned.1.call-update) | async-done | bytes 4194320 | tf_op jit(solution)/shard_map/all_gather | solution.py:49
  160.7 3.2 %fusion.41 = bf16[2,96,512]{2,1,0:T(8,128)(2,1)S(1)} fusion(bf16[4096,512]{1,0:T(8,128)(2,1)} %all-gather.5.cloned.1.call-done, bf16[1,2,96,4096]{3,2,1,0:T(8,128)(2,1)S(1)} %collective-permute-done, f32[4096]{0:T(1024)S(1)} %bitcast.110, f32[2,96]{1,0:T(2,128)S(1)} %add_rsqrt_fusion), kind=kOutput, calls=%fused_computation.43 | convolution fusion | flops 808550400 | bytes 5980928 | tf_op jit(solution)/shard_map/dot_general | solution.py:46
  163.9 0.6 collective-permute-start.1
  164.6 11.7 %collective-permute-done.1 = bf16[2,96,1024]{2,1,0:T(8,128)(2,1)S(1)} collective-permute-done((bf16[2,96,1024]{2,1,0:T(8,128)(2,1)S(1)}, bf16[2,96,1024]{2,1,0:T(8,128)(2,1)S(1)}, u32[]{:S(2)}, u32[]{:S(2)}) %collective-permute-start.1) | collective-permute-done | bytes 393248 | tf_op jit(solution)/shard_map/ppermute | solution.py:18
  176.5 11.4 %collective-permute-done.2 = bf16[2,96,1024]{2,1,0:T(8,128)(2,1)} collective-permute-done((bf16[2,96,1024]{2,1,0:T(8,128)(2,1)S(1)}, bf16[2,96,1024]{2,1,0:T(8,128)(2,1)}, u32[]{:S(2)}, u32[]{:S(2)}) %collective-permute-start.2) | collective-permute-done | bytes 393248 | tf_op jit(solution)/shard_map/ppermute | solution.py:18
  188.5 0.7 broadcast_compare_fusion
  189.3 9.5 %collective-permute-done.3 = bf16[2,96,1024]{2,1,0:T(8,128)(2,1)} collective-permute-done((bf16[2,96,1024]{2,1,0:T(8,128)(2,1)}, bf16[2,96,1024]{2,1,0:T(8,128)(2,1)}, u32[]{:S(2)}, u32[]{:S(2)}) %collective-permute-start.3) | collective-permute-done | bytes 393248 | tf_op jit(solution)/shard_map/ppermute | solution.py:18
  198.8 1.2 pad_maximum_fusion
  200.3 2.0 fusion.8
  202.3 2.1 copy-done.1
  204.4 1.5 fusion.2
  206.1 1.2 fusion.9
  207.3 2.2 copy-done
  209.4 1.5 fusion.4
  211.1 3.7 %fusion.32 = bf16[96,4,8,128]{3,0,2,1:T(8,128)(2,1)S(1)} fusion(f32[4,384,96,8]{1,2,3,0:T(8,128)} %copy-done.1, f32[4,8,96]{2,1,0:T(8,128)S(1)} %get-tuple-element.30, pred[96,384]{1,0:T(8,128)(4,1)S(1)} %copy-done.9, f32[96,4,8]{0,2,1:T(8,128)S(1)} %bitcast.108, bf16[384,4,128,1]{2,1,0,3:T(4,128)(2,1)S(1)} %bitcast.104), kind=kOutput, calls=%fused_computation.38 | convolution fusion | flops 307494912 | bytes 5959680 | tf_op jit(solution)/shard_map/kgtu,ukd->tkgd/dot_general | solution.py:98
  214.8 0.3 copy.17
  215.1 0.3 stack_reshape.6
  215.6 3.7 %fusion.31 = bf16[96,4,8,128]{3,0,2,1:T(8,128)(2,1)S(1)} fusion(f32[4,384,96,8]{1,2,3,0:T(8,128)} %copy-done, f32[4,8,96]{2,1,0:T(8,128)S(1)} %get-tuple-element.28, pred[96,384]{1,0:T(8,128)(4,1)S(1)} %copy-done.7, f32[96,4,8]{0,2,1:T(8,128)S(1)} %bitcast.107, bf16[384,4,128,1]{2,1,0,3:T(4,128)(2,1)S(1)} %bitcast.105), kind=kOutput, calls=%fused_computation.36 | convolution fusion | flops 307494912 | bytes 5959680 | tf_op jit(solution)/shard_map/kgtu,ukd->tkgd/dot_general | solution.py:98
  219.2 0.3 copy.21
  219.5 0.3 stack_reshape.7
  219.9 0.6 maximum_bitcast_fusion.2
  220.5 1.3 maximum_bitcast_fusion
  (62 shorter events, 2.6 us)
Async XLA Ops:
  7.2 3.6 %copy-start.10 = (s32[2,16]{1,0:T(2,128)S(1)}, s32[2,16]{1,0:T(2,128)}, u32[]{:S(2)}) copy-start(s32[2,16]{1,0:T(2,128)} %param.9) | copy-start | bytes 388
  7.2 4.5 %copy-start.11 = (bf16[1,4096]{1,0:T(2,128)(2,1)S(1)}, bf16[1,4096]{1,0:T(2,128)(2,1)}, u32[]{:S(2)}) copy-start(bf16[1,4096]{1,0:T(2,128)(2,1)} %param.6) | copy-start | bytes 24580
  7.2 79.7 %all-gather.3.cloned.1.call-start = ((), (), s32[]{:S(2)}) async-start(), calls=%async_computation | async-start | bytes 4718592 | tf_op jit(solution)/shard_map/all_gather | solution.py:48
  9.5 151.2 %all-gather.5.cloned.1.call-start = ((), (), s32[]{:S(2)}) async-start(), calls=%async_computation.1 | async-start | bytes 4718592 | tf_op jit(solution)/shard_map/all_gather | solution.py:49
  10.3 20.7 %collective-permute-start = (bf16[1,2,96,4096]{3,2,1,0:T(8,128)(2,1)}, bf16[1,2,96,4096]{3,2,1,0:T(8,128)(2,1)S(1)}, u32[]{:S(2)}, u32[]{:S(2)}) collective-permute-start(bf16[1,2,96,4096]{3,2,1,0:T(8,128)(2,1)} %param.5), channel_id=1, source_target_pairs={{24,0},{0,8},{8,16},{16,24},{25,1},{1,9},{9,17},{17,25},{26,2},{2,... | collective-permute-start | bytes 4718600 | tf_op jit(solution)/shard_map/ppermute | solution.py:18
  97.6 78.7 %copy-start.2 = (bf16[1,2,96,4096]{3,2,1,0:T(8,128)(2,1)S(1)}, bf16[1,2,96,4096]{3,2,1,0:T(8,128)(2,1)}, u32[]{:S(2)}) copy-start(bf16[1,2,96,4096]{3,2,1,0:T(8,128)(2,1)} %param.8) | copy-start | bytes 4718596
  163.9 12.6 %copy-start.3 = (bf16[2,96,512]{2,1,0:T(8,128)(2,1)}, bf16[2,96,512]{2,1,0:T(8,128)(2,1)S(1)}, u32[]{:S(2)}) copy-start(bf16[2,96,512]{2,1,0:T(8,128)(2,1)S(1)} %fusion.41) | copy-start | bytes 589828
  163.9 12.4 %collective-permute-start.1 = (bf16[2,96,1024]{2,1,0:T(8,128)(2,1)S(1)}, bf16[2,96,1024]{2,1,0:T(8,128)(2,1)S(1)}, u32[]{:S(2)}, u32[]{:S(2)}) collective-permute-start(bf16[2,96,1024]{2,1,0:T(8,128)(2,1)S(1)} %pad_maximum_fusion.1), channel_id=1, source_target_pairs={{7,0},{0,1},{1,2},{2,3},{3,4},{4,5},{5,6},{6,7},{15,8},{8,9},{9,10... | collective-permute-start | bytes 1179656 | tf_op jit(solution)/shard_map/ppermute | solution.py:18
  176.4 11.6 %copy-start.5 = (bf16[2,96,1024]{2,1,0:T(8,128)(2,1)}, bf16[2,96,1024]{2,1,0:T(8,128)(2,1)S(1)}, u32[]{:S(2)}) copy-start(bf16[2,96,1024]{2,1,0:T(8,128)(2,1)S(1)} %collective-permute-done.1) | copy-start | bytes 1179652
  176.4 11.6 %collective-permute-start.2 = (bf16[2,96,1024]{2,1,0:T(8,128)(2,1)S(1)}, bf16[2,96,1024]{2,1,0:T(8,128)(2,1)}, u32[]{:S(2)}, u32[]{:S(2)}) collective-permute-start(bf16[2,96,1024]{2,1,0:T(8,128)(2,1)S(1)} %collective-permute-done.1), channel_id=1, source_target_pairs={{7,0},{0,1},{1,2},{2,3},{3,4},{4,5},{5,6},{6,7},{15,8},{8,9},{9,10... | collective-permute-start | bytes 1179656 | tf_op jit(solution)/shard_map/ppermute | solution.py:18
  187.9 10.8 %copy-start.4 = (bf16[2,96,512]{2,1,0:T(8,128)(2,1)S(1)}, bf16[2,96,512]{2,1,0:T(8,128)(2,1)}, u32[]{:S(2)}) copy-start(bf16[2,96,512]{2,1,0:T(8,128)(2,1)} %copy-done.3) | copy-start | bytes 589828
  187.9 10.8 %collective-permute-start.3 = (bf16[2,96,1024]{2,1,0:T(8,128)(2,1)}, bf16[2,96,1024]{2,1,0:T(8,128)(2,1)}, u32[]{:S(2)}, u32[]{:S(2)}) collective-permute-start(bf16[2,96,1024]{2,1,0:T(8,128)(2,1)} %collective-permute-done.2), channel_id=1, source_target_pairs={{7,0},{0,1},{1,2},{2,3},{3,4},{4,5},{5,6},{6,7},{15,8},{8,9},{9,10... | collective-permute-start | bytes 1179656 | tf_op jit(solution)/shard_map/ppermute | solution.py:18
  188.2 10.6 %copy-start.6 = (bf16[2,96,1024]{2,1,0:T(8,128)(2,1)S(1)}, bf16[2,96,1024]{2,1,0:T(8,128)(2,1)}, u32[]{:S(2)}) copy-start(bf16[2,96,1024]{2,1,0:T(8,128)(2,1)} %copy-done.5) | copy-start | bytes 1179652
  200.2 4.1 %copy-start.8 = (pred[96,384]{1,0:T(8,128)(4,1)S(1)}, pred[96,384]{1,0:T(8,128)(4,1)}, u32[]{:S(2)}) copy-start(pred[96,384]{1,0:T(8,128)(4,1)} %get-tuple-element.33) | copy-start | bytes 110596
  202.3 2.1 copy-start.1
  202.3 3.8 %copy-start.7 = (pred[96,384]{1,0:T(8,128)(4,1)S(1)}, pred[96,384]{1,0:T(8,128)(4,1)}, u32[]{:S(2)}) copy-start(pred[96,384]{1,0:T(8,128)(4,1)} %get-tuple-element.32) | copy-start | bytes 110596
  207.3 2.2 copy-start
  207.3 3.9 %copy-start.9 = (pred[96,384]{1,0:T(8,128)(4,1)S(1)}, pred[96,384]{1,0:T(8,128)(4,1)}, u32[]{:S(2)}) copy-start(pred[96,384]{1,0:T(8,128)(4,1)} %get-tuple-element.33) | copy-start | bytes 110596
Sparse Core Ops, SparseCore 0:
  10.7 76.0 all-gather.2
  89.0 71.6 all-gather.4
where the time goes:
time: 229 us
  waiting for transfers between devices  171 us (75%)
  matrix products  17.8 us (8%)
  local copies, waits for them, and re-layouts  16.3 us (7%)
  between operations  14.4 us (6%)
  other arithmetic  8.45 us (4%)
    all_gather x1, waiting for transfers between devices, on_device(): lax.all_gather(weight[:, kv_width:], 'ctx', axis=0, tiled=True)  63 us
    all_gather x1, waiting for transfers between devices, on_device(): lax.all_gather(weight[:, :kv_width], 'ctx', axis=0, tiled=True)  55.4 us
    ppermute x4, waiting for transfers between devices, passed_along(): return lax.ppermute(block, axis, route)  51.4 us
    dot_general x2, matrix products, on_device(): jnp.einsum('kgtu,ukd->tkgd', weights_bf, value_rows, preferred_element_ty...  7.32 us
    dot_general x2, matrix products, add_rows(): return jnp.dot(flat_rows, shard_rows, preferred_element_type=jnp.float32)  7.24 us
    dot_general x1, local copies, waits for them, and re-layouts, add_rows(): return jnp.dot(flat_rows, shard_rows, preferred_element_type=jnp.float32)  6.39 us
    unnamed x27, local copies, waits for them, and re-layouts  4.8 us
  transfers between devices with their start and end apart: 6, of which 6 were waited for; matrix products, arithmetic and copies ran while one was open for 6% of the time, Pallas kernels for 0%

commit v1 on v0

v1 whole, which is shorter than its diff:
```python
import jax
import jax.numpy as jnp
from jax import lax
from jax.sharding import PartitionSpec as P

QH = 32
KVH = 4
HD = 128
WINDOW = 4
QUAD = 4


rope_base = 500000.0


def moved(block, axis, target):
    size = lax.axis_size(axis)
    return lax.ppermute(block, axis, [(i, target(i) % size) for i in range(size)])


def rope_tables(positions):
    half_dim = HD // 2
    frequency = rope_base ** (-2.0 * jnp.arange(half_dim, dtype=jnp.float32) / HD)
    angles = positions.astype(jnp.float32)[..., None, None] * frequency
    return jnp.cos(angles), jnp.sin(angles)


def rotate(key_vecs, tables):
    cosine, sine_part = tables
    half_dim = HD // 2
    first_half = key_vecs[..., :half_dim]
    second = key_vecs[..., half_dim:]
    return jnp.concatenate(
        [first_half * cosine - second * sine_part, second * cosine + first_half * sine_part],
        axis=-1,
    )


def on_device(handoff, norm_gain, kv_weight, queries, span_order):
    sections = lax.axis_size("section")
    cycle_size = lax.axis_size("ctx")
    own_index = lax.axis_index("ctx")
    quads = cycle_size // QUAD
    own_quad, own_place = own_index // QUAD, own_index % QUAD
    weight = kv_weight[0]
    shard_rows, kv_width = weight.shape[0], weight.shape[1] // 2
    _, micro_count, tok_rows, model_width = handoff.shape
    rows = micro_count * tok_rows

    def same_place_shards(part):
        return [part] + [
            moved(part, "ctx", lambda i, j=j: i + QUAD * j) for j in range(1, quads)
        ]

    key_shards = same_place_shards(weight[:, :kv_width])

    next_gain = moved(norm_gain, "section", lambda i: i - 1)
    activations = handoff[0].astype(jnp.float32)
    scale = lax.rsqrt(jnp.mean(activations * activations, axis=-1, keepdims=True) + 1e-05)
    normed = (activations * scale * next_gain[0].astype(jnp.float32)).astype(jnp.bfloat16)
    normed = normed.reshape(rows, model_width)

    def to_next_section(part, flip):
        route = [
            (s * cycle_size + i, (s + 1) % sections * cycle_size + (i ^ flip))
            for s in range(sections)
            for i in range(cycle_size)
        ]
        return lax.ppermute(part, ("section", "ctx"), route)

    arrived = []
    for flip in range(QUAD):
        pieces = [
            lax.dynamic_slice_in_dim(
                normed,
                ((own_quad - j) % quads * QUAD + (own_place ^ flip)) * shard_rows,
                shard_rows,
                1,
            )
            for j in range(quads)
        ]
        arrived.append(to_next_section(jnp.concatenate(pieces, axis=1), flip))
    flat_rows = jnp.concatenate(arrived, axis=0)

    def partial_product(shards):
        total = 0.0
        for j, shard in enumerate(shards):
            total = total + jnp.dot(
                flat_rows[:, j * shard_rows : (j + 1) * shard_rows],
                shard,
                preferred_element_type=jnp.float32,
            )
        return total

    def own_rows_total(product):
        total = product[:rows]
        for flip in range(1, QUAD):
            part = product[flip * rows : (flip + 1) * rows].astype(jnp.bfloat16)
            total = total + moved(part, "ctx", lambda i, flip=flip: i ^ flip).astype(jnp.float32)
        return total

    def window_of(block):
        two_back = moved(block, "ctx", lambda i: i + 2)
        beside = moved(two_back, "ctx", lambda i: i ^ 1)
        onward = jnp.where(own_index % 2 == 0, block, two_back)
        last = moved(onward, "ctx", lambda i: i + 1)
        return jnp.concatenate([block, two_back, beside, last], axis=1)

    odd = own_index % 2
    distances = [0, 2, 1 + 2 * odd, 3 - 2 * odd]
    span_len = tok_rows // 2

    def device_positions(device):
        span_ids = lax.dynamic_slice_in_dim(span_order, 2 * device, 2, 1)
        spread = (
            span_ids[:, :, None] * span_len + jnp.arange(span_len, dtype=jnp.int32)[None, None, :]
        )
        return spread.reshape(micro_count, tok_rows)

    own_pos = device_positions(own_index)
    window_pos = jnp.concatenate(
        [device_positions((own_index - d) % cycle_size) for d in distances], axis=1
    )
    tables = rope_tables(own_pos)

    key_total = own_rows_total(partial_product(key_shards))
    value_part, _ = lax.optimization_barrier((weight[:, kv_width:], key_shards[-1]))
    value_shards = same_place_shards(value_part)
    key_vecs = rotate(key_total.reshape(micro_count, tok_rows, KVH, HD), tables)
    key_block = key_vecs.reshape(micro_count, tok_rows, kv_width).astype(jnp.bfloat16)
    window_keys = window_of(key_block)

    group_size = QH // KVH
    query_block = queries[0].reshape(micro_count, tok_rows, KVH, group_size, HD)
    weights, sums, log_sums = [], [], []
    for micro_idx in range(micro_count):
        key_rows = window_keys[micro_idx].reshape(-1, KVH, HD)
        scores = jnp.einsum(
            "tkgd,ukd->kgtu", query_block[micro_idx], key_rows, preferred_element_type=jnp.float32
        ) * HD ** (-0.5)
        visible = (
            window_pos[micro_idx][None, None, None, :] <= own_pos[micro_idx][None, None, :, None]
        )
        scores = jnp.where(visible, scores, -jnp.inf)
        row_max = jnp.max(scores, axis=-1, keepdims=True)
        exps = jnp.exp(scores - row_max)
        running = jnp.sum(exps, axis=-1, keepdims=True)
        weights.append(exps.astype(jnp.bfloat16))
        sums.append(jnp.moveaxis(running[..., 0], 2, 0)[..., None])
        log_sums.append((row_max + jnp.log(running))[..., 0].reshape(QH, tok_rows))

    value_total = own_rows_total(partial_product(value_shards))
    value_block = value_total.astype(jnp.bfloat16).reshape(micro_count, tok_rows, kv_width)
    window_values = window_of(value_block)
    results = []
    for micro_idx in range(micro_count):
        value_rows = window_values[micro_idx].reshape(-1, KVH, HD)
        mixed = jnp.einsum(
            "kgtu,ukd->tkgd", weights[micro_idx], value_rows, preferred_element_type=jnp.float32
        )
        results.append((mixed / sums[micro_idx]).astype(jnp.bfloat16).reshape(tok_rows, QH * HD))
    return (jnp.stack(results)[None], jnp.stack(log_sums)[None])


def solution(mesh):
    placed = (
        P("section", None, "ctx", None),
        P("section", None),
        P("section", "ctx", None),
        P("section", None, "ctx", None),
        P(),
    )
    return jax.shard_map(
        on_device,
        mesh=mesh,
        in_specs=placed,
        out_specs=(P("section", None, "ctx", None), P("section", None, None, "ctx")),
        check_vma=False,
    )
```

time: 229 us -> 145 us (0.63)
  waiting for transfers between devices: 171 us -> 70.7 us
  starting transfers between devices: 1.19 us -> 24 us
  between operations: 14.4 us -> 1.11 us
  other arithmetic: 8.45 us -> 14.6 us
  matrix products: 17.8 us -> 15.2 us
    all_gather x2 -> x0, waiting for transfers between devices: 118 us -> none  [the longest x1 63 us: on_device(): lax.all_gather(weight[:, kv_width:], 'ctx', axis=0, tiled=True)]
    ppermute x4 -> x19, starting transfers between devices: 1.11 us -> 24 us  [the longest x15 19.6 us: moved(): lax.ppermute(block, axis, [(i, target(i) % size) for i in range(size)])]
    ppermute x4 -> x19, waiting for transfers between devices: 51.4 us -> 70.7 us  [the longest x15 48 us: moved(): lax.ppermute(block, axis, [(i, target(i) % size) for i in range(size)])]
    dot_general x1 -> x0, local copies, waits for them, and re-layouts: 6.39 us -> none  [add_rows(): return jnp.dot(flat_rows, shard_rows, preferred_element_type=jnp.float32)]
    concatenate x3 -> x8, other arithmetic: 1.36 us -> 4.4 us  [the longest x4 2.41 us: on_device(): arrived.append(to_next_section(jnp.concatenate(pieces, axis=1), flip))]
    unnamed x27 -> x26, local copies, waits for them, and re-layouts: 4.8 us -> 7 us
    dot_general x4 -> x6, matrix products: 14.6 us -> 12.9 us  [the longest x2 7.4 us: on_device(): jnp.einsum('kgtu,ukd->tkgd', weights[micro_idx], value_rows, preferred_el...]
  transfers between devices with their start and end apart: 6 -> 19, of which waited for: 6 -> 12; matrix products, arithmetic and copies ran while one was open for 6% -> 23% of each run, Pallas kernels for 0% -> 0%
where the time goes in v1:
time: 145 us; the launch traced here: 143 us
  waiting for transfers between devices  70.7 us (49%)
  starting transfers between devices  24 us (17%)
  local copies, waits for them, and re-layouts  17.1 us (12%)
  matrix products  15.2 us (10%)
  other arithmetic  14.6 us (10%)
    ppermute x15, waiting for transfers between devices, moved(): lax.ppermute(block, axis, [(i, target(i) % size) for i in range(size)])  48 us
    ppermute x4, waiting for transfers between devices, to_next_section(): return lax.ppermute(part, ('section', 'ctx'), route)  22.7 us
    ppermute x15, starting transfers between devices, moved(): lax.ppermute(block, axis, [(i, target(i) % size) for i in range(size)])  19.6 us
    dot_general x2, matrix products, on_device(): jnp.einsum('kgtu,ukd->tkgd', weights[micro_idx], value_rows, preferred_el...  7.4 us
    unnamed x26, local copies, waits for them, and re-layouts  7 us
    dot_general x4, matrix products, partial_product(): jnp.dot(flat_rows[:, j * shard_rows:(j + 1) * shard_rows], shard, preferr...  5.5 us
    ppermute x4, starting transfers between devices, to_next_section(): return lax.ppermute(part, ('section', 'ctx'), route)  4.43 us
    reduce_sum x2, other arithmetic, on_device(): running = jnp.sum(exps, axis=-1, keepdims=True)  3.12 us
  transfers between devices with their start and end apart: 19, of which 12 were waited for; matrix products, arithmetic and copies ran while one was open for 23% of the time, Pallas kernels for 0%

profile of v1, /device:TPU:0, one launch (start us, length us, event | category | flops | bytes accessed | tf_op | source)
XLA Modules:
  0.0 142.7 jit_solution(15876128314889194159)
XLA Ops:
  0.6 2.4 %collective-permute-start = (bf16[1,4096]{1,0:T(2,128)(2,1)}, bf16[1,4096]{1,0:T(2,128)(2,1)S(1)}, u32[]{:S(2)}, u32[]{:S(2)}) collective-permute-start(bf16[1,4096]{1,0:T(2,128)(2,1)} %param.6), channel_id=1, source_target_pairs={{0,24},{8,0},{16,8},{24,16},{1,25},{9,1},{17,9},{25,17},{2,26},{10... | collective-permute-start | bytes 24584 | tf_op jit(solution)/shard_map/ppermute | solution.py:18
  3.1 2.3 %fusion.51 = (bf16[512,512]{1,0:T(8,128)(2,1)}, bf16[512,512]{1,0:T(8,128)(2,1)}) fusion(bf16[512,1024]{1,0:T(8,128)(2,1)} %bitcast.96), kind=kLoop, calls=%fused_computation.106 | loop fusion | bytes 2097152 | tf_op jit(solution)/shard_map/slice | solution.py:55
  5.4 2.6 %collective-permute-start.5 = (bf16[512,512]{1,0:T(8,128)(2,1)}, bf16[512,512]{1,0:T(8,128)(2,1)}, u32[]{:S(2)}, u32[]{:S(2)}) collective-permute-start(bf16[512,512]{1,0:T(8,128)(2,1)} %get-tuple-element.16), channel_id=1, source_target_pairs={{0,4},{1,5},{2,6},{3,7},{4,0},{5,1},{6,2},{7,3},{8,12},{9,13},{10,... | collective-permute-start | bytes 1572872 | tf_op jit(solution)/shard_map/ppermute | solution.py:18
  10.0 2.4 %slice_bitcast_fusion.1 = (bf16[12,8,32,128]{3,1,2,0:T(8,128)(2,1)S(1)}, bf16[12,8,32,128]{3,1,2,0:T(8,128)(2,1)}) fusion(bf16[1,2,96,4096]{3,2,1,0:T(8,128)(2,1)} %param.8), kind=kLoop, calls=%fused_computation.38 | loop fusion | bytes 3145728
  14.2 1.9 %collective-permute-start.2 = (bf16[192,1024]{1,0:T(8,128)(2,1)}, bf16[192,1024]{1,0:T(8,128)(2,1)}, u32[]{:S(2)}, u32[]{:S(2)}) collective-permute-start(bf16[192,1024]{1,0:T(8,128)(2,1)} %pad_maximum_fusion.3), channel_id=1, source_target_pairs={{0,9},{1,8},{2,11},{3,10},{4,13},{5,12},{6,15},{7,14},{8,17},{9,16... | collective-permute-start | bytes 1179656 | tf_op jit(solution)/shard_map/ppermute | solution.py:69
  16.9 1.2 collective-permute-start.3
  18.9 1.3 collective-permute-start.4
  23.3 3.6 %collective-permute-done.2 = bf16[192,1024]{1,0:T(8,128)(2,1)} collective-permute-done((bf16[192,1024]{1,0:T(8,128)(2,1)}, bf16[192,1024]{1,0:T(8,128)(2,1)}, u32[]{:S(2)}, u32[]{:S(2)}) %collective-permute-start.2) | collective-permute-done | bytes 393248 | tf_op jit(solution)/shard_map/ppermute | solution.py:69
  28.0 11.7 %collective-permute-done.3 = bf16[192,1024]{1,0:T(8,128)(2,1)} collective-permute-done((bf16[192,1024]{1,0:T(8,128)(2,1)}, bf16[192,1024]{1,0:T(8,128)(2,1)}, u32[]{:S(2)}, u32[]{:S(2)}) %collective-permute-start.3) | collective-permute-done | bytes 393248 | tf_op jit(solution)/shard_map/ppermute | solution.py:69
  40.7 7.3 %collective-permute-done.4 = bf16[192,1024]{1,0:T(8,128)(2,1)} collective-permute-done((bf16[192,1024]{1,0:T(8,128)(2,1)}, bf16[192,1024]{1,0:T(8,128)(2,1)}, u32[]{:S(2)}, u32[]{:S(2)}) %collective-permute-start.4) | collective-permute-done | bytes 393248 | tf_op jit(solution)/shard_map/ppermute | solution.py:69
  49.1 1.7 %fusion.30 = f32[768,512]{1,0:T(8,128)S(1)} fusion(bf16[512,512]{1,0:T(8,128)(2,1)} %collective-permute-done.5, bf16[768,1024]{1,0:T(8,128)(2,1)S(1)} %constant_dynamic-update-slice_fusion), kind=kOutput, calls=%fused_computation.39 | convolution fusion | flops 402653184 | bytes 2883584 | tf_op jit(solution)/shard_map/dot_general | solution.py:88
  51.4 1.6 %collective-permute-start.13 = (bf16[192,512]{1,0:T(8,128)(2,1)S(1)}, bf16[192,512]{1,0:T(8,128)(2,1)S(1)}, u32[]{:S(2)}, u32[]{:S(2)}) collective-permute-start(bf16[192,512]{1,0:T(8,128)(2,1)S(1)} %get-tuple-element.22), channel_id=1, source_target_pairs={{0,1},{1,0},{2,3},{3,2},{4,5},{5,4},{6,7},{7,6},{8,9},{9,8},{10,11... | collective-permute-start | bytes 589832 | tf_op jit(solution)/shard_map/ppermute | solution.py:18
  53.0 2.0 %collective-permute-start.14 = (bf16[192,512]{1,0:T(8,128)(2,1)S(1)}, bf16[192,512]{1,0:T(8,128)(2,1)S(1)}, u32[]{:S(2)}, u32[]{:S(2)}) collective-permute-start(bf16[192,512]{1,0:T(8,128)(2,1)S(1)} %get-tuple-element.24), channel_id=1, source_target_pairs={{0,2},{1,3},{2,0},{3,1},{4,6},{5,7},{6,4},{7,5},{8,10},{9,11},{10,... | collective-permute-start | bytes 589832 | tf_op jit(solution)/shard_map/ppermute | solution.py:18
  57.0 2.9 %collective-permute-done.13 = bf16[192,512]{1,0:T(8,128)(2,1)S(1)} collective-permute-done((bf16[192,512]{1,0:T(8,128)(2,1)S(1)}, bf16[192,512]{1,0:T(8,128)(2,1)S(1)}, u32[]{:S(2)}, u32[]{:S(2)}) %collective-permute-start.13) | collective-permute-done | bytes 196640 | tf_op jit(solution)/shard_map/ppermute | solution.py:18
  59.9 6.0 %collective-permute-done.15 = bf16[192,512]{1,0:T(8,128)(2,1)S(1)} collective-permute-done((bf16[192,512]{1,0:T(8,128)(2,1)S(1)}, bf16[192,512]{1,0:T(8,128)(2,1)S(1)}, u32[]{:S(2)}, u32[]{:S(2)}) %collective-permute-start.15) | collective-permute-done | bytes 196640 | tf_op jit(solution)/shard_map/ppermute | solution.py:18
  66.0 2.2 %collective-permute-done.14 = bf16[192,512]{1,0:T(8,128)(2,1)S(1)} collective-permute-done((bf16[192,512]{1,0:T(8,128)(2,1)S(1)}, bf16[192,512]{1,0:T(8,128)(2,1)S(1)}, u32[]{:S(2)}, u32[]{:S(2)}) %collective-permute-start.14) | collective-permute-done | bytes 196640 | tf_op jit(solution)/shard_map/ppermute | solution.py:18
  70.1 1.3 subtract_convert_fusion
  73.7 8.0 %collective-permute-done.16 = bf16[2,96,512]{1,2,0:T(8,128)(2,1)S(1)} collective-permute-done((bf16[2,96,512]{1,2,0:T(8,128)(2,1)S(1)}, bf16[2,96,512]{1,2,0:T(8,128)(2,1)S(1)}, u32[]{:S(2)}, u32[]{:S(2)}) %collective-permute-start.16) | collective-permute-done | bytes 196640 | tf_op jit(solution)/shard_map/ppermute | solution.py:18
  82.3 4.8 %collective-permute-start.17 = (bf16[2,96,512]{1,2,0:T(8,128)(2,1)S(1)}, bf16[2,96,512]{1,2,0:T(8,128)(2,1)S(1)}, u32[]{:S(2)}, u32[]{:S(2)}) collective-permute-start(bf16[2,96,512]{1,2,0:T(8,128)(2,1)S(1)} %collective-permute-done.16), channel_id=1, source_target_pairs={{0,1},{1,0},{2,3},{3,2},{4,5},{5,4},{6,7},{7,6},{8,9},{9,8},{10,11... | collective-permute-start | bytes 589832 | tf_op jit(solution)/shard_map/ppermute | solution.py:18
  87.1 1.6 %fusion.32 = f32[768,512]{1,0:T(8,128)S(1)} fusion(bf16[512,512]{1,0:T(8,128)(2,1)} %collective-permute-done.6, bf16[768,1024]{1,0:T(8,128)(2,1)S(1)} %constant_dynamic-update-slice_fusion), kind=kOutput, calls=%fused_computation.41 | convolution fusion | flops 402653184 | bytes 2883584 | tf_op jit(solution)/shard_map/dot_general | solution.py:88
  88.7 1.6 %fusion.57 = (bf16[768,512]{1,0:T(8,128)(2,1)S(1)}, f32[768,512]{1,0:T(8,128)S(1)}) fusion(f32[768,512]{1,0:T(8,128)S(1)} %fusion.32, bf16[512,512]{1,0:T(8,128)(2,1)} %get-tuple-element.3, bf16[768,1024]{1,0:T(8,128)(2,1)S(1)} %constant_dynamic-update-slice_fusion), kind=kOutput, calls=%fused_computation.112 | convolution fusion | flops 403439616 | bytes 5242880 | tf_op jit(solution)/shard_map/dot_general | solution.py:88
  90.9 3.5 %collective-permute-start.9 = (bf16[192,512]{1,0:T(8,128)(2,1)S(1)}, bf16[192,512]{1,0:T(8,128)(2,1)S(1)}, u32[]{:S(2)}, u32[]{:S(2)}) collective-permute-start(bf16[192,512]{1,0:T(8,128)(2,1)S(1)} %get-tuple-element.26), channel_id=1, source_target_pairs={{0,3},{1,2},{2,1},{3,0},{4,7},{5,6},{6,5},{7,4},{8,11},{9,10},{10,... | collective-permute-start | bytes 589832 | tf_op jit(solution)/shard_map/ppermute | solution.py:18
  94.6 8.7 %collective-permute-done.17 = bf16[2,96,512]{1,2,0:T(8,128)(2,1)S(1)} collective-permute-done((bf16[2,96,512]{1,2,0:T(8,128)(2,1)S(1)}, bf16[2,96,512]{1,2,0:T(8,128)(2,1)S(1)}, u32[]{:S(2)}, u32[]{:S(2)}) %collective-permute-start.17) | collective-permute-done | bytes 196640 | tf_op jit(solution)/shard_map/ppermute | solution.py:18
  103.9 1.2 fusion.5
  105.1 1.6 %fusion.2 = f32[4,8,96]{2,1,0:T(8,128)S(1)} fusion(f32[4,384,96,8]{1,2,3,0:T(8,128)S(1)} %get-tuple-element.49, f32[4,8,96]{2,1,0:T(8,128)S(1)} %get-tuple-element.48, pred[96,384]{1,0:T(8,128)(4,1)S(1)} %get-tuple-element.52), kind=kLoop, calls=%fused_computation.6 | loop fusion | flops 4715520 | bytes 4780032 | tf_op jit(solution)/shard_map/reduce_sum | solution.py:147
  108.4 1.6 %fusion = f32[4,8,96]{2,1,0:T(8,128)S(1)} fusion(f32[4,384,96,8]{1,2,3,0:T(8,128)S(1)} %get-tuple-element.51, f32[4,8,96]{2,1,0:T(8,128)S(1)} %get-tuple-element.50, pred[96,384]{1,0:T(8,128)(4,1)S(1)} %get-tuple-element.53), kind=kLoop, calls=%fused_computation.4 | loop fusion | flops 4715520 | bytes 4780032 | tf_op jit(solution)/shard_map/reduce_sum | solution.py:147
  111.0 9.0 %collective-permute-done.10 = bf16[2,96,512]{1,2,0:T(8,128)(2,1)S(1)} collective-permute-done((bf16[2,96,512]{1,2,0:T(8,128)(2,1)S(1)}, bf16[2,96,512]{1,2,0:T(8,128)(2,1)S(1)}, u32[]{:S(2)}, u32[]{:S(2)}) %collective-permute-start.10) | collective-permute-done | bytes 196640 | tf_op jit(solution)/shard_map/ppermute | solution.py:18
  121.2 8.1 %collective-permute-done.12 = bf16[2,96,512]{1,2,0:T(8,128)(2,1)S(1)} collective-permute-done((bf16[2,96,512]{1,2,0:T(8,128)(2,1)S(1)}, bf16[2,96,512]{1,2,0:T(8,128)(2,1)S(1)}, u32[]{:S(2)}, u32[]{:S(2)}) %collective-permute-start.12) | collective-permute-done | bytes 196640 | tf_op jit(solution)/shard_map/ppermute | solution.py:18
  129.3 2.8 %collective-permute-done.11 = bf16[2,96,512]{1,2,0:T(8,128)(2,1)S(1)} collective-permute-done((bf16[2,96,512]{1,2,0:T(8,128)(2,1)S(1)}, bf16[2,96,512]{1,2,0:T(8,128)(2,1)S(1)}, u32[]{:S(2)}, u32[]{:S(2)}) %collective-permute-start.11) | collective-permute-done | bytes 196640 | tf_op jit(solution)/shard_map/ppermute | solution.py:18
  132.7 3.7 %fusion.20 = bf16[96,4,8,128]{3,0,2,1:T(8,128)(2,1)S(1)} fusion(bf16[384,4,128,1]{0,2,3,1:T(8,128)(2,1)S(1)} %bitcast.104, f32[4,384,96,8]{1,2,3,0:T(8,128)} %copy-done.1, f32[4,8,96]{2,1,0:T(8,128)S(1)} %get-tuple-element.48, pred[96,384]{1,0:T(8,128)(4,1)S(1)} %get-tuple-element.52, f32[96,4,8]{0,2,1:T(8,128)S(1)} %bitcast.106), kind=kOutput, calls=%fused_computation.26 | convolution fusion | flops 307494912 | bytes 5959680 | tf_op jit(solution)/shard_map/kgtu,ukd->tkgd/dot_general | solution.py:158
  137.1 3.7 %fusion.21 = bf16[96,4,8,128]{3,0,2,1:T(8,128)(2,1)S(1)} fusion(bf16[384,4,128,1]{0,2,3,1:T(8,128)(2,1)S(1)} %bitcast.103, f32[4,384,96,8]{1,2,3,0:T(8,128)} %copy-done, f32[4,8,96]{2,1,0:T(8,128)S(1)} %get-tuple-element.50, pred[96,384]{1,0:T(8,128)(4,1)S(1)} %get-tuple-element.53, f32[96,4,8]{0,2,1:T(8,128)S(1)} %bitcast.105), kind=kOutput, calls=%fused_computation.28 | convolution fusion | flops 307494912 | bytes 5959680 | tf_op jit(solution)/shard_map/kgtu,ukd->tkgd/dot_general | solution.py:158
  141.5 1.3 maximum_bitcast_fusion
  (100 shorter events, 26.2 us)
Async XLA Ops:
  0.6 7.3 %copy-start.2 = (bf16[1,2,96,4096]{3,2,1,0:T(8,128)(2,1)S(1)}, bf16[1,2,96,4096]{3,2,1,0:T(8,128)(2,1)}, u32[]{:S(2)}) copy-start(bf16[1,2,96,4096]{3,2,1,0:T(8,128)(2,1)} %param.5) | copy-start | bytes 4718596
  0.6 12.0 %collective-permute-start = (bf16[1,4096]{1,0:T(2,128)(2,1)}, bf16[1,4096]{1,0:T(2,128)(2,1)S(1)}, u32[]{:S(2)}, u32[]{:S(2)}) collective-permute-start(bf16[1,4096]{1,0:T(2,128)(2,1)} %param.6), channel_id=1, source_target_pairs={{0,24},{8,0},{16,8},{24,16},{1,25},{9,1},{17,9},{25,17},{2,26},{10... | collective-permute-start | bytes 24584 | tf_op jit(solution)/shard_map/ppermute | solution.py:18
  3.1 5.4 %copy-start.5 = (s32[2,16]{1,0:T(2,128)S(1)}, s32[2,16]{1,0:T(2,128)}, u32[]{:S(2)}) copy-start(s32[2,16]{1,0:T(2,128)} %param.9) | copy-start | bytes 388
  5.4 43.7 %collective-permute-start.5 = (bf16[512,512]{1,0:T(8,128)(2,1)}, bf16[512,512]{1,0:T(8,128)(2,1)}, u32[]{:S(2)}, u32[]{:S(2)}) collective-permute-start(bf16[512,512]{1,0:T(8,128)(2,1)} %get-tuple-element.16), channel_id=1, source_target_pairs={{0,4},{1,5},{2,6},{3,7},{4,0},{5,1},{6,2},{7,3},{8,12},{9,13},{10,... | collective-permute-start | bytes 1572872 | tf_op jit(solution)/shard_map/ppermute | solution.py:18
  13.4 7.4 %copy-start.6 = (s32[1,2,48]{2,1,0:T(2,128)S(1)}, s32[1,2,48]{2,1,0:T(2,128)}, u32[]{:S(2)}) copy-start(s32[1,2,48]{2,1,0:T(2,128)} %get-tuple-element.30) | copy-start | bytes 1156
  13.4 8.9 %collective-permute-start.1 = (bf16[192,1024]{1,0:T(8,128)(2,1)S(1)}, bf16[192,1024]{1,0:T(8,128)(2,1)}, u32[]{:S(2)}, u32[]{:S(2)}) collective-permute-start(bf16[192,1024]{1,0:T(8,128)(2,1)S(1)} %pad_maximum_fusion.2), channel_id=1, source_target_pairs={{0,8},{1,9},{2,10},{3,11},{4,12},{5,13},{6,14},{7,15},{8,16},{9,17... | collective-permute-start | bytes 1179656 | tf_op jit(solution)/shard_map/ppermute | solution.py:69
  14.2 12.7 %collective-permute-start.2 = (bf16[192,1024]{1,0:T(8,128)(2,1)}, bf16[192,1024]{1,0:T(8,128)(2,1)}, u32[]{:S(2)}, u32[]{:S(2)}) collective-permute-start(bf16[192,1024]{1,0:T(8,128)(2,1)} %pad_maximum_fusion.3), channel_id=1, source_target_pairs={{0,9},{1,8},{2,11},{3,10},{4,13},{5,12},{6,15},{7,14},{8,17},{9,16... | collective-permute-start | bytes 1179656 | tf_op jit(solution)/shard_map/ppermute | solution.py:69
  16.1 6.0 %copy-start.3 = (bf16[12,8,32,128]{3,1,2,0:T(8,128)(2,1)S(1)}, bf16[12,8,32,128]{3,1,2,0:T(8,128)(2,1)}, u32[]{:S(2)}) copy-start(bf16[12,8,32,128]{3,1,2,0:T(8,128)(2,1)} %get-tuple-element.7) | copy-start | bytes 2359300
  16.9 22.7 %collective-permute-start.3 = (bf16[192,1024]{1,0:T(8,128)(2,1)}, bf16[192,1024]{1,0:T(8,128)(2,1)}, u32[]{:S(2)}, u32[]{:S(2)}) collective-permute-start(bf16[192,1024]{1,0:T(8,128)(2,1)} %pad_maximum_fusion.4), channel_id=1, source_target_pairs={{0,10},{1,11},{2,8},{3,9},{4,14},{5,15},{6,12},{7,13},{8,18},{9,19... | collective-permute-start | bytes 1179656 | tf_op jit(solution)/shard_map/ppermute | solution.py:69
  18.9 29.1 %collective-permute-start.4 = (bf16[192,1024]{1,0:T(8,128)(2,1)}, bf16[192,1024]{1,0:T(8,128)(2,1)}, u32[]{:S(2)}, u32[]{:S(2)}) collective-permute-start(bf16[192,1024]{1,0:T(8,128)(2,1)} %pad_maximum_fusion.5), channel_id=1, source_target_pairs={{0,11},{1,10},{2,9},{3,8},{4,15},{5,14},{6,13},{7,12},{8,19},{9,18... | collective-permute-start | bytes 1179656 | tf_op jit(solution)/shard_map/ppermute | solution.py:69
  49.1 1.7 %copy-start.4 = (bf16[1,512,1024]{2,1,0:T(8,128)(2,1)S(1)}, bf16[1,512,1024]{2,1,0:T(8,128)(2,1)}, u32[]{:S(2)}) copy-start(bf16[1,512,1024]{2,1,0:T(8,128)(2,1)} %param.7) | copy-start | bytes 3145732
  50.8 4.2 %copy-start.9 = (f32[64]{0:T(128)S(1)}, f32[64]{0:T(128)}, u32[]{:S(2)}) copy-start(f32[64]{0:T(128)} %multiply_power_fusion) | copy-start | bytes 772
  51.4 8.5 %collective-permute-start.13 = (bf16[192,512]{1,0:T(8,128)(2,1)S(1)}, bf16[192,512]{1,0:T(8,128)(2,1)S(1)}, u32[]{:S(2)}, u32[]{:S(2)}) collective-permute-start(bf16[192,512]{1,0:T(8,128)(2,1)S(1)} %get-tuple-element.22), channel_id=1, source_target_pairs={{0,1},{1,0},{2,3},{3,2},{4,5},{5,4},{6,7},{7,6},{8,9},{9,8},{10,11... | collective-permute-start | bytes 589832 | tf_op jit(solution)/shard_map/ppermute | solution.py:18
  53.0 12.9 %collective-permute-start.15 = (bf16[192,512]{1,0:T(8,128)(2,1)S(1)}, bf16[192,512]{1,0:T(8,128)(2,1)S(1)}, u32[]{:S(2)}, u32[]{:S(2)}) collective-permute-start(bf16[192,512]{1,0:T(8,128)(2,1)S(1)} %get-tuple-element.23), channel_id=1, source_target_pairs={{0,3},{1,2},{2,1},{3,0},{4,7},{5,6},{6,5},{7,4},{8,11},{9,10},{10,... | collective-permute-start | bytes 589832 | tf_op jit(solution)/shard_map/ppermute | solution.py:18
  53.0 15.1 %collective-permute-start.14 = (bf16[192,512]{1,0:T(8,128)(2,1)S(1)}, bf16[192,512]{1,0:T(8,128)(2,1)S(1)}, u32[]{:S(2)}, u32[]{:S(2)}) collective-permute-start(bf16[192,512]{1,0:T(8,128)(2,1)S(1)} %get-tuple-element.24), channel_id=1, source_target_pairs={{0,2},{1,3},{2,0},{3,1},{4,6},{5,7},{6,4},{7,5},{8,10},{9,11},{10,... | collective-permute-start | bytes 589832 | tf_op jit(solution)/shard_map/ppermute | solution.py:18
  56.1 31.0 %collective-permute-start.6 = (bf16[512,512]{1,0:T(8,128)(2,1)}, bf16[512,512]{1,0:T(8,128)(2,1)}, u32[]{:S(2)}, u32[]{:S(2)}) collective-permute-start(bf16[512,512]{1,0:T(8,128)(2,1)} %get-tuple-element.3), channel_id=1, source_target_pairs={{0,4},{1,5},{2,6},{3,7},{4,0},{5,1},{6,2},{7,3},{8,12},{9,13},{10,... | collective-permute-start | bytes 1572872 | tf_op jit(solution)/shard_map/ppermute | solution.py:18
  69.0 4.6 %copy-start.7 = (s32[96]{0:T(128)S(1)}, s32[96]{0:T(128)}, u32[]{:S(2)}) copy-start(s32[96]{0:T(128)} %le.41) | copy-start | bytes 1156
  69.0 4.6 %copy-start.8 = (s32[96]{0:T(128)S(1)}, s32[96]{0:T(128)}, u32[]{:S(2)}) copy-start(s32[96]{0:T(128)} %le.45) | copy-start | bytes 1156
  73.5 8.2 %collective-permute-start.16 = (bf16[2,96,512]{1,2,0:T(8,128)(2,1)S(1)}, bf16[2,96,512]{1,2,0:T(8,128)(2,1)S(1)}, u32[]{:S(2)}, u32[]{:S(2)}) collective-permute-start(bf16[2,96,512]{1,2,0:T(8,128)(2,1)S(1)} %bitcast.98), channel_id=1, source_target_pairs={{0,2},{1,3},{2,4},{3,5},{4,6},{5,7},{6,0},{7,1},{8,10},{9,11},{10,... | collective-permute-start | bytes 589832 | tf_op jit(solution)/shard_map/ppermute | solution.py:18
  81.7 12.9 %collective-permute-start.18 = (bf16[2,96,512]{1,2,0:T(8,128)(2,1)S(1)}, bf16[2,96,512]{1,2,0:T(8,128)(2,1)S(1)}, u32[]{:S(2)}, u32[]{:S(2)}) collective-permute-start(bf16[2,96,512]{1,2,0:T(8,128)(2,1)S(1)} %broadcast_select_fusion), channel_id=1, source_target_pairs={{0,1},{1,2},{2,3},{3,4},{4,5},{5,6},{6,7},{7,0},{8,9},{9,10},{10,1... | collective-permute-start | bytes 589832 | tf_op jit(solution)/shard_map/ppermute | solution.py:18
  82.3 21.1 %collective-permute-start.17 = (bf16[2,96,512]{1,2,0:T(8,128)(2,1)S(1)}, bf16[2,96,512]{1,2,0:T(8,128)(2,1)S(1)}, u32[]{:S(2)}, u32[]{:S(2)}) collective-permute-start(bf16[2,96,512]{1,2,0:T(8,128)(2,1)S(1)} %collective-permute-done.16), channel_id=1, source_target_pairs={{0,1},{1,0},{2,3},{3,2},{4,5},{5,4},{6,7},{7,6},{8,9},{9,8},{10,11... | collective-permute-start | bytes 589832 | tf_op jit(solution)/shard_map/ppermute | solution.py:18
  90.4 20.2 %collective-permute-start.7 = (bf16[192,512]{1,0:T(8,128)(2,1)S(1)}, bf16[192,512]{1,0:T(8,128)(2,1)S(1)}, u32[]{:S(2)}, u32[]{:S(2)}) collective-permute-start(bf16[192,512]{1,0:T(8,128)(2,1)S(1)} %get-tuple-element.25), channel_id=1, source_target_pairs={{0,1},{1,0},{2,3},{3,2},{4,5},{5,4},{6,7},{7,6},{8,9},{9,8},{10,11... | collective-permute-start | bytes 589832 | tf_op jit(solution)/shard_map/ppermute | solution.py:18
  90.9 19.7 %collective-permute-start.9 = (bf16[192,512]{1,0:T(8,128)(2,1)S(1)}, bf16[192,512]{1,0:T(8,128)(2,1)S(1)}, u32[]{:S(2)}, u32[]{:S(2)}) collective-permute-start(bf16[192,512]{1,0:T(8,128)(2,1)S(1)} %get-tuple-element.26), channel_id=1, source_target_pairs={{0,3},{1,2},{2,1},{3,0},{4,7},{5,6},{6,5},{7,4},{8,11},{9,10},{10,... | collective-permute-start | bytes 589832 | tf_op jit(solution)/shard_map/ppermute | solution.py:18
  94.4 16.2 %collective-permute-start.8 = (bf16[192,512]{1,0:T(8,128)(2,1)S(1)}, bf16[192,512]{1,0:T(8,128)(2,1)S(1)}, u32[]{:S(2)}, u32[]{:S(2)}) collective-permute-start(bf16[192,512]{1,0:T(8,128)(2,1)S(1)} %get-tuple-element.27), channel_id=1, source_target_pairs={{0,2},{1,3},{2,0},{3,1},{4,6},{5,7},{6,4},{7,5},{8,10},{9,11},{10,... | collective-permute-start | bytes 589832 | tf_op jit(solution)/shard_map/ppermute | solution.py:18
  105.1 2.1 %copy-start.1 = (f32[4,384,96,8]{1,2,3,0:T(8,128)}, f32[4,384,96,8]{1,2,3,0:T(8,128)S(1)}, u32[]{:S(2)}) copy-start(f32[4,384,96,8]{1,2,3,0:T(8,128)S(1)} %get-tuple-element.49) | copy-start | bytes 14155780
  108.4 2.2 %copy-start = (f32[4,384,96,8]{1,2,3,0:T(8,128)}, f32[4,384,96,8]{1,2,3,0:T(8,128)S(1)}, u32[]{:S(2)}) copy-start(f32[4,384,96,8]{1,2,3,0:T(8,128)S(1)} %get-tuple-element.51) | copy-start | bytes 14155780
  110.9 9.0 %collective-permute-start.10 = (bf16[2,96,512]{1,2,0:T(8,128)(2,1)S(1)}, bf16[2,96,512]{1,2,0:T(8,128)(2,1)S(1)}, u32[]{:S(2)}, u32[]{:S(2)}) collective-permute-start(bf16[2,96,512]{1,2,0:T(8,128)(2,1)S(1)} %copy.9), channel_id=1, source_target_pairs={{0,2},{1,3},{2,4},{3,5},{4,6},{5,7},{6,0},{7,1},{8,10},{9,11},{10,... | collective-permute-start | bytes 589832 | tf_op jit(solution)/shard_map/ppermute | solution.py:18
  120.0 9.4 %collective-permute-start.12 = (bf16[2,96,512]{1,2,0:T(8,128)(2,1)S(1)}, bf16[2,96,512]{1,2,0:T(8,128)(2,1)S(1)}, u32[]{:S(2)}, u32[]{:S(2)}) collective-permute-start(bf16[2,96,512]{1,2,0:T(8,128)(2,1)S(1)} %broadcast_select_fusion.1), channel_id=1, source_target_pairs={{0,1},{1,2},{2,3},{3,4},{4,5},{5,6},{6,7},{7,0},{8,9},{9,10},{10,1... | collective-permute-start | bytes 589832 | tf_op jit(solution)/shard_map/ppermute | solution.py:18
  120.5 11.6 %collective-permute-start.11 = (bf16[2,96,512]{1,2,0:T(8,128)(2,1)S(1)}, bf16[2,96,512]{1,2,0:T(8,128)(2,1)S(1)}, u32[]{:S(2)}, u32[]{:S(2)}) collective-permute-start(bf16[2,96,512]{1,2,0:T(8,128)(2,1)S(1)} %collective-permute-done.10), channel_id=1, source_target_pairs={{0,1},{1,0},{2,3},{3,2},{4,5},{5,4},{6,7},{7,6},{8,9},{9,8},{10,11... | collective-permute-start | bytes 589832 | tf_op jit(solution)/shard_map/ppermute | solution.py:18

commit v2 on v1

v2 whole, which is shorter than its diff:
```python
import jax
import jax.numpy as jnp
from jax import lax
from jax.experimental import pallas as pl
from jax.experimental.pallas import tpu as pltpu
from jax.sharding import PartitionSpec as P

QH = 32
KVH = 4
HD = 128
WINDOW = 4
QUAD = 4
GROUP = QH // KVH
LANES = 128
ROW_STEP = 16


rope_base = 500000.0


def moved(block, axis, target):
    size = lax.axis_size(axis)
    return lax.ppermute(block, axis, [(i, target(i) % size) for i in range(size)])


def params(mib):
    return pltpu.CompilerParams(vmem_limit_bytes=mib * 1024 * 1024)


def cost(flops, bytes_accessed):
    return pl.CostEstimate(flops=flops, bytes_accessed=bytes_accessed, transcendentals=0)


def norm_kernel(starts_ref, x_ref, gain_ref, *outs):
    rows, width = x_ref.shape[1], x_ref.shape[2]
    pieces = starts_ref.shape[1]
    piece_width = outs[0].shape[1] // pieces
    for r in range(0, rows, ROW_STEP):
        x = x_ref[0, r : r + ROW_STEP, :].astype(jnp.float32)
        scale = lax.rsqrt(jnp.sum(x * x, axis=-1, keepdims=True) / width + 1e-05)
        for flip, out in enumerate(outs):
            for j in range(pieces):
                start = pl.multiple_of(starts_ref[flip, j], LANES)
                xs = x_ref[0, r : r + ROW_STEP, pl.ds(start, piece_width)].astype(jnp.float32)
                gain = gain_ref[:, pl.ds(start, piece_width)]
                out[r : r + ROW_STEP, j * piece_width : (j + 1) * piece_width] = (
                    xs * scale * gain
                ).astype(jnp.bfloat16)


def normed_cuts(activations, gain, starts):
    micro_count, tok_rows, width = activations.shape
    rows = micro_count * tok_rows
    part = width // QUAD
    return pl.pallas_call(
        norm_kernel,
        grid=(micro_count,),
        in_specs=[
            pl.BlockSpec(memory_space=pltpu.SMEM),
            pl.BlockSpec((1, tok_rows, width), lambda m: (m, 0, 0)),
            pl.BlockSpec((1, width), lambda m: (0, 0)),
        ],
        out_specs=[pl.BlockSpec((tok_rows, part), lambda m: (m, 0))] * QUAD,
        out_shape=[jax.ShapeDtypeStruct((rows, part), jnp.bfloat16)] * QUAD,
        compiler_params=params(16),
        cost_estimate=cost(6 * rows * width, 4 * rows * width),
        name="norm_cuts",
    )(starts, activations, gain)


def product_kernel(quads, *refs):
    xs, shards, outs = refs[:QUAD], refs[QUAD : QUAD + quads], refs[QUAD + quads :]
    shard_rows = shards[0].shape[0]
    for x, out in zip(xs, outs):
        total = jnp.dot(x[:, :shard_rows], shards[0][...], preferred_element_type=jnp.float32)
        for j in range(1, quads):
            total = total + jnp.dot(
                x[:, j * shard_rows : (j + 1) * shard_rows],
                shards[j][...],
                preferred_element_type=jnp.float32,
            )
        out[...] = total.astype(out.dtype)


def partial_products(xs, shards):
    rows, part = xs[0].shape
    width = shards[0].shape[1]
    return pl.pallas_call(
        lambda *refs: product_kernel(len(shards), *refs),
        out_shape=[jax.ShapeDtypeStruct((rows, width), jnp.float32)]
        + [jax.ShapeDtypeStruct((rows, width), jnp.bfloat16)] * (QUAD - 1),
        compiler_params=params(24),
        cost_estimate=cost(2 * QUAD * rows * part * width, 2 * QUAD * rows * part + 2 * part * width),
        name="partial_products",
    )(*xs, *shards)


def added(own, one, two, three):
    return own + one.astype(jnp.float32) + two.astype(jnp.float32) + three.astype(jnp.float32)


def key_sum_kernel(own, one, two, three, cosine, sine_part, out):
    for h in range(out.shape[1] // HD):
        cols = slice(h * HD, (h + 1) * HD)
        total = added(own[:, cols], one[:, cols], two[:, cols], three[:, cols])
        turned = pltpu.roll(total, HD // 2, 1)
        out[:, cols] = (total * cosine[...] + turned * sine_part[...]).astype(jnp.bfloat16)


def value_sum_kernel(own, one, two, three, out):
    out[...] = added(own[...], one[...], two[...], three[...]).astype(jnp.bfloat16)


def block_sum(kernel, name, own, parts, *tables):
    return pl.pallas_call(
        kernel,
        out_shape=jax.ShapeDtypeStruct(own.shape, jnp.bfloat16),
        compiler_params=params(16),
        cost_estimate=cost(10 * own.size, 12 * own.size),
        name=name,
    )(own, *parts, *tables)


def stacked(refs, odd):
    own, two_back, three_back, beside, from_even = refs
    one_back = jnp.where(odd == 1, beside[...], from_even[...])
    return jnp.concatenate([own[...], one_back, two_back[...], three_back[...]], axis=0)


def score_kernel(odd_ref, q_ref, *refs):
    key_refs, (row_pos, col_pos, weights, sums, log_sums) = refs[:5], refs[5:]
    keys = stacked(key_refs, odd_ref[0])
    tok_rows = q_ref.shape[2]
    visible = col_pos[0] <= row_pos[0]
    lane = lax.broadcasted_iota(jnp.int32, (tok_rows, LANES), 1)
    all_sums = jnp.ones((tok_rows, LANES), jnp.float32)
    all_max = jnp.zeros((tok_rows, LANES), jnp.float32)
    for h in range(GROUP):
        scores = lax.dot_general(
            q_ref[0, 0, :, h * HD : (h + 1) * HD],
            keys,
            (((1,), (1,)), ((), ())),
            preferred_element_type=jnp.float32,
        ) * HD ** (-0.5)
        scores = jnp.where(visible, scores, -jnp.inf)
        row_max = jnp.max(scores, axis=-1, keepdims=True)
        exps = jnp.exp(scores - row_max)
        running = jnp.sum(exps, axis=-1, keepdims=True)
        weights[0, 0, h * tok_rows : (h + 1) * tok_rows, :] = exps.astype(jnp.bfloat16)
        all_sums = jnp.where(lane == h, running, all_sums)
        all_max = jnp.where(lane == h, row_max, all_max)
    sums[0, 0] = all_sums
    log_sums[0] = jnp.transpose(all_max + jnp.log(all_sums))[:GROUP]


def window_specs(tok_rows):
    return [pl.BlockSpec((tok_rows, HD), lambda m, k: (m, k))] * 5


def scored(odd, queries, window, row_pos, col_pos):
    _, micro_count, tok_rows, width = queries.shape
    keys = WINDOW * tok_rows
    return pl.pallas_call(
        score_kernel,
        grid=(micro_count, KVH),
        in_specs=[
            pl.BlockSpec(memory_space=pltpu.SMEM),
            pl.BlockSpec((1, 1, tok_rows, GROUP * HD), lambda m, k: (0, m, 0, k)),
            *window_specs(tok_rows),
            pl.BlockSpec((1, tok_rows, 1), lambda m, k: (m, 0, 0)),
            pl.BlockSpec((1, 1, keys), lambda m, k: (m, 0, 0)),
        ],
        out_specs=[
            pl.BlockSpec((1, 1, GROUP * tok_rows, keys), lambda m, k: (m, k, 0, 0)),
            pl.BlockSpec((1, 1, tok_rows, LANES), lambda m, k: (m, k, 0, 0)),
            pl.BlockSpec((1, GROUP, tok_rows), lambda m, k: (m, k, 0)),
        ],
        out_shape=[
            jax.ShapeDtypeStruct((micro_count, KVH, GROUP * tok_rows, keys), jnp.bfloat16),
            jax.ShapeDtypeStruct((micro_count, KVH, tok_rows, LANES), jnp.float32),
            jax.ShapeDtypeStruct((micro_count, QH, tok_rows), jnp.float32),
        ],
        compiler_params=params(24),
        cost_estimate=cost(2 * micro_count * QH * tok_rows * keys * HD, 8 * 2**20),
        name="scores",
    )(odd, queries, *window, row_pos, col_pos)


def mix_kernel(odd_ref, weights, sums, *refs):
    values = stacked(refs[:5], odd_ref[0])
    out = refs[5]
    tok_rows = out.shape[2]
    mixed = jnp.dot(weights[0, 0], values, preferred_element_type=jnp.float32)
    share = 1.0 / sums[0, 0]
    for h in range(GROUP):
        out[0, 0, :, h * HD : (h + 1) * HD] = (
            mixed[h * tok_rows : (h + 1) * tok_rows] * share[:, h : h + 1]
        ).astype(jnp.bfloat16)


def mixed_values(odd, weights, sums, window):
    micro_count, _, group_rows, keys = weights.shape
    tok_rows = group_rows // GROUP
    return pl.pallas_call(
        mix_kernel,
        grid=(micro_count, KVH),
        in_specs=[
            pl.BlockSpec(memory_space=pltpu.SMEM),
            pl.BlockSpec((1, 1, group_rows, keys), lambda m, k: (m, k, 0, 0)),
            pl.BlockSpec((1, 1, tok_rows, LANES), lambda m, k: (m, k, 0, 0)),
            *window_specs(tok_rows),
        ],
        out_specs=pl.BlockSpec((1, 1, tok_rows, GROUP * HD), lambda m, k: (0, m, 0, k)),
        out_shape=jax.ShapeDtypeStruct((1, micro_count, tok_rows, QH * HD), jnp.bfloat16),
        compiler_params=params(24),
        cost_estimate=cost(2 * micro_count * QH * tok_rows * keys * HD, 8 * 2**20),
        name="mixed_values",
    )(odd, weights, sums, *window)


def on_device(handoff, norm_gain, kv_weight, queries, span_order):
    sections = lax.axis_size("section")
    cycle_size = lax.axis_size("ctx")
    own_index = lax.axis_index("ctx")
    quads = cycle_size // QUAD
    own_quad, own_place = own_index // QUAD, own_index % QUAD
    weight = kv_weight[0]
    shard_rows, kv_width = weight.shape[0], weight.shape[1] // 2
    _, micro_count, tok_rows, _ = handoff.shape

    def same_place_shards(part):
        return [part] + [
            moved(part, "ctx", lambda i, j=j: i + QUAD * j) for j in range(1, quads)
        ]

    key_shards = same_place_shards(weight[:, :kv_width])
    value_part, _ = lax.optimization_barrier((weight[:, kv_width:], key_shards[-1]))
    value_shards = same_place_shards(value_part)

    next_gain = moved(norm_gain, "section", lambda i: i - 1).astype(jnp.float32)
    starts = jnp.stack(
        [
            jnp.stack(
                [
                    ((own_quad - j) % quads * QUAD + (own_place ^ flip)) * shard_rows
                    for j in range(quads)
                ]
            )
            for flip in range(QUAD)
        ]
    ).astype(jnp.int32)
    cuts = normed_cuts(handoff[0], next_gain, starts)

    def to_next_section(part, flip):
        route = [
            (s * cycle_size + i, (s + 1) % sections * cycle_size + (i ^ flip))
            for s in range(sections)
            for i in range(cycle_size)
        ]
        return lax.ppermute(part, ("section", "ctx"), route)

    arrived = [to_next_section(cuts[flip], flip) for flip in range(QUAD)]

    def swapped(parts):
        return [
            moved(part, "ctx", lambda i, flip=flip: i ^ flip)
            for flip, part in enumerate(parts, start=1)
        ]

    def window_of(block):
        two_back = moved(block, "ctx", lambda i: i + 2)
        beside = moved(block, "ctx", lambda i: i ^ 1)
        three_back = moved(two_back, "ctx", lambda i: i + 1)
        from_even = lax.ppermute(
            beside, "ctx", [(i, (i + 2) % cycle_size) for i in range(0, cycle_size, 2)]
        )
        return [block, two_back, three_back, beside, from_even]

    span_len = tok_rows // 2

    def device_positions(device):
        span_ids = lax.dynamic_slice_in_dim(span_order, 2 * device, 2, 1)
        spread = (
            span_ids[:, :, None] * span_len + jnp.arange(span_len, dtype=jnp.int32)[None, None, :]
        )
        return spread.reshape(micro_count, tok_rows)

    own_pos = device_positions(own_index)
    col_pos = jnp.concatenate(
        [device_positions((own_index - d) % cycle_size) for d in range(WINDOW)], axis=1
    )[:, None, :]
    half_dim = HD // 2
    frequency = rope_base ** (-2.0 * jnp.arange(half_dim, dtype=jnp.float32) / HD)
    angles = own_pos.reshape(-1, 1).astype(jnp.float32) * frequency
    cosine, sine_part = jnp.cos(angles), jnp.sin(angles)
    cosine = jnp.concatenate([cosine, cosine], axis=1)
    sine_part = jnp.concatenate([-sine_part, sine_part], axis=1)
    odd = (own_index % 2).astype(jnp.int32).reshape(1)

    own_keys, *key_parts = partial_products(arrived, key_shards)
    key_parts, value_shards = lax.optimization_barrier((swapped(key_parts), value_shards))
    key_block = block_sum(key_sum_kernel, "key_sum", own_keys, key_parts, cosine, sine_part)
    key_window = window_of(key_block)
    weights, sums, log_sums = scored(odd, queries, key_window, own_pos[:, :, None], col_pos)

    own_values, *value_parts = partial_products(arrived, value_shards)
    value_block = block_sum(value_sum_kernel, "value_sum", own_values, swapped(value_parts))
    out = mixed_values(odd, weights, sums, window_of(value_block))
    return (out, log_sums[None])


def solution(mesh):
    placed = (
        P("section", None, "ctx", None),
        P("section", None),
        P("section", "ctx", None),
        P("section", None, "ctx", None),
        P(),
    )
    return jax.shard_map(
        on_device,
        mesh=mesh,
        in_specs=placed,
        out_specs=(P("section", None, "ctx", None), P("section", None, None, "ctx")),
        check_vma=False,
    )
```

time: 145 us -> 111 us (0.77); the launches traced: 143 us -> 110 us
  waiting for transfers between devices: 70.7 us -> 50.7 us
  Pallas kernels: 0 us -> 18.8 us
  matrix products: 15.2 us -> 0 us
  other arithmetic: 14.6 us -> 1.04 us
  local copies, waits for them, and re-layouts: 17.1 us -> 11 us
  starting transfers between devices: 24 us -> 28 us
    pallas_call x0 -> x7, Pallas kernels: none -> 18.8 us  [the longest x1 6.5 us: scored(): pl.pallas_call(score_kernel, grid=(micro_count, KVH), in_specs=[pl.BlockS...]
    ppermute x15, waiting for transfers between devices: 48 us -> 32.8 us  [moved(): lax.ppermute(block, axis, [(i, target(i) % size) for i in range(size)])]
    dot_general x8 -> x0, matrix products: 15.2 us -> none  [the longest x2 7.4 us: on_device(): jnp.einsum('kgtu,ukd->tkgd', weights[micro_idx], value_rows, preferred_el...]
    ppermute x0 -> x2, starting transfers between devices: none -> 8.98 us  [window_of(): lax.ppermute(beside, 'ctx', [(i, (i + 2) % cycle_size) for i in range(0,...]
    ppermute x4, waiting for transfers between devices: 22.7 us -> 15.1 us  [to_next_section(): return lax.ppermute(part, ('section', 'ctx'), route)]
    ppermute x15, starting transfers between devices: 19.6 us -> 14.6 us  [moved(): lax.ppermute(block, axis, [(i, target(i) % size) for i in range(size)])]
    concatenate x7 -> x1, other arithmetic: 4.33 us -> 0.12 us  [on_device(): cosine = jnp.concatenate([cosine, cosine], axis=1)]
    reduce_sum x3 -> x0, other arithmetic: 3.52 us -> none  [the longest x2 3.12 us: on_device(): running = jnp.sum(exps, axis=-1, keepdims=True)]
  transfers between devices with their start and end apart: 19 -> 21, of which waited for: 12 -> 10; matrix products, arithmetic and copies ran while one was open for 23% -> 3% of each run, Pallas kernels for 0% -> 11%
where the time goes in v2:
time: 111 us; the launch traced here: 110 us
  waiting for transfers between devices  50.7 us (46%)
  starting transfers between devices  28 us (25%)
  Pallas kernels  18.8 us (17%)
  local copies, waits for them, and re-layouts  11 us (10%)
    ppermute x15, waiting for transfers between devices, moved(): lax.ppermute(block, axis, [(i, target(i) % size) for i in range(size)])  32.8 us
    ppermute x4, waiting for transfers between devices, to_next_section(): return lax.ppermute(part, ('section', 'ctx'), route)  15.1 us
    ppermute x15, starting transfers between devices, moved(): lax.ppermute(block, axis, [(i, target(i) % size) for i in range(size)])  14.6 us
    ppermute x2, starting transfers between devices, window_of(): lax.ppermute(beside, 'ctx', [(i, (i + 2) % cycle_size) for i in range(0,...  8.98 us
    unnamed x28, local copies, waits for them, and re-layouts  8.69 us
    pallas_call x1, Pallas kernels, scored(): pl.pallas_call(score_kernel, grid=(micro_count, KVH), in_specs=[pl.BlockS...  6.5 us
    pallas_call x2, Pallas kernels, partial_products(): pl.pallas_call(lambda *refs: product_kernel(len(shards), *refs), out_shap...  5.31 us
    pallas_call x1, Pallas kernels, mixed_values(): pl.pallas_call(mix_kernel, grid=(micro_count, KVH), in_specs=[pl.BlockSpe...  4.59 us
  transfers between devices with their start and end apart: 21, of which 10 were waited for; matrix products, arithmetic and copies ran while one was open for 3% of the time, Pallas kernels for 11%

profile of v2, /device:TPU:0, one launch (start us, length us, event | category | flops | bytes accessed | tf_op | source)
XLA Modules:
  0.0 110.3 jit_solution(9953939300025076878)
XLA Ops:
  0.6 2.4 %collective-permute-start = (bf16[1,4096]{1,0:T(2,128)(2,1)}, bf16[1,4096]{1,0:T(2,128)(2,1)S(1)}, u32[]{:S(2)}, u32[]{:S(2)}) collective-permute-start(bf16[1,4096]{1,0:T(2,128)(2,1)} %param.6), channel_id=1, source_target_pairs={{0,24},{8,0},{16,8},{24,16},{1,25},{9,1},{17,9},{25,17},{2,26},{10... | collective-permute-start | bytes 24584 | tf_op jit(solution)/shard_map/ppermute | solution.py:23
  3.1 1.3 %fusion.6 = (bf16[512,512]{1,0:T(8,128)(2,1)S(1)}, bf16[512,512]{1,0:T(8,128)(2,1)S(1)}) fusion(bf16[512,1024]{1,0:T(8,128)(2,1)} %bitcast.21), kind=kLoop, calls=%fused_computation.28 | loop fusion | bytes 2097152 | tf_op jit(solution)/shard_map/slice | solution.py:237
  4.4 2.7 %collective-permute-start.5 = (bf16[512,512]{1,0:T(8,128)(2,1)S(1)}, bf16[512,512]{1,0:T(8,128)(2,1)S(1)}, u32[]{:S(2)}, u32[]{:S(2)}) collective-permute-start(bf16[512,512]{1,0:T(8,128)(2,1)S(1)} %get-tuple-element.45.refs_4_), channel_id=1, source_target_pairs={{0,4},{1,5},{2,6},{3,7},{4,0},{5,1},{6,2},{7,3},{8,12},{9,13},{10,... | collective-permute-start | bytes 1572872 | tf_op jit(solution)/shard_map/ppermute | solution.py:23
  7.2 2.2 %norm_cuts.1 = (bf16[192,1024]{1,0:T(8,128)(2,1)}, bf16[192,1024]{1,0:T(8,128)(2,1)}, bf16[192,1024]{1,0:T(8,128)(2,1)}, bf16[192,1024]{1,0:T(8,128)(2,1)}) custom-call(s32[4,2]{1,0:T(4,128)S(1)} %pad_add_fusion.1.starts_ref, bf16[2,96,4096]{2,1,0:T(8,128)(2,1)S(1)} %bitcast.20, f32[1,4096]{1,0:T(1,128)S(1)} %convert_element_type.14.gain_ref), custom_call_target="tpu_custom_call" | custom-call | flops 4718592 | bytes 3145728 | tf_op jit(solution)/shard_map/norm_cuts/pallas_call | solution.py:55
  9.4 1.9 %collective-permute-start.2 = (bf16[192,1024]{1,0:T(8,128)(2,1)}, bf16[192,1024]{1,0:T(8,128)(2,1)S(1)}, u32[]{:S(2)}, u32[]{:S(2)}) collective-permute-start(bf16[192,1024]{1,0:T(8,128)(2,1)} %get-tuple-element.24), channel_id=1, source_target_pairs={{0,9},{1,8},{2,11},{3,10},{4,13},{5,12},{6,15},{7,14},{8,17},{9,16... | collective-permute-start | bytes 1179656 | tf_op jit(solution)/shard_map/ppermute | solution.py:260
  11.3 1.2 %collective-permute-start.3 = (bf16[192,1024]{1,0:T(8,128)(2,1)}, bf16[192,1024]{1,0:T(8,128)(2,1)S(1)}, u32[]{:S(2)}, u32[]{:S(2)}) collective-permute-start(bf16[192,1024]{1,0:T(8,128)(2,1)} %get-tuple-element.25), channel_id=1, source_target_pairs={{0,10},{1,11},{2,8},{3,9},{4,14},{5,15},{6,12},{7,13},{8,18},{9,19... | collective-permute-start | bytes 1179656 | tf_op jit(solution)/shard_map/ppermute | solution.py:260
  12.5 1.3 %collective-permute-start.4 = (bf16[192,1024]{1,0:T(8,128)(2,1)}, bf16[192,1024]{1,0:T(8,128)(2,1)}, u32[]{:S(2)}, u32[]{:S(2)}) collective-permute-start(bf16[192,1024]{1,0:T(8,128)(2,1)} %get-tuple-element.26), channel_id=1, source_target_pairs={{0,11},{1,10},{2,9},{3,8},{4,15},{5,14},{6,13},{7,12},{8,19},{9,18... | collective-permute-start | bytes 1179656 | tf_op jit(solution)/shard_map/ppermute | solution.py:260
  13.8 16.2 %collective-permute-done.5.refs_5_ = bf16[512,512]{1,0:T(8,128)(2,1)S(1)} collective-permute-done((bf16[512,512]{1,0:T(8,128)(2,1)S(1)}, bf16[512,512]{1,0:T(8,128)(2,1)S(1)}, u32[]{:S(2)}, u32[]{:S(2)}) %collective-permute-start.5) | collective-permute-done | bytes 524320 | tf_op jit(solution)/shard_map/ppermute | solution.py:23
  30.1 3.8 %collective-permute-done.3.refs_2_ = bf16[192,1024]{1,0:T(8,128)(2,1)S(1)} collective-permute-done((bf16[192,1024]{1,0:T(8,128)(2,1)}, bf16[192,1024]{1,0:T(8,128)(2,1)S(1)}, u32[]{:S(2)}, u32[]{:S(2)}) %collective-permute-start.3) | collective-permute-done | bytes 393248 | tf_op jit(solution)/shard_map/ppermute | solution.py:260
  34.7 11.3 %collective-permute-done.4.refs_3_ = bf16[192,1024]{1,0:T(8,128)(2,1)} collective-permute-done((bf16[192,1024]{1,0:T(8,128)(2,1)}, bf16[192,1024]{1,0:T(8,128)(2,1)}, u32[]{:S(2)}, u32[]{:S(2)}) %collective-permute-start.4) | collective-permute-done | bytes 393248 | tf_op jit(solution)/shard_map/ppermute | solution.py:260
  46.0 1.0 copy-done.11
  47.0 2.7 %partial_products.2 = (f32[192,512]{1,0:T(8,128)S(1)}, bf16[192,512]{1,0:T(8,128)(2,1)}, bf16[192,512]{1,0:T(8,128)(2,1)}, bf16[192,512]{1,0:T(8,128)(2,1)}) custom-call(bf16[192,1024]{1,0:T(8,128)(2,1)S(1)} %collective-permute-done.1.refs_0_, bf16[192,1024]{1,0:T(8,128)(2,1)S(1)} %collective-permute-done.2.refs_1_, bf16[192,1024]{1,0:T(8,128)(2,1)S(1)} %copy-done.11, ...), custom_call_target="tpu_custom_call" | custom-call | flops 805306368 | bytes 2621440 | tf_op jit(solution)/shard_map/partial_products/pallas_call | solution.py:88
  49.6 1.5 %collective-permute-start.6 = (bf16[192,512]{1,0:T(8,128)(2,1)}, bf16[192,512]{1,0:T(8,128)(2,1)S(1)}, u32[]{:S(2)}, u32[]{:S(2)}) collective-permute-start(bf16[192,512]{1,0:T(8,128)(2,1)} %get-tuple-element.28), channel_id=1, source_target_pairs={{0,1},{1,0},{2,3},{3,2},{4,5},{5,4},{6,7},{7,6},{8,9},{9,8},{10,11... | collective-permute-start | bytes 589832 | tf_op jit(solution)/shard_map/ppermute | solution.py:23
  51.1 2.0 %collective-permute-start.8 = (bf16[192,512]{1,0:T(8,128)(2,1)}, bf16[192,512]{1,0:T(8,128)(2,1)S(1)}, u32[]{:S(2)}, u32[]{:S(2)}) collective-permute-start(bf16[192,512]{1,0:T(8,128)(2,1)} %get-tuple-element.30), channel_id=1, source_target_pairs={{0,3},{1,2},{2,1},{3,0},{4,7},{5,6},{6,5},{7,4},{8,11},{9,10},{10,... | collective-permute-start | bytes 589832 | tf_op jit(solution)/shard_map/ppermute | solution.py:23
  53.3 2.9 %collective-permute-done.6.one = bf16[192,512]{1,0:T(8,128)(2,1)S(1)} collective-permute-done((bf16[192,512]{1,0:T(8,128)(2,1)}, bf16[192,512]{1,0:T(8,128)(2,1)S(1)}, u32[]{:S(2)}, u32[]{:S(2)}) %collective-permute-start.6) | collective-permute-done | bytes 196640 | tf_op jit(solution)/shard_map/ppermute | solution.py:23
  56.8 2.3 %collective-permute-done.7.two = bf16[192,512]{1,0:T(8,128)(2,1)S(1)} collective-permute-done((bf16[192,512]{1,0:T(8,128)(2,1)}, bf16[192,512]{1,0:T(8,128)(2,1)S(1)}, u32[]{:S(2)}, u32[]{:S(2)}) %collective-permute-start.7) | collective-permute-done | bytes 196640 | tf_op jit(solution)/shard_map/ppermute | solution.py:23
  59.9 4.5 %collective-permute-done.8.three = bf16[192,512]{1,0:T(8,128)(2,1)S(1)} collective-permute-done((bf16[192,512]{1,0:T(8,128)(2,1)}, bf16[192,512]{1,0:T(8,128)(2,1)S(1)}, u32[]{:S(2)}, u32[]{:S(2)}) %collective-permute-start.8) | collective-permute-done | bytes 196640 | tf_op jit(solution)/shard_map/ppermute | solution.py:23
  64.4 1.1 copy-done.12
  65.4 2.7 %partial_products.3 = (f32[192,512]{1,0:T(8,128)S(1)}, bf16[192,512]{1,0:T(8,128)(2,1)}, bf16[192,512]{1,0:T(8,128)(2,1)}, bf16[192,512]{1,0:T(8,128)(2,1)}) custom-call(bf16[192,1024]{1,0:T(8,128)(2,1)S(1)} %collective-permute-done.1.refs_0_, bf16[192,1024]{1,0:T(8,128)(2,1)S(1)} %collective-permute-done.2.refs_1_, bf16[192,1024]{1,0:T(8,128)(2,1)S(1)} %copy-done.12, ...), custom_call_target="tpu_custom_call" | custom-call | flops 805306368 | bytes 2621440 | tf_op jit(solution)/shard_map/partial_products/pallas_call | solution.py:88
  68.5 3.1 %collective-permute-start.16 = (bf16[192,512]{1,0:T(8,128)(2,1)}, bf16[192,512]{1,0:T(8,128)(2,1)S(1)}, u32[]{:S(2)}, u32[]{:S(2)}) collective-permute-start(bf16[192,512]{1,0:T(8,128)(2,1)} %get-tuple-element.42), channel_id=1, source_target_pairs={{0,3},{1,2},{2,1},{3,0},{4,7},{5,6},{6,5},{7,4},{8,11},{9,10},{10,... | collective-permute-start | bytes 589832 | tf_op jit(solution)/shard_map/ppermute | solution.py:23
  72.9 1.0 copy-done.5
  73.9 0.9 copy-done.7
  74.8 0.9 copy-done.9
  76.6 4.0 %collective-permute-done.16.three = bf16[192,512]{1,0:T(8,128)(2,1)S(1)} collective-permute-done((bf16[192,512]{1,0:T(8,128)(2,1)}, bf16[192,512]{1,0:T(8,128)(2,1)S(1)}, u32[]{:S(2)}, u32[]{:S(2)}) %collective-permute-start.16) | collective-permute-done | bytes 196640 | tf_op jit(solution)/shard_map/ppermute | solution.py:23
  81.3 0.9 copy-done.3
  82.8 1.1 %collective-permute-start.17 = (bf16[192,512]{1,0:T(8,128)(2,1)S(1)}, bf16[192,512]{1,0:T(8,128)(2,1)S(1)}, u32[]{:S(2)}, u32[]{:S(2)}) collective-permute-start(bf16[192,512]{1,0:T(8,128)(2,1)S(1)} %value_sum.1.refs_0_), channel_id=1, source_target_pairs={{0,2},{1,3},{2,4},{3,5},{4,6},{5,7},{6,0},{7,1},{8,10},{9,11},{10,... | collective-permute-start | bytes 589832 | tf_op jit(solution)/shard_map/ppermute | solution.py:23
  84.8 5.0 %collective-permute-start.13 = (bf16[192,512]{1,0:T(8,128)(2,1)S(1)}, bf16[192,512]{1,0:T(8,128)(2,1)S(1)}, u32[]{:S(2)}, u32[]{:S(2)}) collective-permute-start(bf16[192,512]{1,0:T(8,128)(2,1)S(1)} %collective-permute-done.12.refs_3_), channel_id=1, source_target_pairs={{0,2},{2,4},{4,6},{6,0},{8,10},{10,12},{12,14},{14,8},{16,18},{18,... | collective-permute-start | bytes 589832 | tf_op jit(solution)/shard_map/ppermute | solution.py:274
  90.0 3.9 %collective-permute-start.20 = (bf16[192,512]{1,0:T(8,128)(2,1)S(1)}, bf16[192,512]{1,0:T(8,128)(2,1)S(1)}, u32[]{:S(2)}, u32[]{:S(2)}) collective-permute-start(bf16[192,512]{1,0:T(8,128)(2,1)S(1)} %collective-permute-done.19.refs_3_), channel_id=1, source_target_pairs={{0,2},{2,4},{4,6},{6,0},{8,10},{10,12},{12,14},{14,8},{16,18},{18,... | collective-permute-start | bytes 589832 | tf_op jit(solution)/shard_map/ppermute | solution.py:274
  94.2 2.8 %collective-permute-done.13.refs_4_ = bf16[192,512]{1,0:T(8,128)(2,1)S(1)} collective-permute-done((bf16[192,512]{1,0:T(8,128)(2,1)S(1)}, bf16[192,512]{1,0:T(8,128)(2,1)S(1)}, u32[]{:S(2)}, u32[]{:S(2)}) %collective-permute-start.13) | collective-permute-done | bytes 196640 | tf_op jit(solution)/shard_map/ppermute | solution.py:274
  97.0 2.2 %collective-permute-done.11.refs_2_ = bf16[192,512]{1,0:T(8,128)(2,1)S(1)} collective-permute-done((bf16[192,512]{1,0:T(8,128)(2,1)S(1)}, bf16[192,512]{1,0:T(8,128)(2,1)S(1)}, u32[]{:S(2)}, u32[]{:S(2)}) %collective-permute-start.11) | collective-permute-done | bytes 196640 | tf_op jit(solution)/shard_map/ppermute | solution.py:23
  99.2 6.5 %scores.1 = (bf16[2,4,768,384]{3,2,1,0:T(8,128)(2,1)S(1)}, f32[2,4,96,128]{3,2,1,0:T(8,128)S(1)}, f32[2,32,96]{2,1,0:T(8,128)}) custom-call(s32[1]{0:T(128)} %bitcast.odd_ref, bf16[1,2,96,4096]{3,2,1,0:T(8,128)(2,1)S(1)} %copy-done.1, bf16[192,512]{1,0:T(8,128)(2,1)S(1)} %key_sum.1.refs_0_, bf16[192,512]{1,0:T(8,128)(2,1)S(1)} %collective-permute-done.10.refs_1_, ...), custom_call_target="tpu_custom_call" | custom-call | flops 603979776 | bytes 8388608 | tf_op jit(solution)/shard_map/scores/pallas_call | solution.py:163
  105.7 4.6 %mixed_values.1 = bf16[1,2,96,4096]{3,2,1,0:T(8,128)(2,1)} custom-call(s32[1]{0:T(128)} %bitcast.odd_ref, bf16[2,4,768,384]{3,2,1,0:T(8,128)(2,1)S(1)} %get-tuple-element.35.weights, f32[2,4,96,128]{3,2,1,0:T(8,128)S(1)} %get-tuple-element.36.sums, bf16[192,512]{1,0:T(8,128)(2,1)S(1)} %value_sum.1.refs_0_, ...), custom_call_target="tpu_custom_call" | custom-call | flops 603979776 | bytes 8388608 | tf_op jit(solution)/shard_map/mixed_values/pallas_call | solution.py:204
  (72 shorter events, 7.6 us)
Async XLA Ops:
  0.6 6.6 %copy-start = (bf16[1,2,96,4096]{3,2,1,0:T(8,128)(2,1)S(1)}, bf16[1,2,96,4096]{3,2,1,0:T(8,128)(2,1)}, u32[]{:S(2)}) copy-start(bf16[1,2,96,4096]{3,2,1,0:T(8,128)(2,1)} %param.5) | copy-start | bytes 4718596
  0.6 6.5 %collective-permute-start = (bf16[1,4096]{1,0:T(2,128)(2,1)}, bf16[1,4096]{1,0:T(2,128)(2,1)S(1)}, u32[]{:S(2)}, u32[]{:S(2)}) collective-permute-start(bf16[1,4096]{1,0:T(2,128)(2,1)} %param.6), channel_id=1, source_target_pairs={{0,24},{8,0},{16,8},{24,16},{1,25},{9,1},{17,9},{25,17},{2,26},{10... | collective-permute-start | bytes 24584 | tf_op jit(solution)/shard_map/ppermute | solution.py:23
  3.1 27.0 %copy-start.13 = (s32[2,16]{1,0:T(2,128)S(1)}, s32[2,16]{1,0:T(2,128)}, u32[]{:S(2)}) copy-start(s32[2,16]{1,0:T(2,128)} %param.9) | copy-start | bytes 388
  4.4 25.7 %collective-permute-start.5 = (bf16[512,512]{1,0:T(8,128)(2,1)S(1)}, bf16[512,512]{1,0:T(8,128)(2,1)S(1)}, u32[]{:S(2)}, u32[]{:S(2)}) collective-permute-start(bf16[512,512]{1,0:T(8,128)(2,1)S(1)} %get-tuple-element.45.refs_4_), channel_id=1, source_target_pairs={{0,4},{1,5},{2,6},{3,7},{4,0},{5,1},{6,2},{7,3},{8,12},{9,13},{10,... | collective-permute-start | bytes 1572872 | tf_op jit(solution)/shard_map/ppermute | solution.py:23
  9.4 20.7 %collective-permute-start.1 = (bf16[192,1024]{1,0:T(8,128)(2,1)}, bf16[192,1024]{1,0:T(8,128)(2,1)S(1)}, u32[]{:S(2)}, u32[]{:S(2)}) collective-permute-start(bf16[192,1024]{1,0:T(8,128)(2,1)} %get-tuple-element.23), channel_id=1, source_target_pairs={{0,8},{1,9},{2,10},{3,11},{4,12},{5,13},{6,14},{7,15},{8,16},{9,17... | collective-permute-start | bytes 1179656 | tf_op jit(solution)/shard_map/ppermute | solution.py:260
  9.4 20.7 %collective-permute-start.2 = (bf16[192,1024]{1,0:T(8,128)(2,1)}, bf16[192,1024]{1,0:T(8,128)(2,1)S(1)}, u32[]{:S(2)}, u32[]{:S(2)}) collective-permute-start(bf16[192,1024]{1,0:T(8,128)(2,1)} %get-tuple-element.24), channel_id=1, source_target_pairs={{0,9},{1,8},{2,11},{3,10},{4,13},{5,12},{6,15},{7,14},{8,17},{9,16... | collective-permute-start | bytes 1179656 | tf_op jit(solution)/shard_map/ppermute | solution.py:260
  11.3 22.6 %collective-permute-start.3 = (bf16[192,1024]{1,0:T(8,128)(2,1)}, bf16[192,1024]{1,0:T(8,128)(2,1)S(1)}, u32[]{:S(2)}, u32[]{:S(2)}) collective-permute-start(bf16[192,1024]{1,0:T(8,128)(2,1)} %get-tuple-element.25), channel_id=1, source_target_pairs={{0,10},{1,11},{2,8},{3,9},{4,14},{5,15},{6,12},{7,13},{8,18},{9,19... | collective-permute-start | bytes 1179656 | tf_op jit(solution)/shard_map/ppermute | solution.py:260
  12.5 33.5 %collective-permute-start.4 = (bf16[192,1024]{1,0:T(8,128)(2,1)}, bf16[192,1024]{1,0:T(8,128)(2,1)}, u32[]{:S(2)}, u32[]{:S(2)}) collective-permute-start(bf16[192,1024]{1,0:T(8,128)(2,1)} %get-tuple-element.26), channel_id=1, source_target_pairs={{0,11},{1,10},{2,9},{3,8},{4,15},{5,14},{6,13},{7,12},{8,19},{9,18... | collective-permute-start | bytes 1179656 | tf_op jit(solution)/shard_map/ppermute | solution.py:260
  30.0 34.3 %collective-permute-start.9 = (bf16[512,512]{1,0:T(8,128)(2,1)S(1)}, bf16[512,512]{1,0:T(8,128)(2,1)S(1)}, u32[]{:S(2)}, u32[]{:S(2)}) collective-permute-start(bf16[512,512]{1,0:T(8,128)(2,1)S(1)} %get-tuple-element.37.refs_4_), channel_id=1, source_target_pairs={{0,4},{1,5},{2,6},{3,7},{4,0},{5,1},{6,2},{7,3},{8,12},{9,13},{10,... | collective-permute-start | bytes 1572872 | tf_op jit(solution)/shard_map/ppermute | solution.py:23
  33.9 0.7 copy-start.10
  46.0 1.0 copy-start.11
  49.6 6.5 %collective-permute-start.6 = (bf16[192,512]{1,0:T(8,128)(2,1)}, bf16[192,512]{1,0:T(8,128)(2,1)S(1)}, u32[]{:S(2)}, u32[]{:S(2)}) collective-permute-start(bf16[192,512]{1,0:T(8,128)(2,1)} %get-tuple-element.28), channel_id=1, source_target_pairs={{0,1},{1,0},{2,3},{3,2},{4,5},{5,4},{6,7},{7,6},{8,9},{9,8},{10,11... | collective-permute-start | bytes 589832 | tf_op jit(solution)/shard_map/ppermute | solution.py:23
  51.1 8.0 %collective-permute-start.7 = (bf16[192,512]{1,0:T(8,128)(2,1)}, bf16[192,512]{1,0:T(8,128)(2,1)S(1)}, u32[]{:S(2)}, u32[]{:S(2)}) collective-permute-start(bf16[192,512]{1,0:T(8,128)(2,1)} %get-tuple-element.29), channel_id=1, source_target_pairs={{0,2},{1,3},{2,0},{3,1},{4,6},{5,7},{6,4},{7,5},{8,10},{9,11},{10,... | collective-permute-start | bytes 589832 | tf_op jit(solution)/shard_map/ppermute | solution.py:23
  51.1 13.2 %collective-permute-start.8 = (bf16[192,512]{1,0:T(8,128)(2,1)}, bf16[192,512]{1,0:T(8,128)(2,1)S(1)}, u32[]{:S(2)}, u32[]{:S(2)}) collective-permute-start(bf16[192,512]{1,0:T(8,128)(2,1)} %get-tuple-element.30), channel_id=1, source_target_pairs={{0,3},{1,2},{2,1},{3,0},{4,7},{5,6},{6,5},{7,4},{8,11},{9,10},{10,... | collective-permute-start | bytes 589832 | tf_op jit(solution)/shard_map/ppermute | solution.py:23
  64.3 7.6 %copy-start.8 = (bf16[192,512]{1,0:T(8,128)(2,1)}, bf16[192,512]{1,0:T(8,128)(2,1)S(1)}, u32[]{:S(2)}) copy-start(bf16[192,512]{1,0:T(8,128)(2,1)S(1)} %collective-permute-done.8.three) | copy-start | bytes 589828
  64.4 1.1 copy-start.12
  68.1 8.5 %collective-permute-start.14 = (bf16[192,512]{1,0:T(8,128)(2,1)}, bf16[192,512]{1,0:T(8,128)(2,1)S(1)}, u32[]{:S(2)}, u32[]{:S(2)}) collective-permute-start(bf16[192,512]{1,0:T(8,128)(2,1)} %get-tuple-element.40), channel_id=1, source_target_pairs={{0,1},{1,0},{2,3},{3,2},{4,5},{5,4},{6,7},{7,6},{8,9},{9,8},{10,11... | collective-permute-start | bytes 589832 | tf_op jit(solution)/shard_map/ppermute | solution.py:23
  68.5 8.1 %collective-permute-start.15 = (bf16[192,512]{1,0:T(8,128)(2,1)}, bf16[192,512]{1,0:T(8,128)(2,1)S(1)}, u32[]{:S(2)}, u32[]{:S(2)}) collective-permute-start(bf16[192,512]{1,0:T(8,128)(2,1)} %get-tuple-element.41), channel_id=1, source_target_pairs={{0,2},{1,3},{2,0},{3,1},{4,6},{5,7},{6,4},{7,5},{8,10},{9,11},{10,... | collective-permute-start | bytes 589832 | tf_op jit(solution)/shard_map/ppermute | solution.py:23
  68.5 12.1 %collective-permute-start.16 = (bf16[192,512]{1,0:T(8,128)(2,1)}, bf16[192,512]{1,0:T(8,128)(2,1)S(1)}, u32[]{:S(2)}, u32[]{:S(2)}) collective-permute-start(bf16[192,512]{1,0:T(8,128)(2,1)} %get-tuple-element.42), channel_id=1, source_target_pairs={{0,3},{1,2},{2,1},{3,0},{4,7},{5,6},{6,5},{7,4},{8,11},{9,10},{10,... | collective-permute-start | bytes 589832 | tf_op jit(solution)/shard_map/ppermute | solution.py:23
  72.8 26.4 %copy-start.1 = (bf16[1,2,96,4096]{3,2,1,0:T(8,128)(2,1)S(1)}, bf16[1,2,96,4096]{3,2,1,0:T(8,128)(2,1)}, u32[]{:S(2)}) copy-start(bf16[1,2,96,4096]{3,2,1,0:T(8,128)(2,1)} %q_ref.1) | copy-start | bytes 4718596
  72.9 1.0 copy-start.5
  73.9 0.9 copy-start.7
  74.8 0.9 copy-start.9
  75.9 8.9 %collective-permute-start.12 = (bf16[192,512]{1,0:T(8,128)(2,1)S(1)}, bf16[192,512]{1,0:T(8,128)(2,1)S(1)}, u32[]{:S(2)}, u32[]{:S(2)}) collective-permute-start(bf16[192,512]{1,0:T(8,128)(2,1)S(1)} %key_sum.1.refs_0_), channel_id=1, source_target_pairs={{0,1},{1,0},{2,3},{3,2},{4,5},{5,4},{6,7},{7,6},{8,9},{9,8},{10,11... | collective-permute-start | bytes 589832 | tf_op jit(solution)/shard_map/ppermute | solution.py:23
  76.4 13.5 %collective-permute-start.10 = (bf16[192,512]{1,0:T(8,128)(2,1)S(1)}, bf16[192,512]{1,0:T(8,128)(2,1)S(1)}, u32[]{:S(2)}, u32[]{:S(2)}) collective-permute-start(bf16[192,512]{1,0:T(8,128)(2,1)S(1)} %key_sum.1.refs_0_), channel_id=1, source_target_pairs={{0,2},{1,3},{2,4},{3,5},{4,6},{5,7},{6,0},{7,1},{8,10},{9,11},{10,... | collective-permute-start | bytes 589832 | tf_op jit(solution)/shard_map/ppermute | solution.py:23
  81.3 0.9 copy-start.3
  82.3 7.6 %collective-permute-start.19 = (bf16[192,512]{1,0:T(8,128)(2,1)S(1)}, bf16[192,512]{1,0:T(8,128)(2,1)S(1)}, u32[]{:S(2)}, u32[]{:S(2)}) collective-permute-start(bf16[192,512]{1,0:T(8,128)(2,1)S(1)} %value_sum.1.refs_0_), channel_id=1, source_target_pairs={{0,1},{1,0},{2,3},{3,2},{4,5},{5,4},{6,7},{7,6},{8,9},{9,8},{10,11... | collective-permute-start | bytes 589832 | tf_op jit(solution)/shard_map/ppermute | solution.py:23
  82.8 11.1 %collective-permute-start.17 = (bf16[192,512]{1,0:T(8,128)(2,1)S(1)}, bf16[192,512]{1,0:T(8,128)(2,1)S(1)}, u32[]{:S(2)}, u32[]{:S(2)}) collective-permute-start(bf16[192,512]{1,0:T(8,128)(2,1)S(1)} %value_sum.1.refs_0_), channel_id=1, source_target_pairs={{0,2},{1,3},{2,4},{3,5},{4,6},{5,7},{6,0},{7,1},{8,10},{9,11},{10,... | collective-permute-start | bytes 589832 | tf_op jit(solution)/shard_map/ppermute | solution.py:23
  84.8 12.2 %collective-permute-start.13 = (bf16[192,512]{1,0:T(8,128)(2,1)S(1)}, bf16[192,512]{1,0:T(8,128)(2,1)S(1)}, u32[]{:S(2)}, u32[]{:S(2)}) collective-permute-start(bf16[192,512]{1,0:T(8,128)(2,1)S(1)} %collective-permute-done.12.refs_3_), channel_id=1, source_target_pairs={{0,2},{2,4},{4,6},{6,0},{8,10},{10,12},{12,14},{14,8},{16,18},{18,... | collective-permute-start | bytes 589832 | tf_op jit(solution)/shard_map/ppermute | solution.py:274
  89.9 9.3 %collective-permute-start.11 = (bf16[192,512]{1,0:T(8,128)(2,1)S(1)}, bf16[192,512]{1,0:T(8,128)(2,1)S(1)}, u32[]{:S(2)}, u32[]{:S(2)}) collective-permute-start(bf16[192,512]{1,0:T(8,128)(2,1)S(1)} %collective-permute-done.10.refs_1_), channel_id=1, source_target_pairs={{0,1},{1,2},{2,3},{3,4},{4,5},{5,6},{6,7},{7,0},{8,9},{9,10},{10,1... | collective-permute-start | bytes 589832 | tf_op jit(solution)/shard_map/ppermute | solution.py:23
  90.0 15.8 %collective-permute-start.20 = (bf16[192,512]{1,0:T(8,128)(2,1)S(1)}, bf16[192,512]{1,0:T(8,128)(2,1)S(1)}, u32[]{:S(2)}, u32[]{:S(2)}) collective-permute-start(bf16[192,512]{1,0:T(8,128)(2,1)S(1)} %collective-permute-done.19.refs_3_), channel_id=1, source_target_pairs={{0,2},{2,4},{4,6},{6,0},{8,10},{10,12},{12,14},{14,8},{16,18},{18,... | collective-permute-start | bytes 589832 | tf_op jit(solution)/shard_map/ppermute | solution.py:274
  93.9 11.8 %collective-permute-start.18 = (bf16[192,512]{1,0:T(8,128)(2,1)S(1)}, bf16[192,512]{1,0:T(8,128)(2,1)S(1)}, u32[]{:S(2)}, u32[]{:S(2)}) collective-permute-start(bf16[192,512]{1,0:T(8,128)(2,1)S(1)} %collective-permute-done.17.refs_1_), channel_id=1, source_target_pairs={{0,1},{1,2},{2,3},{3,4},{4,5},{5,6},{6,7},{7,0},{8,9},{9,10},{10,1... | collective-permute-start | bytes 589832 | tf_op jit(solution)/shard_map/ppermute | solution.py:23
  (3 other events, 2.0 us)

commit v3 on v2

--- a/solution.py
+++ b/solution.py
@@ -33,25 +33,22 @@
 
 def norm_kernel(starts_ref, x_ref, gain_ref, *outs):
     rows, width = x_ref.shape[1], x_ref.shape[2]
-    pieces = starts_ref.shape[1]
-    piece_width = outs[0].shape[1] // pieces
+    piece_width = outs[0].shape[1]
     for r in range(0, rows, ROW_STEP):
         x = x_ref[0, r : r + ROW_STEP, :].astype(jnp.float32)
         scale = lax.rsqrt(jnp.sum(x * x, axis=-1, keepdims=True) / width + 1e-05)
-        for flip, out in enumerate(outs):
-            for j in range(pieces):
-                start = pl.multiple_of(starts_ref[flip, j], LANES)
-                xs = x_ref[0, r : r + ROW_STEP, pl.ds(start, piece_width)].astype(jnp.float32)
-                gain = gain_ref[:, pl.ds(start, piece_width)]
-                out[r : r + ROW_STEP, j * piece_width : (j + 1) * piece_width] = (
-                    xs * scale * gain
-                ).astype(jnp.bfloat16)
+        for j, out in enumerate(outs):
+            start = pl.multiple_of(starts_ref[j], LANES)
+            xs = x_ref[0, r : r + ROW_STEP, pl.ds(start, piece_width)].astype(jnp.float32)
+            gain = gain_ref[:, pl.ds(start, piece_width)]
+            out[r : r + ROW_STEP, :] = (xs * scale * gain).astype(jnp.bfloat16)
 
 
 def normed_cuts(activations, gain, starts):
     micro_count, tok_rows, width = activations.shape
     rows = micro_count * tok_rows
-    part = width // QUAD
+    pieces = starts.shape[0]
+    part = width // pieces
     return pl.pallas_call(
         norm_kernel,
         grid=(micro_count,),
@@ -60,55 +57,59 @@
             pl.BlockSpec((1, tok_rows, width), lambda m: (m, 0, 0)),
             pl.BlockSpec((1, width), lambda m: (0, 0)),
         ],
-        out_specs=[pl.BlockSpec((tok_rows, part), lambda m: (m, 0))] * QUAD,
-        out_shape=[jax.ShapeDtypeStruct((rows, part), jnp.bfloat16)] * QUAD,
+        out_specs=[pl.BlockSpec((tok_rows, part), lambda m: (m, 0))] * pieces,
+        out_shape=[jax.ShapeDtypeStruct((rows, part), jnp.bfloat16)] * pieces,
         compiler_params=params(16),
         cost_estimate=cost(6 * rows * width, 4 * rows * width),
         name="norm_cuts",
     )(starts, activations, gain)
 
 
-def product_kernel(quads, *refs):
-    xs, shards, outs = refs[:QUAD], refs[QUAD : QUAD + quads], refs[QUAD + quads :]
+def product_kernel(starts_ref, x, *refs):
+    shards, out = refs[:QUAD], refs[QUAD]
     shard_rows = shards[0].shape[0]
-    for x, out in zip(xs, outs):
-        total = jnp.dot(x[:, :shard_rows], shards[0][...], preferred_element_type=jnp.float32)
-        for j in range(1, quads):
-            total = total + jnp.dot(
-                x[:, j * shard_rows : (j + 1) * shard_rows],
-                shards[j][...],
-                preferred_element_type=jnp.float32,
-            )
-        out[...] = total.astype(out.dtype)
-
-
-def partial_products(xs, shards):
-    rows, part = xs[0].shape
+    total = 0.0
+    for i, shard in enumerate(shards):
+        start = pl.multiple_of(starts_ref[i], LANES)
+        total = total + jnp.dot(
+            x[:, pl.ds(start, shard_rows)], shard[...], preferred_element_type=jnp.float32
+        )
+    out[...] = total.astype(out.dtype)
+
+
+def product(starts, x, shards, dtype):
+    rows, part = x.shape
     width = shards[0].shape[1]
-    return pl.pallas_call(
-        lambda *refs: product_kernel(len(shards), *refs),
-        out_shape=[jax.ShapeDtypeStruct((rows, width), jnp.float32)]
-        + [jax.ShapeDtypeStruct((rows, width), jnp.bfloat16)] * (QUAD - 1),
+    vmem = pl.BlockSpec(memory_space=pltpu.VMEM)
+    return pl.pallas_call(
+        product_kernel,
+        in_specs=[pl.BlockSpec(memory_space=pltpu.SMEM)] + [vmem] * (1 + QUAD),
+        out_shape=jax.ShapeDtypeStruct((rows, width), dtype),
         compiler_params=params(24),
-        cost_estimate=cost(2 * QUAD * rows * part * width, 2 * QUAD * rows * part + 2 * part * width),
-        name="partial_products",
-    )(*xs, *shards)
-
-
-def added(own, one, two, three):
-    return own + one.astype(jnp.float32) + two.astype(jnp.float32) + three.astype(jnp.float32)
-
-
-def key_sum_kernel(own, one, two, three, cosine, sine_part, out):
+        cost_estimate=cost(2 * rows * part * width, 2 * (rows * part + part * width)),
+        name="product",
+    )(starts, x, *shards)
+
+
+def added(own, parts, cols):
+    total = own[:, cols]
+    for part in parts:
+        total = total + part[:, cols].astype(jnp.float32)
+    return total
+
+
+def key_sum_kernel(cosine, sine_part, own, *refs):
+    parts, out = refs[:-1], refs[-1]
     for h in range(out.shape[1] // HD):
         cols = slice(h * HD, (h + 1) * HD)
-        total = added(own[:, cols], one[:, cols], two[:, cols], three[:, cols])
+        total = added(own, parts, cols)
         turned = pltpu.roll(total, HD // 2, 1)
         out[:, cols] = (total * cosine[...] + turned * sine_part[...]).astype(jnp.bfloat16)
 
 
-def value_sum_kernel(own, one, two, three, out):
-    out[...] = added(own[...], one[...], two[...], three[...]).astype(jnp.bfloat16)
+def value_sum_kernel(own, *refs):
+    parts, out = refs[:-1], refs[-1]
+    out[...] = added(own, parts, slice(None)).astype(jnp.bfloat16)
 
 
 def block_sum(kernel, name, own, parts, *tables):
@@ -118,7 +119,7 @@
         compiler_params=params(16),
         cost_estimate=cost(10 * own.size, 12 * own.size),
         name=name,
-    )(own, *parts, *tables)
+    )(*tables, own, *parts)
 
 
 def stacked(refs, odd):
@@ -190,12 +191,16 @@
     values = stacked(refs[:5], odd_ref[0])
     out = refs[5]
     tok_rows = out.shape[2]
-    mixed = jnp.dot(weights[0, 0], values, preferred_element_type=jnp.float32)
-    share = 1.0 / sums[0, 0]
-    for h in range(GROUP):
-        out[0, 0, :, h * HD : (h + 1) * HD] = (
-            mixed[h * tok_rows : (h + 1) * tok_rows] * share[:, h : h + 1]
-        ).astype(jnp.bfloat16)
+    for k in range(KVH):
+        mixed = jnp.dot(
+            weights[0, k], values[:, k * HD : (k + 1) * HD], preferred_element_type=jnp.float32
+        )
+        share = 1.0 / sums[0, k]
+        for h in range(GROUP):
+            head = k * GROUP + h
+            out[0, 0, :, head * HD : (head + 1) * HD] = (
+                mixed[h * tok_rows : (h + 1) * tok_rows] * share[:, h : h + 1]
+            ).astype(jnp.bfloat16)
 
 
 def mixed_values(odd, weights, sums, window):
@@ -203,16 +208,16 @@
     tok_rows = group_rows // GROUP
     return pl.pallas_call(
         mix_kernel,
-        grid=(micro_count, KVH),
+        grid=(micro_count,),
         in_specs=[
             pl.BlockSpec(memory_space=pltpu.SMEM),
-            pl.BlockSpec((1, 1, group_rows, keys), lambda m, k: (m, k, 0, 0)),
-            pl.BlockSpec((1, 1, tok_rows, LANES), lambda m, k: (m, k, 0, 0)),
-            *window_specs(tok_rows),
-        ],
-        out_specs=pl.BlockSpec((1, 1, tok_rows, GROUP * HD), lambda m, k: (0, m, 0, k)),
+            pl.BlockSpec((1, KVH, group_rows, keys), lambda m: (m, 0, 0, 0)),
+            pl.BlockSpec((1, KVH, tok_rows, LANES), lambda m: (m, 0, 0, 0)),
+            *[pl.BlockSpec((tok_rows, KVH * HD), lambda m: (m, 0))] * 5,
+        ],
+        out_specs=pl.BlockSpec((1, 1, tok_rows, QH * HD), lambda m: (0, m, 0, 0)),
         out_shape=jax.ShapeDtypeStruct((1, micro_count, tok_rows, QH * HD), jnp.bfloat16),
-        compiler_params=params(24),
+        compiler_params=params(32),
         cost_estimate=cost(2 * micro_count * QH * tok_rows * keys * HD, 8 * 2**20),
         name="mixed_values",
     )(odd, weights, sums, *window)
@@ -228,43 +233,43 @@
     shard_rows, kv_width = weight.shape[0], weight.shape[1] // 2
     _, micro_count, tok_rows, _ = handoff.shape
 
-    def same_place_shards(part):
-        return [part] + [
-            moved(part, "ctx", lambda i, j=j: i + QUAD * j) for j in range(1, quads)
-        ]
-
-    key_shards = same_place_shards(weight[:, :kv_width])
-    value_part, _ = lax.optimization_barrier((weight[:, kv_width:], key_shards[-1]))
-    value_shards = same_place_shards(value_part)
+    def over_z(part):
+        return moved(part, "ctx", lambda i: i ^ 2)
+
+    def over_y(part):
+        return moved(part, "ctx", lambda i: i ^ 1)
+
+    places = own_place ^ jnp.array([0, 2, 1, 3], jnp.int32)
+    starts = places * shard_rows
+    key_part, value_part = weight[:, :kv_width], weight[:, kv_width:]
+    key_z = over_z(key_part)
+    key_shards = [key_part, key_z, over_y(key_part), over_y(key_z)]
+    late_part, _ = lax.optimization_barrier((value_part, key_z))
+    value_z = over_z(late_part)
+    value_shards = [value_part, value_z, over_y(value_part), over_y(value_z)]
 
     next_gain = moved(norm_gain, "section", lambda i: i - 1).astype(jnp.float32)
-    starts = jnp.stack(
-        [
-            jnp.stack(
-                [
-                    ((own_quad - j) % quads * QUAD + (own_place ^ flip)) * shard_rows
-                    for j in range(quads)
-                ]
-            )
-            for flip in range(QUAD)
-        ]
-    ).astype(jnp.int32)
-    cuts = normed_cuts(handoff[0], next_gain, starts)
-
-    def to_next_section(part, flip):
+    cut_starts = (own_quad + jnp.arange(quads, dtype=jnp.int32)) % quads * (QUAD * shard_rows)
+    cuts = normed_cuts(handoff[0], next_gain, cut_starts)
+
+    def to_next_section(part, j):
         route = [
-            (s * cycle_size + i, (s + 1) % sections * cycle_size + (i ^ flip))
+            (s * cycle_size + i, (s + 1) % sections * cycle_size + (i + QUAD * j) % cycle_size)
             for s in range(sections)
             for i in range(cycle_size)
         ]
         return lax.ppermute(part, ("section", "ctx"), route)
 
-    arrived = [to_next_section(cuts[flip], flip) for flip in range(QUAD)]
-
-    def swapped(parts):
+    arrived = [to_next_section(cuts[j], j) for j in range(quads)]
+
+    def sent_back(shards):
         return [
-            moved(part, "ctx", lambda i, flip=flip: i ^ flip)
-            for flip, part in enumerate(parts, start=1)
+            moved(
+                product(starts, arrived[j], shards, jnp.bfloat16),
+                "ctx",
+                lambda i, j=j: i - QUAD * j,
+            )
+            for j in range(1, quads)
         ]
 
     def window_of(block):
@@ -297,14 +302,16 @@
     sine_part = jnp.concatenate([-sine_part, sine_part], axis=1)
     odd = (own_index % 2).astype(jnp.int32).reshape(1)
 
-    own_keys, *key_parts = partial_products(arrived, key_shards)
-    key_parts, value_shards = lax.optimization_barrier((swapped(key_parts), value_shards))
+    key_parts = sent_back(key_shards)
+    own_keys = product(starts, arrived[0], key_shards, jnp.float32)
     key_block = block_sum(key_sum_kernel, "key_sum", own_keys, key_parts, cosine, sine_part)
-    key_window = window_of(key_block)
-    weights, sums, log_sums = scored(odd, queries, key_window, own_pos[:, :, None], col_pos)
-
-    own_values, *value_parts = partial_products(arrived, value_shards)
-    value_block = block_sum(value_sum_kernel, "value_sum", own_values, swapped(value_parts))
+    weights, sums, log_sums = scored(
+        odd, queries, window_of(key_block), own_pos[:, :, None], col_pos
+    )
+
+    value_parts = sent_back(value_shards)
+    own_values = product(starts, arrived[0], value_shards, jnp.float32)
+    value_block = block_sum(value_sum_kernel, "value_sum", own_values, value_parts)
     out = mixed_values(odd, weights, sums, window_of(value_block))
     return (out, log_sums[None])
 

time: 111 us -> 113 us (1.018)
  waiting for transfers between devices: 50.7 us -> 52.7 us
  starting transfers between devices: 28 us -> 26.1 us
  Pallas kernels: 18.8 us -> 20.2 us
    ppermute x4 -> x2, waiting for transfers between devices: 15.1 us -> 27.3 us  [to_next_section(): return lax.ppermute(part, ('section', 'ctx'), route)]
    ppermute x15, waiting for transfers between devices: 32.8 us -> 21.2 us  [moved(): lax.ppermute(block, axis, [(i, target(i) % size) for i in range(size)])]
    add x12, local copies, waits for them, and re-layouts: 0.89 us -> 4.53 us  [device_positions(): span_ids[:, :, None] * span_len]
    unnamed x28 -> x24, local copies, waits for them, and re-layouts: 8.69 us -> 5.19 us
    ppermute x2, starting transfers between devices: 8.98 us -> 6.15 us  [window_of(): lax.ppermute(beside, 'ctx', [(i, (i + 2) % cycle_size) for i in range(0,...]
    pallas_call x2, Pallas kernels: 0.27 us -> 2.06 us  [block_sum(): pl.pallas_call(kernel, out_shape=jax.ShapeDtypeStruct(own.shape, jnp.bflo...]
    ppermute x2, waiting for transfers between devices: 2.77 us -> 4.13 us  [window_of(): lax.ppermute(beside, 'ctx', [(i, (i + 2) % cycle_size) for i in range(0,...]
    ppermute x15, starting transfers between devices: 14.6 us -> 15.9 us  [moved(): lax.ppermute(block, axis, [(i, target(i) % size) for i in range(size)])]
  transfers between devices with their start and end apart: 21 -> 19, of which waited for: 10 -> 9; matrix products, arithmetic and copies ran while one was open for 3% -> 5% of each run, Pallas kernels for 11% -> 16%
where the time goes in v3:
time: 113 us
  waiting for transfers between devices  52.7 us (47%)
  starting transfers between devices  26.1 us (23%)
  Pallas kernels  20.2 us (18%)
  local copies, waits for them, and re-layouts  11.2 us (10%)
  other arithmetic  1.46 us (1%)
    ppermute x2, waiting for transfers between devices, to_next_section(): return lax.ppermute(part, ('section', 'ctx'), route)  27.3 us
    ppermute x15, waiting for transfers between devices, moved(): lax.ppermute(block, axis, [(i, target(i) % size) for i in range(size)])  21.2 us
    ppermute x15, starting transfers between devices, moved(): lax.ppermute(block, axis, [(i, target(i) % size) for i in range(size)])  15.9 us
    pallas_call x4, Pallas kernels, product(): pl.pallas_call(product_kernel, in_specs=[pl.BlockSpec(memory_space=pltpu....  7.12 us
    pallas_call x1, Pallas kernels, scored(): pl.pallas_call(score_kernel, grid=(micro_count, KVH), in_specs=[pl.BlockS...  6.5 us
    ppermute x2, starting transfers between devices, window_of(): lax.ppermute(beside, 'ctx', [(i, (i + 2) % cycle_size) for i in range(0,...  6.15 us
    unnamed x24, local copies, waits for them, and re-layouts  5.19 us
    add x12, local copies, waits for them, and re-layouts, device_positions(): span_ids[:, :, None] * span_len  4.53 us
  transfers between devices with their start and end apart: 19, of which 9 were waited for; matrix products, arithmetic and copies ran while one was open for 5% of the time, Pallas kernels for 16%

profile of v3, /device:TPU:0, one launch (start us, length us, event | category | flops | bytes accessed | tf_op | source)
XLA Modules:
  0.0 112.5 jit_solution(14426578147434959733)
XLA Ops:
  0.7 1.4 %fusion.8 = (bf16[512,512]{1,0:T(8,128)(2,1)S(1)}, bf16[512,512]{1,0:T(8,128)(2,1)S(1)}) fusion(bf16[512,1024]{1,0:T(8,128)(2,1)} %bitcast.5), kind=kLoop, calls=%fused_computation.29 | loop fusion | bytes 2097152 | tf_op jit(solution)/shard_map/slice | solution.py:244
  2.1 3.1 %collective-permute-start.2 = (bf16[512,512]{1,0:T(8,128)(2,1)S(1)}, bf16[512,512]{1,0:T(8,128)(2,1)S(1)}, u32[]{:S(2)}, u32[]{:S(2)}) collective-permute-start(bf16[512,512]{1,0:T(8,128)(2,1)S(1)} %get-tuple-element.15.refs_0_), channel_id=1, source_target_pairs={{0,2},{1,3},{2,0},{3,1},{4,6},{5,7},{6,4},{7,5},{8,10},{9,11},{10,... | collective-permute-start | bytes 1572872 | tf_op jit(solution)/shard_map/ppermute | solution.py:23
  5.1 1.5 %collective-permute-start.3 = (bf16[512,512]{1,0:T(8,128)(2,1)S(1)}, bf16[512,512]{1,0:T(8,128)(2,1)}, u32[]{:S(2)}, u32[]{:S(2)}) collective-permute-start(bf16[512,512]{1,0:T(8,128)(2,1)S(1)} %get-tuple-element.15.refs_0_), channel_id=1, source_target_pairs={{0,1},{1,0},{2,3},{3,2},{4,5},{5,4},{6,7},{7,6},{8,9},{9,8},{10,11... | collective-permute-start | bytes 1572872 | tf_op jit(solution)/shard_map/ppermute | solution.py:23
  6.7 10.4 %collective-permute-done.2.refs_1_ = bf16[512,512]{1,0:T(8,128)(2,1)S(1)} collective-permute-done((bf16[512,512]{1,0:T(8,128)(2,1)S(1)}, bf16[512,512]{1,0:T(8,128)(2,1)S(1)}, u32[]{:S(2)}, u32[]{:S(2)}) %collective-permute-start.2) | collective-permute-done | bytes 524320 | tf_op jit(solution)/shard_map/ppermute | solution.py:23
  17.9 1.7 %collective-permute-start.11 = (bf16[512,512]{1,0:T(8,128)(2,1)S(1)}, bf16[512,512]{1,0:T(8,128)(2,1)S(1)}, u32[]{:S(2)}, u32[]{:S(2)}) collective-permute-start(bf16[512,512]{1,0:T(8,128)(2,1)S(1)} %get-tuple-element.12.refs_0_), channel_id=1, source_target_pairs={{0,2},{1,3},{2,0},{3,1},{4,6},{5,7},{6,4},{7,5},{8,10},{9,11},{10,... | collective-permute-start | bytes 1572872 | tf_op jit(solution)/shard_map/ppermute | solution.py:23
  19.6 1.4 %collective-permute-done = bf16[1,4096]{1,0:T(2,128)(2,1)S(1)} collective-permute-done((bf16[1,4096]{1,0:T(2,128)(2,1)S(1)}, bf16[1,4096]{1,0:T(2,128)(2,1)S(1)}, u32[]{:S(2)}, u32[]{:S(2)}) %collective-permute-start) | collective-permute-done | bytes 8224 | tf_op jit(solution)/shard_map/ppermute | solution.py:23
  21.1 2.0 %norm_cuts.1 = (bf16[192,2048]{1,0:T(8,128)(2,1)S(1)}, bf16[192,2048]{1,0:T(8,128)(2,1)}) custom-call(s32[2]{0:T(128)S(1)} %fusion.6.starts_ref, bf16[2,96,4096]{2,1,0:T(8,128)(2,1)S(1)} %bitcast.4, f32[1,4096]{1,0:T(1,128)S(1)} %convert_element_type.16.gain_ref), custom_call_target="tpu_custom_call" | custom-call | flops 4718592 | bytes 3145728 | tf_op jit(solution)/shard_map/norm_cuts/pallas_call | solution.py:52
  24.0 4.1 %collective-permute-start.5 = (bf16[192,2048]{1,0:T(8,128)(2,1)}, bf16[192,2048]{1,0:T(8,128)(2,1)S(1)}, u32[]{:S(2)}, u32[]{:S(2)}) collective-permute-start(bf16[192,2048]{1,0:T(8,128)(2,1)} %get-tuple-element.9), channel_id=1, source_target_pairs={{0,12},{1,13},{2,14},{3,15},{4,8},{5,9},{6,10},{7,11},{8,20},{9,21... | collective-permute-start | bytes 2359304 | tf_op jit(solution)/shard_map/ppermute | solution.py:261
  28.1 1.5 %collective-permute-start.12 = (bf16[512,512]{1,0:T(8,128)(2,1)S(1)}, bf16[512,512]{1,0:T(8,128)(2,1)}, u32[]{:S(2)}, u32[]{:S(2)}) collective-permute-start(bf16[512,512]{1,0:T(8,128)(2,1)S(1)} %get-tuple-element.12.refs_0_), channel_id=1, source_target_pairs={{0,1},{1,0},{2,3},{3,2},{4,5},{5,4},{6,7},{7,6},{8,9},{9,8},{10,11... | collective-permute-start | bytes 1572872 | tf_op jit(solution)/shard_map/ppermute | solution.py:23
  30.8 3.1 %collective-permute-done.11.refs_1_ = bf16[512,512]{1,0:T(8,128)(2,1)S(1)} collective-permute-done((bf16[512,512]{1,0:T(8,128)(2,1)S(1)}, bf16[512,512]{1,0:T(8,128)(2,1)S(1)}, u32[]{:S(2)}, u32[]{:S(2)}) %collective-permute-start.11) | collective-permute-done | bytes 524320 | tf_op jit(solution)/shard_map/ppermute | solution.py:23
  34.0 1.2 %collective-permute-start.13 = (bf16[512,512]{1,0:T(8,128)(2,1)S(1)}, bf16[512,512]{1,0:T(8,128)(2,1)}, u32[]{:S(2)}, u32[]{:S(2)}) collective-permute-start(bf16[512,512]{1,0:T(8,128)(2,1)S(1)} %collective-permute-done.11.refs_1_), channel_id=1, source_target_pairs={{0,1},{1,0},{2,3},{3,2},{4,5},{5,4},{6,7},{7,6},{8,9},{9,8},{10,11... | collective-permute-start | bytes 1572872 | tf_op jit(solution)/shard_map/ppermute | solution.py:23
  35.4 27.3 %collective-permute-done.5.x = bf16[192,2048]{1,0:T(8,128)(2,1)S(1)} collective-permute-done((bf16[192,2048]{1,0:T(8,128)(2,1)}, bf16[192,2048]{1,0:T(8,128)(2,1)S(1)}, u32[]{:S(2)}, u32[]{:S(2)}) %collective-permute-start.5) | collective-permute-done | bytes 786464 | tf_op jit(solution)/shard_map/ppermute | solution.py:261
  62.7 1.0 copy-done.1
  63.7 1.8 %product.5 = bf16[192,512]{1,0:T(8,128)(2,1)S(1)} custom-call(s32[4]{0:T(128)S(1)} %xor_multiply_fusion.starts_ref, bf16[192,2048]{1,0:T(8,128)(2,1)S(1)} %collective-permute-done.5.x, bf16[512,512]{1,0:T(8,128)(2,1)S(1)} %get-tuple-element.15.refs_0_, bf16[512,512]{1,0:T(8,128)(2,1)S(1)} %copy-done.1, bf16[512,512]{1,0:T(8,128)(2,1)} %collective-permute-done.3.refs_2_, ...), custom_call_target="tpu_custom_call" | custom-call | flops 402653184 | bytes 2883584 | tf_op jit(solution)/shard_map/product/pallas_call | solution.py:84
  65.8 1.8 %product.7 = bf16[192,512]{1,0:T(8,128)(2,1)S(1)} custom-call(s32[4]{0:T(128)S(1)} %xor_multiply_fusion.starts_ref, bf16[192,2048]{1,0:T(8,128)(2,1)S(1)} %collective-permute-done.5.x, bf16[512,512]{1,0:T(8,128)(2,1)S(1)} %get-tuple-element.12.refs_0_, bf16[512,512]{1,0:T(8,128)(2,1)S(1)} %collective-permute-done.11.refs_1_, ...), custom_call_target="tpu_custom_call" | custom-call | flops 402653184 | bytes 2883584 | tf_op jit(solution)/shard_map/product/pallas_call | solution.py:84
  67.6 2.7 %collective-permute-start.14 = (bf16[192,512]{1,0:T(8,128)(2,1)S(1)}, bf16[192,512]{1,0:T(8,128)(2,1)}, u32[]{:S(2)}, u32[]{:S(2)}) collective-permute-start(bf16[192,512]{1,0:T(8,128)(2,1)S(1)} %product.7), channel_id=1, source_target_pairs={{0,4},{1,5},{2,6},{3,7},{4,0},{5,1},{6,2},{7,3},{8,12},{9,13},{10,... | collective-permute-start | bytes 589832 | tf_op jit(solution)/shard_map/ppermute | solution.py:23
  75.3 1.0 copy-done.2
  76.3 1.8 %product.4.own = f32[192,512]{1,0:T(8,128)S(1)} custom-call(s32[4]{0:T(128)S(1)} %xor_multiply_fusion.starts_ref, bf16[192,2048]{1,0:T(8,128)(2,1)S(1)} %collective-permute-done.1.x, bf16[512,512]{1,0:T(8,128)(2,1)S(1)} %get-tuple-element.15.refs_0_, bf16[512,512]{1,0:T(8,128)(2,1)S(1)} %copy-done.2, bf16[512,512]{1,0:T(8,128)(2,1)} %collective-permute-done.3.refs_2_, ...), custom_call_target="tpu_custom_call" | custom-call | flops 402653184 | bytes 2883584 | tf_op jit(solution)/shard_map/product/pallas_call | solution.py:84
  78.1 3.5 %collective-permute-done.6.refs_0_ = bf16[192,512]{1,0:T(8,128)(2,1)} collective-permute-done((bf16[192,512]{1,0:T(8,128)(2,1)S(1)}, bf16[192,512]{1,0:T(8,128)(2,1)}, u32[]{:S(2)}, u32[]{:S(2)}) %collective-permute-start.6) | collective-permute-done | bytes 196640 | tf_op jit(solution)/shard_map/ppermute | solution.py:23
  81.6 1.1 key_sum.1.refs_0_
  82.8 1.6 %collective-permute-start.9 = (bf16[192,512]{1,0:T(8,128)(2,1)S(1)}, bf16[192,512]{1,0:T(8,128)(2,1)S(1)}, u32[]{:S(2)}, u32[]{:S(2)}) collective-permute-start(bf16[192,512]{1,0:T(8,128)(2,1)S(1)} %key_sum.1.refs_0_), channel_id=1, source_target_pairs={{0,1},{1,0},{2,3},{3,2},{4,5},{5,4},{6,7},{7,6},{8,9},{9,8},{10,11... | collective-permute-start | bytes 589832 | tf_op jit(solution)/shard_map/ppermute | solution.py:23
  84.4 1.8 %product.6.own = f32[192,512]{1,0:T(8,128)S(1)} custom-call(s32[4]{0:T(128)S(1)} %xor_multiply_fusion.starts_ref, bf16[192,2048]{1,0:T(8,128)(2,1)S(1)} %collective-permute-done.1.x, bf16[512,512]{1,0:T(8,128)(2,1)S(1)} %get-tuple-element.12.refs_0_, bf16[512,512]{1,0:T(8,128)(2,1)S(1)} %collective-permute-done.11.refs_1_, ...), custom_call_target="tpu_custom_call" | custom-call | flops 402653184 | bytes 2883584 | tf_op jit(solution)/shard_map/product/pallas_call | solution.py:84
  86.1 1.0 value_sum.1.refs_0_
  87.1 1.2 %collective-permute-start.17 = (bf16[192,512]{1,0:T(8,128)(2,1)S(1)}, bf16[192,512]{1,0:T(8,128)(2,1)S(1)}, u32[]{:S(2)}, u32[]{:S(2)}) collective-permute-start(bf16[192,512]{1,0:T(8,128)(2,1)S(1)} %value_sum.1.refs_0_), channel_id=1, source_target_pairs={{0,1},{1,0},{2,3},{3,2},{4,5},{5,4},{6,7},{7,6},{8,9},{9,8},{10,11... | collective-permute-start | bytes 589832 | tf_op jit(solution)/shard_map/ppermute | solution.py:23
  88.7 1.1 collective-permute-done.9.refs_3_
  89.7 3.1 %collective-permute-start.10 = (bf16[192,512]{1,0:T(8,128)(2,1)S(1)}, bf16[192,512]{1,0:T(8,128)(2,1)S(1)}, u32[]{:S(2)}, u32[]{:S(2)}) collective-permute-start(bf16[192,512]{1,0:T(8,128)(2,1)S(1)} %collective-permute-done.9.refs_3_), channel_id=1, source_target_pairs={{0,2},{2,4},{4,6},{6,0},{8,10},{10,12},{12,14},{14,8},{16,18},{18,... | collective-permute-start | bytes 589832 | tf_op jit(solution)/shard_map/ppermute | solution.py:279
  93.9 3.0 %collective-permute-start.18 = (bf16[192,512]{1,0:T(8,128)(2,1)S(1)}, bf16[192,512]{1,0:T(8,128)(2,1)S(1)}, u32[]{:S(2)}, u32[]{:S(2)}) collective-permute-start(bf16[192,512]{1,0:T(8,128)(2,1)S(1)} %collective-permute-done.17.refs_3_), channel_id=1, source_target_pairs={{0,2},{2,4},{4,6},{6,0},{8,10},{10,12},{12,14},{14,8},{16,18},{18,... | collective-permute-start | bytes 589832 | tf_op jit(solution)/shard_map/ppermute | solution.py:279
  96.9 1.1 collective-permute-done.15.refs_1_
  98.0 4.1 %collective-permute-done.10.refs_4_ = bf16[192,512]{1,0:T(8,128)(2,1)S(1)} collective-permute-done((bf16[192,512]{1,0:T(8,128)(2,1)S(1)}, bf16[192,512]{1,0:T(8,128)(2,1)S(1)}, u32[]{:S(2)}, u32[]{:S(2)}) %collective-permute-start.10) | collective-permute-done | bytes 196640 | tf_op jit(solution)/shard_map/ppermute | solution.py:279
  102.2 1.4 %copy-done.4 = bf16[1,2,96,4096]{3,2,1,0:T(8,128)(2,1)S(1)} copy-done((bf16[1,2,96,4096]{3,2,1,0:T(8,128)(2,1)S(1)}, bf16[1,2,96,4096]{3,2,1,0:T(8,128)(2,1)}, u32[]{:S(2)}) %copy-start.4) | copy-done | bytes 1572888
  103.6 6.5 %scores.1 = (bf16[2,4,768,384]{3,2,1,0:T(8,128)(2,1)S(1)}, f32[2,4,96,128]{3,2,1,0:T(8,128)S(1)}, f32[2,32,96]{2,1,0:T(8,128)}) custom-call(s32[1]{0:T(128)} %bitcast.odd_ref, bf16[1,2,96,4096]{3,2,1,0:T(8,128)(2,1)S(1)} %copy-done.4, bf16[192,512]{1,0:T(8,128)(2,1)S(1)} %key_sum.1.refs_0_, bf16[192,512]{1,0:T(8,128)(2,1)S(1)} %collective-permute-done.7.refs_1_, ...), custom_call_target="tpu_custom_call" | custom-call | flops 603979776 | bytes 8388608 | tf_op jit(solution)/shard_map/scores/pallas_call | solution.py:164
  110.1 2.5 %mixed_values.1 = bf16[1,2,96,4096]{3,2,1,0:T(8,128)(2,1)} custom-call(s32[1]{0:T(128)} %bitcast.odd_ref, bf16[2,4,768,384]{3,2,1,0:T(8,128)(2,1)S(1)} %get-tuple-element.10.weights, f32[2,4,96,128]{3,2,1,0:T(8,128)S(1)} %get-tuple-element.11.sums, bf16[192,512]{1,0:T(8,128)(2,1)S(1)} %value_sum.1.refs_0_, ...), custom_call_target="tpu_custom_call" | custom-call | flops 603979776 | bytes 8388608 | tf_op jit(solution)/shard_map/mixed_values/pallas_call | solution.py:209
  (65 shorter events, 9.7 us)
Async XLA Ops:
  0.6 19.0 %copy-start.10 = (bf16[1,4096]{1,0:T(2,128)(2,1)S(1)}, bf16[1,4096]{1,0:T(2,128)(2,1)}, u32[]{:S(2)}) copy-start(bf16[1,4096]{1,0:T(2,128)(2,1)} %param.7) | copy-start | bytes 24580
  0.6 20.4 %copy-start.3 = (bf16[1,2,96,4096]{3,2,1,0:T(8,128)(2,1)S(1)}, bf16[1,2,96,4096]{3,2,1,0:T(8,128)(2,1)}, u32[]{:S(2)}) copy-start(bf16[1,2,96,4096]{3,2,1,0:T(8,128)(2,1)} %param.6) | copy-start | bytes 4718596
  0.7 29.0 %copy-start.6 = (s32[2,16]{1,0:T(2,128)S(1)}, s32[2,16]{1,0:T(2,128)}, u32[]{:S(2)}) copy-start(s32[2,16]{1,0:T(2,128)} %param.10) | copy-start | bytes 388
  0.7 34.7 %copy-start.11 = (s32[4]{0:T(128)S(1)}, s32[4]{0:T(128)}, u32[]{:S(2)}) copy-start(s32[4]{0:T(128)} %constant.93.clone) | copy-start | bytes 52
  2.1 15.0 %collective-permute-start.2 = (bf16[512,512]{1,0:T(8,128)(2,1)S(1)}, bf16[512,512]{1,0:T(8,128)(2,1)S(1)}, u32[]{:S(2)}, u32[]{:S(2)}) collective-permute-start(bf16[512,512]{1,0:T(8,128)(2,1)S(1)} %get-tuple-element.15.refs_0_), channel_id=1, source_target_pairs={{0,2},{1,3},{2,0},{3,1},{4,6},{5,7},{6,4},{7,5},{8,10},{9,11},{10,... | collective-permute-start | bytes 1572872 | tf_op jit(solution)/shard_map/ppermute | solution.py:23
  5.1 25.1 %collective-permute-start.3 = (bf16[512,512]{1,0:T(8,128)(2,1)S(1)}, bf16[512,512]{1,0:T(8,128)(2,1)}, u32[]{:S(2)}, u32[]{:S(2)}) collective-permute-start(bf16[512,512]{1,0:T(8,128)(2,1)S(1)} %get-tuple-element.15.refs_0_), channel_id=1, source_target_pairs={{0,1},{1,0},{2,3},{3,2},{4,5},{5,4},{6,7},{7,6},{8,9},{9,8},{10,11... | collective-permute-start | bytes 1572872 | tf_op jit(solution)/shard_map/ppermute | solution.py:23
  17.1 0.8 copy-start
  17.9 16.1 %collective-permute-start.11 = (bf16[512,512]{1,0:T(8,128)(2,1)S(1)}, bf16[512,512]{1,0:T(8,128)(2,1)S(1)}, u32[]{:S(2)}, u32[]{:S(2)}) collective-permute-start(bf16[512,512]{1,0:T(8,128)(2,1)S(1)} %get-tuple-element.12.refs_0_), channel_id=1, source_target_pairs={{0,2},{1,3},{2,0},{3,1},{4,6},{5,7},{6,4},{7,5},{8,10},{9,11},{10,... | collective-permute-start | bytes 1572872 | tf_op jit(solution)/shard_map/ppermute | solution.py:23
  19.6 1.4 %collective-permute-start = (bf16[1,4096]{1,0:T(2,128)(2,1)S(1)}, bf16[1,4096]{1,0:T(2,128)(2,1)S(1)}, u32[]{:S(2)}, u32[]{:S(2)}) collective-permute-start(bf16[1,4096]{1,0:T(2,128)(2,1)S(1)} %copy-done.10), channel_id=1, source_target_pairs={{0,24},{8,0},{16,8},{24,16},{1,25},{9,1},{17,9},{25,17},{2,26},{10... | collective-permute-start | bytes 24584 | tf_op jit(solution)/shard_map/ppermute | solution.py:23
  23.1 0.9 copy-start.5
  24.0 38.7 %collective-permute-start.5 = (bf16[192,2048]{1,0:T(8,128)(2,1)}, bf16[192,2048]{1,0:T(8,128)(2,1)S(1)}, u32[]{:S(2)}, u32[]{:S(2)}) collective-permute-start(bf16[192,2048]{1,0:T(8,128)(2,1)} %get-tuple-element.9), channel_id=1, source_target_pairs={{0,12},{1,13},{2,14},{3,15},{4,8},{5,9},{6,10},{7,11},{8,20},{9,21... | collective-permute-start | bytes 2359304 | tf_op jit(solution)/shard_map/ppermute | solution.py:261
  28.1 37.8 %collective-permute-start.12 = (bf16[512,512]{1,0:T(8,128)(2,1)S(1)}, bf16[512,512]{1,0:T(8,128)(2,1)}, u32[]{:S(2)}, u32[]{:S(2)}) collective-permute-start(bf16[512,512]{1,0:T(8,128)(2,1)S(1)} %get-tuple-element.12.refs_0_), channel_id=1, source_target_pairs={{0,1},{1,0},{2,3},{3,2},{4,5},{5,4},{6,7},{7,6},{8,9},{9,8},{10,11... | collective-permute-start | bytes 1572872 | tf_op jit(solution)/shard_map/ppermute | solution.py:23
  30.3 45.0 %collective-permute-start.1 = (bf16[192,2048]{1,0:T(8,128)(2,1)}, bf16[192,2048]{1,0:T(8,128)(2,1)S(1)}, u32[]{:S(2)}, u32[]{:S(2)}) collective-permute-start(bf16[192,2048]{1,0:T(8,128)(2,1)} %copy-done.5), channel_id=1, source_target_pairs={{0,8},{1,9},{2,10},{3,11},{4,12},{5,13},{6,14},{7,15},{8,16},{9,17... | collective-permute-start | bytes 2359304 | tf_op jit(solution)/shard_map/ppermute | solution.py:261
  30.3 32.4 %collective-permute-start.4 = (bf16[512,512]{1,0:T(8,128)(2,1)}, bf16[512,512]{1,0:T(8,128)(2,1)}, u32[]{:S(2)}, u32[]{:S(2)}) collective-permute-start(bf16[512,512]{1,0:T(8,128)(2,1)} %copy-done), channel_id=1, source_target_pairs={{0,1},{1,0},{2,3},{3,2},{4,5},{5,4},{6,7},{7,6},{8,9},{9,8},{10,11... | collective-permute-start | bytes 1572872 | tf_op jit(solution)/shard_map/ppermute | solution.py:23
  34.0 31.9 %collective-permute-start.13 = (bf16[512,512]{1,0:T(8,128)(2,1)S(1)}, bf16[512,512]{1,0:T(8,128)(2,1)}, u32[]{:S(2)}, u32[]{:S(2)}) collective-permute-start(bf16[512,512]{1,0:T(8,128)(2,1)S(1)} %collective-permute-done.11.refs_1_), channel_id=1, source_target_pairs={{0,1},{1,0},{2,3},{3,2},{4,5},{5,4},{6,7},{7,6},{8,9},{9,8},{10,11... | collective-permute-start | bytes 1572872 | tf_op jit(solution)/shard_map/ppermute | solution.py:23
  62.7 1.0 copy-start.1
  65.5 16.1 %collective-permute-start.6 = (bf16[192,512]{1,0:T(8,128)(2,1)S(1)}, bf16[192,512]{1,0:T(8,128)(2,1)}, u32[]{:S(2)}, u32[]{:S(2)}) collective-permute-start(bf16[192,512]{1,0:T(8,128)(2,1)S(1)} %product.5), channel_id=1, source_target_pairs={{0,4},{1,5},{2,6},{3,7},{4,0},{5,1},{6,2},{7,3},{8,12},{9,13},{10,... | collective-permute-start | bytes 589832 | tf_op jit(solution)/shard_map/ppermute | solution.py:23
  67.6 18.5 %collective-permute-start.14 = (bf16[192,512]{1,0:T(8,128)(2,1)S(1)}, bf16[192,512]{1,0:T(8,128)(2,1)}, u32[]{:S(2)}, u32[]{:S(2)}) collective-permute-start(bf16[192,512]{1,0:T(8,128)(2,1)S(1)} %product.7), channel_id=1, source_target_pairs={{0,4},{1,5},{2,6},{3,7},{4,0},{5,1},{6,2},{7,3},{8,12},{9,13},{10,... | collective-permute-start | bytes 589832 | tf_op jit(solution)/shard_map/ppermute | solution.py:23
  75.3 1.0 copy-start.2
  82.7 5.6 %copy-start.7 = (s32[2,96]{1,0:T(2,128)S(1)}, s32[2,96]{1,0:T(2,128)}, u32[]{:S(2)}) copy-start(s32[2,96]{1,0:T(2,128)} %add.189) | copy-start | bytes 2308
  82.7 5.6 %copy-start.8 = (s32[2,96]{1,0:T(2,128)S(1)}, s32[2,96]{1,0:T(2,128)}, u32[]{:S(2)}) copy-start(s32[2,96]{1,0:T(2,128)} %add.199) | copy-start | bytes 2308
  82.8 5.6 %copy-start.9 = (s32[96]{0:T(128)S(1)}, s32[96]{0:T(128)}, u32[]{:S(2)}) copy-start(s32[96]{0:T(128)} %add.177) | copy-start | bytes 1156
  82.8 7.0 %collective-permute-start.9 = (bf16[192,512]{1,0:T(8,128)(2,1)S(1)}, bf16[192,512]{1,0:T(8,128)(2,1)S(1)}, u32[]{:S(2)}, u32[]{:S(2)}) collective-permute-start(bf16[192,512]{1,0:T(8,128)(2,1)S(1)} %key_sum.1.refs_0_), channel_id=1, source_target_pairs={{0,1},{1,0},{2,3},{3,2},{4,5},{5,4},{6,7},{7,6},{8,9},{9,8},{10,11... | collective-permute-start | bytes 589832 | tf_op jit(solution)/shard_map/ppermute | solution.py:23
  84.3 8.5 %collective-permute-start.7 = (bf16[192,512]{1,0:T(8,128)(2,1)S(1)}, bf16[192,512]{1,0:T(8,128)(2,1)S(1)}, u32[]{:S(2)}, u32[]{:S(2)}) collective-permute-start(bf16[192,512]{1,0:T(8,128)(2,1)S(1)} %key_sum.1.refs_0_), channel_id=1, source_target_pairs={{0,2},{1,3},{2,4},{3,5},{4,6},{5,7},{6,0},{7,1},{8,10},{9,11},{10,... | collective-permute-start | bytes 589832 | tf_op jit(solution)/shard_map/ppermute | solution.py:23
  87.1 6.8 %collective-permute-start.17 = (bf16[192,512]{1,0:T(8,128)(2,1)S(1)}, bf16[192,512]{1,0:T(8,128)(2,1)S(1)}, u32[]{:S(2)}, u32[]{:S(2)}) collective-permute-start(bf16[192,512]{1,0:T(8,128)(2,1)S(1)} %value_sum.1.refs_0_), channel_id=1, source_target_pairs={{0,1},{1,0},{2,3},{3,2},{4,5},{5,4},{6,7},{7,6},{8,9},{9,8},{10,11... | collective-permute-start | bytes 589832 | tf_op jit(solution)/shard_map/ppermute | solution.py:23
  88.3 9.6 %collective-permute-start.15 = (bf16[192,512]{1,0:T(8,128)(2,1)S(1)}, bf16[192,512]{1,0:T(8,128)(2,1)S(1)}, u32[]{:S(2)}, u32[]{:S(2)}) collective-permute-start(bf16[192,512]{1,0:T(8,128)(2,1)S(1)} %value_sum.1.refs_0_), channel_id=1, source_target_pairs={{0,2},{1,3},{2,4},{3,5},{4,6},{5,7},{6,0},{7,1},{8,10},{9,11},{10,... | collective-permute-start | bytes 589832 | tf_op jit(solution)/shard_map/ppermute | solution.py:23
  89.7 12.4 %collective-permute-start.10 = (bf16[192,512]{1,0:T(8,128)(2,1)S(1)}, bf16[192,512]{1,0:T(8,128)(2,1)S(1)}, u32[]{:S(2)}, u32[]{:S(2)}) collective-permute-start(bf16[192,512]{1,0:T(8,128)(2,1)S(1)} %collective-permute-done.9.refs_3_), channel_id=1, source_target_pairs={{0,2},{2,4},{4,6},{6,0},{8,10},{10,12},{12,14},{14,8},{16,18},{18,... | collective-permute-start | bytes 589832 | tf_op jit(solution)/shard_map/ppermute | solution.py:279
  92.9 9.3 %collective-permute-start.8 = (bf16[192,512]{1,0:T(8,128)(2,1)S(1)}, bf16[192,512]{1,0:T(8,128)(2,1)S(1)}, u32[]{:S(2)}, u32[]{:S(2)}) collective-permute-start(bf16[192,512]{1,0:T(8,128)(2,1)S(1)} %collective-permute-done.7.refs_1_), channel_id=1, source_target_pairs={{0,1},{1,2},{2,3},{3,4},{4,5},{5,6},{6,7},{7,0},{8,9},{9,10},{10,1... | collective-permute-start | bytes 589832 | tf_op jit(solution)/shard_map/ppermute | solution.py:23
  93.9 16.2 %collective-permute-start.18 = (bf16[192,512]{1,0:T(8,128)(2,1)S(1)}, bf16[192,512]{1,0:T(8,128)(2,1)S(1)}, u32[]{:S(2)}, u32[]{:S(2)}) collective-permute-start(bf16[192,512]{1,0:T(8,128)(2,1)S(1)} %collective-permute-done.17.refs_3_), channel_id=1, source_target_pairs={{0,2},{2,4},{4,6},{6,0},{8,10},{10,12},{12,14},{14,8},{16,18},{18,... | collective-permute-start | bytes 589832 | tf_op jit(solution)/shard_map/ppermute | solution.py:279
  97.9 12.1 %collective-permute-start.16 = (bf16[192,512]{1,0:T(8,128)(2,1)S(1)}, bf16[192,512]{1,0:T(8,128)(2,1)S(1)}, u32[]{:S(2)}, u32[]{:S(2)}) collective-permute-start(bf16[192,512]{1,0:T(8,128)(2,1)S(1)} %collective-permute-done.15.refs_1_), channel_id=1, source_target_pairs={{0,1},{1,2},{2,3},{3,4},{4,5},{5,6},{6,7},{7,0},{8,9},{9,10},{10,1... | collective-permute-start | bytes 589832 | tf_op jit(solution)/shard_map/ppermute | solution.py:23
  102.2 1.4 %copy-start.4 = (bf16[1,2,96,4096]{3,2,1,0:T(8,128)(2,1)S(1)}, bf16[1,2,96,4096]{3,2,1,0:T(8,128)(2,1)}, u32[]{:S(2)}) copy-start(bf16[1,2,96,4096]{3,2,1,0:T(8,128)(2,1)} %q_ref.1) | copy-start | bytes 4718596

commit v4 on v3

--- a/solution.py
+++ b/solution.py
@@ -125,7 +125,7 @@
 def stacked(refs, odd):
     own, two_back, three_back, beside, from_even = refs
     one_back = jnp.where(odd == 1, beside[...], from_even[...])
-    return jnp.concatenate([own[...], one_back, two_back[...], three_back[...]], axis=0)
+    return jnp.concatenate([three_back[...], two_back[...], one_back, own[...]], axis=0)
 
 
 def score_kernel(odd_ref, q_ref, *refs):
@@ -159,7 +159,7 @@
 
 
 def scored(odd, queries, window, row_pos, col_pos):
-    _, micro_count, tok_rows, width = queries.shape
+    _, micro_count, tok_rows, _ = queries.shape
     keys = WINDOW * tok_rows
     return pl.pallas_call(
         score_kernel,
@@ -233,6 +233,10 @@
     shard_rows, kv_width = weight.shape[0], weight.shape[1] // 2
     _, micro_count, tok_rows, _ = handoff.shape
 
+    next_gain = moved(norm_gain, "section", lambda i: i - 1).astype(jnp.float32)
+    cut_starts = (own_quad + jnp.arange(quads, dtype=jnp.int32)) % quads * (QUAD * shard_rows)
+    cuts = normed_cuts(handoff[0], next_gain, cut_starts)
+
     def over_z(part):
         return moved(part, "ctx", lambda i: i ^ 2)
 
@@ -241,16 +245,14 @@
 
     places = own_place ^ jnp.array([0, 2, 1, 3], jnp.int32)
     starts = places * shard_rows
-    key_part, value_part = weight[:, :kv_width], weight[:, kv_width:]
+    key_part, value_part, cuts = lax.optimization_barrier(
+        (weight[:, :kv_width], weight[:, kv_width:], cuts)
+    )
     key_z = over_z(key_part)
     key_shards = [key_part, key_z, over_y(key_part), over_y(key_z)]
     late_part, _ = lax.optimization_barrier((value_part, key_z))
     value_z = over_z(late_part)
     value_shards = [value_part, value_z, over_y(value_part), over_y(value_z)]
-
-    next_gain = moved(norm_gain, "section", lambda i: i - 1).astype(jnp.float32)
-    cut_starts = (own_quad + jnp.arange(quads, dtype=jnp.int32)) % quads * (QUAD * shard_rows)
-    cuts = normed_cuts(handoff[0], next_gain, cut_starts)
 
     def to_next_section(part, j):
         route = [
@@ -262,19 +264,18 @@
 
     arrived = [to_next_section(cuts[j], j) for j in range(quads)]
 
-    def sent_back(shards):
+    def partials(shards):
+        return [product(starts, arrived[j], shards, jnp.bfloat16) for j in range(1, quads)]
+
+    def sent_back(parts):
         return [
-            moved(
-                product(starts, arrived[j], shards, jnp.bfloat16),
-                "ctx",
-                lambda i, j=j: i - QUAD * j,
-            )
-            for j in range(1, quads)
+            moved(part, "ctx", lambda i, j=j: i - QUAD * j) for j, part in enumerate(parts, start=1)
         ]
 
-    def window_of(block):
-        two_back = moved(block, "ctx", lambda i: i + 2)
-        beside = moved(block, "ctx", lambda i: i ^ 1)
+    def near_blocks(block):
+        return [moved(block, "ctx", lambda i: i + 2), moved(block, "ctx", lambda i: i ^ 1)]
+
+    def window_of(block, two_back, beside):
         three_back = moved(two_back, "ctx", lambda i: i + 1)
         from_even = lax.ppermute(
             beside, "ctx", [(i, (i + 2) % cycle_size) for i in range(0, cycle_size, 2)]
@@ -282,18 +283,15 @@
         return [block, two_back, three_back, beside, from_even]
 
     span_len = tok_rows // 2
-
-    def device_positions(device):
-        span_ids = lax.dynamic_slice_in_dim(span_order, 2 * device, 2, 1)
-        spread = (
-            span_ids[:, :, None] * span_len + jnp.arange(span_len, dtype=jnp.int32)[None, None, :]
-        )
-        return spread.reshape(micro_count, tok_rows)
-
-    own_pos = device_positions(own_index)
-    col_pos = jnp.concatenate(
-        [device_positions((own_index - d) % cycle_size) for d in range(WINDOW)], axis=1
-    )[:, None, :]
+    places_of = span_order[:, :, None] * span_len + jnp.arange(span_len, dtype=jnp.int32)
+    all_pos = places_of.reshape(micro_count, cycle_size * tok_rows)
+    col_pos = lax.dynamic_slice_in_dim(
+        jnp.concatenate([all_pos[:, -(WINDOW - 1) * tok_rows :], all_pos], axis=1),
+        own_index * tok_rows,
+        WINDOW * tok_rows,
+        1,
+    )
+    own_pos = col_pos[:, -tok_rows:]
     half_dim = HD // 2
     frequency = rope_base ** (-2.0 * jnp.arange(half_dim, dtype=jnp.float32) / HD)
     angles = own_pos.reshape(-1, 1).astype(jnp.float32) * frequency
@@ -302,17 +300,22 @@
     sine_part = jnp.concatenate([-sine_part, sine_part], axis=1)
     odd = (own_index % 2).astype(jnp.int32).reshape(1)
 
-    key_parts = sent_back(key_shards)
+    key_parts = sent_back(partials(key_shards))
     own_keys = product(starts, arrived[0], key_shards, jnp.float32)
+    own_values = product(starts, arrived[0], value_shards, jnp.float32)
+    value_partials, key_parts, own_values = lax.optimization_barrier(
+        (partials(value_shards), key_parts, own_values)
+    )
+    value_parts = sent_back(value_partials)
     key_block = block_sum(key_sum_kernel, "key_sum", own_keys, key_parts, cosine, sine_part)
+    key_near, value_parts = lax.optimization_barrier((near_blocks(key_block), value_parts))
+    key_window = window_of(key_block, *key_near)
     weights, sums, log_sums = scored(
-        odd, queries, window_of(key_block), own_pos[:, :, None], col_pos
-    )
-
-    value_parts = sent_back(value_shards)
-    own_values = product(starts, arrived[0], value_shards, jnp.float32)
+        odd, queries, key_window, own_pos[:, :, None], col_pos[:, None, :]
+    )
     value_block = block_sum(value_sum_kernel, "value_sum", own_values, value_parts)
-    out = mixed_values(odd, weights, sums, window_of(value_block))
+    value_window = window_of(value_block, *near_blocks(value_block))
+    out = mixed_values(odd, weights, sums, value_window)
     return (out, log_sums[None])
 
 

time: 113 us -> 119 us (1.053)
  waiting for transfers between devices: 52.7 us -> 69.4 us
  local copies, waits for them, and re-layouts: 11.2 us -> 3.6 us
  Pallas kernels: 20.2 us -> 18.4 us
    ppermute x15, waiting for transfers between devices: 21.2 us -> 54.9 us  [moved(): lax.ppermute(block, axis, [(i, target(i) % size) for i in range(size)])]
    ppermute x2, waiting for transfers between devices: 27.3 us -> 14.5 us  [to_next_section(): return lax.ppermute(part, ('section', 'ctx'), route)]
    add x12 -> x4, local copies, waits for them, and re-layouts: 4.53 us -> 0.24 us  [on_device(): span_order[:, :, None] * span_len + jnp.arange(span_len, dtype=jnp.int32)]
    ppermute x2, waiting for transfers between devices: 4.13 us -> 0.01 us  [window_of(): lax.ppermute(beside, 'ctx', [(i, (i + 2) % cycle_size) for i in range(0,...]
    unnamed x24 -> x12, local copies, waits for them, and re-layouts: 5.19 us -> 1.8 us
    ppermute x15, starting transfers between devices: 15.9 us -> 18.9 us  [moved(): lax.ppermute(block, axis, [(i, target(i) % size) for i in range(size)])]
    ppermute x2, starting transfers between devices: 6.15 us -> 3.91 us  [window_of(): lax.ppermute(beside, 'ctx', [(i, (i + 2) % cycle_size) for i in range(0,...]
    pallas_call x2, Pallas kernels: 2.06 us -> 0.22 us  [block_sum(): pl.pallas_call(kernel, out_shape=jax.ShapeDtypeStruct(own.shape, jnp.bflo...]
  transfers between devices with their start and end apart: 19 -> 19, of which waited for: 9 -> 11; matrix products, arithmetic and copies ran while one was open for 5% -> 2% of each run, Pallas kernels for 16% -> 11%
where the time goes in v4:
time: 119 us; the launch traced here: 118 us
  waiting for transfers between devices  69.4 us (58%)
  starting transfers between devices  25.5 us (21%)
  Pallas kernels  18.4 us (15%)
  local copies, waits for them, and re-layouts  3.6 us (3%)
    ppermute x15, waiting for transfers between devices, moved(): lax.ppermute(block, axis, [(i, target(i) % size) for i in range(size)])  54.9 us
    ppermute x15, starting transfers between devices, moved(): lax.ppermute(block, axis, [(i, target(i) % size) for i in range(size)])  18.9 us
    ppermute x2, waiting for transfers between devices, to_next_section(): return lax.ppermute(part, ('section', 'ctx'), route)  14.5 us
    pallas_call x1, Pallas kernels, scored(): pl.pallas_call(score_kernel, grid=(micro_count, KVH), in_specs=[pl.BlockS...  6.95 us
    pallas_call x4, Pallas kernels, product(): pl.pallas_call(product_kernel, in_specs=[pl.BlockSpec(memory_space=pltpu....  6.53 us
    ppermute x2, starting transfers between devices, window_of(): lax.ppermute(beside, 'ctx', [(i, (i + 2) % cycle_size) for i in range(0,...  3.91 us
    pallas_call x1, Pallas kernels, mixed_values(): pl.pallas_call(mix_kernel, grid=(micro_count,), in_specs=[pl.BlockSpec(me...  3.36 us
    ppermute x2, starting transfers between devices, to_next_section(): return lax.ppermute(part, ('section', 'ctx'), route)  2.67 us
  transfers between devices with their start and end apart: 19, of which 11 were waited for; matrix products, arithmetic and copies ran while one was open for 2% of the time, Pallas kernels for 11%

profile of v4, /device:TPU:0, one launch (start us, length us, event | category | flops | bytes accessed | tf_op | source)
XLA Modules:
  0.0 118.5 jit_solution(11141800673651533107)
XLA Ops:
  0.6 2.4 %collective-permute-start = (bf16[1,4096]{1,0:T(2,128)(2,1)}, bf16[1,4096]{1,0:T(2,128)(2,1)S(1)}, u32[]{:S(2)}, u32[]{:S(2)}) collective-permute-start(bf16[1,4096]{1,0:T(2,128)(2,1)} %param.7), channel_id=1, source_target_pairs={{0,24},{8,0},{16,8},{24,16},{1,25},{9,1},{17,9},{25,17},{2,26},{10... | collective-permute-start | bytes 24584 | tf_op jit(solution)/shard_map/ppermute | solution.py:23
  3.1 1.3 %fusion.4 = (bf16[512,512]{1,0:T(8,128)(2,1)S(1)}, bf16[512,512]{1,0:T(8,128)(2,1)S(1)}) fusion(bf16[512,1024]{1,0:T(8,128)(2,1)} %bitcast.7), kind=kLoop, calls=%fused_computation.19 | loop fusion | bytes 2097152 | tf_op jit(solution)/shard_map/slice | solution.py:249
  4.8 1.3 %norm_cuts.1 = (bf16[192,2048]{1,0:T(8,128)(2,1)S(1)}, bf16[192,2048]{1,0:T(8,128)(2,1)S(1)}) custom-call(s32[2]{0:T(128)S(1)} %fusion.2.starts_ref, bf16[2,96,4096]{2,1,0:T(8,128)(2,1)S(1)} %bitcast.6, f32[1,4096]{1,0:T(1,128)S(1)} %convert_element_type.16.gain_ref), custom_call_target="tpu_custom_call" | custom-call | flops 4718592 | bytes 3145728 | tf_op jit(solution)/shard_map/norm_cuts/pallas_call | solution.py:52
  6.9 0.9 copy-done.3
  7.8 1.6 %collective-permute-start.2 = (bf16[512,512]{1,0:T(8,128)(2,1)S(1)}, bf16[512,512]{1,0:T(8,128)(2,1)S(1)}, u32[]{:S(2)}, u32[]{:S(2)}) collective-permute-start(bf16[512,512]{1,0:T(8,128)(2,1)S(1)} %get-tuple-element.21.refs_0_), channel_id=1, source_target_pairs={{0,2},{1,3},{2,0},{3,1},{4,6},{5,7},{6,4},{7,5},{8,10},{9,11},{10,... | collective-permute-start | bytes 1572872 | tf_op jit(solution)/shard_map/ppermute | solution.py:23
  9.8 1.5 %collective-permute-start.3 = (bf16[512,512]{1,0:T(8,128)(2,1)S(1)}, bf16[512,512]{1,0:T(8,128)(2,1)}, u32[]{:S(2)}, u32[]{:S(2)}) collective-permute-start(bf16[512,512]{1,0:T(8,128)(2,1)S(1)} %get-tuple-element.21.refs_0_), channel_id=1, source_target_pairs={{0,1},{1,0},{2,3},{3,2},{4,5},{5,4},{6,7},{7,6},{8,9},{9,8},{10,11... | collective-permute-start | bytes 1572872 | tf_op jit(solution)/shard_map/ppermute | solution.py:23
  11.3 11.0 %collective-permute-done.2.refs_1_ = bf16[512,512]{1,0:T(8,128)(2,1)S(1)} collective-permute-done((bf16[512,512]{1,0:T(8,128)(2,1)S(1)}, bf16[512,512]{1,0:T(8,128)(2,1)S(1)}, u32[]{:S(2)}, u32[]{:S(2)}) %collective-permute-start.2) | collective-permute-done | bytes 524320 | tf_op jit(solution)/shard_map/ppermute | solution.py:23
  22.3 1.6 %collective-permute-start.6 = (bf16[512,512]{1,0:T(8,128)(2,1)S(1)}, bf16[512,512]{1,0:T(8,128)(2,1)}, u32[]{:S(2)}, u32[]{:S(2)}) collective-permute-start(bf16[512,512]{1,0:T(8,128)(2,1)S(1)} %get-tuple-element.24.refs_0_), channel_id=1, source_target_pairs={{0,2},{1,3},{2,0},{3,1},{4,6},{5,7},{6,4},{7,5},{8,10},{9,11},{10,... | collective-permute-start | bytes 1572872 | tf_op jit(solution)/shard_map/ppermute | solution.py:23
  24.0 2.7 %collective-permute-start.5 = (bf16[192,2048]{1,0:T(8,128)(2,1)}, bf16[192,2048]{1,0:T(8,128)(2,1)S(1)}, u32[]{:S(2)}, u32[]{:S(2)}) collective-permute-start(bf16[192,2048]{1,0:T(8,128)(2,1)} %copy-done.3), channel_id=1, source_target_pairs={{0,12},{1,13},{2,14},{3,15},{4,8},{5,9},{6,10},{7,11},{8,20},{9,21... | collective-permute-start | bytes 2359304 | tf_op jit(solution)/shard_map/ppermute | solution.py:263
  26.8 1.5 %collective-permute-start.4 = (bf16[512,512]{1,0:T(8,128)(2,1)S(1)}, bf16[512,512]{1,0:T(8,128)(2,1)S(1)}, u32[]{:S(2)}, u32[]{:S(2)}) collective-permute-start(bf16[512,512]{1,0:T(8,128)(2,1)S(1)} %collective-permute-done.2.refs_1_), channel_id=1, source_target_pairs={{0,1},{1,0},{2,3},{3,2},{4,5},{5,4},{6,7},{7,6},{8,9},{9,8},{10,11... | collective-permute-start | bytes 1572872 | tf_op jit(solution)/shard_map/ppermute | solution.py:23
  28.9 17.0 %collective-permute-done.6.refs_1_ = bf16[512,512]{1,0:T(8,128)(2,1)} collective-permute-done((bf16[512,512]{1,0:T(8,128)(2,1)S(1)}, bf16[512,512]{1,0:T(8,128)(2,1)}, u32[]{:S(2)}, u32[]{:S(2)}) %collective-permute-start.6) | collective-permute-done | bytes 524320 | tf_op jit(solution)/shard_map/ppermute | solution.py:23
  46.0 1.5 %collective-permute-start.8 = (bf16[512,512]{1,0:T(8,128)(2,1)}, bf16[512,512]{1,0:T(8,128)(2,1)S(1)}, u32[]{:S(2)}, u32[]{:S(2)}) collective-permute-start(bf16[512,512]{1,0:T(8,128)(2,1)} %collective-permute-done.6.refs_1_), channel_id=1, source_target_pairs={{0,1},{1,0},{2,3},{3,2},{4,5},{5,4},{6,7},{7,6},{8,9},{9,8},{10,11... | collective-permute-start | bytes 1572872 | tf_op jit(solution)/shard_map/ppermute | solution.py:23
  47.9 14.5 %collective-permute-done.5.x = bf16[192,2048]{1,0:T(8,128)(2,1)S(1)} collective-permute-done((bf16[192,2048]{1,0:T(8,128)(2,1)}, bf16[192,2048]{1,0:T(8,128)(2,1)S(1)}, u32[]{:S(2)}, u32[]{:S(2)}) %collective-permute-start.5) | collective-permute-done | bytes 786464 | tf_op jit(solution)/shard_map/ppermute | solution.py:263
  62.4 1.6 %product.6 = bf16[192,512]{1,0:T(8,128)(2,1)S(1)} custom-call(s32[4]{0:T(128)S(1)} %xor_multiply_fusion.starts_ref, bf16[192,2048]{1,0:T(8,128)(2,1)S(1)} %collective-permute-done.5.x, bf16[512,512]{1,0:T(8,128)(2,1)S(1)} %get-tuple-element.21.refs_0_, bf16[512,512]{1,0:T(8,128)(2,1)S(1)} %collective-permute-done.2.refs_1_, ...), custom_call_target="tpu_custom_call" | custom-call | flops 402653184 | bytes 2883584 | tf_op jit(solution)/shard_map/product/pallas_call | solution.py:84
  64.3 1.6 %product.4.own = f32[192,512]{1,0:T(8,128)S(1)} custom-call(s32[4]{0:T(128)S(1)} %xor_multiply_fusion.starts_ref, bf16[192,2048]{1,0:T(8,128)(2,1)S(1)} %collective-permute-done.1.x, bf16[512,512]{1,0:T(8,128)(2,1)S(1)} %get-tuple-element.21.refs_0_, bf16[512,512]{1,0:T(8,128)(2,1)S(1)} %collective-permute-done.2.refs_1_, ...), custom_call_target="tpu_custom_call" | custom-call | flops 402653184 | bytes 2883584 | tf_op jit(solution)/shard_map/product/pallas_call | solution.py:84
  65.9 1.6 %product.7.own = f32[192,512]{1,0:T(8,128)S(1)} custom-call(s32[4]{0:T(128)S(1)} %xor_multiply_fusion.starts_ref, bf16[192,2048]{1,0:T(8,128)(2,1)S(1)} %collective-permute-done.1.x, bf16[512,512]{1,0:T(8,128)(2,1)S(1)} %get-tuple-element.24.refs_0_, bf16[512,512]{1,0:T(8,128)(2,1)} %collective-permute-done.6.refs_1_, ...), custom_call_target="tpu_custom_call" | custom-call | flops 402653184 | bytes 2883584 | tf_op jit(solution)/shard_map/product/pallas_call | solution.py:84
  67.6 1.6 %product.5 = bf16[192,512]{1,0:T(8,128)(2,1)S(1)} custom-call(s32[4]{0:T(128)S(1)} %xor_multiply_fusion.starts_ref, bf16[192,2048]{1,0:T(8,128)(2,1)S(1)} %collective-permute-done.5.x, bf16[512,512]{1,0:T(8,128)(2,1)S(1)} %get-tuple-element.24.refs_0_, bf16[512,512]{1,0:T(8,128)(2,1)} %collective-permute-done.6.refs_1_, ...), custom_call_target="tpu_custom_call" | custom-call | flops 402653184 | bytes 2883584 | tf_op jit(solution)/shard_map/product/pallas_call | solution.py:84
  69.2 6.4 %collective-permute-done.9.refs_0_ = bf16[192,512]{1,0:T(8,128)(2,1)S(1)} collective-permute-done((bf16[192,512]{1,0:T(8,128)(2,1)S(1)}, bf16[192,512]{1,0:T(8,128)(2,1)S(1)}, u32[]{:S(2)}, u32[]{:S(2)}) %collective-permute-start.9) | collective-permute-done | bytes 196640 | tf_op jit(solution)/shard_map/ppermute | solution.py:23
  75.8 1.6 %collective-permute-start.11 = (bf16[192,512]{1,0:T(8,128)(2,1)S(1)}, bf16[192,512]{1,0:T(8,128)(2,1)S(1)}, u32[]{:S(2)}, u32[]{:S(2)}) collective-permute-start(bf16[192,512]{1,0:T(8,128)(2,1)S(1)} %key_sum.1.refs_0_), channel_id=1, source_target_pairs={{0,1},{1,0},{2,3},{3,2},{4,5},{5,4},{6,7},{7,6},{8,9},{9,8},{10,11... | collective-permute-start | bytes 589832 | tf_op jit(solution)/shard_map/ppermute | solution.py:23
  77.4 2.0 %collective-permute-start.12 = (bf16[192,512]{1,0:T(8,128)(2,1)S(1)}, bf16[192,512]{1,0:T(8,128)(2,1)S(1)}, u32[]{:S(2)}, u32[]{:S(2)}) collective-permute-start(bf16[192,512]{1,0:T(8,128)(2,1)S(1)} %product.5), channel_id=1, source_target_pairs={{0,4},{1,5},{2,6},{3,7},{4,0},{5,1},{6,2},{7,3},{8,12},{9,13},{10,... | collective-permute-start | bytes 589832 | tf_op jit(solution)/shard_map/ppermute | solution.py:23
  79.4 3.3 %collective-permute-done.11.refs_3_ = bf16[192,512]{1,0:T(8,128)(2,1)S(1)} collective-permute-done((bf16[192,512]{1,0:T(8,128)(2,1)S(1)}, bf16[192,512]{1,0:T(8,128)(2,1)S(1)}, u32[]{:S(2)}, u32[]{:S(2)}) %collective-permute-start.11) | collective-permute-done | bytes 196640 | tf_op jit(solution)/shard_map/ppermute | solution.py:23
  82.7 4.4 %collective-permute-done.10.refs_1_ = bf16[192,512]{1,0:T(8,128)(2,1)S(1)} collective-permute-done((bf16[192,512]{1,0:T(8,128)(2,1)S(1)}, bf16[192,512]{1,0:T(8,128)(2,1)S(1)}, u32[]{:S(2)}, u32[]{:S(2)}) %collective-permute-start.10) | collective-permute-done | bytes 196640 | tf_op jit(solution)/shard_map/ppermute | solution.py:23
  87.0 6.2 %collective-permute-done.12.refs_0_ = bf16[192,512]{1,0:T(8,128)(2,1)S(1)} collective-permute-done((bf16[192,512]{1,0:T(8,128)(2,1)S(1)}, bf16[192,512]{1,0:T(8,128)(2,1)S(1)}, u32[]{:S(2)}, u32[]{:S(2)}) %collective-permute-start.12) | collective-permute-done | bytes 196640 | tf_op jit(solution)/shard_map/ppermute | solution.py:23
  93.9 1.5 %collective-permute-start.13 = (bf16[192,512]{1,0:T(8,128)(2,1)S(1)}, bf16[192,512]{1,0:T(8,128)(2,1)S(1)}, u32[]{:S(2)}, u32[]{:S(2)}) collective-permute-start(bf16[192,512]{1,0:T(8,128)(2,1)S(1)} %collective-permute-done.10.refs_1_), channel_id=1, source_target_pairs={{0,1},{1,2},{2,3},{3,4},{4,5},{5,6},{6,7},{7,0},{8,9},{9,10},{10,1... | collective-permute-start | bytes 589832 | tf_op jit(solution)/shard_map/ppermute | solution.py:23
  95.4 2.0 %collective-permute-start.14 = (bf16[192,512]{1,0:T(8,128)(2,1)S(1)}, bf16[192,512]{1,0:T(8,128)(2,1)S(1)}, u32[]{:S(2)}, u32[]{:S(2)}) collective-permute-start(bf16[192,512]{1,0:T(8,128)(2,1)S(1)} %collective-permute-done.11.refs_3_), channel_id=1, source_target_pairs={{0,2},{2,4},{4,6},{6,0},{8,10},{10,12},{12,14},{14,8},{16,18},{18,... | collective-permute-start | bytes 589832 | tf_op jit(solution)/shard_map/ppermute | solution.py:280
  97.4 1.9 %collective-permute-done.17.refs_3_ = bf16[192,512]{1,0:T(8,128)(2,1)S(1)} collective-permute-done((bf16[192,512]{1,0:T(8,128)(2,1)S(1)}, bf16[192,512]{1,0:T(8,128)(2,1)S(1)}, u32[]{:S(2)}, u32[]{:S(2)}) %collective-permute-start.17) | collective-permute-done | bytes 196640 | tf_op jit(solution)/shard_map/ppermute | solution.py:23
  99.3 1.9 %collective-permute-start.18 = (bf16[192,512]{1,0:T(8,128)(2,1)S(1)}, bf16[192,512]{1,0:T(8,128)(2,1)S(1)}, u32[]{:S(2)}, u32[]{:S(2)}) collective-permute-start(bf16[192,512]{1,0:T(8,128)(2,1)S(1)} %collective-permute-done.17.refs_3_), channel_id=1, source_target_pairs={{0,2},{2,4},{4,6},{6,0},{8,10},{10,12},{12,14},{14,8},{16,18},{18,... | collective-permute-start | bytes 589832 | tf_op jit(solution)/shard_map/ppermute | solution.py:280
  101.2 1.3 %collective-permute-done.15.refs_1_ = bf16[192,512]{1,0:T(8,128)(2,1)S(1)} collective-permute-done((bf16[192,512]{1,0:T(8,128)(2,1)S(1)}, bf16[192,512]{1,0:T(8,128)(2,1)S(1)}, u32[]{:S(2)}, u32[]{:S(2)}) %collective-permute-start.15) | collective-permute-done | bytes 196640 | tf_op jit(solution)/shard_map/ppermute | solution.py:23
  102.5 2.4 %collective-permute-start.16 = (bf16[192,512]{1,0:T(8,128)(2,1)S(1)}, bf16[192,512]{1,0:T(8,128)(2,1)}, u32[]{:S(2)}, u32[]{:S(2)}) collective-permute-start(bf16[192,512]{1,0:T(8,128)(2,1)S(1)} %collective-permute-done.15.refs_1_), channel_id=1, source_target_pairs={{0,1},{1,2},{2,3},{3,4},{4,5},{5,6},{6,7},{7,0},{8,9},{9,10},{10,1... | collective-permute-start | bytes 589832 | tf_op jit(solution)/shard_map/ppermute | solution.py:23
  105.0 3.1 %collective-permute-done.13.refs_2_ = bf16[192,512]{1,0:T(8,128)(2,1)S(1)} collective-permute-done((bf16[192,512]{1,0:T(8,128)(2,1)S(1)}, bf16[192,512]{1,0:T(8,128)(2,1)S(1)}, u32[]{:S(2)}, u32[]{:S(2)}) %collective-permute-start.13) | collective-permute-done | bytes 196640 | tf_op jit(solution)/shard_map/ppermute | solution.py:23
  108.1 6.9 %scores.1 = (bf16[2,4,768,384]{3,2,1,0:T(8,128)(2,1)S(1)}, f32[2,4,96,128]{3,2,1,0:T(8,128)S(1)}, f32[2,32,96]{2,1,0:T(8,128)}) custom-call(s32[1]{0:T(128)} %bitcast.odd_ref, bf16[1,2,96,4096]{3,2,1,0:T(8,128)(2,1)S(1)} %copy-done.1, bf16[192,512]{1,0:T(8,128)(2,1)S(1)} %key_sum.1.refs_0_, bf16[192,512]{1,0:T(8,128)(2,1)S(1)} %collective-permute-done.10.refs_1_, ...), custom_call_target="tpu_custom_call" | custom-call | flops 603979776 | bytes 8388608 | tf_op jit(solution)/shard_map/scores/pallas_call | solution.py:164
  115.1 3.4 %mixed_values.1 = bf16[1,2,96,4096]{3,2,1,0:T(8,128)(2,1)} custom-call(s32[1]{0:T(128)} %bitcast.odd_ref, bf16[2,4,768,384]{3,2,1,0:T(8,128)(2,1)S(1)} %get-tuple-element.29.weights, f32[2,4,96,128]{3,2,1,0:T(8,128)S(1)} %get-tuple-element.30.sums, bf16[192,512]{1,0:T(8,128)(2,1)S(1)} %value_sum.1.refs_0_, ...), custom_call_target="tpu_custom_call" | custom-call | flops 603979776 | bytes 8388608 | tf_op jit(solution)/shard_map/mixed_values/pallas_call | solution.py:209
  (46 shorter events, 3.9 us)
Async XLA Ops:
  0.6 4.1 %copy-start = (bf16[1,2,96,4096]{3,2,1,0:T(8,128)(2,1)S(1)}, bf16[1,2,96,4096]{3,2,1,0:T(8,128)(2,1)}, u32[]{:S(2)}) copy-start(bf16[1,2,96,4096]{3,2,1,0:T(8,128)(2,1)} %param.6) | copy-start | bytes 4718596
  0.6 4.1 %collective-permute-start = (bf16[1,4096]{1,0:T(2,128)(2,1)}, bf16[1,4096]{1,0:T(2,128)(2,1)S(1)}, u32[]{:S(2)}, u32[]{:S(2)}) collective-permute-start(bf16[1,4096]{1,0:T(2,128)(2,1)} %param.7), channel_id=1, source_target_pairs={{0,24},{8,0},{16,8},{24,16},{1,25},{9,1},{17,9},{25,17},{2,26},{10... | collective-permute-start | bytes 24584 | tf_op jit(solution)/shard_map/ppermute | solution.py:23
  3.1 6.4 %copy-start.4 = (s32[2,16]{1,0:T(2,128)S(1)}, s32[2,16]{1,0:T(2,128)}, u32[]{:S(2)}) copy-start(s32[2,16]{1,0:T(2,128)} %param.10) | copy-start | bytes 388
  3.1 25.3 %copy-start.5 = (s32[4]{0:T(128)S(1)}, s32[4]{0:T(128)}, u32[]{:S(2)}) copy-start(s32[4]{0:T(128)} %constant.66.clone) | copy-start | bytes 52
  6.1 0.9 copy-start.2
  6.9 0.9 copy-start.3
  7.8 14.5 %collective-permute-start.2 = (bf16[512,512]{1,0:T(8,128)(2,1)S(1)}, bf16[512,512]{1,0:T(8,128)(2,1)S(1)}, u32[]{:S(2)}, u32[]{:S(2)}) collective-permute-start(bf16[512,512]{1,0:T(8,128)(2,1)S(1)} %get-tuple-element.21.refs_0_), channel_id=1, source_target_pairs={{0,2},{1,3},{2,0},{3,1},{4,6},{5,7},{6,4},{7,5},{8,10},{9,11},{10,... | collective-permute-start | bytes 1572872 | tf_op jit(solution)/shard_map/ppermute | solution.py:23
  9.8 18.6 %collective-permute-start.3 = (bf16[512,512]{1,0:T(8,128)(2,1)S(1)}, bf16[512,512]{1,0:T(8,128)(2,1)}, u32[]{:S(2)}, u32[]{:S(2)}) collective-permute-start(bf16[512,512]{1,0:T(8,128)(2,1)S(1)} %get-tuple-element.21.refs_0_), channel_id=1, source_target_pairs={{0,1},{1,0},{2,3},{3,2},{4,5},{5,4},{6,7},{7,6},{8,9},{9,8},{10,11... | collective-permute-start | bytes 1572872 | tf_op jit(solution)/shard_map/ppermute | solution.py:23
  22.3 23.6 %collective-permute-start.6 = (bf16[512,512]{1,0:T(8,128)(2,1)S(1)}, bf16[512,512]{1,0:T(8,128)(2,1)}, u32[]{:S(2)}, u32[]{:S(2)}) collective-permute-start(bf16[512,512]{1,0:T(8,128)(2,1)S(1)} %get-tuple-element.24.refs_0_), channel_id=1, source_target_pairs={{0,2},{1,3},{2,0},{3,1},{4,6},{5,7},{6,4},{7,5},{8,10},{9,11},{10,... | collective-permute-start | bytes 1572872 | tf_op jit(solution)/shard_map/ppermute | solution.py:23
  24.0 40.3 %collective-permute-start.1 = (bf16[192,2048]{1,0:T(8,128)(2,1)}, bf16[192,2048]{1,0:T(8,128)(2,1)S(1)}, u32[]{:S(2)}, u32[]{:S(2)}) collective-permute-start(bf16[192,2048]{1,0:T(8,128)(2,1)} %copy-done.2), channel_id=1, source_target_pairs={{0,8},{1,9},{2,10},{3,11},{4,12},{5,13},{6,14},{7,15},{8,16},{9,17... | collective-permute-start | bytes 2359304 | tf_op jit(solution)/shard_map/ppermute | solution.py:263
  24.0 38.4 %collective-permute-start.5 = (bf16[192,2048]{1,0:T(8,128)(2,1)}, bf16[192,2048]{1,0:T(8,128)(2,1)S(1)}, u32[]{:S(2)}, u32[]{:S(2)}) collective-permute-start(bf16[192,2048]{1,0:T(8,128)(2,1)} %copy-done.3), channel_id=1, source_target_pairs={{0,12},{1,13},{2,14},{3,15},{4,8},{5,9},{6,10},{7,11},{8,20},{9,21... | collective-permute-start | bytes 2359304 | tf_op jit(solution)/shard_map/ppermute | solution.py:263
  26.8 35.6 %collective-permute-start.4 = (bf16[512,512]{1,0:T(8,128)(2,1)S(1)}, bf16[512,512]{1,0:T(8,128)(2,1)S(1)}, u32[]{:S(2)}, u32[]{:S(2)}) collective-permute-start(bf16[512,512]{1,0:T(8,128)(2,1)S(1)} %collective-permute-done.2.refs_1_), channel_id=1, source_target_pairs={{0,1},{1,0},{2,3},{3,2},{4,5},{5,4},{6,7},{7,6},{8,9},{9,8},{10,11... | collective-permute-start | bytes 1572872 | tf_op jit(solution)/shard_map/ppermute | solution.py:23
  28.4 37.5 %collective-permute-start.7 = (bf16[512,512]{1,0:T(8,128)(2,1)S(1)}, bf16[512,512]{1,0:T(8,128)(2,1)S(1)}, u32[]{:S(2)}, u32[]{:S(2)}) collective-permute-start(bf16[512,512]{1,0:T(8,128)(2,1)S(1)} %get-tuple-element.24.refs_0_), channel_id=1, source_target_pairs={{0,1},{1,0},{2,3},{3,2},{4,5},{5,4},{6,7},{7,6},{8,9},{9,8},{10,11... | collective-permute-start | bytes 1572872 | tf_op jit(solution)/shard_map/ppermute | solution.py:23
  46.0 19.9 %collective-permute-start.8 = (bf16[512,512]{1,0:T(8,128)(2,1)}, bf16[512,512]{1,0:T(8,128)(2,1)S(1)}, u32[]{:S(2)}, u32[]{:S(2)}) collective-permute-start(bf16[512,512]{1,0:T(8,128)(2,1)} %collective-permute-done.6.refs_1_), channel_id=1, source_target_pairs={{0,1},{1,0},{2,3},{3,2},{4,5},{5,4},{6,7},{7,6},{8,9},{9,8},{10,11... | collective-permute-start | bytes 1572872 | tf_op jit(solution)/shard_map/ppermute | solution.py:23
  64.0 11.6 %collective-permute-start.9 = (bf16[192,512]{1,0:T(8,128)(2,1)S(1)}, bf16[192,512]{1,0:T(8,128)(2,1)S(1)}, u32[]{:S(2)}, u32[]{:S(2)}) collective-permute-start(bf16[192,512]{1,0:T(8,128)(2,1)S(1)} %product.6), channel_id=1, source_target_pairs={{0,4},{1,5},{2,6},{3,7},{4,0},{5,1},{6,2},{7,3},{8,12},{9,13},{10,... | collective-permute-start | bytes 589832 | tf_op jit(solution)/shard_map/ppermute | solution.py:23
  69.2 38.9 %copy-start.1 = (bf16[1,2,96,4096]{3,2,1,0:T(8,128)(2,1)S(1)}, bf16[1,2,96,4096]{3,2,1,0:T(8,128)(2,1)}, u32[]{:S(2)}) copy-start(bf16[1,2,96,4096]{3,2,1,0:T(8,128)(2,1)} %q_ref.1) | copy-start | bytes 4718596
  75.8 6.9 %collective-permute-start.11 = (bf16[192,512]{1,0:T(8,128)(2,1)S(1)}, bf16[192,512]{1,0:T(8,128)(2,1)S(1)}, u32[]{:S(2)}, u32[]{:S(2)}) collective-permute-start(bf16[192,512]{1,0:T(8,128)(2,1)S(1)} %key_sum.1.refs_0_), channel_id=1, source_target_pairs={{0,1},{1,0},{2,3},{3,2},{4,5},{5,4},{6,7},{7,6},{8,9},{9,8},{10,11... | collective-permute-start | bytes 589832 | tf_op jit(solution)/shard_map/ppermute | solution.py:23
  77.4 9.7 %collective-permute-start.10 = (bf16[192,512]{1,0:T(8,128)(2,1)S(1)}, bf16[192,512]{1,0:T(8,128)(2,1)S(1)}, u32[]{:S(2)}, u32[]{:S(2)}) collective-permute-start(bf16[192,512]{1,0:T(8,128)(2,1)S(1)} %key_sum.1.refs_0_), channel_id=1, source_target_pairs={{0,2},{1,3},{2,4},{3,5},{4,6},{5,7},{6,0},{7,1},{8,10},{9,11},{10,... | collective-permute-start | bytes 589832 | tf_op jit(solution)/shard_map/ppermute | solution.py:23
  77.4 15.9 %collective-permute-start.12 = (bf16[192,512]{1,0:T(8,128)(2,1)S(1)}, bf16[192,512]{1,0:T(8,128)(2,1)S(1)}, u32[]{:S(2)}, u32[]{:S(2)}) collective-permute-start(bf16[192,512]{1,0:T(8,128)(2,1)S(1)} %product.5), channel_id=1, source_target_pairs={{0,4},{1,5},{2,6},{3,7},{4,0},{5,1},{6,2},{7,3},{8,12},{9,13},{10,... | collective-permute-start | bytes 589832 | tf_op jit(solution)/shard_map/ppermute | solution.py:23
  93.3 6.0 %collective-permute-start.17 = (bf16[192,512]{1,0:T(8,128)(2,1)S(1)}, bf16[192,512]{1,0:T(8,128)(2,1)S(1)}, u32[]{:S(2)}, u32[]{:S(2)}) collective-permute-start(bf16[192,512]{1,0:T(8,128)(2,1)S(1)} %value_sum.1.refs_0_), channel_id=1, source_target_pairs={{0,1},{1,0},{2,3},{3,2},{4,5},{5,4},{6,7},{7,6},{8,9},{9,8},{10,11... | collective-permute-start | bytes 589832 | tf_op jit(solution)/shard_map/ppermute | solution.py:23
  93.9 8.6 %collective-permute-start.15 = (bf16[192,512]{1,0:T(8,128)(2,1)S(1)}, bf16[192,512]{1,0:T(8,128)(2,1)S(1)}, u32[]{:S(2)}, u32[]{:S(2)}) collective-permute-start(bf16[192,512]{1,0:T(8,128)(2,1)S(1)} %value_sum.1.refs_0_), channel_id=1, source_target_pairs={{0,2},{1,3},{2,4},{3,5},{4,6},{5,7},{6,0},{7,1},{8,10},{9,11},{10,... | collective-permute-start | bytes 589832 | tf_op jit(solution)/shard_map/ppermute | solution.py:23
  93.9 14.3 %collective-permute-start.13 = (bf16[192,512]{1,0:T(8,128)(2,1)S(1)}, bf16[192,512]{1,0:T(8,128)(2,1)S(1)}, u32[]{:S(2)}, u32[]{:S(2)}) collective-permute-start(bf16[192,512]{1,0:T(8,128)(2,1)S(1)} %collective-permute-done.10.refs_1_), channel_id=1, source_target_pairs={{0,1},{1,2},{2,3},{3,4},{4,5},{5,6},{6,7},{7,0},{8,9},{9,10},{10,1... | collective-permute-start | bytes 589832 | tf_op jit(solution)/shard_map/ppermute | solution.py:23
  95.4 12.7 %collective-permute-start.14 = (bf16[192,512]{1,0:T(8,128)(2,1)S(1)}, bf16[192,512]{1,0:T(8,128)(2,1)S(1)}, u32[]{:S(2)}, u32[]{:S(2)}) collective-permute-start(bf16[192,512]{1,0:T(8,128)(2,1)S(1)} %collective-permute-done.11.refs_3_), channel_id=1, source_target_pairs={{0,2},{2,4},{4,6},{6,0},{8,10},{10,12},{12,14},{14,8},{16,18},{18,... | collective-permute-start | bytes 589832 | tf_op jit(solution)/shard_map/ppermute | solution.py:280
  99.3 15.8 %collective-permute-start.18 = (bf16[192,512]{1,0:T(8,128)(2,1)S(1)}, bf16[192,512]{1,0:T(8,128)(2,1)S(1)}, u32[]{:S(2)}, u32[]{:S(2)}) collective-permute-start(bf16[192,512]{1,0:T(8,128)(2,1)S(1)} %collective-permute-done.17.refs_3_), channel_id=1, source_target_pairs={{0,2},{2,4},{4,6},{6,0},{8,10},{10,12},{12,14},{14,8},{16,18},{18,... | collective-permute-start | bytes 589832 | tf_op jit(solution)/shard_map/ppermute | solution.py:280
  102.5 12.6 %collective-permute-start.16 = (bf16[192,512]{1,0:T(8,128)(2,1)S(1)}, bf16[192,512]{1,0:T(8,128)(2,1)}, u32[]{:S(2)}, u32[]{:S(2)}) collective-permute-start(bf16[192,512]{1,0:T(8,128)(2,1)S(1)} %collective-permute-done.15.refs_1_), channel_id=1, source_target_pairs={{0,1},{1,2},{2,3},{3,4},{4,5},{5,6},{6,7},{7,0},{8,9},{9,10},{10,1... | collective-permute-start | bytes 589832 | tf_op jit(solution)/shard_map/ppermute | solution.py:23

commit v5 on v4

--- a/solution.py
+++ b/solution.py
@@ -86,7 +86,7 @@
         in_specs=[pl.BlockSpec(memory_space=pltpu.SMEM)] + [vmem] * (1 + QUAD),
         out_shape=jax.ShapeDtypeStruct((rows, width), dtype),
         compiler_params=params(24),
-        cost_estimate=cost(2 * rows * part * width, 2 * (rows * part + part * width)),
+        cost_estimate=cost(8 * rows * part * width, 8 * (rows * part + part * width)),
         name="product",
     )(starts, x, *shards)
 

time: 119 us -> 114 us (0.958)
  waiting for transfers between devices: 69.4 us -> 64.6 us
    ppermute x2, waiting for transfers between devices: 14.5 us -> 0.01 us  [to_next_section(): return lax.ppermute(part, ('section', 'ctx'), route)]
    ppermute x15, waiting for transfers between devices: 54.9 us -> 64.6 us  [moved(): lax.ppermute(block, axis, [(i, target(i) % size) for i in range(size)])]
  transfers between devices with their start and end apart: 19 -> 19, of which waited for: 11 -> 10; matrix products, arithmetic and copies ran while one was open for 2% -> 2% of each run, Pallas kernels for 11% -> 12%
where the time goes in v5:
time: 114 us
  waiting for transfers between devices  64.6 us (57%)
  starting transfers between devices  26.5 us (23%)
  Pallas kernels  18.3 us (16%)
  local copies, waits for them, and re-layouts  2.69 us (2%)
    ppermute x15, waiting for transfers between devices, moved(): lax.ppermute(block, axis, [(i, target(i) % size) for i in range(size)])  64.6 us
    ppermute x15, starting transfers between devices, moved(): lax.ppermute(block, axis, [(i, target(i) % size) for i in range(size)])  19.9 us
    pallas_call x1, Pallas kernels, scored(): pl.pallas_call(score_kernel, grid=(micro_count, KVH), in_specs=[pl.BlockS...  6.94 us
    pallas_call x4, Pallas kernels, product(): pl.pallas_call(product_kernel, in_specs=[pl.BlockSpec(memory_space=pltpu....  6.49 us
    ppermute x2, starting transfers between devices, window_of(): lax.ppermute(beside, 'ctx', [(i, (i + 2) % cycle_size) for i in range(0,...  4.27 us
    pallas_call x1, Pallas kernels, mixed_values(): pl.pallas_call(mix_kernel, grid=(micro_count,), in_specs=[pl.BlockSpec(me...  3.36 us
  transfers between devices with their start and end apart: 19, of which 10 were waited for; matrix products, arithmetic and copies ran while one was open for 2% of the time, Pallas kernels for 12%

profile of v5, /device:TPU:0, one launch (start us, length us, event | category | flops | bytes accessed | tf_op | source)
XLA Modules:
  0.0 113.7 jit_solution(7668567063972895262)
XLA Ops:
  0.6 2.4 %collective-permute-start = (bf16[1,4096]{1,0:T(2,128)(2,1)}, bf16[1,4096]{1,0:T(2,128)(2,1)S(1)}, u32[]{:S(2)}, u32[]{:S(2)}) collective-permute-start(bf16[1,4096]{1,0:T(2,128)(2,1)} %param.7), channel_id=1, source_target_pairs={{0,24},{8,0},{16,8},{24,16},{1,25},{9,1},{17,9},{25,17},{2,26},{10... | collective-permute-start | bytes 24584 | tf_op jit(solution)/shard_map/ppermute | solution.py:23
  3.1 1.3 %fusion.4 = (bf16[512,512]{1,0:T(8,128)(2,1)S(1)}, bf16[512,512]{1,0:T(8,128)(2,1)S(1)}) fusion(bf16[512,1024]{1,0:T(8,128)(2,1)} %bitcast.7), kind=kLoop, calls=%fused_computation.19 | loop fusion | bytes 2097152 | tf_op jit(solution)/shard_map/slice | solution.py:249
  4.8 1.3 %norm_cuts.1 = (bf16[192,2048]{1,0:T(8,128)(2,1)S(1)}, bf16[192,2048]{1,0:T(8,128)(2,1)S(1)}) custom-call(s32[2]{0:T(128)S(1)} %fusion.2.starts_ref, bf16[2,96,4096]{2,1,0:T(8,128)(2,1)S(1)} %bitcast.6, f32[1,4096]{1,0:T(1,128)S(1)} %convert_element_type.16.gain_ref), custom_call_target="tpu_custom_call" | custom-call | flops 4718592 | bytes 3145728 | tf_op jit(solution)/shard_map/norm_cuts/pallas_call | solution.py:52
  6.1 0.9 copy-done.2
  6.9 1.6 %collective-permute-start.2 = (bf16[512,512]{1,0:T(8,128)(2,1)S(1)}, bf16[512,512]{1,0:T(8,128)(2,1)S(1)}, u32[]{:S(2)}, u32[]{:S(2)}) collective-permute-start(bf16[512,512]{1,0:T(8,128)(2,1)S(1)} %get-tuple-element.21.refs_0_), channel_id=1, source_target_pairs={{0,2},{1,3},{2,0},{3,1},{4,6},{5,7},{6,4},{7,5},{8,10},{9,11},{10,... | collective-permute-start | bytes 1572872 | tf_op jit(solution)/shard_map/ppermute | solution.py:23
  8.9 1.5 %collective-permute-start.3 = (bf16[512,512]{1,0:T(8,128)(2,1)S(1)}, bf16[512,512]{1,0:T(8,128)(2,1)}, u32[]{:S(2)}, u32[]{:S(2)}) collective-permute-start(bf16[512,512]{1,0:T(8,128)(2,1)S(1)} %get-tuple-element.21.refs_0_), channel_id=1, source_target_pairs={{0,1},{1,0},{2,3},{3,2},{4,5},{5,4},{6,7},{7,6},{8,9},{9,8},{10,11... | collective-permute-start | bytes 1572872 | tf_op jit(solution)/shard_map/ppermute | solution.py:23
  10.4 2.3 %collective-permute-start.5 = (bf16[192,2048]{1,0:T(8,128)(2,1)}, bf16[192,2048]{1,0:T(8,128)(2,1)S(1)}, u32[]{:S(2)}, u32[]{:S(2)}) collective-permute-start(bf16[192,2048]{1,0:T(8,128)(2,1)} %copy-done.2), channel_id=1, source_target_pairs={{0,12},{1,13},{2,14},{3,15},{4,8},{5,9},{6,10},{7,11},{8,20},{9,21... | collective-permute-start | bytes 2359304 | tf_op jit(solution)/shard_map/ppermute | solution.py:263
  12.7 17.8 %collective-permute-done.2.refs_1_ = bf16[512,512]{1,0:T(8,128)(2,1)S(1)} collective-permute-done((bf16[512,512]{1,0:T(8,128)(2,1)S(1)}, bf16[512,512]{1,0:T(8,128)(2,1)S(1)}, u32[]{:S(2)}, u32[]{:S(2)}) %collective-permute-start.2) | collective-permute-done | bytes 524320 | tf_op jit(solution)/shard_map/ppermute | solution.py:23
  30.6 2.6 %collective-permute-start.4 = (bf16[512,512]{1,0:T(8,128)(2,1)S(1)}, bf16[512,512]{1,0:T(8,128)(2,1)S(1)}, u32[]{:S(2)}, u32[]{:S(2)}) collective-permute-start(bf16[512,512]{1,0:T(8,128)(2,1)S(1)} %collective-permute-done.2.refs_1_), channel_id=1, source_target_pairs={{0,1},{1,0},{2,3},{3,2},{4,5},{5,4},{6,7},{7,6},{8,9},{9,8},{10,11... | collective-permute-start | bytes 1572872 | tf_op jit(solution)/shard_map/ppermute | solution.py:23
  33.9 18.2 %collective-permute-done.6.refs_1_ = bf16[512,512]{1,0:T(8,128)(2,1)} collective-permute-done((bf16[512,512]{1,0:T(8,128)(2,1)S(1)}, bf16[512,512]{1,0:T(8,128)(2,1)}, u32[]{:S(2)}, u32[]{:S(2)}) %collective-permute-start.6) | collective-permute-done | bytes 524320 | tf_op jit(solution)/shard_map/ppermute | solution.py:23
  52.0 1.5 %collective-permute-start.8 = (bf16[512,512]{1,0:T(8,128)(2,1)}, bf16[512,512]{1,0:T(8,128)(2,1)S(1)}, u32[]{:S(2)}, u32[]{:S(2)}) collective-permute-start(bf16[512,512]{1,0:T(8,128)(2,1)} %collective-permute-done.6.refs_1_), channel_id=1, source_target_pairs={{0,1},{1,0},{2,3},{3,2},{4,5},{5,4},{6,7},{7,6},{8,9},{9,8},{10,11... | collective-permute-start | bytes 1572872 | tf_op jit(solution)/shard_map/ppermute | solution.py:23
  53.6 1.6 %product.6 = bf16[192,512]{1,0:T(8,128)(2,1)S(1)} custom-call(s32[4]{0:T(128)S(1)} %xor_multiply_fusion.starts_ref, bf16[192,2048]{1,0:T(8,128)(2,1)S(1)} %collective-permute-done.5.x, bf16[512,512]{1,0:T(8,128)(2,1)S(1)} %get-tuple-element.21.refs_0_, bf16[512,512]{1,0:T(8,128)(2,1)S(1)} %collective-permute-done.2.refs_1_, ...), custom_call_target="tpu_custom_call" | custom-call | flops 1610612736 | bytes 11534336 | tf_op jit(solution)/shard_map/product/pallas_call | solution.py:84
  55.2 1.6 %collective-permute-start.9 = (bf16[192,512]{1,0:T(8,128)(2,1)S(1)}, bf16[192,512]{1,0:T(8,128)(2,1)S(1)}, u32[]{:S(2)}, u32[]{:S(2)}) collective-permute-start(bf16[192,512]{1,0:T(8,128)(2,1)S(1)} %product.6), channel_id=1, source_target_pairs={{0,4},{1,5},{2,6},{3,7},{4,0},{5,1},{6,2},{7,3},{8,12},{9,13},{10,... | collective-permute-start | bytes 589832 | tf_op jit(solution)/shard_map/ppermute | solution.py:23
  56.8 1.6 %product.4.own = f32[192,512]{1,0:T(8,128)S(1)} custom-call(s32[4]{0:T(128)S(1)} %xor_multiply_fusion.starts_ref, bf16[192,2048]{1,0:T(8,128)(2,1)S(1)} %collective-permute-done.1.x, bf16[512,512]{1,0:T(8,128)(2,1)S(1)} %get-tuple-element.21.refs_0_, bf16[512,512]{1,0:T(8,128)(2,1)S(1)} %collective-permute-done.2.refs_1_, ...), custom_call_target="tpu_custom_call" | custom-call | flops 1610612736 | bytes 11534336 | tf_op jit(solution)/shard_map/product/pallas_call | solution.py:84
  58.5 9.1 %collective-permute-done.8.refs_3_ = bf16[512,512]{1,0:T(8,128)(2,1)S(1)} collective-permute-done((bf16[512,512]{1,0:T(8,128)(2,1)}, bf16[512,512]{1,0:T(8,128)(2,1)S(1)}, u32[]{:S(2)}, u32[]{:S(2)}) %collective-permute-start.8) | collective-permute-done | bytes 524320 | tf_op jit(solution)/shard_map/ppermute | solution.py:23
  67.6 1.6 %product.7.own = f32[192,512]{1,0:T(8,128)S(1)} custom-call(s32[4]{0:T(128)S(1)} %xor_multiply_fusion.starts_ref, bf16[192,2048]{1,0:T(8,128)(2,1)S(1)} %collective-permute-done.1.x, bf16[512,512]{1,0:T(8,128)(2,1)S(1)} %get-tuple-element.24.refs_0_, bf16[512,512]{1,0:T(8,128)(2,1)} %collective-permute-done.6.refs_1_, ...), custom_call_target="tpu_custom_call" | custom-call | flops 1610612736 | bytes 11534336 | tf_op jit(solution)/shard_map/product/pallas_call | solution.py:84
  69.2 1.6 %product.5 = bf16[192,512]{1,0:T(8,128)(2,1)S(1)} custom-call(s32[4]{0:T(128)S(1)} %xor_multiply_fusion.starts_ref, bf16[192,2048]{1,0:T(8,128)(2,1)S(1)} %collective-permute-done.5.x, bf16[512,512]{1,0:T(8,128)(2,1)S(1)} %get-tuple-element.24.refs_0_, bf16[512,512]{1,0:T(8,128)(2,1)} %collective-permute-done.6.refs_1_, ...), custom_call_target="tpu_custom_call" | custom-call | flops 1610612736 | bytes 11534336 | tf_op jit(solution)/shard_map/product/pallas_call | solution.py:84
  71.1 1.8 %collective-permute-start.11 = (bf16[192,512]{1,0:T(8,128)(2,1)S(1)}, bf16[192,512]{1,0:T(8,128)(2,1)S(1)}, u32[]{:S(2)}, u32[]{:S(2)}) collective-permute-start(bf16[192,512]{1,0:T(8,128)(2,1)S(1)} %key_sum.1.refs_0_), channel_id=1, source_target_pairs={{0,1},{1,0},{2,3},{3,2},{4,5},{5,4},{6,7},{7,6},{8,9},{9,8},{10,11... | collective-permute-start | bytes 589832 | tf_op jit(solution)/shard_map/ppermute | solution.py:23
  72.9 2.0 %collective-permute-start.10 = (bf16[192,512]{1,0:T(8,128)(2,1)S(1)}, bf16[192,512]{1,0:T(8,128)(2,1)S(1)}, u32[]{:S(2)}, u32[]{:S(2)}) collective-permute-start(bf16[192,512]{1,0:T(8,128)(2,1)S(1)} %key_sum.1.refs_0_), channel_id=1, source_target_pairs={{0,2},{1,3},{2,4},{3,5},{4,6},{5,7},{6,0},{7,1},{8,10},{9,11},{10,... | collective-permute-start | bytes 589832 | tf_op jit(solution)/shard_map/ppermute | solution.py:23
  74.9 1.0 collective-permute-start.12
  75.9 1.3 %collective-permute-done.11.refs_3_ = bf16[192,512]{1,0:T(8,128)(2,1)S(1)} collective-permute-done((bf16[192,512]{1,0:T(8,128)(2,1)S(1)}, bf16[192,512]{1,0:T(8,128)(2,1)S(1)}, u32[]{:S(2)}, u32[]{:S(2)}) %collective-permute-start.11) | collective-permute-done | bytes 196640 | tf_op jit(solution)/shard_map/ppermute | solution.py:23
  77.2 5.1 %collective-permute-done.10.refs_1_ = bf16[192,512]{1,0:T(8,128)(2,1)S(1)} collective-permute-done((bf16[192,512]{1,0:T(8,128)(2,1)S(1)}, bf16[192,512]{1,0:T(8,128)(2,1)S(1)}, u32[]{:S(2)}, u32[]{:S(2)}) %collective-permute-start.10) | collective-permute-done | bytes 196640 | tf_op jit(solution)/shard_map/ppermute | solution.py:23
  82.4 6.2 %collective-permute-done.12.refs_0_ = bf16[192,512]{1,0:T(8,128)(2,1)S(1)} collective-permute-done((bf16[192,512]{1,0:T(8,128)(2,1)S(1)}, bf16[192,512]{1,0:T(8,128)(2,1)S(1)}, u32[]{:S(2)}, u32[]{:S(2)}) %collective-permute-start.12) | collective-permute-done | bytes 196640 | tf_op jit(solution)/shard_map/ppermute | solution.py:23
  89.3 1.4 %collective-permute-start.13 = (bf16[192,512]{1,0:T(8,128)(2,1)S(1)}, bf16[192,512]{1,0:T(8,128)(2,1)S(1)}, u32[]{:S(2)}, u32[]{:S(2)}) collective-permute-start(bf16[192,512]{1,0:T(8,128)(2,1)S(1)} %collective-permute-done.10.refs_1_), channel_id=1, source_target_pairs={{0,1},{1,2},{2,3},{3,4},{4,5},{5,6},{6,7},{7,0},{8,9},{9,10},{10,1... | collective-permute-start | bytes 589832 | tf_op jit(solution)/shard_map/ppermute | solution.py:23
  90.7 2.0 %collective-permute-start.14 = (bf16[192,512]{1,0:T(8,128)(2,1)S(1)}, bf16[192,512]{1,0:T(8,128)(2,1)S(1)}, u32[]{:S(2)}, u32[]{:S(2)}) collective-permute-start(bf16[192,512]{1,0:T(8,128)(2,1)S(1)} %collective-permute-done.11.refs_3_), channel_id=1, source_target_pairs={{0,2},{2,4},{4,6},{6,0},{8,10},{10,12},{12,14},{14,8},{16,18},{18,... | collective-permute-start | bytes 589832 | tf_op jit(solution)/shard_map/ppermute | solution.py:280
  92.7 2.8 %collective-permute-done.17.refs_3_ = bf16[192,512]{1,0:T(8,128)(2,1)S(1)} collective-permute-done((bf16[192,512]{1,0:T(8,128)(2,1)S(1)}, bf16[192,512]{1,0:T(8,128)(2,1)S(1)}, u32[]{:S(2)}, u32[]{:S(2)}) %collective-permute-start.17) | collective-permute-done | bytes 196640 | tf_op jit(solution)/shard_map/ppermute | solution.py:23
  95.5 2.3 %collective-permute-start.18 = (bf16[192,512]{1,0:T(8,128)(2,1)S(1)}, bf16[192,512]{1,0:T(8,128)(2,1)S(1)}, u32[]{:S(2)}, u32[]{:S(2)}) collective-permute-start(bf16[192,512]{1,0:T(8,128)(2,1)S(1)} %collective-permute-done.17.refs_3_), channel_id=1, source_target_pairs={{0,2},{2,4},{4,6},{6,0},{8,10},{10,12},{12,14},{14,8},{16,18},{18,... | collective-permute-start | bytes 589832 | tf_op jit(solution)/shard_map/ppermute | solution.py:280
  97.8 1.0 collective-permute-done.15.refs_1_
  98.7 1.6 %collective-permute-start.16 = (bf16[192,512]{1,0:T(8,128)(2,1)S(1)}, bf16[192,512]{1,0:T(8,128)(2,1)}, u32[]{:S(2)}, u32[]{:S(2)}) collective-permute-start(bf16[192,512]{1,0:T(8,128)(2,1)S(1)} %collective-permute-done.15.refs_1_), channel_id=1, source_target_pairs={{0,1},{1,2},{2,3},{3,4},{4,5},{5,6},{6,7},{7,0},{8,9},{9,10},{10,1... | collective-permute-start | bytes 589832 | tf_op jit(solution)/shard_map/ppermute | solution.py:23
  100.5 2.9 %collective-permute-done.13.refs_2_ = bf16[192,512]{1,0:T(8,128)(2,1)S(1)} collective-permute-done((bf16[192,512]{1,0:T(8,128)(2,1)S(1)}, bf16[192,512]{1,0:T(8,128)(2,1)S(1)}, u32[]{:S(2)}, u32[]{:S(2)}) %collective-permute-start.13) | collective-permute-done | bytes 196640 | tf_op jit(solution)/shard_map/ppermute | solution.py:23
  103.4 6.9 %scores.1 = (bf16[2,4,768,384]{3,2,1,0:T(8,128)(2,1)S(1)}, f32[2,4,96,128]{3,2,1,0:T(8,128)S(1)}, f32[2,32,96]{2,1,0:T(8,128)}) custom-call(s32[1]{0:T(128)} %bitcast.odd_ref, bf16[1,2,96,4096]{3,2,1,0:T(8,128)(2,1)S(1)} %copy-done.1, bf16[192,512]{1,0:T(8,128)(2,1)S(1)} %key_sum.1.refs_0_, bf16[192,512]{1,0:T(8,128)(2,1)S(1)} %collective-permute-done.10.refs_1_, ...), custom_call_target="tpu_custom_call" | custom-call | flops 603979776 | bytes 8388608 | tf_op jit(solution)/shard_map/scores/pallas_call | solution.py:164
  110.3 3.4 %mixed_values.1 = bf16[1,2,96,4096]{3,2,1,0:T(8,128)(2,1)} custom-call(s32[1]{0:T(128)} %bitcast.odd_ref, bf16[2,4,768,384]{3,2,1,0:T(8,128)(2,1)S(1)} %get-tuple-element.29.weights, f32[2,4,96,128]{3,2,1,0:T(8,128)S(1)} %get-tuple-element.30.sums, bf16[192,512]{1,0:T(8,128)(2,1)S(1)} %value_sum.1.refs_0_, ...), custom_call_target="tpu_custom_call" | custom-call | flops 603979776 | bytes 8388608 | tf_op jit(solution)/shard_map/mixed_values/pallas_call | solution.py:209
  (44 shorter events, 2.5 us)
Async XLA Ops:
  0.6 4.1 %copy-start = (bf16[1,2,96,4096]{3,2,1,0:T(8,128)(2,1)S(1)}, bf16[1,2,96,4096]{3,2,1,0:T(8,128)(2,1)}, u32[]{:S(2)}) copy-start(bf16[1,2,96,4096]{3,2,1,0:T(8,128)(2,1)} %param.6) | copy-start | bytes 4718596
  0.6 4.1 %collective-permute-start = (bf16[1,4096]{1,0:T(2,128)(2,1)}, bf16[1,4096]{1,0:T(2,128)(2,1)S(1)}, u32[]{:S(2)}, u32[]{:S(2)}) collective-permute-start(bf16[1,4096]{1,0:T(2,128)(2,1)} %param.7), channel_id=1, source_target_pairs={{0,24},{8,0},{16,8},{24,16},{1,25},{9,1},{17,9},{25,17},{2,26},{10... | collective-permute-start | bytes 24584 | tf_op jit(solution)/shard_map/ppermute | solution.py:23
  3.1 5.4 %copy-start.3 = (s32[2,16]{1,0:T(2,128)S(1)}, s32[2,16]{1,0:T(2,128)}, u32[]{:S(2)}) copy-start(s32[2,16]{1,0:T(2,128)} %param.10) | copy-start | bytes 388
  4.4 49.2 %copy-start.4 = (s32[4]{0:T(128)S(1)}, s32[4]{0:T(128)}, u32[]{:S(2)}) copy-start(s32[4]{0:T(128)} %constant.66.clone) | copy-start | bytes 52
  6.1 0.9 copy-start.2
  6.9 23.5 %collective-permute-start.2 = (bf16[512,512]{1,0:T(8,128)(2,1)S(1)}, bf16[512,512]{1,0:T(8,128)(2,1)S(1)}, u32[]{:S(2)}, u32[]{:S(2)}) collective-permute-start(bf16[512,512]{1,0:T(8,128)(2,1)S(1)} %get-tuple-element.21.refs_0_), channel_id=1, source_target_pairs={{0,2},{1,3},{2,0},{3,1},{4,6},{5,7},{6,4},{7,5},{8,10},{9,11},{10,... | collective-permute-start | bytes 1572872 | tf_op jit(solution)/shard_map/ppermute | solution.py:23
  8.9 24.9 %collective-permute-start.3 = (bf16[512,512]{1,0:T(8,128)(2,1)S(1)}, bf16[512,512]{1,0:T(8,128)(2,1)}, u32[]{:S(2)}, u32[]{:S(2)}) collective-permute-start(bf16[512,512]{1,0:T(8,128)(2,1)S(1)} %get-tuple-element.21.refs_0_), channel_id=1, source_target_pairs={{0,1},{1,0},{2,3},{3,2},{4,5},{5,4},{6,7},{7,6},{8,9},{9,8},{10,11... | collective-permute-start | bytes 1572872 | tf_op jit(solution)/shard_map/ppermute | solution.py:23
  10.4 43.1 %collective-permute-start.5 = (bf16[192,2048]{1,0:T(8,128)(2,1)}, bf16[192,2048]{1,0:T(8,128)(2,1)S(1)}, u32[]{:S(2)}, u32[]{:S(2)}) collective-permute-start(bf16[192,2048]{1,0:T(8,128)(2,1)} %copy-done.2), channel_id=1, source_target_pairs={{0,12},{1,13},{2,14},{3,15},{4,8},{5,9},{6,10},{7,11},{8,20},{9,21... | collective-permute-start | bytes 2359304 | tf_op jit(solution)/shard_map/ppermute | solution.py:263
  30.4 21.6 %collective-permute-start.6 = (bf16[512,512]{1,0:T(8,128)(2,1)S(1)}, bf16[512,512]{1,0:T(8,128)(2,1)}, u32[]{:S(2)}, u32[]{:S(2)}) collective-permute-start(bf16[512,512]{1,0:T(8,128)(2,1)S(1)} %get-tuple-element.24.refs_0_), channel_id=1, source_target_pairs={{0,2},{1,3},{2,0},{3,1},{4,6},{5,7},{6,4},{7,5},{8,10},{9,11},{10,... | collective-permute-start | bytes 1572872 | tf_op jit(solution)/shard_map/ppermute | solution.py:23
  30.6 26.2 %collective-permute-start.1 = (bf16[192,2048]{1,0:T(8,128)(2,1)S(1)}, bf16[192,2048]{1,0:T(8,128)(2,1)S(1)}, u32[]{:S(2)}, u32[]{:S(2)}) collective-permute-start(bf16[192,2048]{1,0:T(8,128)(2,1)S(1)} %get-tuple-element.20), channel_id=1, source_target_pairs={{0,8},{1,9},{2,10},{3,11},{4,12},{5,13},{6,14},{7,15},{8,16},{9,17... | collective-permute-start | bytes 2359304 | tf_op jit(solution)/shard_map/ppermute | solution.py:263
  30.6 22.9 %collective-permute-start.4 = (bf16[512,512]{1,0:T(8,128)(2,1)S(1)}, bf16[512,512]{1,0:T(8,128)(2,1)S(1)}, u32[]{:S(2)}, u32[]{:S(2)}) collective-permute-start(bf16[512,512]{1,0:T(8,128)(2,1)S(1)} %collective-permute-done.2.refs_1_), channel_id=1, source_target_pairs={{0,1},{1,0},{2,3},{3,2},{4,5},{5,4},{6,7},{7,6},{8,9},{9,8},{10,11... | collective-permute-start | bytes 1572872 | tf_op jit(solution)/shard_map/ppermute | solution.py:23
  33.8 24.7 %collective-permute-start.7 = (bf16[512,512]{1,0:T(8,128)(2,1)S(1)}, bf16[512,512]{1,0:T(8,128)(2,1)S(1)}, u32[]{:S(2)}, u32[]{:S(2)}) collective-permute-start(bf16[512,512]{1,0:T(8,128)(2,1)S(1)} %get-tuple-element.24.refs_0_), channel_id=1, source_target_pairs={{0,1},{1,0},{2,3},{3,2},{4,5},{5,4},{6,7},{7,6},{8,9},{9,8},{10,11... | collective-permute-start | bytes 1572872 | tf_op jit(solution)/shard_map/ppermute | solution.py:23
  52.0 15.6 %collective-permute-start.8 = (bf16[512,512]{1,0:T(8,128)(2,1)}, bf16[512,512]{1,0:T(8,128)(2,1)S(1)}, u32[]{:S(2)}, u32[]{:S(2)}) collective-permute-start(bf16[512,512]{1,0:T(8,128)(2,1)} %collective-permute-done.6.refs_1_), channel_id=1, source_target_pairs={{0,1},{1,0},{2,3},{3,2},{4,5},{5,4},{6,7},{7,6},{8,9},{9,8},{10,11... | collective-permute-start | bytes 1572872 | tf_op jit(solution)/shard_map/ppermute | solution.py:23
  55.2 15.7 %collective-permute-start.9 = (bf16[192,512]{1,0:T(8,128)(2,1)S(1)}, bf16[192,512]{1,0:T(8,128)(2,1)S(1)}, u32[]{:S(2)}, u32[]{:S(2)}) collective-permute-start(bf16[192,512]{1,0:T(8,128)(2,1)S(1)} %product.6), channel_id=1, source_target_pairs={{0,4},{1,5},{2,6},{3,7},{4,0},{5,1},{6,2},{7,3},{8,12},{9,13},{10,... | collective-permute-start | bytes 589832 | tf_op jit(solution)/shard_map/ppermute | solution.py:23
  70.9 32.5 %copy-start.1 = (bf16[1,2,96,4096]{3,2,1,0:T(8,128)(2,1)S(1)}, bf16[1,2,96,4096]{3,2,1,0:T(8,128)(2,1)}, u32[]{:S(2)}) copy-start(bf16[1,2,96,4096]{3,2,1,0:T(8,128)(2,1)} %q_ref.1) | copy-start | bytes 4718596
  71.1 6.1 %collective-permute-start.11 = (bf16[192,512]{1,0:T(8,128)(2,1)S(1)}, bf16[192,512]{1,0:T(8,128)(2,1)S(1)}, u32[]{:S(2)}, u32[]{:S(2)}) collective-permute-start(bf16[192,512]{1,0:T(8,128)(2,1)S(1)} %key_sum.1.refs_0_), channel_id=1, source_target_pairs={{0,1},{1,0},{2,3},{3,2},{4,5},{5,4},{6,7},{7,6},{8,9},{9,8},{10,11... | collective-permute-start | bytes 589832 | tf_op jit(solution)/shard_map/ppermute | solution.py:23
  72.9 9.5 %collective-permute-start.10 = (bf16[192,512]{1,0:T(8,128)(2,1)S(1)}, bf16[192,512]{1,0:T(8,128)(2,1)S(1)}, u32[]{:S(2)}, u32[]{:S(2)}) collective-permute-start(bf16[192,512]{1,0:T(8,128)(2,1)S(1)} %key_sum.1.refs_0_), channel_id=1, source_target_pairs={{0,2},{1,3},{2,4},{3,5},{4,6},{5,7},{6,0},{7,1},{8,10},{9,11},{10,... | collective-permute-start | bytes 589832 | tf_op jit(solution)/shard_map/ppermute | solution.py:23
  74.9 13.7 %collective-permute-start.12 = (bf16[192,512]{1,0:T(8,128)(2,1)S(1)}, bf16[192,512]{1,0:T(8,128)(2,1)S(1)}, u32[]{:S(2)}, u32[]{:S(2)}) collective-permute-start(bf16[192,512]{1,0:T(8,128)(2,1)S(1)} %product.5), channel_id=1, source_target_pairs={{0,4},{1,5},{2,6},{3,7},{4,0},{5,1},{6,2},{7,3},{8,12},{9,13},{10,... | collective-permute-start | bytes 589832 | tf_op jit(solution)/shard_map/ppermute | solution.py:23
  88.6 6.9 %collective-permute-start.17 = (bf16[192,512]{1,0:T(8,128)(2,1)S(1)}, bf16[192,512]{1,0:T(8,128)(2,1)S(1)}, u32[]{:S(2)}, u32[]{:S(2)}) collective-permute-start(bf16[192,512]{1,0:T(8,128)(2,1)S(1)} %value_sum.1.refs_0_), channel_id=1, source_target_pairs={{0,1},{1,0},{2,3},{3,2},{4,5},{5,4},{6,7},{7,6},{8,9},{9,8},{10,11... | collective-permute-start | bytes 589832 | tf_op jit(solution)/shard_map/ppermute | solution.py:23
  89.3 9.4 %collective-permute-start.15 = (bf16[192,512]{1,0:T(8,128)(2,1)S(1)}, bf16[192,512]{1,0:T(8,128)(2,1)S(1)}, u32[]{:S(2)}, u32[]{:S(2)}) collective-permute-start(bf16[192,512]{1,0:T(8,128)(2,1)S(1)} %value_sum.1.refs_0_), channel_id=1, source_target_pairs={{0,2},{1,3},{2,4},{3,5},{4,6},{5,7},{6,0},{7,1},{8,10},{9,11},{10,... | collective-permute-start | bytes 589832 | tf_op jit(solution)/shard_map/ppermute | solution.py:23
  89.3 14.1 %collective-permute-start.13 = (bf16[192,512]{1,0:T(8,128)(2,1)S(1)}, bf16[192,512]{1,0:T(8,128)(2,1)S(1)}, u32[]{:S(2)}, u32[]{:S(2)}) collective-permute-start(bf16[192,512]{1,0:T(8,128)(2,1)S(1)} %collective-permute-done.10.refs_1_), channel_id=1, source_target_pairs={{0,1},{1,2},{2,3},{3,4},{4,5},{5,6},{6,7},{7,0},{8,9},{9,10},{10,1... | collective-permute-start | bytes 589832 | tf_op jit(solution)/shard_map/ppermute | solution.py:23
  90.7 12.7 %collective-permute-start.14 = (bf16[192,512]{1,0:T(8,128)(2,1)S(1)}, bf16[192,512]{1,0:T(8,128)(2,1)S(1)}, u32[]{:S(2)}, u32[]{:S(2)}) collective-permute-start(bf16[192,512]{1,0:T(8,128)(2,1)S(1)} %collective-permute-done.11.refs_3_), channel_id=1, source_target_pairs={{0,2},{2,4},{4,6},{6,0},{8,10},{10,12},{12,14},{14,8},{16,18},{18,... | collective-permute-start | bytes 589832 | tf_op jit(solution)/shard_map/ppermute | solution.py:280
  95.5 14.8 %collective-permute-start.18 = (bf16[192,512]{1,0:T(8,128)(2,1)S(1)}, bf16[192,512]{1,0:T(8,128)(2,1)S(1)}, u32[]{:S(2)}, u32[]{:S(2)}) collective-permute-start(bf16[192,512]{1,0:T(8,128)(2,1)S(1)} %collective-permute-done.17.refs_3_), channel_id=1, source_target_pairs={{0,2},{2,4},{4,6},{6,0},{8,10},{10,12},{12,14},{14,8},{16,18},{18,... | collective-permute-start | bytes 589832 | tf_op jit(solution)/shard_map/ppermute | solution.py:280
  98.7 11.6 %collective-permute-start.16 = (bf16[192,512]{1,0:T(8,128)(2,1)S(1)}, bf16[192,512]{1,0:T(8,128)(2,1)}, u32[]{:S(2)}, u32[]{:S(2)}) collective-permute-start(bf16[192,512]{1,0:T(8,128)(2,1)S(1)} %collective-permute-done.15.refs_1_), channel_id=1, source_target_pairs={{0,1},{1,2},{2,3},{3,4},{4,5},{5,6},{6,7},{7,0},{8,9},{9,10},{10,1... | collective-permute-start | bytes 589832 | tf_op jit(solution)/shard_map/ppermute | solution.py:23

commit v6 on v5

--- a/solution.py
+++ b/solution.py
@@ -33,22 +33,26 @@
 
 def norm_kernel(starts_ref, x_ref, gain_ref, *outs):
     rows, width = x_ref.shape[1], x_ref.shape[2]
-    piece_width = outs[0].shape[1]
+    pieces = starts_ref.shape[1]
+    piece_width = outs[0].shape[1] // pieces
     for r in range(0, rows, ROW_STEP):
         x = x_ref[0, r : r + ROW_STEP, :].astype(jnp.float32)
         scale = lax.rsqrt(jnp.sum(x * x, axis=-1, keepdims=True) / width + 1e-05)
-        for j, out in enumerate(outs):
-            start = pl.multiple_of(starts_ref[j], LANES)
-            xs = x_ref[0, r : r + ROW_STEP, pl.ds(start, piece_width)].astype(jnp.float32)
-            gain = gain_ref[:, pl.ds(start, piece_width)]
-            out[r : r + ROW_STEP, :] = (xs * scale * gain).astype(jnp.bfloat16)
+        for i, out in enumerate(outs):
+            for j in range(pieces):
+                start = pl.multiple_of(starts_ref[i, j], LANES)
+                xs = x_ref[0, r : r + ROW_STEP, pl.ds(start, piece_width)].astype(jnp.float32)
+                gain = gain_ref[:, pl.ds(start, piece_width)]
+                out[r : r + ROW_STEP, j * piece_width : (j + 1) * piece_width] = (
+                    xs * scale * gain
+                ).astype(jnp.bfloat16)
 
 
 def normed_cuts(activations, gain, starts):
     micro_count, tok_rows, width = activations.shape
     rows = micro_count * tok_rows
-    pieces = starts.shape[0]
-    part = width // pieces
+    cuts = starts.shape[0]
+    part = width // cuts
     return pl.pallas_call(
         norm_kernel,
         grid=(micro_count,),
@@ -57,8 +61,8 @@
             pl.BlockSpec((1, tok_rows, width), lambda m: (m, 0, 0)),
             pl.BlockSpec((1, width), lambda m: (0, 0)),
         ],
-        out_specs=[pl.BlockSpec((tok_rows, part), lambda m: (m, 0))] * pieces,
-        out_shape=[jax.ShapeDtypeStruct((rows, part), jnp.bfloat16)] * pieces,
+        out_specs=[pl.BlockSpec((tok_rows, part), lambda m: (m, 0))] * cuts,
+        out_shape=[jax.ShapeDtypeStruct((rows, part), jnp.bfloat16)] * cuts,
         compiler_params=params(16),
         cost_estimate=cost(6 * rows * width, 4 * rows * width),
         name="norm_cuts",
@@ -66,13 +70,12 @@
 
 
 def product_kernel(starts_ref, x, *refs):
-    shards, out = refs[:QUAD], refs[QUAD]
-    shard_rows = shards[0].shape[0]
+    shards, out = refs[:-1], refs[-1]
     total = 0.0
     for i, shard in enumerate(shards):
         start = pl.multiple_of(starts_ref[i], LANES)
         total = total + jnp.dot(
-            x[:, pl.ds(start, shard_rows)], shard[...], preferred_element_type=jnp.float32
+            x[:, pl.ds(start, shard.shape[0])], shard[...], preferred_element_type=jnp.float32
         )
     out[...] = total.astype(out.dtype)
 
@@ -83,7 +86,7 @@
     vmem = pl.BlockSpec(memory_space=pltpu.VMEM)
     return pl.pallas_call(
         product_kernel,
-        in_specs=[pl.BlockSpec(memory_space=pltpu.SMEM)] + [vmem] * (1 + QUAD),
+        in_specs=[pl.BlockSpec(memory_space=pltpu.SMEM)] + [vmem] * (1 + len(shards)),
         out_shape=jax.ShapeDtypeStruct((rows, width), dtype),
         compiler_params=params(24),
         cost_estimate=cost(8 * rows * part * width, 8 * (rows * part + part * width)),
@@ -234,43 +237,47 @@
     _, micro_count, tok_rows, _ = handoff.shape
 
     next_gain = moved(norm_gain, "section", lambda i: i - 1).astype(jnp.float32)
-    cut_starts = (own_quad + jnp.arange(quads, dtype=jnp.int32)) % quads * (QUAD * shard_rows)
+    parity, own_y = own_place // 2, own_place % 2
+    quad_ids = jnp.arange(quads, dtype=jnp.int32)
+    cut_starts = jnp.stack(
+        [(quad_ids * QUAD + 2 * p) * shard_rows for p in (parity, 1 - parity)]
+    )
     cuts = normed_cuts(handoff[0], next_gain, cut_starts)
 
-    def over_z(part):
-        return moved(part, "ctx", lambda i: i ^ 2)
-
-    def over_y(part):
-        return moved(part, "ctx", lambda i: i ^ 1)
-
-    places = own_place ^ jnp.array([0, 2, 1, 3], jnp.int32)
-    starts = places * shard_rows
-    key_part, value_part, cuts = lax.optimization_barrier(
-        (weight[:, :kv_width], weight[:, kv_width:], cuts)
-    )
-    key_z = over_z(key_part)
-    key_shards = [key_part, key_z, over_y(key_part), over_y(key_z)]
-    late_part, _ = lax.optimization_barrier((value_part, key_z))
-    value_z = over_z(late_part)
-    value_shards = [value_part, value_z, over_y(value_part), over_y(value_z)]
-
-    def to_next_section(part, j):
+    def to_next_section(part, flip):
         route = [
-            (s * cycle_size + i, (s + 1) % sections * cycle_size + (i + QUAD * j) % cycle_size)
+            (s * cycle_size + i, (s + 1) % sections * cycle_size + (i ^ flip))
             for s in range(sections)
             for i in range(cycle_size)
         ]
         return lax.ppermute(part, ("section", "ctx"), route)
 
-    arrived = [to_next_section(cuts[j], j) for j in range(quads)]
-
-    def partials(shards):
-        return [product(starts, arrived[j], shards, jnp.bfloat16) for j in range(1, quads)]
-
-    def sent_back(parts):
-        return [
-            moved(part, "ctx", lambda i, j=j: i - QUAD * j) for j, part in enumerate(parts, start=1)
-        ]
+    own_rows, next_rows = to_next_section(cuts[0], 0), to_next_section(cuts[1], 2)
+
+    def along_z(part):
+        return [moved(part, "ctx", lambda i, j=j: i + QUAD * j) for j in range(1, quads)]
+
+    def over_y(part):
+        return moved(part, "ctx", lambda i: i ^ 1)
+
+    key_part, value_part, _ = lax.optimization_barrier(
+        (weight[:, :kv_width], weight[:, kv_width:], cuts)
+    )
+    key_line = along_z(key_part)
+    late_part, _ = lax.optimization_barrier((value_part, key_line[-1]))
+    value_line = along_z(late_part)
+    key_y, value_y = over_y(key_part), over_y(value_part)
+    passed_on, _ = lax.optimization_barrier((key_line, value_y))
+    key_shards = [key_part, *key_line, key_y, *map(over_y, passed_on)]
+    value_shards = [value_part, *value_line, value_y]
+    line = (own_quad - quad_ids) % quads * 2
+    starts = jnp.concatenate([line + own_y, line + 1 - own_y]) * shard_rows
+
+    def partial(shards):
+        return product(starts, next_rows, shards, jnp.bfloat16)
+
+    def sent_back(part):
+        return [moved(part, "ctx", lambda i: i ^ 2)]
 
     def near_blocks(block):
         return [moved(block, "ctx", lambda i: i + 2), moved(block, "ctx", lambda i: i ^ 1)]
@@ -300,15 +307,16 @@
     sine_part = jnp.concatenate([-sine_part, sine_part], axis=1)
     odd = (own_index % 2).astype(jnp.int32).reshape(1)
 
-    key_parts = sent_back(partials(key_shards))
-    own_keys = product(starts, arrived[0], key_shards, jnp.float32)
-    own_values = product(starts, arrived[0], value_shards, jnp.float32)
-    value_partials, key_parts, own_values = lax.optimization_barrier(
-        (partials(value_shards), key_parts, own_values)
-    )
-    value_parts = sent_back(value_partials)
+    key_parts = sent_back(partial(key_shards))
+    own_keys = product(starts, own_rows, key_shards, jnp.float32)
     key_block = block_sum(key_sum_kernel, "key_sum", own_keys, key_parts, cosine, sine_part)
-    key_near, value_parts = lax.optimization_barrier((near_blocks(key_block), value_parts))
+    value_line, _ = lax.optimization_barrier((value_line, key_parts))
+    value_shards += map(over_y, value_line)
+    value_shards, _ = lax.optimization_barrier((value_shards, key_block))
+    value_parts = sent_back(partial(value_shards))
+    own_values = product(starts, own_rows, value_shards, jnp.float32)
+    key_near = near_blocks(key_block)
+    value_parts, _ = lax.optimization_barrier((value_parts, key_near))
     key_window = window_of(key_block, *key_near)
     weights, sums, log_sums = scored(
         odd, queries, key_window, own_pos[:, :, None], col_pos[:, None, :]

time: 114 us -> 115 us (level)
  starting transfers between devices: 26.5 us -> 23.9 us
  waiting for transfers between devices: 64.6 us -> 66.1 us
  Pallas kernels: 18.3 us -> 19.7 us
    ppermute x15, waiting for transfers between devices: 64.6 us -> 54.6 us  [moved(): lax.ppermute(block, axis, [(i, target(i) % size) for i in range(size)])]
    ppermute x2, waiting for transfers between devices: 0.01 us -> 8.76 us  [to_next_section(): return lax.ppermute(part, ('section', 'ctx'), route)]
    ppermute x15, starting transfers between devices: 19.9 us -> 14.8 us  [moved(): lax.ppermute(block, axis, [(i, target(i) % size) for i in range(size)])]
    ppermute x2, starting transfers between devices: 4.27 us -> 7.81 us  [window_of(): lax.ppermute(beside, 'ctx', [(i, (i + 2) % cycle_size) for i in range(0,...]
    ppermute x2, waiting for transfers between devices: 0.01 us -> 2.77 us  [window_of(): lax.ppermute(beside, 'ctx', [(i, (i + 2) % cycle_size) for i in range(0,...]
    pallas_call x4, Pallas kernels: 6.49 us -> 7.84 us  [product(): pl.pallas_call(product_kernel, in_specs=[pl.BlockSpec(memory_space=pltpu....]
  transfers between devices with their start and end apart: 19 -> 19, of which waited for: 10 -> 11; matrix products, arithmetic and copies ran while one was open for 2% -> 2% of each run, Pallas kernels for 12% -> 13%
where the time goes in v6:
time: 115 us
  waiting for transfers between devices  66.1 us (57%)
  starting transfers between devices  23.9 us (21%)
  Pallas kernels  19.7 us (17%)
  local copies, waits for them, and re-layouts  3.59 us (3%)
    ppermute x15, waiting for transfers between devices, moved(): lax.ppermute(block, axis, [(i, target(i) % size) for i in range(size)])  54.6 us
    ppermute x15, starting transfers between devices, moved(): lax.ppermute(block, axis, [(i, target(i) % size) for i in range(size)])  14.8 us
    ppermute x2, waiting for transfers between devices, to_next_section(): return lax.ppermute(part, ('section', 'ctx'), route)  8.76 us
    pallas_call x4, Pallas kernels, product(): pl.pallas_call(product_kernel, in_specs=[pl.BlockSpec(memory_space=pltpu....  7.84 us
    ppermute x2, starting transfers between devices, window_of(): lax.ppermute(beside, 'ctx', [(i, (i + 2) % cycle_size) for i in range(0,...  7.81 us
    pallas_call x1, Pallas kernels, scored(): pl.pallas_call(score_kernel, grid=(micro_count, KVH), in_specs=[pl.BlockS...  6.92 us
    pallas_call x1, Pallas kernels, mixed_values(): pl.pallas_call(mix_kernel, grid=(micro_count,), in_specs=[pl.BlockSpec(me...  3.41 us
    ppermute x2, waiting for transfers between devices, window_of(): lax.ppermute(beside, 'ctx', [(i, (i + 2) % cycle_size) for i in range(0,...  2.77 us
  transfers between devices with their start and end apart: 19, of which 11 were waited for; matrix products, arithmetic and copies ran while one was open for 2% of the time, Pallas kernels for 13%

profile of v6, /device:TPU:0, one launch (start us, length us, event | category | flops | bytes accessed | tf_op | source)
XLA Modules:
  0.0 115.1 jit_solution(15153733446101954944)
XLA Ops:
  0.6 2.4 %collective-permute-start = (bf16[1,4096]{1,0:T(2,128)(2,1)}, bf16[1,4096]{1,0:T(2,128)(2,1)S(1)}, u32[]{:S(2)}, u32[]{:S(2)}) collective-permute-start(bf16[1,4096]{1,0:T(2,128)(2,1)} %param.6), channel_id=1, source_target_pairs={{0,24},{8,0},{16,8},{24,16},{1,25},{9,1},{17,9},{25,17},{2,26},{10... | collective-permute-start | bytes 24584 | tf_op jit(solution)/shard_map/ppermute | solution.py:23
  3.1 1.3 %fusion.4 = (bf16[512,512]{1,0:T(8,128)(2,1)S(1)}, bf16[512,512]{1,0:T(8,128)(2,1)S(1)}) fusion(bf16[512,1024]{1,0:T(8,128)(2,1)} %bitcast.7), kind=kLoop, calls=%fused_computation.25 | loop fusion | bytes 2097152 | tf_op jit(solution)/shard_map/slice | solution.py:264
  4.8 1.3 %norm_cuts.1 = (bf16[192,2048]{1,0:T(8,128)(2,1)S(1)}, bf16[192,2048]{1,0:T(8,128)(2,1)S(1)}) custom-call(s32[2,2]{1,0:T(2,128)S(1)} %pad_add_fusion.starts_ref, bf16[2,96,4096]{2,1,0:T(8,128)(2,1)S(1)} %bitcast.6, f32[1,4096]{1,0:T(1,128)S(1)} %convert_element_type.16.gain_ref), custom_call_target="tpu_custom_call" | custom-call | flops 4718592 | bytes 3145728 | tf_op jit(solution)/shard_map/norm_cuts/pallas_call | solution.py:56
  6.1 0.9 copy-done.2
  7.0 0.9 copy-done.3
  7.9 1.5 %collective-permute-start.4 = (bf16[512,512]{1,0:T(8,128)(2,1)S(1)}, bf16[512,512]{1,0:T(8,128)(2,1)S(1)}, u32[]{:S(2)}, u32[]{:S(2)}) collective-permute-start(bf16[512,512]{1,0:T(8,128)(2,1)S(1)} %get-tuple-element.26.refs_0_), channel_id=1, source_target_pairs={{0,1},{1,0},{2,3},{3,2},{4,5},{5,4},{6,7},{7,6},{8,9},{9,8},{10,11... | collective-permute-start | bytes 1572872 | tf_op jit(solution)/shard_map/ppermute | solution.py:23
  9.4 2.6 %collective-permute-start.2 = (bf16[512,512]{1,0:T(8,128)(2,1)S(1)}, bf16[512,512]{1,0:T(8,128)(2,1)}, u32[]{:S(2)}, u32[]{:S(2)}) collective-permute-start(bf16[512,512]{1,0:T(8,128)(2,1)S(1)} %get-tuple-element.19.refs_0_), channel_id=1, source_target_pairs={{0,4},{1,5},{2,6},{3,7},{4,0},{5,1},{6,2},{7,3},{8,12},{9,13},{10,... | collective-permute-start | bytes 1572872 | tf_op jit(solution)/shard_map/ppermute | solution.py:23
  12.0 1.3 %collective-permute-start.6 = (bf16[192,2048]{1,0:T(8,128)(2,1)}, bf16[192,2048]{1,0:T(8,128)(2,1)S(1)}, u32[]{:S(2)}, u32[]{:S(2)}) collective-permute-start(bf16[192,2048]{1,0:T(8,128)(2,1)} %copy-done.3), channel_id=1, source_target_pairs={{0,10},{1,11},{2,8},{3,9},{4,14},{5,15},{6,12},{7,13},{8,18},{9,19... | collective-permute-start | bytes 2359304 | tf_op jit(solution)/shard_map/ppermute | solution.py:253
  13.5 0.6 collective-permute-start.3
  14.1 8.6 %collective-permute-done.4.refs_2_ = bf16[512,512]{1,0:T(8,128)(2,1)S(1)} collective-permute-done((bf16[512,512]{1,0:T(8,128)(2,1)S(1)}, bf16[512,512]{1,0:T(8,128)(2,1)S(1)}, u32[]{:S(2)}, u32[]{:S(2)}) %collective-permute-start.4) | collective-permute-done | bytes 524320 | tf_op jit(solution)/shard_map/ppermute | solution.py:23
  22.7 13.3 %collective-permute-done.2.refs_1_ = bf16[512,512]{1,0:T(8,128)(2,1)} collective-permute-done((bf16[512,512]{1,0:T(8,128)(2,1)S(1)}, bf16[512,512]{1,0:T(8,128)(2,1)}, u32[]{:S(2)}, u32[]{:S(2)}) %collective-permute-start.2) | collective-permute-done | bytes 524320 | tf_op jit(solution)/shard_map/ppermute | solution.py:23
  36.8 8.8 %collective-permute-done.6.x = bf16[192,2048]{1,0:T(8,128)(2,1)S(1)} collective-permute-done((bf16[192,2048]{1,0:T(8,128)(2,1)}, bf16[192,2048]{1,0:T(8,128)(2,1)S(1)}, u32[]{:S(2)}, u32[]{:S(2)}) %collective-permute-start.6) | collective-permute-done | bytes 786464 | tf_op jit(solution)/shard_map/ppermute | solution.py:253
  45.6 4.0 %collective-permute-done.5.refs_3_ = bf16[512,512]{1,0:T(8,128)(2,1)} collective-permute-done((bf16[512,512]{1,0:T(8,128)(2,1)}, bf16[512,512]{1,0:T(8,128)(2,1)}, u32[]{:S(2)}, u32[]{:S(2)}) %collective-permute-start.5) | collective-permute-done | bytes 524320 | tf_op jit(solution)/shard_map/ppermute | solution.py:23
  49.6 1.9 %product.5 = bf16[192,512]{1,0:T(8,128)(2,1)S(1)} custom-call(s32[4]{0:T(128)S(1)} %add_multiply_fusion.starts_ref, bf16[192,2048]{1,0:T(8,128)(2,1)S(1)} %collective-permute-done.6.x, bf16[512,512]{1,0:T(8,128)(2,1)S(1)} %get-tuple-element.19.refs_0_, bf16[512,512]{1,0:T(8,128)(2,1)} %collective-permute-done.2.refs_1_, ...), custom_call_target="tpu_custom_call" | custom-call | flops 1610612736 | bytes 11534336 | tf_op jit(solution)/shard_map/product/pallas_call | solution.py:87
  51.5 1.1 collective-permute-start.7
  52.7 9.3 %collective-permute-done.12.refs_1_ = bf16[512,512]{1,0:T(8,128)(2,1)} collective-permute-done((bf16[512,512]{1,0:T(8,128)(2,1)S(1)}, bf16[512,512]{1,0:T(8,128)(2,1)}, u32[]{:S(2)}, u32[]{:S(2)}) %collective-permute-start.12) | collective-permute-done | bytes 524320 | tf_op jit(solution)/shard_map/ppermute | solution.py:23
  62.0 3.0 %collective-permute-done.7.refs_0_ = bf16[192,512]{1,0:T(8,128)(2,1)S(1)} collective-permute-done((bf16[192,512]{1,0:T(8,128)(2,1)S(1)}, bf16[192,512]{1,0:T(8,128)(2,1)S(1)}, u32[]{:S(2)}, u32[]{:S(2)}) %collective-permute-start.7) | collective-permute-done | bytes 196640 | tf_op jit(solution)/shard_map/ppermute | solution.py:23
  65.0 1.5 %collective-permute-start.13 = (bf16[512,512]{1,0:T(8,128)(2,1)}, bf16[512,512]{1,0:T(8,128)(2,1)}, u32[]{:S(2)}, u32[]{:S(2)}) collective-permute-start(bf16[512,512]{1,0:T(8,128)(2,1)} %collective-permute-done.12.refs_1_), channel_id=1, source_target_pairs={{0,1},{1,0},{2,3},{3,2},{4,5},{5,4},{6,7},{7,6},{8,9},{9,8},{10,11... | collective-permute-start | bytes 1572872 | tf_op jit(solution)/shard_map/ppermute | solution.py:23
  67.2 2.2 %product.4.own = f32[192,512]{1,0:T(8,128)S(1)} custom-call(s32[4]{0:T(128)S(1)} %add_multiply_fusion.starts_ref, bf16[192,2048]{1,0:T(8,128)(2,1)S(1)} %collective-permute-done.1.x, bf16[512,512]{1,0:T(8,128)(2,1)S(1)} %get-tuple-element.19.refs_0_, bf16[512,512]{1,0:T(8,128)(2,1)} %collective-permute-done.2.refs_1_, ...), custom_call_target="tpu_custom_call" | custom-call | flops 1610612736 | bytes 11534336 | tf_op jit(solution)/shard_map/product/pallas_call | solution.py:87
  69.7 0.6 collective-permute-start.10
  70.2 10.0 %collective-permute-done.13.refs_3_ = bf16[512,512]{1,0:T(8,128)(2,1)} collective-permute-done((bf16[512,512]{1,0:T(8,128)(2,1)}, bf16[512,512]{1,0:T(8,128)(2,1)}, u32[]{:S(2)}, u32[]{:S(2)}) %collective-permute-start.13) | collective-permute-done | bytes 524320 | tf_op jit(solution)/shard_map/ppermute | solution.py:23
  80.2 1.8 %product.7 = bf16[192,512]{1,0:T(8,128)(2,1)S(1)} custom-call(s32[4]{0:T(128)S(1)} %add_multiply_fusion.starts_ref, bf16[192,2048]{1,0:T(8,128)(2,1)S(1)} %collective-permute-done.6.x, bf16[512,512]{1,0:T(8,128)(2,1)S(1)} %get-tuple-element.26.refs_0_, bf16[512,512]{1,0:T(8,128)(2,1)} %collective-permute-done.12.refs_1_, ...), custom_call_target="tpu_custom_call" | custom-call | flops 1610612736 | bytes 11534336 | tf_op jit(solution)/shard_map/product/pallas_call | solution.py:87
  82.1 1.9 %product.6.own = f32[192,512]{1,0:T(8,128)S(1)} custom-call(s32[4]{0:T(128)S(1)} %add_multiply_fusion.starts_ref, bf16[192,2048]{1,0:T(8,128)(2,1)S(1)} %copy-done.5, bf16[512,512]{1,0:T(8,128)(2,1)S(1)} %get-tuple-element.26.refs_0_, bf16[512,512]{1,0:T(8,128)(2,1)} %collective-permute-done.12.refs_1_, bf16[512,512]{1,0:T(8,128)(2,1)S(1)} %collective-permute-done.4.refs_2_, ...), custom_call_target="tpu_custom_call" | custom-call | flops 1610612736 | bytes 11534336 | tf_op jit(solution)/shard_map/product/pallas_call | solution.py:87
  84.0 3.7 %collective-permute-done.14.refs_0_ = bf16[192,512]{1,0:T(8,128)(2,1)S(1)} collective-permute-done((bf16[192,512]{1,0:T(8,128)(2,1)S(1)}, bf16[192,512]{1,0:T(8,128)(2,1)S(1)}, u32[]{:S(2)}, u32[]{:S(2)}) %collective-permute-start.14) | collective-permute-done | bytes 196640 | tf_op jit(solution)/shard_map/ppermute | solution.py:23
  87.8 1.6 %collective-permute-start.17 = (bf16[192,512]{1,0:T(8,128)(2,1)S(1)}, bf16[192,512]{1,0:T(8,128)(2,1)S(1)}, u32[]{:S(2)}, u32[]{:S(2)}) collective-permute-start(bf16[192,512]{1,0:T(8,128)(2,1)S(1)} %value_sum.1.refs_0_), channel_id=1, source_target_pairs={{0,1},{1,0},{2,3},{3,2},{4,5},{5,4},{6,7},{7,6},{8,9},{9,8},{10,11... | collective-permute-start | bytes 589832 | tf_op jit(solution)/shard_map/ppermute | solution.py:23
  89.4 1.9 %collective-permute-start.15 = (bf16[192,512]{1,0:T(8,128)(2,1)S(1)}, bf16[192,512]{1,0:T(8,128)(2,1)S(1)}, u32[]{:S(2)}, u32[]{:S(2)}) collective-permute-start(bf16[192,512]{1,0:T(8,128)(2,1)S(1)} %value_sum.1.refs_0_), channel_id=1, source_target_pairs={{0,2},{1,3},{2,4},{3,5},{4,6},{5,7},{6,0},{7,1},{8,10},{9,11},{10,... | collective-permute-start | bytes 589832 | tf_op jit(solution)/shard_map/ppermute | solution.py:23
  91.3 3.9 %collective-permute-start.11 = (bf16[192,512]{1,0:T(8,128)(2,1)S(1)}, bf16[192,512]{1,0:T(8,128)(2,1)S(1)}, u32[]{:S(2)}, u32[]{:S(2)}) collective-permute-start(bf16[192,512]{1,0:T(8,128)(2,1)S(1)} %collective-permute-done.10.refs_3_), channel_id=1, source_target_pairs={{0,2},{2,4},{4,6},{6,0},{8,10},{10,12},{12,14},{14,8},{16,18},{18,... | collective-permute-start | bytes 589832 | tf_op jit(solution)/shard_map/ppermute | solution.py:287
  95.3 3.9 %collective-permute-start.18 = (bf16[192,512]{1,0:T(8,128)(2,1)S(1)}, bf16[192,512]{1,0:T(8,128)(2,1)S(1)}, u32[]{:S(2)}, u32[]{:S(2)}) collective-permute-start(bf16[192,512]{1,0:T(8,128)(2,1)S(1)} %collective-permute-done.17.refs_3_), channel_id=1, source_target_pairs={{0,2},{2,4},{4,6},{6,0},{8,10},{10,12},{12,14},{14,8},{16,18},{18,... | collective-permute-start | bytes 589832 | tf_op jit(solution)/shard_map/ppermute | solution.py:287
  99.6 2.8 %collective-permute-done.11.refs_4_ = bf16[192,512]{1,0:T(8,128)(2,1)S(1)} collective-permute-done((bf16[192,512]{1,0:T(8,128)(2,1)S(1)}, bf16[192,512]{1,0:T(8,128)(2,1)S(1)}, u32[]{:S(2)}, u32[]{:S(2)}) %collective-permute-start.11) | collective-permute-done | bytes 196640 | tf_op jit(solution)/shard_map/ppermute | solution.py:287
  102.4 2.4 %collective-permute-done.9.refs_2_ = bf16[192,512]{1,0:T(8,128)(2,1)S(1)} collective-permute-done((bf16[192,512]{1,0:T(8,128)(2,1)S(1)}, bf16[192,512]{1,0:T(8,128)(2,1)S(1)}, u32[]{:S(2)}, u32[]{:S(2)}) %collective-permute-start.9) | collective-permute-done | bytes 196640 | tf_op jit(solution)/shard_map/ppermute | solution.py:23
  104.7 6.9 %scores.1 = (bf16[2,4,768,384]{3,2,1,0:T(8,128)(2,1)S(1)}, f32[2,4,96,128]{3,2,1,0:T(8,128)S(1)}, f32[2,32,96]{2,1,0:T(8,128)}) custom-call(s32[1]{0:T(128)} %bitcast.odd_ref, bf16[1,2,96,4096]{3,2,1,0:T(8,128)(2,1)S(1)} %copy-done, bf16[192,512]{1,0:T(8,128)(2,1)S(1)} %key_sum.1.refs_0_, bf16[192,512]{1,0:T(8,128)(2,1)S(1)} %collective-permute-done.8.refs_1_, ...), custom_call_target="tpu_custom_call" | custom-call | flops 603979776 | bytes 8388608 | tf_op jit(solution)/shard_map/scores/pallas_call | solution.py:167
  111.7 3.4 %mixed_values.1 = bf16[1,2,96,4096]{3,2,1,0:T(8,128)(2,1)} custom-call(s32[1]{0:T(128)} %bitcast.odd_ref, bf16[2,4,768,384]{3,2,1,0:T(8,128)(2,1)S(1)} %get-tuple-element.22.weights, f32[2,4,96,128]{3,2,1,0:T(8,128)S(1)} %get-tuple-element.23.sums, bf16[192,512]{1,0:T(8,128)(2,1)S(1)} %value_sum.1.refs_0_, ...), custom_call_target="tpu_custom_call" | custom-call | flops 603979776 | bytes 8388608 | tf_op jit(solution)/shard_map/mixed_values/pallas_call | solution.py:212
  (50 shorter events, 2.9 us)
Async XLA Ops:
  0.6 4.1 %copy-start.1 = (bf16[1,2,96,4096]{3,2,1,0:T(8,128)(2,1)S(1)}, bf16[1,2,96,4096]{3,2,1,0:T(8,128)(2,1)}, u32[]{:S(2)}) copy-start(bf16[1,2,96,4096]{3,2,1,0:T(8,128)(2,1)} %param.5) | copy-start | bytes 4718596
  0.6 4.1 %collective-permute-start = (bf16[1,4096]{1,0:T(2,128)(2,1)}, bf16[1,4096]{1,0:T(2,128)(2,1)S(1)}, u32[]{:S(2)}, u32[]{:S(2)}) collective-permute-start(bf16[1,4096]{1,0:T(2,128)(2,1)} %param.6), channel_id=1, source_target_pairs={{0,24},{8,0},{16,8},{24,16},{1,25},{9,1},{17,9},{25,17},{2,26},{10... | collective-permute-start | bytes 24584 | tf_op jit(solution)/shard_map/ppermute | solution.py:23
  3.1 10.3 %copy-start.6 = (s32[2,16]{1,0:T(2,128)S(1)}, s32[2,16]{1,0:T(2,128)}, u32[]{:S(2)}) copy-start(s32[2,16]{1,0:T(2,128)} %param.9) | copy-start | bytes 388
  6.1 0.9 copy-start.2
  7.0 0.9 copy-start.3
  7.9 14.8 %collective-permute-start.4 = (bf16[512,512]{1,0:T(8,128)(2,1)S(1)}, bf16[512,512]{1,0:T(8,128)(2,1)S(1)}, u32[]{:S(2)}, u32[]{:S(2)}) collective-permute-start(bf16[512,512]{1,0:T(8,128)(2,1)S(1)} %get-tuple-element.26.refs_0_), channel_id=1, source_target_pairs={{0,1},{1,0},{2,3},{3,2},{4,5},{5,4},{6,7},{7,6},{8,9},{9,8},{10,11... | collective-permute-start | bytes 1572872 | tf_op jit(solution)/shard_map/ppermute | solution.py:23
  9.4 26.5 %collective-permute-start.2 = (bf16[512,512]{1,0:T(8,128)(2,1)S(1)}, bf16[512,512]{1,0:T(8,128)(2,1)}, u32[]{:S(2)}, u32[]{:S(2)}) collective-permute-start(bf16[512,512]{1,0:T(8,128)(2,1)S(1)} %get-tuple-element.19.refs_0_), channel_id=1, source_target_pairs={{0,4},{1,5},{2,6},{3,7},{4,0},{5,1},{6,2},{7,3},{8,12},{9,13},{10,... | collective-permute-start | bytes 1572872 | tf_op jit(solution)/shard_map/ppermute | solution.py:23
  12.0 33.6 %collective-permute-start.6 = (bf16[192,2048]{1,0:T(8,128)(2,1)}, bf16[192,2048]{1,0:T(8,128)(2,1)S(1)}, u32[]{:S(2)}, u32[]{:S(2)}) collective-permute-start(bf16[192,2048]{1,0:T(8,128)(2,1)} %copy-done.3), channel_id=1, source_target_pairs={{0,10},{1,11},{2,8},{3,9},{4,14},{5,15},{6,12},{7,13},{8,18},{9,19... | collective-permute-start | bytes 2359304 | tf_op jit(solution)/shard_map/ppermute | solution.py:253
  13.5 23.3 %collective-permute-start.3 = (bf16[512,512]{1,0:T(8,128)(2,1)S(1)}, bf16[512,512]{1,0:T(8,128)(2,1)}, u32[]{:S(2)}, u32[]{:S(2)}) collective-permute-start(bf16[512,512]{1,0:T(8,128)(2,1)S(1)} %get-tuple-element.19.refs_0_), channel_id=1, source_target_pairs={{0,1},{1,0},{2,3},{3,2},{4,5},{5,4},{6,7},{7,6},{8,9},{9,8},{10,11... | collective-permute-start | bytes 1572872 | tf_op jit(solution)/shard_map/ppermute | solution.py:23
  35.9 13.7 %collective-permute-start.5 = (bf16[512,512]{1,0:T(8,128)(2,1)}, bf16[512,512]{1,0:T(8,128)(2,1)}, u32[]{:S(2)}, u32[]{:S(2)}) collective-permute-start(bf16[512,512]{1,0:T(8,128)(2,1)} %collective-permute-done.2.refs_1_), channel_id=1, source_target_pairs={{0,1},{1,0},{2,3},{3,2},{4,5},{5,4},{6,7},{7,6},{8,9},{9,8},{10,11... | collective-permute-start | bytes 1572872 | tf_op jit(solution)/shard_map/ppermute | solution.py:23
  36.5 25.5 %collective-permute-start.12 = (bf16[512,512]{1,0:T(8,128)(2,1)S(1)}, bf16[512,512]{1,0:T(8,128)(2,1)}, u32[]{:S(2)}, u32[]{:S(2)}) collective-permute-start(bf16[512,512]{1,0:T(8,128)(2,1)S(1)} %get-tuple-element.26.refs_0_), channel_id=1, source_target_pairs={{0,4},{1,5},{2,6},{3,7},{4,0},{5,1},{6,2},{7,3},{8,12},{9,13},{10,... | collective-permute-start | bytes 1572872 | tf_op jit(solution)/shard_map/ppermute | solution.py:23
  36.8 30.4 %collective-permute-start.1 = (bf16[192,2048]{1,0:T(8,128)(2,1)}, bf16[192,2048]{1,0:T(8,128)(2,1)S(1)}, u32[]{:S(2)}, u32[]{:S(2)}) collective-permute-start(bf16[192,2048]{1,0:T(8,128)(2,1)} %copy-done.2), channel_id=1, source_target_pairs={{0,8},{1,9},{2,10},{3,11},{4,12},{5,13},{6,14},{7,15},{8,16},{9,17... | collective-permute-start | bytes 2359304 | tf_op jit(solution)/shard_map/ppermute | solution.py:253
  51.5 13.5 %collective-permute-start.7 = (bf16[192,512]{1,0:T(8,128)(2,1)S(1)}, bf16[192,512]{1,0:T(8,128)(2,1)S(1)}, u32[]{:S(2)}, u32[]{:S(2)}) collective-permute-start(bf16[192,512]{1,0:T(8,128)(2,1)S(1)} %product.5), channel_id=1, source_target_pairs={{0,2},{1,3},{2,0},{3,1},{4,6},{5,7},{6,4},{7,5},{8,10},{9,11},{10,... | collective-permute-start | bytes 589832 | tf_op jit(solution)/shard_map/ppermute | solution.py:23
  65.0 15.2 %collective-permute-start.13 = (bf16[512,512]{1,0:T(8,128)(2,1)}, bf16[512,512]{1,0:T(8,128)(2,1)}, u32[]{:S(2)}, u32[]{:S(2)}) collective-permute-start(bf16[512,512]{1,0:T(8,128)(2,1)} %collective-permute-done.12.refs_1_), channel_id=1, source_target_pairs={{0,1},{1,0},{2,3},{3,2},{4,5},{5,4},{6,7},{7,6},{8,9},{9,8},{10,11... | collective-permute-start | bytes 1572872 | tf_op jit(solution)/shard_map/ppermute | solution.py:23
  67.2 2.2 %copy-start.4 = (bf16[192,2048]{1,0:T(8,128)(2,1)}, bf16[192,2048]{1,0:T(8,128)(2,1)S(1)}, u32[]{:S(2)}) copy-start(bf16[192,2048]{1,0:T(8,128)(2,1)S(1)} %collective-permute-done.1.x) | copy-start | bytes 2359300
  69.6 12.4 %copy-start.5 = (bf16[192,2048]{1,0:T(8,128)(2,1)S(1)}, bf16[192,2048]{1,0:T(8,128)(2,1)}, u32[]{:S(2)}) copy-start(bf16[192,2048]{1,0:T(8,128)(2,1)} %copy-done.4) | copy-start | bytes 2359300
  69.7 14.3 %collective-permute-start.10 = (bf16[192,512]{1,0:T(8,128)(2,1)S(1)}, bf16[192,512]{1,0:T(8,128)(2,1)S(1)}, u32[]{:S(2)}, u32[]{:S(2)}) collective-permute-start(bf16[192,512]{1,0:T(8,128)(2,1)S(1)} %key_sum.1.refs_0_), channel_id=1, source_target_pairs={{0,1},{1,0},{2,3},{3,2},{4,5},{5,4},{6,7},{7,6},{8,9},{9,8},{10,11... | collective-permute-start | bytes 589832 | tf_op jit(solution)/shard_map/ppermute | solution.py:23
  70.2 13.8 %collective-permute-start.8 = (bf16[192,512]{1,0:T(8,128)(2,1)S(1)}, bf16[192,512]{1,0:T(8,128)(2,1)S(1)}, u32[]{:S(2)}, u32[]{:S(2)}) collective-permute-start(bf16[192,512]{1,0:T(8,128)(2,1)S(1)} %key_sum.1.refs_0_), channel_id=1, source_target_pairs={{0,2},{1,3},{2,4},{3,5},{4,6},{5,7},{6,0},{7,1},{8,10},{9,11},{10,... | collective-permute-start | bytes 589832 | tf_op jit(solution)/shard_map/ppermute | solution.py:23
  82.0 22.8 %copy-start = (bf16[1,2,96,4096]{3,2,1,0:T(8,128)(2,1)S(1)}, bf16[1,2,96,4096]{3,2,1,0:T(8,128)(2,1)}, u32[]{:S(2)}) copy-start(bf16[1,2,96,4096]{3,2,1,0:T(8,128)(2,1)} %q_ref.1) | copy-start | bytes 4718596
  82.0 5.7 %collective-permute-start.14 = (bf16[192,512]{1,0:T(8,128)(2,1)S(1)}, bf16[192,512]{1,0:T(8,128)(2,1)S(1)}, u32[]{:S(2)}, u32[]{:S(2)}) collective-permute-start(bf16[192,512]{1,0:T(8,128)(2,1)S(1)} %product.7), channel_id=1, source_target_pairs={{0,2},{1,3},{2,0},{3,1},{4,6},{5,7},{6,4},{7,5},{8,10},{9,11},{10,... | collective-permute-start | bytes 589832 | tf_op jit(solution)/shard_map/ppermute | solution.py:23
  87.8 7.5 %collective-permute-start.17 = (bf16[192,512]{1,0:T(8,128)(2,1)S(1)}, bf16[192,512]{1,0:T(8,128)(2,1)S(1)}, u32[]{:S(2)}, u32[]{:S(2)}) collective-permute-start(bf16[192,512]{1,0:T(8,128)(2,1)S(1)} %value_sum.1.refs_0_), channel_id=1, source_target_pairs={{0,1},{1,0},{2,3},{3,2},{4,5},{5,4},{6,7},{7,6},{8,9},{9,8},{10,11... | collective-permute-start | bytes 589832 | tf_op jit(solution)/shard_map/ppermute | solution.py:23
  89.4 9.8 %collective-permute-start.15 = (bf16[192,512]{1,0:T(8,128)(2,1)S(1)}, bf16[192,512]{1,0:T(8,128)(2,1)S(1)}, u32[]{:S(2)}, u32[]{:S(2)}) collective-permute-start(bf16[192,512]{1,0:T(8,128)(2,1)S(1)} %value_sum.1.refs_0_), channel_id=1, source_target_pairs={{0,2},{1,3},{2,4},{3,5},{4,6},{5,7},{6,0},{7,1},{8,10},{9,11},{10,... | collective-permute-start | bytes 589832 | tf_op jit(solution)/shard_map/ppermute | solution.py:23
  91.3 11.1 %collective-permute-start.11 = (bf16[192,512]{1,0:T(8,128)(2,1)S(1)}, bf16[192,512]{1,0:T(8,128)(2,1)S(1)}, u32[]{:S(2)}, u32[]{:S(2)}) collective-permute-start(bf16[192,512]{1,0:T(8,128)(2,1)S(1)} %collective-permute-done.10.refs_3_), channel_id=1, source_target_pairs={{0,2},{2,4},{4,6},{6,0},{8,10},{10,12},{12,14},{14,8},{16,18},{18,... | collective-permute-start | bytes 589832 | tf_op jit(solution)/shard_map/ppermute | solution.py:287
  95.2 9.5 %collective-permute-start.9 = (bf16[192,512]{1,0:T(8,128)(2,1)S(1)}, bf16[192,512]{1,0:T(8,128)(2,1)S(1)}, u32[]{:S(2)}, u32[]{:S(2)}) collective-permute-start(bf16[192,512]{1,0:T(8,128)(2,1)S(1)} %collective-permute-done.8.refs_1_), channel_id=1, source_target_pairs={{0,1},{1,2},{2,3},{3,4},{4,5},{5,6},{6,7},{7,0},{8,9},{9,10},{10,1... | collective-permute-start | bytes 589832 | tf_op jit(solution)/shard_map/ppermute | solution.py:23
  95.3 16.4 %collective-permute-start.18 = (bf16[192,512]{1,0:T(8,128)(2,1)S(1)}, bf16[192,512]{1,0:T(8,128)(2,1)S(1)}, u32[]{:S(2)}, u32[]{:S(2)}) collective-permute-start(bf16[192,512]{1,0:T(8,128)(2,1)S(1)} %collective-permute-done.17.refs_3_), channel_id=1, source_target_pairs={{0,2},{2,4},{4,6},{6,0},{8,10},{10,12},{12,14},{14,8},{16,18},{18,... | collective-permute-start | bytes 589832 | tf_op jit(solution)/shard_map/ppermute | solution.py:287
  99.2 12.4 %collective-permute-start.16 = (bf16[192,512]{1,0:T(8,128)(2,1)S(1)}, bf16[192,512]{1,0:T(8,128)(2,1)}, u32[]{:S(2)}, u32[]{:S(2)}) collective-permute-start(bf16[192,512]{1,0:T(8,128)(2,1)S(1)} %collective-permute-done.15.refs_1_), channel_id=1, source_target_pairs={{0,1},{1,2},{2,3},{3,4},{4,5},{5,6},{6,7},{7,0},{8,9},{9,10},{10,1... | collective-permute-start | bytes 589832 | tf_op jit(solution)/shard_map/ppermute | solution.py:23

commit v7 on v6

--- a/solution.py
+++ b/solution.py
@@ -69,29 +69,32 @@
     )(starts, activations, gain)
 
 
-def product_kernel(starts_ref, x, *refs):
-    shards, out = refs[:-1], refs[-1]
-    total = 0.0
-    for i, shard in enumerate(shards):
-        start = pl.multiple_of(starts_ref[i], LANES)
-        total = total + jnp.dot(
-            x[:, pl.ds(start, shard.shape[0])], shard[...], preferred_element_type=jnp.float32
-        )
-    out[...] = total.astype(out.dtype)
-
-
-def product(starts, x, shards, dtype):
-    rows, part = x.shape
+def product_kernel(blocks, *refs):
+    xs, shards, outs = refs[:blocks], refs[blocks:-blocks], refs[-blocks:]
+    shard_rows = shards[0].shape[0]
+    for x, out in zip(xs, outs):
+        total = 0.0
+        for j, shard in enumerate(shards):
+            total = total + jnp.dot(
+                x[:, j * shard_rows : (j + 1) * shard_rows],
+                shard[...],
+                preferred_element_type=jnp.float32,
+            )
+        out[...] = total.astype(out.dtype)
+
+
+def products(xs, shards, dtype):
+    rows, part = xs[0].shape
     width = shards[0].shape[1]
-    vmem = pl.BlockSpec(memory_space=pltpu.VMEM)
-    return pl.pallas_call(
-        product_kernel,
-        in_specs=[pl.BlockSpec(memory_space=pltpu.SMEM)] + [vmem] * (1 + len(shards)),
-        out_shape=jax.ShapeDtypeStruct((rows, width), dtype),
+    blocks = len(xs)
+    size = 8 * blocks * rows * part
+    return pl.pallas_call(
+        lambda *refs: product_kernel(blocks, *refs),
+        out_shape=[jax.ShapeDtypeStruct((rows, width), dtype)] * blocks,
         compiler_params=params(24),
-        cost_estimate=cost(8 * rows * part * width, 8 * (rows * part + part * width)),
-        name="product",
-    )(starts, x, *shards)
+        cost_estimate=cost(size * width, size),
+        name="products",
+    )(*xs, *shards)
 
 
 def added(own, parts, cols):
@@ -237,11 +240,9 @@
     _, micro_count, tok_rows, _ = handoff.shape
 
     next_gain = moved(norm_gain, "section", lambda i: i - 1).astype(jnp.float32)
-    parity, own_y = own_place // 2, own_place % 2
-    quad_ids = jnp.arange(quads, dtype=jnp.int32)
-    cut_starts = jnp.stack(
-        [(quad_ids * QUAD + 2 * p) * shard_rows for p in (parity, 1 - parity)]
-    )
+    quad_order = (own_quad - jnp.arange(quads, dtype=jnp.int32)) % quads * QUAD
+    flips = jnp.arange(QUAD, dtype=jnp.int32)
+    cut_starts = (quad_order[None, :] + (own_place ^ flips)[:, None]) * shard_rows
     cuts = normed_cuts(handoff[0], next_gain, cut_starts)
 
     def to_next_section(part, flip):
@@ -252,32 +253,22 @@
         ]
         return lax.ppermute(part, ("section", "ctx"), route)
 
-    own_rows, next_rows = to_next_section(cuts[0], 0), to_next_section(cuts[1], 2)
-
-    def along_z(part):
-        return [moved(part, "ctx", lambda i, j=j: i + QUAD * j) for j in range(1, quads)]
-
-    def over_y(part):
-        return moved(part, "ctx", lambda i: i ^ 1)
-
-    key_part, value_part, _ = lax.optimization_barrier(
-        (weight[:, :kv_width], weight[:, kv_width:], cuts)
-    )
-    key_line = along_z(key_part)
-    late_part, _ = lax.optimization_barrier((value_part, key_line[-1]))
-    value_line = along_z(late_part)
-    key_y, value_y = over_y(key_part), over_y(value_part)
-    passed_on, _ = lax.optimization_barrier((key_line, value_y))
-    key_shards = [key_part, *key_line, key_y, *map(over_y, passed_on)]
-    value_shards = [value_part, *value_line, value_y]
-    line = (own_quad - quad_ids) % quads * 2
-    starts = jnp.concatenate([line + own_y, line + 1 - own_y]) * shard_rows
-
-    def partial(shards):
-        return product(starts, next_rows, shards, jnp.bfloat16)
-
-    def sent_back(part):
-        return [moved(part, "ctx", lambda i: i ^ 2)]
+    arrived = [to_next_section(cuts[flip], flip) for flip in range(QUAD)]
+
+    def same_place(part):
+        return [part] + [
+            moved(part, "ctx", lambda i, j=j: i + QUAD * j) for j in range(1, quads)
+        ]
+
+    key_shards = same_place(weight[:, :kv_width])
+    late_part, _ = lax.optimization_barrier((weight[:, kv_width:], key_shards[-1]))
+    value_shards = same_place(late_part)
+
+    def sent_back(parts):
+        return [
+            moved(part, "ctx", lambda i, flip=flip: i ^ flip)
+            for flip, part in enumerate(parts, start=1)
+        ]
 
     def near_blocks(block):
         return [moved(block, "ctx", lambda i: i + 2), moved(block, "ctx", lambda i: i ^ 1)]
@@ -307,14 +298,14 @@
     sine_part = jnp.concatenate([-sine_part, sine_part], axis=1)
     odd = (own_index % 2).astype(jnp.int32).reshape(1)
 
-    key_parts = sent_back(partial(key_shards))
-    own_keys = product(starts, own_rows, key_shards, jnp.float32)
+    key_parts = sent_back(products(arrived[1:], key_shards, jnp.bfloat16))
+    (own_keys,) = products(arrived[:1], key_shards, jnp.float32)
+    value_products = products(arrived[1:], value_shards, jnp.bfloat16)
+    key_parts, value_products = lax.optimization_barrier((key_parts, value_products))
     key_block = block_sum(key_sum_kernel, "key_sum", own_keys, key_parts, cosine, sine_part)
-    value_line, _ = lax.optimization_barrier((value_line, key_parts))
-    value_shards += map(over_y, value_line)
-    value_shards, _ = lax.optimization_barrier((value_shards, key_block))
-    value_parts = sent_back(partial(value_shards))
-    own_values = product(starts, own_rows, value_shards, jnp.float32)
+    value_products, _ = lax.optimization_barrier((value_products, key_block))
+    value_parts = sent_back(value_products)
+    (own_values,) = products(arrived[:1], value_shards, jnp.float32)
     key_near = near_blocks(key_block)
     value_parts, _ = lax.optimization_barrier((value_parts, key_near))
     key_window = window_of(key_block, *key_near)
@@ -322,7 +313,8 @@
         odd, queries, key_window, own_pos[:, :, None], col_pos[:, None, :]
     )
     value_block = block_sum(value_sum_kernel, "value_sum", own_values, value_parts)
-    value_window = window_of(value_block, *near_blocks(value_block))
+    value_near, weights = lax.optimization_barrier((near_blocks(value_block), weights))
+    value_window = window_of(value_block, *value_near)
     out = mixed_values(odd, weights, sums, value_window)
     return (out, log_sums[None])
 

time: 115 us -> 109 us (0.948)
  Pallas kernels: 19.7 us -> 14.1 us
    ppermute x15, waiting for transfers between devices: 54.6 us -> 46 us  [moved(): lax.ppermute(block, axis, [(i, target(i) % size) for i in range(size)])]
    ppermute x2 -> x4, waiting for transfers between devices: 8.76 us -> 14.9 us  [to_next_section(): return lax.ppermute(part, ('section', 'ctx'), route)]
    pallas_call x4, Pallas kernels: 7.84 us -> 2.31 us  [products(): pl.pallas_call(lambda *refs: product_kernel(blocks, *refs), out_shape=[ja...]
    ppermute x2, starting transfers between devices: 7.81 us -> 4.04 us  [window_of(): lax.ppermute(beside, 'ctx', [(i, (i + 2) % cycle_size) for i in range(0,...]
    ppermute x2 -> x4, starting transfers between devices: 1.27 us -> 4.23 us  [to_next_section(): return lax.ppermute(part, ('section', 'ctx'), route)]
    ppermute x2, waiting for transfers between devices: 2.77 us -> 5.64 us  [window_of(): lax.ppermute(beside, 'ctx', [(i, (i + 2) % cycle_size) for i in range(0,...]
    ppermute x15, starting transfers between devices: 14.8 us -> 16.1 us  [moved(): lax.ppermute(block, axis, [(i, target(i) % size) for i in range(size)])]
  transfers between devices with their start and end apart: 19 -> 21, of which waited for: 11 -> 14; matrix products, arithmetic and copies ran while one was open for 2% -> 2% of each run, Pallas kernels for 13% -> 10%
where the time goes in v7:
time: 109 us
  waiting for transfers between devices  66.6 us (61%)
  starting transfers between devices  24.4 us (22%)
  Pallas kernels  14.1 us (13%)
  local copies, waits for them, and re-layouts  2.55 us (2%)
    ppermute x15, waiting for transfers between devices, moved(): lax.ppermute(block, axis, [(i, target(i) % size) for i in range(size)])  46 us
    ppermute x15, starting transfers between devices, moved(): lax.ppermute(block, axis, [(i, target(i) % size) for i in range(size)])  16.1 us
    ppermute x4, waiting for transfers between devices, to_next_section(): return lax.ppermute(part, ('section', 'ctx'), route)  14.9 us
    pallas_call x1, Pallas kernels, scored(): pl.pallas_call(score_kernel, grid=(micro_count, KVH), in_specs=[pl.BlockS...  6.92 us
    ppermute x2, waiting for transfers between devices, window_of(): lax.ppermute(beside, 'ctx', [(i, (i + 2) % cycle_size) for i in range(0,...  5.64 us
    ppermute x4, starting transfers between devices, to_next_section(): return lax.ppermute(part, ('section', 'ctx'), route)  4.23 us
    ppermute x2, starting transfers between devices, window_of(): lax.ppermute(beside, 'ctx', [(i, (i + 2) % cycle_size) for i in range(0,...  4.04 us
    pallas_call x1, Pallas kernels, mixed_values(): pl.pallas_call(mix_kernel, grid=(micro_count,), in_specs=[pl.BlockSpec(me...  2.49 us
  transfers between devices with their start and end apart: 21, of which 14 were waited for; matrix products, arithmetic and copies ran while one was open for 2% of the time, Pallas kernels for 10%

profile of v7, /device:TPU:0, one launch (start us, length us, event | category | flops | bytes accessed | tf_op | source)
XLA Modules:
  0.0 109.3 jit_solution(12524409969710066620)
XLA Ops:
  0.7 2.4 %collective-permute-start = (bf16[1,4096]{1,0:T(2,128)(2,1)}, bf16[1,4096]{1,0:T(2,128)(2,1)S(1)}, u32[]{:S(2)}, u32[]{:S(2)}) collective-permute-start(bf16[1,4096]{1,0:T(2,128)(2,1)} %param.6), channel_id=1, source_target_pairs={{0,24},{8,0},{16,8},{24,16},{1,25},{9,1},{17,9},{25,17},{2,26},{10... | collective-permute-start | bytes 24584 | tf_op jit(solution)/shard_map/ppermute | solution.py:23
  3.1 1.3 %fusion.4 = (bf16[512,512]{1,0:T(8,128)(2,1)S(1)}, bf16[512,512]{1,0:T(8,128)(2,1)S(1)}) fusion(bf16[512,1024]{1,0:T(8,128)(2,1)} %bitcast.7), kind=kLoop, calls=%fused_computation.20 | loop fusion | bytes 2097152 | tf_op jit(solution)/shard_map/slice | solution.py:263
  4.3 2.7 %collective-permute-start.2 = (bf16[512,512]{1,0:T(8,128)(2,1)S(1)}, bf16[512,512]{1,0:T(8,128)(2,1)S(1)}, u32[]{:S(2)}, u32[]{:S(2)}) collective-permute-start(bf16[512,512]{1,0:T(8,128)(2,1)S(1)} %get-tuple-element.60.refs_3_.refs_1_), channel_id=1, source_target_pairs={{0,4},{1,5},{2,6},{3,7},{4,0},{5,1},{6,2},{7,3},{8,12},{9,13},{10,... | collective-permute-start | bytes 1572872 | tf_op jit(solution)/shard_map/ppermute | solution.py:23
  7.6 2.1 %norm_cuts.1 = (bf16[192,1024]{1,0:T(8,128)(2,1)S(1)}, bf16[192,1024]{1,0:T(8,128)(2,1)}, bf16[192,1024]{1,0:T(8,128)(2,1)}, bf16[192,1024]{1,0:T(8,128)(2,1)}) custom-call(s32[4,2]{1,0:T(4,128)S(1)} %add_multiply_fusion.starts_ref, bf16[2,96,4096]{2,1,0:T(8,128)(2,1)S(1)} %bitcast.6, f32[1,4096]{1,0:T(1,128)S(1)} %convert_element_type.14.gain_ref), custom_call_target="tpu_custom_call" | custom-call | flops 4718592 | bytes 3145728 | tf_op jit(solution)/shard_map/norm_cuts/pallas_call | solution.py:56
  10.9 2.5 %collective-permute-start.5 = (bf16[192,1024]{1,0:T(8,128)(2,1)}, bf16[192,1024]{1,0:T(8,128)(2,1)S(1)}, u32[]{:S(2)}, u32[]{:S(2)}) collective-permute-start(bf16[192,1024]{1,0:T(8,128)(2,1)} %get-tuple-element.34), channel_id=1, source_target_pairs={{0,10},{1,11},{2,8},{3,9},{4,14},{5,15},{6,12},{7,13},{8,18},{9,19... | collective-permute-start | bytes 1179656 | tf_op jit(solution)/shard_map/ppermute | solution.py:254
  13.6 1.2 %collective-permute-start.1 = (bf16[192,1024]{1,0:T(8,128)(2,1)}, bf16[192,1024]{1,0:T(8,128)(2,1)S(1)}, u32[]{:S(2)}, u32[]{:S(2)}) collective-permute-start(bf16[192,1024]{1,0:T(8,128)(2,1)} %copy-done.2), channel_id=1, source_target_pairs={{0,8},{1,9},{2,10},{3,11},{4,12},{5,13},{6,14},{7,15},{8,16},{9,17... | collective-permute-start | bytes 1179656 | tf_op jit(solution)/shard_map/ppermute | solution.py:254
  14.8 15.2 %collective-permute-done.2.refs_4_.refs_2_ = bf16[512,512]{1,0:T(8,128)(2,1)S(1)} collective-permute-done((bf16[512,512]{1,0:T(8,128)(2,1)S(1)}, bf16[512,512]{1,0:T(8,128)(2,1)S(1)}, u32[]{:S(2)}, u32[]{:S(2)}) %collective-permute-start.2) | collective-permute-done | bytes 524320 | tf_op jit(solution)/shard_map/ppermute | solution.py:23
  30.6 2.9 %collective-permute-done.5.refs_1_ = bf16[192,1024]{1,0:T(8,128)(2,1)S(1)} collective-permute-done((bf16[192,1024]{1,0:T(8,128)(2,1)}, bf16[192,1024]{1,0:T(8,128)(2,1)S(1)}, u32[]{:S(2)}, u32[]{:S(2)}) %collective-permute-start.5) | collective-permute-done | bytes 393248 | tf_op jit(solution)/shard_map/ppermute | solution.py:254
  33.5 12.0 %collective-permute-done.6.refs_2_ = bf16[192,1024]{1,0:T(8,128)(2,1)S(1)} collective-permute-done((bf16[192,1024]{1,0:T(8,128)(2,1)}, bf16[192,1024]{1,0:T(8,128)(2,1)S(1)}, u32[]{:S(2)}, u32[]{:S(2)}) %collective-permute-start.6) | collective-permute-done | bytes 393248 | tf_op jit(solution)/shard_map/ppermute | solution.py:254
  45.5 0.8 products.5
  46.3 1.6 %collective-permute-start.7 = (bf16[192,512]{1,0:T(8,128)(2,1)S(1)}, bf16[192,512]{1,0:T(8,128)(2,1)S(1)}, u32[]{:S(2)}, u32[]{:S(2)}) collective-permute-start(bf16[192,512]{1,0:T(8,128)(2,1)S(1)} %get-tuple-element.36), channel_id=1, source_target_pairs={{0,1},{1,0},{2,3},{3,2},{4,5},{5,4},{6,7},{7,6},{8,9},{9,8},{10,11... | collective-permute-start | bytes 589832 | tf_op jit(solution)/shard_map/ppermute | solution.py:23
  47.9 2.0 %collective-permute-start.9 = (bf16[192,512]{1,0:T(8,128)(2,1)S(1)}, bf16[192,512]{1,0:T(8,128)(2,1)S(1)}, u32[]{:S(2)}, u32[]{:S(2)}) collective-permute-start(bf16[192,512]{1,0:T(8,128)(2,1)S(1)} %get-tuple-element.38), channel_id=1, source_target_pairs={{0,3},{1,2},{2,1},{3,0},{4,7},{5,6},{6,5},{7,4},{8,11},{9,10},{10,... | collective-permute-start | bytes 589832 | tf_op jit(solution)/shard_map/ppermute | solution.py:23
  50.2 4.7 %collective-permute-done.3.refs_2_.refs_4_ = bf16[512,512]{1,0:T(8,128)(2,1)S(1)} collective-permute-done((bf16[512,512]{1,0:T(8,128)(2,1)S(1)}, bf16[512,512]{1,0:T(8,128)(2,1)S(1)}, u32[]{:S(2)}, u32[]{:S(2)}) %collective-permute-start.3) | collective-permute-done | bytes 524320 | tf_op jit(solution)/shard_map/ppermute | solution.py:23
  55.0 0.8 products.6
  55.8 3.3 %collective-permute-done.8.refs_1_ = bf16[192,512]{1,0:T(8,128)(2,1)S(1)} collective-permute-done((bf16[192,512]{1,0:T(8,128)(2,1)S(1)}, bf16[192,512]{1,0:T(8,128)(2,1)S(1)}, u32[]{:S(2)}, u32[]{:S(2)}) %collective-permute-start.8) | collective-permute-done | bytes 196640 | tf_op jit(solution)/shard_map/ppermute | solution.py:23
  59.1 5.2 %collective-permute-done.9.refs_2_ = bf16[192,512]{1,0:T(8,128)(2,1)S(1)} collective-permute-done((bf16[192,512]{1,0:T(8,128)(2,1)S(1)}, bf16[192,512]{1,0:T(8,128)(2,1)S(1)}, u32[]{:S(2)}, u32[]{:S(2)}) %collective-permute-start.9) | collective-permute-done | bytes 196640 | tf_op jit(solution)/shard_map/ppermute | solution.py:23
  65.0 1.6 %collective-permute-start.10 = (bf16[192,512]{1,0:T(8,128)(2,1)S(1)}, bf16[192,512]{1,0:T(8,128)(2,1)S(1)}, u32[]{:S(2)}, u32[]{:S(2)}) collective-permute-start(bf16[192,512]{1,0:T(8,128)(2,1)S(1)} %get-tuple-element.48), channel_id=1, source_target_pairs={{0,1},{1,0},{2,3},{3,2},{4,5},{5,4},{6,7},{7,6},{8,9},{9,8},{10,11... | collective-permute-start | bytes 589832 | tf_op jit(solution)/shard_map/ppermute | solution.py:23
  66.6 2.2 %collective-permute-start.11 = (bf16[192,512]{1,0:T(8,128)(2,1)S(1)}, bf16[192,512]{1,0:T(8,128)(2,1)S(1)}, u32[]{:S(2)}, u32[]{:S(2)}) collective-permute-start(bf16[192,512]{1,0:T(8,128)(2,1)S(1)} %get-tuple-element.49), channel_id=1, source_target_pairs={{0,2},{1,3},{2,0},{3,1},{4,6},{5,7},{6,4},{7,5},{8,10},{9,11},{10,... | collective-permute-start | bytes 589832 | tf_op jit(solution)/shard_map/ppermute | solution.py:23
  68.9 1.0 collective-permute-start.12
  69.8 2.5 %collective-permute-done.14.refs_3_ = bf16[192,512]{1,0:T(8,128)(2,1)S(1)} collective-permute-done((bf16[192,512]{1,0:T(8,128)(2,1)S(1)}, bf16[192,512]{1,0:T(8,128)(2,1)S(1)}, u32[]{:S(2)}, u32[]{:S(2)}) %collective-permute-start.14) | collective-permute-done | bytes 196640 | tf_op jit(solution)/shard_map/ppermute | solution.py:23
  72.4 1.9 %collective-permute-start.18 = (bf16[192,512]{1,0:T(8,128)(2,1)S(1)}, bf16[192,512]{1,0:T(8,128)(2,1)S(1)}, u32[]{:S(2)}, u32[]{:S(2)}) collective-permute-start(bf16[192,512]{1,0:T(8,128)(2,1)S(1)} %collective-permute-done.14.refs_3_), channel_id=1, source_target_pairs={{0,2},{2,4},{4,6},{6,0},{8,10},{10,12},{12,14},{14,8},{16,18},{18,... | collective-permute-start | bytes 589832 | tf_op jit(solution)/shard_map/ppermute | solution.py:278
  74.3 1.1 collective-permute-done.13.refs_1_
  75.4 1.5 %collective-permute-start.17 = (bf16[192,512]{1,0:T(8,128)(2,1)S(1)}, bf16[192,512]{1,0:T(8,128)(2,1)S(1)}, u32[]{:S(2)}, u32[]{:S(2)}) collective-permute-start(bf16[192,512]{1,0:T(8,128)(2,1)S(1)} %collective-permute-done.13.refs_1_), channel_id=1, source_target_pairs={{0,1},{1,2},{2,3},{3,4},{4,5},{5,6},{6,7},{7,0},{8,9},{9,10},{10,1... | collective-permute-start | bytes 589832 | tf_op jit(solution)/shard_map/ppermute | solution.py:23
  77.3 1.6 %collective-permute-done.11.refs_1_ = bf16[192,512]{1,0:T(8,128)(2,1)S(1)} collective-permute-done((bf16[192,512]{1,0:T(8,128)(2,1)S(1)}, bf16[192,512]{1,0:T(8,128)(2,1)S(1)}, u32[]{:S(2)}, u32[]{:S(2)}) %collective-permute-start.11) | collective-permute-done | bytes 196640 | tf_op jit(solution)/shard_map/ppermute | solution.py:23
  78.8 3.7 %collective-permute-done.12.refs_2_ = bf16[192,512]{1,0:T(8,128)(2,1)S(1)} collective-permute-done((bf16[192,512]{1,0:T(8,128)(2,1)S(1)}, bf16[192,512]{1,0:T(8,128)(2,1)S(1)}, u32[]{:S(2)}, u32[]{:S(2)}) %collective-permute-start.12) | collective-permute-done | bytes 196640 | tf_op jit(solution)/shard_map/ppermute | solution.py:23
  83.4 4.6 %collective-permute-done.18.refs_4_ = bf16[192,512]{1,0:T(8,128)(2,1)S(1)} collective-permute-done((bf16[192,512]{1,0:T(8,128)(2,1)S(1)}, bf16[192,512]{1,0:T(8,128)(2,1)S(1)}, u32[]{:S(2)}, u32[]{:S(2)}) %collective-permute-start.18) | collective-permute-done | bytes 196640 | tf_op jit(solution)/shard_map/ppermute | solution.py:278
  88.0 2.4 %collective-permute-done.17.refs_2_ = bf16[192,512]{1,0:T(8,128)(2,1)S(1)} collective-permute-done((bf16[192,512]{1,0:T(8,128)(2,1)S(1)}, bf16[192,512]{1,0:T(8,128)(2,1)S(1)}, u32[]{:S(2)}, u32[]{:S(2)}) %collective-permute-start.17) | collective-permute-done | bytes 196640 | tf_op jit(solution)/shard_map/ppermute | solution.py:23
  90.5 6.9 %scores.1 = (bf16[2,4,768,384]{3,2,1,0:T(8,128)(2,1)S(1)}, f32[2,4,96,128]{3,2,1,0:T(8,128)S(1)}, f32[2,32,96]{2,1,0:T(8,128)}) custom-call(s32[1]{0:T(128)} %bitcast.odd_ref, bf16[1,2,96,4096]{3,2,1,0:T(8,128)(2,1)S(1)} %copy-done.1, bf16[192,512]{1,0:T(8,128)(2,1)S(1)} %key_sum.1.refs_0_, bf16[192,512]{1,0:T(8,128)(2,1)S(1)} %collective-permute-done.13.refs_1_, ...), custom_call_target="tpu_custom_call" | custom-call | flops 603979776 | bytes 8388608 | tf_op jit(solution)/shard_map/scores/pallas_call | solution.py:170
  97.4 2.1 %collective-permute-start.20 = (bf16[192,512]{1,0:T(8,128)(2,1)S(1)}, bf16[192,512]{1,0:T(8,128)(2,1)S(1)}, u32[]{:S(2)}, u32[]{:S(2)}) collective-permute-start(bf16[192,512]{1,0:T(8,128)(2,1)S(1)} %collective-permute-done.16.refs_3_), channel_id=1, source_target_pairs={{0,2},{2,4},{4,6},{6,0},{8,10},{10,12},{12,14},{14,8},{16,18},{18,... | collective-permute-start | bytes 589832 | tf_op jit(solution)/shard_map/ppermute | solution.py:278
  99.6 6.2 %collective-permute-done.19.refs_2_ = bf16[192,512]{1,0:T(8,128)(2,1)S(1)} collective-permute-done((bf16[192,512]{1,0:T(8,128)(2,1)S(1)}, bf16[192,512]{1,0:T(8,128)(2,1)S(1)}, u32[]{:S(2)}, u32[]{:S(2)}) %collective-permute-start.19) | collective-permute-done | bytes 196640 | tf_op jit(solution)/shard_map/ppermute | solution.py:23
  105.8 1.0 collective-permute-done.20.refs_4_
  106.8 2.5 %mixed_values.1 = bf16[1,2,96,4096]{3,2,1,0:T(8,128)(2,1)} custom-call(s32[1]{0:T(128)} %bitcast.odd_ref, bf16[2,4,768,384]{3,2,1,0:T(8,128)(2,1)S(1)} %get-tuple-element.55.weights, f32[2,4,96,128]{3,2,1,0:T(8,128)S(1)} %get-tuple-element.56.sums, bf16[192,512]{1,0:T(8,128)(2,1)S(1)} %value_sum.1.refs_0_, ...), custom_call_target="tpu_custom_call" | custom-call | flops 603979776 | bytes 8388608 | tf_op jit(solution)/shard_map/mixed_values/pallas_call | solution.py:215
  (47 shorter events, 4.8 us)
Async XLA Ops:
  0.6 6.4 %copy-start.3 = (s32[2,16]{1,0:T(2,128)S(1)}, s32[2,16]{1,0:T(2,128)}, u32[]{:S(2)}) copy-start(s32[2,16]{1,0:T(2,128)} %param.9) | copy-start | bytes 388
  0.6 7.0 %copy-start = (bf16[1,2,96,4096]{3,2,1,0:T(8,128)(2,1)S(1)}, bf16[1,2,96,4096]{3,2,1,0:T(8,128)(2,1)}, u32[]{:S(2)}) copy-start(bf16[1,2,96,4096]{3,2,1,0:T(8,128)(2,1)} %param.5) | copy-start | bytes 4718596
  0.7 7.0 %collective-permute-start = (bf16[1,4096]{1,0:T(2,128)(2,1)}, bf16[1,4096]{1,0:T(2,128)(2,1)S(1)}, u32[]{:S(2)}, u32[]{:S(2)}) collective-permute-start(bf16[1,4096]{1,0:T(2,128)(2,1)} %param.6), channel_id=1, source_target_pairs={{0,24},{8,0},{16,8},{24,16},{1,25},{9,1},{17,9},{25,17},{2,26},{10... | collective-permute-start | bytes 24584 | tf_op jit(solution)/shard_map/ppermute | solution.py:23
  4.3 25.7 %collective-permute-start.2 = (bf16[512,512]{1,0:T(8,128)(2,1)S(1)}, bf16[512,512]{1,0:T(8,128)(2,1)S(1)}, u32[]{:S(2)}, u32[]{:S(2)}) collective-permute-start(bf16[512,512]{1,0:T(8,128)(2,1)S(1)} %get-tuple-element.60.refs_3_.refs_1_), channel_id=1, source_target_pairs={{0,4},{1,5},{2,6},{3,7},{4,0},{5,1},{6,2},{7,3},{8,12},{9,13},{10,... | collective-permute-start | bytes 1572872 | tf_op jit(solution)/shard_map/ppermute | solution.py:23
  9.7 0.8 copy-start.2
  10.5 20.1 %collective-permute-start.4 = (bf16[192,1024]{1,0:T(8,128)(2,1)}, bf16[192,1024]{1,0:T(8,128)(2,1)S(1)}, u32[]{:S(2)}, u32[]{:S(2)}) collective-permute-start(bf16[192,1024]{1,0:T(8,128)(2,1)} %get-tuple-element.33), channel_id=1, source_target_pairs={{0,9},{1,8},{2,11},{3,10},{4,13},{5,12},{6,15},{7,14},{8,17},{9,16... | collective-permute-start | bytes 1179656 | tf_op jit(solution)/shard_map/ppermute | solution.py:254
  10.9 22.6 %collective-permute-start.5 = (bf16[192,1024]{1,0:T(8,128)(2,1)}, bf16[192,1024]{1,0:T(8,128)(2,1)S(1)}, u32[]{:S(2)}, u32[]{:S(2)}) collective-permute-start(bf16[192,1024]{1,0:T(8,128)(2,1)} %get-tuple-element.34), channel_id=1, source_target_pairs={{0,10},{1,11},{2,8},{3,9},{4,14},{5,15},{6,12},{7,13},{8,18},{9,19... | collective-permute-start | bytes 1179656 | tf_op jit(solution)/shard_map/ppermute | solution.py:254
  13.5 32.0 %collective-permute-start.6 = (bf16[192,1024]{1,0:T(8,128)(2,1)}, bf16[192,1024]{1,0:T(8,128)(2,1)S(1)}, u32[]{:S(2)}, u32[]{:S(2)}) collective-permute-start(bf16[192,1024]{1,0:T(8,128)(2,1)} %get-tuple-element.35), channel_id=1, source_target_pairs={{0,11},{1,10},{2,9},{3,8},{4,15},{5,14},{6,13},{7,12},{8,19},{9,18... | collective-permute-start | bytes 1179656 | tf_op jit(solution)/shard_map/ppermute | solution.py:254
  13.6 36.2 %collective-permute-start.1 = (bf16[192,1024]{1,0:T(8,128)(2,1)}, bf16[192,1024]{1,0:T(8,128)(2,1)S(1)}, u32[]{:S(2)}, u32[]{:S(2)}) collective-permute-start(bf16[192,1024]{1,0:T(8,128)(2,1)} %copy-done.2), channel_id=1, source_target_pairs={{0,8},{1,9},{2,10},{3,11},{4,12},{5,13},{6,14},{7,15},{8,16},{9,17... | collective-permute-start | bytes 1179656 | tf_op jit(solution)/shard_map/ppermute | solution.py:254
  30.0 24.9 %collective-permute-start.3 = (bf16[512,512]{1,0:T(8,128)(2,1)S(1)}, bf16[512,512]{1,0:T(8,128)(2,1)S(1)}, u32[]{:S(2)}, u32[]{:S(2)}) collective-permute-start(bf16[512,512]{1,0:T(8,128)(2,1)S(1)} %get-tuple-element.32.refs_1_.refs_3_), channel_id=1, source_target_pairs={{0,4},{1,5},{2,6},{3,7},{4,0},{5,1},{6,2},{7,3},{8,12},{9,13},{10,... | collective-permute-start | bytes 1572872 | tf_op jit(solution)/shard_map/ppermute | solution.py:23
  46.3 9.4 %collective-permute-start.7 = (bf16[192,512]{1,0:T(8,128)(2,1)S(1)}, bf16[192,512]{1,0:T(8,128)(2,1)S(1)}, u32[]{:S(2)}, u32[]{:S(2)}) collective-permute-start(bf16[192,512]{1,0:T(8,128)(2,1)S(1)} %get-tuple-element.36), channel_id=1, source_target_pairs={{0,1},{1,0},{2,3},{3,2},{4,5},{5,4},{6,7},{7,6},{8,9},{9,8},{10,11... | collective-permute-start | bytes 589832 | tf_op jit(solution)/shard_map/ppermute | solution.py:23
  47.9 11.2 %collective-permute-start.8 = (bf16[192,512]{1,0:T(8,128)(2,1)S(1)}, bf16[192,512]{1,0:T(8,128)(2,1)S(1)}, u32[]{:S(2)}, u32[]{:S(2)}) collective-permute-start(bf16[192,512]{1,0:T(8,128)(2,1)S(1)} %get-tuple-element.37), channel_id=1, source_target_pairs={{0,2},{1,3},{2,0},{3,1},{4,6},{5,7},{6,4},{7,5},{8,10},{9,11},{10,... | collective-permute-start | bytes 589832 | tf_op jit(solution)/shard_map/ppermute | solution.py:23
  47.9 16.5 %collective-permute-start.9 = (bf16[192,512]{1,0:T(8,128)(2,1)S(1)}, bf16[192,512]{1,0:T(8,128)(2,1)S(1)}, u32[]{:S(2)}, u32[]{:S(2)}) collective-permute-start(bf16[192,512]{1,0:T(8,128)(2,1)S(1)} %get-tuple-element.38), channel_id=1, source_target_pairs={{0,3},{1,2},{2,1},{3,0},{4,7},{5,6},{6,5},{7,4},{8,11},{9,10},{10,... | collective-permute-start | bytes 589832 | tf_op jit(solution)/shard_map/ppermute | solution.py:23
  64.5 26.0 %copy-start.1 = (bf16[1,2,96,4096]{3,2,1,0:T(8,128)(2,1)S(1)}, bf16[1,2,96,4096]{3,2,1,0:T(8,128)(2,1)}, u32[]{:S(2)}) copy-start(bf16[1,2,96,4096]{3,2,1,0:T(8,128)(2,1)} %q_ref.1) | copy-start | bytes 4718596
  64.5 7.8 %collective-permute-start.14 = (bf16[192,512]{1,0:T(8,128)(2,1)S(1)}, bf16[192,512]{1,0:T(8,128)(2,1)S(1)}, u32[]{:S(2)}, u32[]{:S(2)}) collective-permute-start(bf16[192,512]{1,0:T(8,128)(2,1)S(1)} %key_sum.1.refs_0_), channel_id=1, source_target_pairs={{0,1},{1,0},{2,3},{3,2},{4,5},{5,4},{6,7},{7,6},{8,9},{9,8},{10,11... | collective-permute-start | bytes 589832 | tf_op jit(solution)/shard_map/ppermute | solution.py:23
  65.0 10.3 %collective-permute-start.13 = (bf16[192,512]{1,0:T(8,128)(2,1)S(1)}, bf16[192,512]{1,0:T(8,128)(2,1)S(1)}, u32[]{:S(2)}, u32[]{:S(2)}) collective-permute-start(bf16[192,512]{1,0:T(8,128)(2,1)S(1)} %key_sum.1.refs_0_), channel_id=1, source_target_pairs={{0,2},{1,3},{2,4},{3,5},{4,6},{5,7},{6,0},{7,1},{8,10},{9,11},{10,... | collective-permute-start | bytes 589832 | tf_op jit(solution)/shard_map/ppermute | solution.py:23
  65.0 12.3 %collective-permute-start.10 = (bf16[192,512]{1,0:T(8,128)(2,1)S(1)}, bf16[192,512]{1,0:T(8,128)(2,1)S(1)}, u32[]{:S(2)}, u32[]{:S(2)}) collective-permute-start(bf16[192,512]{1,0:T(8,128)(2,1)S(1)} %get-tuple-element.48), channel_id=1, source_target_pairs={{0,1},{1,0},{2,3},{3,2},{4,5},{5,4},{6,7},{7,6},{8,9},{9,8},{10,11... | collective-permute-start | bytes 589832 | tf_op jit(solution)/shard_map/ppermute | solution.py:23
  66.6 12.2 %collective-permute-start.11 = (bf16[192,512]{1,0:T(8,128)(2,1)S(1)}, bf16[192,512]{1,0:T(8,128)(2,1)S(1)}, u32[]{:S(2)}, u32[]{:S(2)}) collective-permute-start(bf16[192,512]{1,0:T(8,128)(2,1)S(1)} %get-tuple-element.49), channel_id=1, source_target_pairs={{0,2},{1,3},{2,0},{3,1},{4,6},{5,7},{6,4},{7,5},{8,10},{9,11},{10,... | collective-permute-start | bytes 589832 | tf_op jit(solution)/shard_map/ppermute | solution.py:23
  68.9 13.6 %collective-permute-start.12 = (bf16[192,512]{1,0:T(8,128)(2,1)S(1)}, bf16[192,512]{1,0:T(8,128)(2,1)S(1)}, u32[]{:S(2)}, u32[]{:S(2)}) collective-permute-start(bf16[192,512]{1,0:T(8,128)(2,1)S(1)} %get-tuple-element.50), channel_id=1, source_target_pairs={{0,3},{1,2},{2,1},{3,0},{4,7},{5,6},{6,5},{7,4},{8,11},{9,10},{10,... | collective-permute-start | bytes 589832 | tf_op jit(solution)/shard_map/ppermute | solution.py:23
  72.4 15.7 %collective-permute-start.18 = (bf16[192,512]{1,0:T(8,128)(2,1)S(1)}, bf16[192,512]{1,0:T(8,128)(2,1)S(1)}, u32[]{:S(2)}, u32[]{:S(2)}) collective-permute-start(bf16[192,512]{1,0:T(8,128)(2,1)S(1)} %collective-permute-done.14.refs_3_), channel_id=1, source_target_pairs={{0,2},{2,4},{4,6},{6,0},{8,10},{10,12},{12,14},{14,8},{16,18},{18,... | collective-permute-start | bytes 589832 | tf_op jit(solution)/shard_map/ppermute | solution.py:278
  75.4 15.1 %collective-permute-start.17 = (bf16[192,512]{1,0:T(8,128)(2,1)S(1)}, bf16[192,512]{1,0:T(8,128)(2,1)S(1)}, u32[]{:S(2)}, u32[]{:S(2)}) collective-permute-start(bf16[192,512]{1,0:T(8,128)(2,1)S(1)} %collective-permute-done.13.refs_1_), channel_id=1, source_target_pairs={{0,1},{1,2},{2,3},{3,4},{4,5},{5,6},{6,7},{7,0},{8,9},{9,10},{10,1... | collective-permute-start | bytes 589832 | tf_op jit(solution)/shard_map/ppermute | solution.py:23
  82.6 14.8 %collective-permute-start.16 = (bf16[192,512]{1,0:T(8,128)(2,1)S(1)}, bf16[192,512]{1,0:T(8,128)(2,1)S(1)}, u32[]{:S(2)}, u32[]{:S(2)}) collective-permute-start(bf16[192,512]{1,0:T(8,128)(2,1)S(1)} %value_sum.1.refs_0_), channel_id=1, source_target_pairs={{0,1},{1,0},{2,3},{3,2},{4,5},{5,4},{6,7},{7,6},{8,9},{9,8},{10,11... | collective-permute-start | bytes 589832 | tf_op jit(solution)/shard_map/ppermute | solution.py:23
  83.3 14.1 %collective-permute-start.15 = (bf16[192,512]{1,0:T(8,128)(2,1)S(1)}, bf16[192,512]{1,0:T(8,128)(2,1)S(1)}, u32[]{:S(2)}, u32[]{:S(2)}) collective-permute-start(bf16[192,512]{1,0:T(8,128)(2,1)S(1)} %value_sum.1.refs_0_), channel_id=1, source_target_pairs={{0,2},{1,3},{2,4},{3,5},{4,6},{5,7},{6,0},{7,1},{8,10},{9,11},{10,... | collective-permute-start | bytes 589832 | tf_op jit(solution)/shard_map/ppermute | solution.py:23
  97.4 8.4 %collective-permute-start.19 = (bf16[192,512]{1,0:T(8,128)(2,1)S(1)}, bf16[192,512]{1,0:T(8,128)(2,1)S(1)}, u32[]{:S(2)}, u32[]{:S(2)}) collective-permute-start(bf16[192,512]{1,0:T(8,128)(2,1)S(1)} %collective-permute-done.15.refs_1_), channel_id=1, source_target_pairs={{0,1},{1,2},{2,3},{3,4},{4,5},{5,6},{6,7},{7,0},{8,9},{9,10},{10,1... | collective-permute-start | bytes 589832 | tf_op jit(solution)/shard_map/ppermute | solution.py:23
  97.4 9.4 %collective-permute-start.20 = (bf16[192,512]{1,0:T(8,128)(2,1)S(1)}, bf16[192,512]{1,0:T(8,128)(2,1)S(1)}, u32[]{:S(2)}, u32[]{:S(2)}) collective-permute-start(bf16[192,512]{1,0:T(8,128)(2,1)S(1)} %collective-permute-done.16.refs_3_), channel_id=1, source_target_pairs={{0,2},{2,4},{4,6},{6,0},{8,10},{10,12},{12,14},{14,8},{16,18},{18,... | collective-permute-start | bytes 589832 | tf_op jit(solution)/shard_map/ppermute | solution.py:278

commit v8 on v7

--- a/solution.py
+++ b/solution.py
@@ -11,6 +11,8 @@
 WINDOW = 4
 QUAD = 4
 GROUP = QH // KVH
+SCALE = HD**-0.5
+LOG2_E = 1.4426950408889634
 LANES = 128
 ROW_STEP = 16
 
@@ -128,50 +130,43 @@
     )(*tables, own, *parts)
 
 
-def stacked(refs, odd):
-    own, two_back, three_back, beside, from_even = refs
-    one_back = jnp.where(odd == 1, beside[...], from_even[...])
-    return jnp.concatenate([three_back[...], two_back[...], one_back, own[...]], axis=0)
-
-
-def score_kernel(odd_ref, q_ref, *refs):
-    key_refs, (row_pos, col_pos, weights, sums, log_sums) = refs[:5], refs[5:]
-    keys = stacked(key_refs, odd_ref[0])
+def score_kernel(q_ref, *refs):
+    key_refs, (row_pos, col_pos, weights, sums, log_sums) = refs[:WINDOW], refs[WINDOW:]
+    keys = jnp.concatenate([ref[...] for ref in key_refs], axis=0)
     tok_rows = q_ref.shape[2]
     visible = col_pos[0] <= row_pos[0]
     lane = lax.broadcasted_iota(jnp.int32, (tok_rows, LANES), 1)
     all_sums = jnp.ones((tok_rows, LANES), jnp.float32)
     all_max = jnp.zeros((tok_rows, LANES), jnp.float32)
     for h in range(GROUP):
-        scores = lax.dot_general(
+        dots = lax.dot_general(
             q_ref[0, 0, :, h * HD : (h + 1) * HD],
             keys,
             (((1,), (1,)), ((), ())),
             preferred_element_type=jnp.float32,
-        ) * HD ** (-0.5)
-        scores = jnp.where(visible, scores, -jnp.inf)
-        row_max = jnp.max(scores, axis=-1, keepdims=True)
-        exps = jnp.exp(scores - row_max)
+        )
+        dots = jnp.where(visible, dots, -jnp.inf)
+        row_max = jnp.max(dots, axis=-1, keepdims=True)
+        exps = jnp.exp2((dots - row_max) * (SCALE * LOG2_E))
         running = jnp.sum(exps, axis=-1, keepdims=True)
         weights[0, 0, h * tok_rows : (h + 1) * tok_rows, :] = exps.astype(jnp.bfloat16)
         all_sums = jnp.where(lane == h, running, all_sums)
         all_max = jnp.where(lane == h, row_max, all_max)
     sums[0, 0] = all_sums
-    log_sums[0] = jnp.transpose(all_max + jnp.log(all_sums))[:GROUP]
+    log_sums[0] = jnp.transpose(all_max * SCALE + jnp.log(all_sums))[:GROUP]
 
 
 def window_specs(tok_rows):
-    return [pl.BlockSpec((tok_rows, HD), lambda m, k: (m, k))] * 5
-
-
-def scored(odd, queries, window, row_pos, col_pos):
+    return [pl.BlockSpec((tok_rows, HD), lambda m, k: (m, k))] * WINDOW
+
+
+def scored(queries, window, row_pos, col_pos):
     _, micro_count, tok_rows, _ = queries.shape
     keys = WINDOW * tok_rows
     return pl.pallas_call(
         score_kernel,
         grid=(micro_count, KVH),
         in_specs=[
-            pl.BlockSpec(memory_space=pltpu.SMEM),
             pl.BlockSpec((1, 1, tok_rows, GROUP * HD), lambda m, k: (0, m, 0, k)),
             *window_specs(tok_rows),
             pl.BlockSpec((1, tok_rows, 1), lambda m, k: (m, 0, 0)),
@@ -190,12 +185,12 @@
         compiler_params=params(24),
         cost_estimate=cost(2 * micro_count * QH * tok_rows * keys * HD, 8 * 2**20),
         name="scores",
-    )(odd, queries, *window, row_pos, col_pos)
-
-
-def mix_kernel(odd_ref, weights, sums, *refs):
-    values = stacked(refs[:5], odd_ref[0])
-    out = refs[5]
+    )(queries, *window, row_pos, col_pos)
+
+
+def mix_kernel(weights, sums, *refs):
+    values = jnp.concatenate([ref[...] for ref in refs[:WINDOW]], axis=0)
+    out = refs[WINDOW]
     tok_rows = out.shape[2]
     for k in range(KVH):
         mixed = jnp.dot(
@@ -209,24 +204,23 @@
             ).astype(jnp.bfloat16)
 
 
-def mixed_values(odd, weights, sums, window):
+def mixed_values(weights, sums, window):
     micro_count, _, group_rows, keys = weights.shape
     tok_rows = group_rows // GROUP
     return pl.pallas_call(
         mix_kernel,
         grid=(micro_count,),
         in_specs=[
-            pl.BlockSpec(memory_space=pltpu.SMEM),
             pl.BlockSpec((1, KVH, group_rows, keys), lambda m: (m, 0, 0, 0)),
             pl.BlockSpec((1, KVH, tok_rows, LANES), lambda m: (m, 0, 0, 0)),
-            *[pl.BlockSpec((tok_rows, KVH * HD), lambda m: (m, 0))] * 5,
+            *[pl.BlockSpec((tok_rows, KVH * HD), lambda m: (m, 0))] * WINDOW,
         ],
         out_specs=pl.BlockSpec((1, 1, tok_rows, QH * HD), lambda m: (0, m, 0, 0)),
         out_shape=jax.ShapeDtypeStruct((1, micro_count, tok_rows, QH * HD), jnp.bfloat16),
         compiler_params=params(32),
         cost_estimate=cost(2 * micro_count * QH * tok_rows * keys * HD, 8 * 2**20),
         name="mixed_values",
-    )(odd, weights, sums, *window)
+    )(weights, sums, *window)
 
 
 def on_device(handoff, norm_gain, kv_weight, queries, span_order):
@@ -261,7 +255,7 @@
         ]
 
     key_shards = same_place(weight[:, :kv_width])
-    late_part, _ = lax.optimization_barrier((weight[:, kv_width:], key_shards[-1]))
+    late_part, _ = lax.optimization_barrier((weight[:, kv_width:], (key_shards[-1], arrived)))
     value_shards = same_place(late_part)
 
     def sent_back(parts):
@@ -271,14 +265,10 @@
         ]
 
     def near_blocks(block):
-        return [moved(block, "ctx", lambda i: i + 2), moved(block, "ctx", lambda i: i ^ 1)]
-
-    def window_of(block, two_back, beside):
-        three_back = moved(two_back, "ctx", lambda i: i + 1)
-        from_even = lax.ppermute(
-            beside, "ctx", [(i, (i + 2) % cycle_size) for i in range(0, cycle_size, 2)]
-        )
-        return [block, two_back, three_back, beside, from_even]
+        return [moved(block, "ctx", lambda i, d=d: i + d) for d in (1, 2)]
+
+    def window_of(block, one_back, two_back):
+        return [moved(one_back, "ctx", lambda i: i + 2), two_back, one_back, block]
 
     span_len = tok_rows // 2
     places_of = span_order[:, :, None] * span_len + jnp.arange(span_len, dtype=jnp.int32)
@@ -296,26 +286,23 @@
     cosine, sine_part = jnp.cos(angles), jnp.sin(angles)
     cosine = jnp.concatenate([cosine, cosine], axis=1)
     sine_part = jnp.concatenate([-sine_part, sine_part], axis=1)
-    odd = (own_index % 2).astype(jnp.int32).reshape(1)
 
     key_parts = sent_back(products(arrived[1:], key_shards, jnp.bfloat16))
     (own_keys,) = products(arrived[:1], key_shards, jnp.float32)
-    value_products = products(arrived[1:], value_shards, jnp.bfloat16)
-    key_parts, value_products = lax.optimization_barrier((key_parts, value_products))
     key_block = block_sum(key_sum_kernel, "key_sum", own_keys, key_parts, cosine, sine_part)
-    value_products, _ = lax.optimization_barrier((value_products, key_block))
-    value_parts = sent_back(value_products)
+    value_shards, _ = lax.optimization_barrier((value_shards, key_block))
+    value_parts = sent_back(products(arrived[1:], value_shards, jnp.bfloat16))
     (own_values,) = products(arrived[:1], value_shards, jnp.float32)
     key_near = near_blocks(key_block)
     value_parts, _ = lax.optimization_barrier((value_parts, key_near))
     key_window = window_of(key_block, *key_near)
     weights, sums, log_sums = scored(
-        odd, queries, key_window, own_pos[:, :, None], col_pos[:, None, :]
+        queries, key_window, own_pos[:, :, None], col_pos[:, None, :]
     )
     value_block = block_sum(value_sum_kernel, "value_sum", own_values, value_parts)
     value_near, weights = lax.optimization_barrier((near_blocks(value_block), weights))
     value_window = window_of(value_block, *value_near)
-    out = mixed_values(odd, weights, sums, value_window)
+    out = mixed_values(weights, sums, value_window)
     return (out, log_sums[None])
 
 

time: 109 us -> 116 us (1.064)
  starting transfers between devices: 24.4 us -> 29.7 us
  waiting for transfers between devices: 66.6 us -> 68.5 us
    ppermute x4, waiting for transfers between devices: 14.9 us -> 28.3 us  [to_next_section(): return lax.ppermute(part, ('section', 'ctx'), route)]
    ppermute x15, starting transfers between devices: 16.1 us -> 25.3 us  [moved(): lax.ppermute(block, axis, [(i, target(i) % size) for i in range(size)])]
    ppermute x15, waiting for transfers between devices: 46 us -> 40.2 us  [moved(): lax.ppermute(block, axis, [(i, target(i) % size) for i in range(size)])]
    ppermute x2 -> x0, waiting for transfers between devices: 5.64 us -> none  [window_of(): lax.ppermute(beside, 'ctx', [(i, (i + 2) % cycle_size) for i in range(0,...]
    ppermute x2 -> x0, starting transfers between devices: 4.04 us -> none  [window_of(): lax.ppermute(beside, 'ctx', [(i, (i + 2) % cycle_size) for i in range(0,...]
  transfers between devices with their start and end apart: 21 -> 19, of which waited for: 14 -> 13; matrix products, arithmetic and copies ran while one was open for 2% -> 2% of each run, Pallas kernels for 10% -> 10%
where the time goes in v8:
time: 116 us; the launch traced here: 115 us
  waiting for transfers between devices  68.5 us (59%)
  starting transfers between devices  29.7 us (26%)
  Pallas kernels  13.8 us (12%)
  local copies, waits for them, and re-layouts  1.8 us (2%)
    ppermute x15, waiting for transfers between devices, moved(): lax.ppermute(block, axis, [(i, target(i) % size) for i in range(size)])  40.2 us
    ppermute x4, waiting for transfers between devices, to_next_section(): return lax.ppermute(part, ('section', 'ctx'), route)  28.3 us
    ppermute x15, starting transfers between devices, moved(): lax.ppermute(block, axis, [(i, target(i) % size) for i in range(size)])  25.3 us
    pallas_call x1, Pallas kernels, scored(): pl.pallas_call(score_kernel, grid=(micro_count, KVH), in_specs=[pl.BlockS...  6.6 us
    ppermute x4, starting transfers between devices, to_next_section(): return lax.ppermute(part, ('section', 'ctx'), route)  4.39 us
    pallas_call x1, Pallas kernels, mixed_values(): pl.pallas_call(mix_kernel, grid=(micro_count,), in_specs=[pl.BlockSpec((1...  2.44 us
  transfers between devices with their start and end apart: 19, of which 13 were waited for; matrix products, arithmetic and copies ran while one was open for 2% of the time, Pallas kernels for 10%

profile of v8, /device:TPU:0, one launch (start us, length us, event | category | flops | bytes accessed | tf_op | source)
XLA Modules:
  0.0 115.5 jit_solution(6005980689406571335)
XLA Ops:
  0.7 2.4 %collective-permute-start = (bf16[1,4096]{1,0:T(2,128)(2,1)}, bf16[1,4096]{1,0:T(2,128)(2,1)S(1)}, u32[]{:S(2)}, u32[]{:S(2)}) collective-permute-start(bf16[1,4096]{1,0:T(2,128)(2,1)} %param.6), channel_id=1, source_target_pairs={{0,24},{8,0},{16,8},{24,16},{1,25},{9,1},{17,9},{25,17},{2,26},{10... | collective-permute-start | bytes 24584 | tf_op jit(solution)/shard_map/ppermute | solution.py:25
  3.1 1.3 %fusion.4 = (bf16[512,512]{1,0:T(8,128)(2,1)S(1)}, bf16[512,512]{1,0:T(8,128)(2,1)S(1)}) fusion(bf16[512,1024]{1,0:T(8,128)(2,1)} %bitcast.6), kind=kLoop, calls=%fused_computation.20 | loop fusion | bytes 2097152 | tf_op jit(solution)/shard_map/slice | solution.py:257
  4.3 2.7 %collective-permute-start.2 = (bf16[512,512]{1,0:T(8,128)(2,1)S(1)}, bf16[512,512]{1,0:T(8,128)(2,1)S(1)}, u32[]{:S(2)}, u32[]{:S(2)}) collective-permute-start(bf16[512,512]{1,0:T(8,128)(2,1)S(1)} %get-tuple-element.46.refs_1_.refs_3_), channel_id=1, source_target_pairs={{0,4},{1,5},{2,6},{3,7},{4,0},{5,1},{6,2},{7,3},{8,12},{9,13},{10,... | collective-permute-start | bytes 1572872 | tf_op jit(solution)/shard_map/ppermute | solution.py:25
  7.5 2.1 %norm_cuts.1 = (bf16[192,1024]{1,0:T(8,128)(2,1)}, bf16[192,1024]{1,0:T(8,128)(2,1)}, bf16[192,1024]{1,0:T(8,128)(2,1)}, bf16[192,1024]{1,0:T(8,128)(2,1)}) custom-call(s32[4,2]{1,0:T(4,128)S(1)} %add_multiply_fusion.starts_ref, bf16[2,96,4096]{2,1,0:T(8,128)(2,1)S(1)} %bitcast.5, f32[1,4096]{1,0:T(1,128)S(1)} %convert_element_type.14.gain_ref), custom_call_target="tpu_custom_call" | custom-call | flops 4718592 | bytes 3145728 | tf_op jit(solution)/shard_map/norm_cuts/pallas_call | solution.py:58
  9.6 1.9 %collective-permute-start.3 = (bf16[192,1024]{1,0:T(8,128)(2,1)}, bf16[192,1024]{1,0:T(8,128)(2,1)S(1)}, u32[]{:S(2)}, u32[]{:S(2)}) collective-permute-start(bf16[192,1024]{1,0:T(8,128)(2,1)} %get-tuple-element.25), channel_id=1, source_target_pairs={{0,9},{1,8},{2,11},{3,10},{4,13},{5,12},{6,15},{7,14},{8,17},{9,16... | collective-permute-start | bytes 1179656 | tf_op jit(solution)/shard_map/ppermute | solution.py:248
  11.6 1.1 collective-permute-start.4
  12.7 1.3 %collective-permute-start.5 = (bf16[192,1024]{1,0:T(8,128)(2,1)}, bf16[192,1024]{1,0:T(8,128)(2,1)S(1)}, u32[]{:S(2)}, u32[]{:S(2)}) collective-permute-start(bf16[192,1024]{1,0:T(8,128)(2,1)} %get-tuple-element.27), channel_id=1, source_target_pairs={{0,11},{1,10},{2,9},{3,8},{4,15},{5,14},{6,13},{7,12},{8,19},{9,18... | collective-permute-start | bytes 1179656 | tf_op jit(solution)/shard_map/ppermute | solution.py:248
  14.3 4.1 %collective-permute-done.1.refs_0_ = bf16[192,1024]{1,0:T(8,128)(2,1)S(1)} collective-permute-done((bf16[192,1024]{1,0:T(8,128)(2,1)}, bf16[192,1024]{1,0:T(8,128)(2,1)S(1)}, u32[]{:S(2)}, u32[]{:S(2)}) %collective-permute-start.1) | collective-permute-done | bytes 393248 | tf_op jit(solution)/shard_map/ppermute | solution.py:248
  18.4 6.9 %collective-permute-done.3.refs_0_ = bf16[192,1024]{1,0:T(8,128)(2,1)S(1)} collective-permute-done((bf16[192,1024]{1,0:T(8,128)(2,1)}, bf16[192,1024]{1,0:T(8,128)(2,1)S(1)}, u32[]{:S(2)}, u32[]{:S(2)}) %collective-permute-start.3) | collective-permute-done | bytes 393248 | tf_op jit(solution)/shard_map/ppermute | solution.py:248
  25.3 8.9 %collective-permute-done.4.refs_1_ = bf16[192,1024]{1,0:T(8,128)(2,1)S(1)} collective-permute-done((bf16[192,1024]{1,0:T(8,128)(2,1)}, bf16[192,1024]{1,0:T(8,128)(2,1)S(1)}, u32[]{:S(2)}, u32[]{:S(2)}) %collective-permute-start.4) | collective-permute-done | bytes 393248 | tf_op jit(solution)/shard_map/ppermute | solution.py:248
  34.2 8.4 %collective-permute-done.5.refs_2_ = bf16[192,1024]{1,0:T(8,128)(2,1)S(1)} collective-permute-done((bf16[192,1024]{1,0:T(8,128)(2,1)}, bf16[192,1024]{1,0:T(8,128)(2,1)S(1)}, u32[]{:S(2)}, u32[]{:S(2)}) %collective-permute-start.5) | collective-permute-done | bytes 393248 | tf_op jit(solution)/shard_map/ppermute | solution.py:248
  43.1 0.8 products.5
  43.8 1.1 collective-permute-start.7
  45.0 2.9 %collective-permute-start.8 = (bf16[192,512]{1,0:T(8,128)(2,1)S(1)}, bf16[192,512]{1,0:T(8,128)(2,1)S(1)}, u32[]{:S(2)}, u32[]{:S(2)}) collective-permute-start(bf16[192,512]{1,0:T(8,128)(2,1)S(1)} %get-tuple-element.30), channel_id=1, source_target_pairs={{0,2},{1,3},{2,0},{3,1},{4,6},{5,7},{6,4},{7,5},{8,10},{9,11},{10,... | collective-permute-start | bytes 589832 | tf_op jit(solution)/shard_map/ppermute | solution.py:25
  48.8 1.5 %collective-permute-done.7.refs_0_ = bf16[192,512]{1,0:T(8,128)(2,1)S(1)} collective-permute-done((bf16[192,512]{1,0:T(8,128)(2,1)S(1)}, bf16[192,512]{1,0:T(8,128)(2,1)S(1)}, u32[]{:S(2)}, u32[]{:S(2)}) %collective-permute-start.7) | collective-permute-done | bytes 196640 | tf_op jit(solution)/shard_map/ppermute | solution.py:25
  50.3 9.3 %collective-permute-done.8.refs_1_ = bf16[192,512]{1,0:T(8,128)(2,1)S(1)} collective-permute-done((bf16[192,512]{1,0:T(8,128)(2,1)S(1)}, bf16[192,512]{1,0:T(8,128)(2,1)S(1)}, u32[]{:S(2)}, u32[]{:S(2)}) %collective-permute-start.8) | collective-permute-done | bytes 196640 | tf_op jit(solution)/shard_map/ppermute | solution.py:25
  59.6 3.2 %collective-permute-done.9.refs_2_ = bf16[192,512]{1,0:T(8,128)(2,1)S(1)} collective-permute-done((bf16[192,512]{1,0:T(8,128)(2,1)S(1)}, bf16[192,512]{1,0:T(8,128)(2,1)S(1)}, u32[]{:S(2)}, u32[]{:S(2)}) %collective-permute-start.9) | collective-permute-done | bytes 196640 | tf_op jit(solution)/shard_map/ppermute | solution.py:25
  63.0 2.5 %collective-permute-start.14 = (bf16[192,512]{1,0:T(8,128)(2,1)S(1)}, bf16[192,512]{1,0:T(8,128)(2,1)S(1)}, u32[]{:S(2)}, u32[]{:S(2)}) collective-permute-start(bf16[192,512]{1,0:T(8,128)(2,1)S(1)} %key_sum.1.refs_3_), channel_id=1, source_target_pairs={{0,2},{1,3},{2,4},{3,5},{4,6},{5,7},{6,0},{7,1},{8,10},{9,11},{10,... | collective-permute-start | bytes 589832 | tf_op jit(solution)/shard_map/ppermute | solution.py:25
  65.5 1.5 %collective-permute-start.13 = (bf16[192,512]{1,0:T(8,128)(2,1)S(1)}, bf16[192,512]{1,0:T(8,128)(2,1)S(1)}, u32[]{:S(2)}, u32[]{:S(2)}) collective-permute-start(bf16[192,512]{1,0:T(8,128)(2,1)S(1)} %key_sum.1.refs_3_), channel_id=1, source_target_pairs={{0,1},{1,2},{2,3},{3,4},{4,5},{5,6},{6,7},{7,0},{8,9},{9,10},{10,1... | collective-permute-start | bytes 589832 | tf_op jit(solution)/shard_map/ppermute | solution.py:25
  67.0 4.6 %collective-permute-done.6.refs_2_.refs_4_ = bf16[512,512]{1,0:T(8,128)(2,1)S(1)} collective-permute-done((bf16[512,512]{1,0:T(8,128)(2,1)S(1)}, bf16[512,512]{1,0:T(8,128)(2,1)S(1)}, u32[]{:S(2)}, u32[]{:S(2)}) %collective-permute-start.6) | collective-permute-done | bytes 524320 | tf_op jit(solution)/shard_map/ppermute | solution.py:25
  71.5 0.8 products.7
  72.3 5.7 %collective-permute-start.10 = (bf16[192,512]{1,0:T(8,128)(2,1)S(1)}, bf16[192,512]{1,0:T(8,128)(2,1)S(1)}, u32[]{:S(2)}, u32[]{:S(2)}) collective-permute-start(bf16[192,512]{1,0:T(8,128)(2,1)S(1)} %get-tuple-element.34), channel_id=1, source_target_pairs={{0,1},{1,0},{2,3},{3,2},{4,5},{5,4},{6,7},{7,6},{8,9},{9,8},{10,11... | collective-permute-start | bytes 589832 | tf_op jit(solution)/shard_map/ppermute | solution.py:25
  78.1 1.5 %collective-permute-start.12 = (bf16[192,512]{1,0:T(8,128)(2,1)S(1)}, bf16[192,512]{1,0:T(8,128)(2,1)S(1)}, u32[]{:S(2)}, u32[]{:S(2)}) collective-permute-start(bf16[192,512]{1,0:T(8,128)(2,1)S(1)} %get-tuple-element.36), channel_id=1, source_target_pairs={{0,3},{1,2},{2,1},{3,0},{4,7},{5,6},{6,5},{7,4},{8,11},{9,10},{10,... | collective-permute-start | bytes 589832 | tf_op jit(solution)/shard_map/ppermute | solution.py:25
  80.6 2.4 %collective-permute-done.10.refs_0_ = bf16[192,512]{1,0:T(8,128)(2,1)S(1)} collective-permute-done((bf16[192,512]{1,0:T(8,128)(2,1)S(1)}, bf16[192,512]{1,0:T(8,128)(2,1)S(1)}, u32[]{:S(2)}, u32[]{:S(2)}) %collective-permute-start.10) | collective-permute-done | bytes 196640 | tf_op jit(solution)/shard_map/ppermute | solution.py:25
  82.9 4.3 %collective-permute-done.11.refs_1_ = bf16[192,512]{1,0:T(8,128)(2,1)S(1)} collective-permute-done((bf16[192,512]{1,0:T(8,128)(2,1)S(1)}, bf16[192,512]{1,0:T(8,128)(2,1)S(1)}, u32[]{:S(2)}, u32[]{:S(2)}) %collective-permute-start.11) | collective-permute-done | bytes 196640 | tf_op jit(solution)/shard_map/ppermute | solution.py:25
  87.2 4.6 %collective-permute-done.12.refs_2_ = bf16[192,512]{1,0:T(8,128)(2,1)S(1)} collective-permute-done((bf16[192,512]{1,0:T(8,128)(2,1)S(1)}, bf16[192,512]{1,0:T(8,128)(2,1)S(1)}, u32[]{:S(2)}, u32[]{:S(2)}) %collective-permute-start.12) | collective-permute-done | bytes 196640 | tf_op jit(solution)/shard_map/ppermute | solution.py:25
  91.9 1.9 %collective-permute-start.16 = (bf16[192,512]{1,0:T(8,128)(2,1)S(1)}, bf16[192,512]{1,0:T(8,128)(2,1)S(1)}, u32[]{:S(2)}, u32[]{:S(2)}) collective-permute-start(bf16[192,512]{1,0:T(8,128)(2,1)S(1)} %value_sum.1.refs_3_), channel_id=1, source_target_pairs={{0,2},{1,3},{2,4},{3,5},{4,6},{5,7},{6,0},{7,1},{8,10},{9,11},{10,... | collective-permute-start | bytes 589832 | tf_op jit(solution)/shard_map/ppermute | solution.py:25
  93.8 2.0 %collective-permute-start.15 = (bf16[192,512]{1,0:T(8,128)(2,1)S(1)}, bf16[192,512]{1,0:T(8,128)(2,1)S(1)}, u32[]{:S(2)}, u32[]{:S(2)}) collective-permute-start(bf16[192,512]{1,0:T(8,128)(2,1)S(1)} %value_sum.1.refs_3_), channel_id=1, source_target_pairs={{0,1},{1,2},{2,3},{3,4},{4,5},{5,6},{6,7},{7,0},{8,9},{9,10},{10,1... | collective-permute-start | bytes 589832 | tf_op jit(solution)/shard_map/ppermute | solution.py:25
  95.9 6.6 %scores.1 = (bf16[2,4,768,384]{3,2,1,0:T(8,128)(2,1)S(1)}, f32[2,4,96,128]{3,2,1,0:T(8,128)S(1)}, f32[2,32,96]{2,1,0:T(8,128)}) custom-call(bf16[1,2,96,4096]{3,2,1,0:T(8,128)(2,1)S(1)} %copy-done.1, bf16[192,512]{1,0:T(8,128)(2,1)S(1)} %collective-permute-done.17.refs_0_, bf16[192,512]{1,0:T(8,128)(2,1)S(1)} %collective-permute-done.14.refs_1_, ...), custom_call_target="tpu_custom_call" | custom-call | flops 603979776 | bytes 8388608 | tf_op jit(solution)/shard_map/scores/pallas_call | solution.py:166
  102.5 3.0 %collective-permute-done.15.refs_2_ = bf16[192,512]{1,0:T(8,128)(2,1)S(1)} collective-permute-done((bf16[192,512]{1,0:T(8,128)(2,1)S(1)}, bf16[192,512]{1,0:T(8,128)(2,1)S(1)}, u32[]{:S(2)}, u32[]{:S(2)}) %collective-permute-start.15) | collective-permute-done | bytes 196640 | tf_op jit(solution)/shard_map/ppermute | solution.py:25
  105.6 7.5 %collective-permute-done.18.refs_0_ = bf16[192,512]{1,0:T(8,128)(2,1)S(1)} collective-permute-done((bf16[192,512]{1,0:T(8,128)(2,1)S(1)}, bf16[192,512]{1,0:T(8,128)(2,1)S(1)}, u32[]{:S(2)}, u32[]{:S(2)}) %collective-permute-start.18) | collective-permute-done | bytes 196640 | tf_op jit(solution)/shard_map/ppermute | solution.py:25
  113.0 2.4 %mixed_values.1 = bf16[1,2,96,4096]{3,2,1,0:T(8,128)(2,1)} custom-call(bf16[2,4,768,384]{3,2,1,0:T(8,128)(2,1)S(1)} %get-tuple-element.41.weights, f32[2,4,96,128]{3,2,1,0:T(8,128)S(1)} %get-tuple-element.42.sums, bf16[192,512]{1,0:T(8,128)(2,1)S(1)} %collective-permute-done.18.refs_0_, bf16[192,512]{1,0:T(8,128)(2,1)S(1)} %collective-permute-done.16.refs_1_, ...), custom_call_target="tpu_custom_call" | custom-call | flops 603979776 | bytes 8388608 | tf_op jit(solution)/shard_map/mixed_values/pallas_call | solution.py:210
  (45 shorter events, 3.4 us)
Async XLA Ops:
  0.6 6.4 %copy-start.4 = (s32[2,16]{1,0:T(2,128)S(1)}, s32[2,16]{1,0:T(2,128)}, u32[]{:S(2)}) copy-start(s32[2,16]{1,0:T(2,128)} %param.9) | copy-start | bytes 388
  0.6 6.8 %copy-start = (bf16[1,2,96,4096]{3,2,1,0:T(8,128)(2,1)S(1)}, bf16[1,2,96,4096]{3,2,1,0:T(8,128)(2,1)}, u32[]{:S(2)}) copy-start(bf16[1,2,96,4096]{3,2,1,0:T(8,128)(2,1)} %param.5) | copy-start | bytes 4718596
  0.7 6.8 %collective-permute-start = (bf16[1,4096]{1,0:T(2,128)(2,1)}, bf16[1,4096]{1,0:T(2,128)(2,1)S(1)}, u32[]{:S(2)}, u32[]{:S(2)}) collective-permute-start(bf16[1,4096]{1,0:T(2,128)(2,1)} %param.6), channel_id=1, source_target_pairs={{0,24},{8,0},{16,8},{24,16},{1,25},{9,1},{17,9},{25,17},{2,26},{10... | collective-permute-start | bytes 24584 | tf_op jit(solution)/shard_map/ppermute | solution.py:25
  4.3 38.2 %collective-permute-start.2 = (bf16[512,512]{1,0:T(8,128)(2,1)S(1)}, bf16[512,512]{1,0:T(8,128)(2,1)S(1)}, u32[]{:S(2)}, u32[]{:S(2)}) collective-permute-start(bf16[512,512]{1,0:T(8,128)(2,1)S(1)} %get-tuple-element.46.refs_1_.refs_3_), channel_id=1, source_target_pairs={{0,4},{1,5},{2,6},{3,7},{4,0},{5,1},{6,2},{7,3},{8,12},{9,13},{10,... | collective-permute-start | bytes 1572872 | tf_op jit(solution)/shard_map/ppermute | solution.py:25
  9.6 8.8 %collective-permute-start.1 = (bf16[192,1024]{1,0:T(8,128)(2,1)}, bf16[192,1024]{1,0:T(8,128)(2,1)S(1)}, u32[]{:S(2)}, u32[]{:S(2)}) collective-permute-start(bf16[192,1024]{1,0:T(8,128)(2,1)} %get-tuple-element.24), channel_id=1, source_target_pairs={{0,8},{1,9},{2,10},{3,11},{4,12},{5,13},{6,14},{7,15},{8,16},{9,17... | collective-permute-start | bytes 1179656 | tf_op jit(solution)/shard_map/ppermute | solution.py:248
  9.6 15.7 %collective-permute-start.3 = (bf16[192,1024]{1,0:T(8,128)(2,1)}, bf16[192,1024]{1,0:T(8,128)(2,1)S(1)}, u32[]{:S(2)}, u32[]{:S(2)}) collective-permute-start(bf16[192,1024]{1,0:T(8,128)(2,1)} %get-tuple-element.25), channel_id=1, source_target_pairs={{0,9},{1,8},{2,11},{3,10},{4,13},{5,12},{6,15},{7,14},{8,17},{9,16... | collective-permute-start | bytes 1179656 | tf_op jit(solution)/shard_map/ppermute | solution.py:248
  11.6 22.6 %collective-permute-start.4 = (bf16[192,1024]{1,0:T(8,128)(2,1)}, bf16[192,1024]{1,0:T(8,128)(2,1)S(1)}, u32[]{:S(2)}, u32[]{:S(2)}) collective-permute-start(bf16[192,1024]{1,0:T(8,128)(2,1)} %get-tuple-element.26), channel_id=1, source_target_pairs={{0,10},{1,11},{2,8},{3,9},{4,14},{5,15},{6,12},{7,13},{8,18},{9,19... | collective-permute-start | bytes 1179656 | tf_op jit(solution)/shard_map/ppermute | solution.py:248
  12.7 29.9 %collective-permute-start.5 = (bf16[192,1024]{1,0:T(8,128)(2,1)}, bf16[192,1024]{1,0:T(8,128)(2,1)S(1)}, u32[]{:S(2)}, u32[]{:S(2)}) collective-permute-start(bf16[192,1024]{1,0:T(8,128)(2,1)} %get-tuple-element.27), channel_id=1, source_target_pairs={{0,11},{1,10},{2,9},{3,8},{4,15},{5,14},{6,13},{7,12},{8,19},{9,18... | collective-permute-start | bytes 1179656 | tf_op jit(solution)/shard_map/ppermute | solution.py:248
  18.4 30.1 %copy-start.2 = (bf16[192,1024]{1,0:T(8,128)(2,1)}, bf16[192,1024]{1,0:T(8,128)(2,1)S(1)}, u32[]{:S(2)}) copy-start(bf16[192,1024]{1,0:T(8,128)(2,1)S(1)} %collective-permute-done.1.refs_0_) | copy-start | bytes 1179652
  42.6 29.0 %collective-permute-start.6 = (bf16[512,512]{1,0:T(8,128)(2,1)S(1)}, bf16[512,512]{1,0:T(8,128)(2,1)S(1)}, u32[]{:S(2)}, u32[]{:S(2)}) collective-permute-start(bf16[512,512]{1,0:T(8,128)(2,1)S(1)} %get-tuple-element.32.refs_1_.refs_3_), channel_id=1, source_target_pairs={{0,4},{1,5},{2,6},{3,7},{4,0},{5,1},{6,2},{7,3},{8,12},{9,13},{10,... | collective-permute-start | bytes 1572872 | tf_op jit(solution)/shard_map/ppermute | solution.py:25
  43.8 6.5 %collective-permute-start.7 = (bf16[192,512]{1,0:T(8,128)(2,1)S(1)}, bf16[192,512]{1,0:T(8,128)(2,1)S(1)}, u32[]{:S(2)}, u32[]{:S(2)}) collective-permute-start(bf16[192,512]{1,0:T(8,128)(2,1)S(1)} %get-tuple-element.29), channel_id=1, source_target_pairs={{0,1},{1,0},{2,3},{3,2},{4,5},{5,4},{6,7},{7,6},{8,9},{9,8},{10,11... | collective-permute-start | bytes 589832 | tf_op jit(solution)/shard_map/ppermute | solution.py:25
  45.0 14.7 %collective-permute-start.8 = (bf16[192,512]{1,0:T(8,128)(2,1)S(1)}, bf16[192,512]{1,0:T(8,128)(2,1)S(1)}, u32[]{:S(2)}, u32[]{:S(2)}) collective-permute-start(bf16[192,512]{1,0:T(8,128)(2,1)S(1)} %get-tuple-element.30), channel_id=1, source_target_pairs={{0,2},{1,3},{2,0},{3,1},{4,6},{5,7},{6,4},{7,5},{8,10},{9,11},{10,... | collective-permute-start | bytes 589832 | tf_op jit(solution)/shard_map/ppermute | solution.py:25
  47.9 14.9 %collective-permute-start.9 = (bf16[192,512]{1,0:T(8,128)(2,1)S(1)}, bf16[192,512]{1,0:T(8,128)(2,1)S(1)}, u32[]{:S(2)}, u32[]{:S(2)}) collective-permute-start(bf16[192,512]{1,0:T(8,128)(2,1)S(1)} %get-tuple-element.31), channel_id=1, source_target_pairs={{0,3},{1,2},{2,1},{3,0},{4,7},{5,6},{6,5},{7,4},{8,11},{9,10},{10,... | collective-permute-start | bytes 589832 | tf_op jit(solution)/shard_map/ppermute | solution.py:25
  63.0 17.2 %copy-start.3 = (bf16[192,1024]{1,0:T(8,128)(2,1)S(1)}, bf16[192,1024]{1,0:T(8,128)(2,1)}, u32[]{:S(2)}) copy-start(bf16[192,1024]{1,0:T(8,128)(2,1)} %copy-done.2) | copy-start | bytes 1179652
  63.0 17.6 %collective-permute-start.14 = (bf16[192,512]{1,0:T(8,128)(2,1)S(1)}, bf16[192,512]{1,0:T(8,128)(2,1)S(1)}, u32[]{:S(2)}, u32[]{:S(2)}) collective-permute-start(bf16[192,512]{1,0:T(8,128)(2,1)S(1)} %key_sum.1.refs_3_), channel_id=1, source_target_pairs={{0,2},{1,3},{2,4},{3,5},{4,6},{5,7},{6,0},{7,1},{8,10},{9,11},{10,... | collective-permute-start | bytes 589832 | tf_op jit(solution)/shard_map/ppermute | solution.py:25
  65.5 14.2 %collective-permute-start.13 = (bf16[192,512]{1,0:T(8,128)(2,1)S(1)}, bf16[192,512]{1,0:T(8,128)(2,1)S(1)}, u32[]{:S(2)}, u32[]{:S(2)}) collective-permute-start(bf16[192,512]{1,0:T(8,128)(2,1)S(1)} %key_sum.1.refs_3_), channel_id=1, source_target_pairs={{0,1},{1,2},{2,3},{3,4},{4,5},{5,6},{6,7},{7,0},{8,9},{9,10},{10,1... | collective-permute-start | bytes 589832 | tf_op jit(solution)/shard_map/ppermute | solution.py:25
  72.3 10.6 %collective-permute-start.10 = (bf16[192,512]{1,0:T(8,128)(2,1)S(1)}, bf16[192,512]{1,0:T(8,128)(2,1)S(1)}, u32[]{:S(2)}, u32[]{:S(2)}) collective-permute-start(bf16[192,512]{1,0:T(8,128)(2,1)S(1)} %get-tuple-element.34), channel_id=1, source_target_pairs={{0,1},{1,0},{2,3},{3,2},{4,5},{5,4},{6,7},{7,6},{8,9},{9,8},{10,11... | collective-permute-start | bytes 589832 | tf_op jit(solution)/shard_map/ppermute | solution.py:25
  78.1 9.1 %collective-permute-start.11 = (bf16[192,512]{1,0:T(8,128)(2,1)S(1)}, bf16[192,512]{1,0:T(8,128)(2,1)S(1)}, u32[]{:S(2)}, u32[]{:S(2)}) collective-permute-start(bf16[192,512]{1,0:T(8,128)(2,1)S(1)} %get-tuple-element.35), channel_id=1, source_target_pairs={{0,2},{1,3},{2,0},{3,1},{4,6},{5,7},{6,4},{7,5},{8,10},{9,11},{10,... | collective-permute-start | bytes 589832 | tf_op jit(solution)/shard_map/ppermute | solution.py:25
  78.1 17.9 %copy-start.1 = (bf16[1,2,96,4096]{3,2,1,0:T(8,128)(2,1)S(1)}, bf16[1,2,96,4096]{3,2,1,0:T(8,128)(2,1)}, u32[]{:S(2)}) copy-start(bf16[1,2,96,4096]{3,2,1,0:T(8,128)(2,1)} %q_ref.1) | copy-start | bytes 4718596
  78.1 13.7 %collective-permute-start.12 = (bf16[192,512]{1,0:T(8,128)(2,1)S(1)}, bf16[192,512]{1,0:T(8,128)(2,1)S(1)}, u32[]{:S(2)}, u32[]{:S(2)}) collective-permute-start(bf16[192,512]{1,0:T(8,128)(2,1)S(1)} %get-tuple-element.36), channel_id=1, source_target_pairs={{0,3},{1,2},{2,1},{3,0},{4,7},{5,6},{6,5},{7,4},{8,11},{9,10},{10,... | collective-permute-start | bytes 589832 | tf_op jit(solution)/shard_map/ppermute | solution.py:25
  79.6 16.3 %collective-permute-start.17 = (bf16[192,512]{1,0:T(8,128)(2,1)S(1)}, bf16[192,512]{1,0:T(8,128)(2,1)S(1)}, u32[]{:S(2)}, u32[]{:S(2)}) collective-permute-start(bf16[192,512]{1,0:T(8,128)(2,1)S(1)} %collective-permute-done.13.refs_2_), channel_id=1, source_target_pairs={{0,2},{1,3},{2,4},{3,5},{4,6},{5,7},{6,0},{7,1},{8,10},{9,11},{10,... | collective-permute-start | bytes 589832 | tf_op jit(solution)/shard_map/ppermute | solution.py:25
  91.9 10.6 %collective-permute-start.16 = (bf16[192,512]{1,0:T(8,128)(2,1)S(1)}, bf16[192,512]{1,0:T(8,128)(2,1)S(1)}, u32[]{:S(2)}, u32[]{:S(2)}) collective-permute-start(bf16[192,512]{1,0:T(8,128)(2,1)S(1)} %value_sum.1.refs_3_), channel_id=1, source_target_pairs={{0,2},{1,3},{2,4},{3,5},{4,6},{5,7},{6,0},{7,1},{8,10},{9,11},{10,... | collective-permute-start | bytes 589832 | tf_op jit(solution)/shard_map/ppermute | solution.py:25
  93.8 11.7 %collective-permute-start.15 = (bf16[192,512]{1,0:T(8,128)(2,1)S(1)}, bf16[192,512]{1,0:T(8,128)(2,1)S(1)}, u32[]{:S(2)}, u32[]{:S(2)}) collective-permute-start(bf16[192,512]{1,0:T(8,128)(2,1)S(1)} %value_sum.1.refs_3_), channel_id=1, source_target_pairs={{0,1},{1,2},{2,3},{3,4},{4,5},{5,6},{6,7},{7,0},{8,9},{9,10},{10,1... | collective-permute-start | bytes 589832 | tf_op jit(solution)/shard_map/ppermute | solution.py:25
  105.6 7.5 %collective-permute-start.18 = (bf16[192,512]{1,0:T(8,128)(2,1)S(1)}, bf16[192,512]{1,0:T(8,128)(2,1)S(1)}, u32[]{:S(2)}, u32[]{:S(2)}) collective-permute-start(bf16[192,512]{1,0:T(8,128)(2,1)S(1)} %collective-permute-done.15.refs_2_), channel_id=1, source_target_pairs={{0,2},{1,3},{2,4},{3,5},{4,6},{5,7},{6,0},{7,1},{8,10},{9,11},{10,... | collective-permute-start | bytes 589832 | tf_op jit(solution)/shard_map/ppermute | solution.py:25

commit v9 on v8

--- a/solution.py
+++ b/solution.py
@@ -72,9 +72,9 @@
 
 
 def product_kernel(blocks, *refs):
-    xs, shards, outs = refs[:blocks], refs[blocks:-blocks], refs[-blocks:]
-    shard_rows = shards[0].shape[0]
-    for x, out in zip(xs, outs):
+    xs, shards, out = refs[:blocks], refs[blocks:-1], refs[-1]
+    rows, shard_rows = xs[0].shape[0], shards[0].shape[0]
+    for i, x in enumerate(xs):
         total = 0.0
         for j, shard in enumerate(shards):
             total = total + jnp.dot(
@@ -82,7 +82,7 @@
                 shard[...],
                 preferred_element_type=jnp.float32,
             )
-        out[...] = total.astype(out.dtype)
+        out[i * rows : (i + 1) * rows, :] = total.astype(out.dtype)
 
 
 def products(xs, shards, dtype):
@@ -92,11 +92,31 @@
     size = 8 * blocks * rows * part
     return pl.pallas_call(
         lambda *refs: product_kernel(blocks, *refs),
-        out_shape=[jax.ShapeDtypeStruct((rows, width), dtype)] * blocks,
+        out_shape=jax.ShapeDtypeStruct((blocks * rows, width), dtype),
         compiler_params=params(24),
         cost_estimate=cost(size * width, size),
         name="products",
     )(*xs, *shards)
+
+
+def half_sum_kernel(held, arrived, own, onward):
+    rows = own.shape[0]
+    own[...] = held[:rows, :] + arrived[:rows, :].astype(jnp.float32)
+    onward[...] = (held[rows:, :] + arrived[rows:, :].astype(jnp.float32)).astype(jnp.bfloat16)
+
+
+def half_sum(held, arrived):
+    rows, width = held.shape[0] // 2, held.shape[1]
+    return pl.pallas_call(
+        half_sum_kernel,
+        out_shape=[
+            jax.ShapeDtypeStruct((rows, width), jnp.float32),
+            jax.ShapeDtypeStruct((rows, width), jnp.bfloat16),
+        ],
+        compiler_params=params(16),
+        cost_estimate=cost(2 * held.size, 9 * held.size),
+        name="half_sum",
+    )(held, arrived)
 
 
 def added(own, parts, cols):
@@ -255,14 +275,20 @@
         ]
 
     key_shards = same_place(weight[:, :kv_width])
-    late_part, _ = lax.optimization_barrier((weight[:, kv_width:], (key_shards[-1], arrived)))
+    late_part, _ = lax.optimization_barrier((weight[:, kv_width:], key_shards[-1]))
     value_shards = same_place(late_part)
 
-    def sent_back(parts):
-        return [
-            moved(part, "ctx", lambda i, flip=flip: i ^ flip)
-            for flip, part in enumerate(parts, start=1)
-        ]
+    def over_y(part):
+        return moved(part, "ctx", lambda i: i ^ 1)
+
+    def over_z(part):
+        return moved(part, "ctx", lambda i: i ^ 2)
+
+    def for_others(shards):
+        return products([arrived[1], arrived[3]], shards, jnp.bfloat16)
+
+    def held_here(shards):
+        return products([arrived[0], arrived[2]], shards, jnp.float32)
 
     def near_blocks(block):
         return [moved(block, "ctx", lambda i, d=d: i + d) for d in (1, 2)]
@@ -287,21 +313,23 @@
     cosine = jnp.concatenate([cosine, cosine], axis=1)
     sine_part = jnp.concatenate([-sine_part, sine_part], axis=1)
 
-    key_parts = sent_back(products(arrived[1:], key_shards, jnp.bfloat16))
-    (own_keys,) = products(arrived[:1], key_shards, jnp.float32)
-    key_block = block_sum(key_sum_kernel, "key_sum", own_keys, key_parts, cosine, sine_part)
-    value_shards, _ = lax.optimization_barrier((value_shards, key_block))
-    value_parts = sent_back(products(arrived[1:], value_shards, jnp.bfloat16))
-    (own_values,) = products(arrived[:1], value_shards, jnp.float32)
+    key_y = over_y(for_others(key_shards))
+    key_held = held_here(key_shards)
+    value_products, key_y = lax.optimization_barrier((for_others(value_shards), key_y))
+    own_keys, onward_keys = half_sum(key_held, key_y)
+    key_z = over_z(onward_keys)
+    value_y = over_y(value_products)
+    value_held = held_here(value_shards)
+    key_block = block_sum(key_sum_kernel, "key_sum", own_keys, [key_z], cosine, sine_part)
     key_near = near_blocks(key_block)
-    value_parts, _ = lax.optimization_barrier((value_parts, key_near))
+    own_values, onward_values = half_sum(value_held, value_y)
+    value_z = over_z(onward_values)
     key_window = window_of(key_block, *key_near)
     weights, sums, log_sums = scored(
         queries, key_window, own_pos[:, :, None], col_pos[:, None, :]
     )
-    value_block = block_sum(value_sum_kernel, "value_sum", own_values, value_parts)
-    value_near, weights = lax.optimization_barrier((near_blocks(value_block), weights))
-    value_window = window_of(value_block, *value_near)
+    value_block = block_sum(value_sum_kernel, "value_sum", own_values, [value_z])
+    value_window = window_of(value_block, *near_blocks(value_block))
     out = mixed_values(weights, sums, value_window)
     return (out, log_sums[None])
 

time: 116 us -> 101 us (0.87); the launches traced: 115 us -> 98.8 us
  waiting for transfers between devices: 68.5 us -> 54.8 us
  starting transfers between devices: 29.7 us -> 22 us
  Pallas kernels: 13.8 us -> 16.8 us
  local copies, waits for them, and re-layouts: 1.8 us -> 3.55 us
    ppermute x4, waiting for transfers between devices: 28.3 us -> 0.01 us  [to_next_section(): return lax.ppermute(part, ('section', 'ctx'), route)]
    ppermute x15 -> x13, waiting for transfers between devices: 40.2 us -> 54.7 us  [moved(): lax.ppermute(block, axis, [(i, target(i) % size) for i in range(size)])]
    ppermute x15 -> x13, starting transfers between devices: 25.3 us -> 16.3 us  [moved(): lax.ppermute(block, axis, [(i, target(i) % size) for i in range(size)])]
    pallas_call x4 -> x6, Pallas kernels: 2.31 us -> 5.45 us  [the longest x4 5.32 us: products(): pl.pallas_call(lambda *refs: product_kernel(blocks, *refs), out_shape=jax...]
    unnamed x10, local copies, waits for them, and re-layouts: 0.02 us -> 1.76 us
    ppermute x4, starting transfers between devices: 4.39 us -> 5.76 us  [to_next_section(): return lax.ppermute(part, ('section', 'ctx'), route)]
  transfers between devices with their start and end apart: 19 -> 17, of which waited for: 13 -> 8; matrix products, arithmetic and copies ran while one was open for 2% -> 3% of each run, Pallas kernels for 10% -> 15%
where the time goes in v9:
time: 101 us; the launch traced here: 98.8 us
  waiting for transfers between devices  54.8 us (54%)
  starting transfers between devices  22 us (22%)
  Pallas kernels  16.8 us (17%)
  local copies, waits for them, and re-layouts  3.55 us (4%)
    ppermute x13, waiting for transfers between devices, moved(): lax.ppermute(block, axis, [(i, target(i) % size) for i in range(size)])  54.7 us
    ppermute x13, starting transfers between devices, moved(): lax.ppermute(block, axis, [(i, target(i) % size) for i in range(size)])  16.3 us
    pallas_call x1, Pallas kernels, scored(): pl.pallas_call(score_kernel, grid=(micro_count, KVH), in_specs=[pl.BlockS...  6.58 us
    ppermute x4, starting transfers between devices, to_next_section(): return lax.ppermute(part, ('section', 'ctx'), route)  5.76 us
    pallas_call x4, Pallas kernels, products(): pl.pallas_call(lambda *refs: product_kernel(blocks, *refs), out_shape=jax...  5.32 us
    pallas_call x1, Pallas kernels, mixed_values(): pl.pallas_call(mix_kernel, grid=(micro_count,), in_specs=[pl.BlockSpec((1...  2.46 us
    pallas_call x1, Pallas kernels, normed_cuts(): pl.pallas_call(norm_kernel, grid=(micro_count,), in_specs=[pl.BlockSpec(m...  2.09 us
  transfers between devices with their start and end apart: 17, of which 8 were waited for; matrix products, arithmetic and copies ran while one was open for 3% of the time, Pallas kernels for 15%

profile of v9, /device:TPU:0, one launch (start us, length us, event | category | flops | bytes accessed | tf_op | source)
XLA Modules:
  0.0 98.8 jit_solution(14741939163120624815)
XLA Ops:
  0.6 2.4 %collective-permute-start = (bf16[1,4096]{1,0:T(2,128)(2,1)}, bf16[1,4096]{1,0:T(2,128)(2,1)S(1)}, u32[]{:S(2)}, u32[]{:S(2)}) collective-permute-start(bf16[1,4096]{1,0:T(2,128)(2,1)} %param.6), channel_id=1, source_target_pairs={{0,24},{8,0},{16,8},{24,16},{1,25},{9,1},{17,9},{25,17},{2,26},{10... | collective-permute-start | bytes 24584 | tf_op jit(solution)/shard_map/ppermute | solution.py:25
  3.1 1.3 %fusion.4 = (bf16[512,512]{1,0:T(8,128)(2,1)S(1)}, bf16[512,512]{1,0:T(8,128)(2,1)S(1)}) fusion(bf16[512,1024]{1,0:T(8,128)(2,1)} %bitcast.6), kind=kLoop, calls=%fused_computation.20 | loop fusion | bytes 2097152 | tf_op jit(solution)/shard_map/slice | solution.py:278
  4.4 2.7 %collective-permute-start.3 = (bf16[512,512]{1,0:T(8,128)(2,1)S(1)}, bf16[512,512]{1,0:T(8,128)(2,1)S(1)}, u32[]{:S(2)}, u32[]{:S(2)}) collective-permute-start(bf16[512,512]{1,0:T(8,128)(2,1)S(1)} %get-tuple-element.31.refs_2_), channel_id=1, source_target_pairs={{0,4},{1,5},{2,6},{3,7},{4,0},{5,1},{6,2},{7,3},{8,12},{9,13},{10,... | collective-permute-start | bytes 1572872 | tf_op jit(solution)/shard_map/ppermute | solution.py:25
  7.2 2.1 %norm_cuts.1 = (bf16[192,1024]{1,0:T(8,128)(2,1)}, bf16[192,1024]{1,0:T(8,128)(2,1)}, bf16[192,1024]{1,0:T(8,128)(2,1)S(1)}, bf16[192,1024]{1,0:T(8,128)(2,1)}) custom-call(s32[4,2]{1,0:T(4,128)S(1)} %add_multiply_fusion.starts_ref, bf16[2,96,4096]{2,1,0:T(8,128)(2,1)S(1)} %bitcast.5, f32[1,4096]{1,0:T(1,128)S(1)} %convert_element_type.16.gain_ref), custom_call_target="tpu_custom_call" | custom-call | flops 4718592 | bytes 3145728 | tf_op jit(solution)/shard_map/norm_cuts/pallas_call | solution.py:58
  9.3 0.4 collective-permute-start.4
  9.7 2.4 %collective-permute-start.5 = (bf16[192,1024]{1,0:T(8,128)(2,1)}, bf16[192,1024]{1,0:T(8,128)(2,1)S(1)}, u32[]{:S(2)}, u32[]{:S(2)}) collective-permute-start(bf16[192,1024]{1,0:T(8,128)(2,1)} %get-tuple-element.19), channel_id=1, source_target_pairs={{0,11},{1,10},{2,9},{3,8},{4,15},{5,14},{6,13},{7,12},{8,19},{9,18... | collective-permute-start | bytes 1179656 | tf_op jit(solution)/shard_map/ppermute | solution.py:268
  12.4 17.7 %collective-permute-done.3.refs_3_ = bf16[512,512]{1,0:T(8,128)(2,1)S(1)} collective-permute-done((bf16[512,512]{1,0:T(8,128)(2,1)S(1)}, bf16[512,512]{1,0:T(8,128)(2,1)S(1)}, u32[]{:S(2)}, u32[]{:S(2)}) %collective-permute-start.3) | collective-permute-done | bytes 524320 | tf_op jit(solution)/shard_map/ppermute | solution.py:25
  30.1 1.4 %products.6 = bf16[384,512]{1,0:T(8,128)(2,1)} custom-call(bf16[192,1024]{1,0:T(8,128)(2,1)S(1)} %collective-permute-done.4.refs_0_, bf16[192,1024]{1,0:T(8,128)(2,1)S(1)} %collective-permute-done.5.refs_1_, bf16[512,512]{1,0:T(8,128)(2,1)S(1)} %get-tuple-element.31.refs_2_, bf16[512,512]{1,0:T(8,128)(2,1)S(1)} %collective-permute-done.3.refs_3_), custom_call_target="tpu_custom_call" | custom-call | flops 1610612736 | bytes 3145728 | tf_op jit(solution)/shard_map/products/pallas_call | solution.py:93
  31.5 0.7 copy-done.2
  32.2 4.0 %collective-permute-start.7 = (bf16[384,512]{1,0:T(8,128)(2,1)}, bf16[384,512]{1,0:T(8,128)(2,1)S(1)}, u32[]{:S(2)}, u32[]{:S(2)}) collective-permute-start(bf16[384,512]{1,0:T(8,128)(2,1)} %products.6), channel_id=1, source_target_pairs={{0,1},{1,0},{2,3},{3,2},{4,5},{5,4},{6,7},{7,6},{8,9},{9,8},{10,11... | collective-permute-start | bytes 1179656 | tf_op jit(solution)/shard_map/ppermute | solution.py:25
  36.3 2.9 %collective-permute-start.2 = (bf16[192,1024]{1,0:T(8,128)(2,1)S(1)}, bf16[192,1024]{1,0:T(8,128)(2,1)}, u32[]{:S(2)}, u32[]{:S(2)}) collective-permute-start(bf16[192,1024]{1,0:T(8,128)(2,1)S(1)} %get-tuple-element.17), channel_id=1, source_target_pairs={{0,10},{1,11},{2,8},{3,9},{4,14},{5,15},{6,12},{7,13},{8,18},{9,19... | collective-permute-start | bytes 1179656 | tf_op jit(solution)/shard_map/ppermute | solution.py:268
  39.3 15.6 %collective-permute-done.6.refs_3_ = bf16[512,512]{1,0:T(8,128)(2,1)S(1)} collective-permute-done((bf16[512,512]{1,0:T(8,128)(2,1)S(1)}, bf16[512,512]{1,0:T(8,128)(2,1)S(1)}, u32[]{:S(2)}, u32[]{:S(2)}) %collective-permute-start.6) | collective-permute-done | bytes 524320 | tf_op jit(solution)/shard_map/ppermute | solution.py:25
  54.9 1.0 %copy-done.3 = bf16[192,1024]{1,0:T(8,128)(2,1)S(1)} copy-done((bf16[192,1024]{1,0:T(8,128)(2,1)S(1)}, bf16[192,1024]{1,0:T(8,128)(2,1)}, u32[]{:S(2)}) %copy-start.3) | copy-done | bytes 393240
  55.9 0.6 products.5
  56.5 1.7 %collective-permute-start.12 = (bf16[384,512]{1,0:T(8,128)(2,1)S(1)}, bf16[384,512]{1,0:T(8,128)(2,1)S(1)}, u32[]{:S(2)}, u32[]{:S(2)}) collective-permute-start(bf16[384,512]{1,0:T(8,128)(2,1)S(1)} %products.5), channel_id=1, source_target_pairs={{0,1},{1,0},{2,3},{3,2},{4,5},{5,4},{6,7},{7,6},{8,9},{9,8},{10,11... | collective-permute-start | bytes 1179656 | tf_op jit(solution)/shard_map/ppermute | solution.py:25
  58.2 1.7 %products.4.held = f32[384,512]{1,0:T(8,128)S(1)} custom-call(bf16[192,1024]{1,0:T(8,128)(2,1)} %collective-permute-done.1.refs_0_, bf16[192,1024]{1,0:T(8,128)(2,1)} %collective-permute-done.2.refs_1_, bf16[512,512]{1,0:T(8,128)(2,1)S(1)} %get-tuple-element.31.refs_2_, bf16[512,512]{1,0:T(8,128)(2,1)S(1)} %collective-permute-done.3.refs_3_), custom_call_target="tpu_custom_call" | custom-call | flops 1610612736 | bytes 3145728 | tf_op jit(solution)/shard_map/products/pallas_call | solution.py:93
  60.1 1.7 %products.7.held = f32[384,512]{1,0:T(8,128)S(1)} custom-call(bf16[192,1024]{1,0:T(8,128)(2,1)} %collective-permute-done.1.refs_0_, bf16[192,1024]{1,0:T(8,128)(2,1)} %collective-permute-done.2.refs_1_, bf16[512,512]{1,0:T(8,128)(2,1)S(1)} %get-tuple-element.20.refs_2_, bf16[512,512]{1,0:T(8,128)(2,1)S(1)} %collective-permute-done.6.refs_3_), custom_call_target="tpu_custom_call" | custom-call | flops 1610612736 | bytes 3145728 | tf_op jit(solution)/shard_map/products/pallas_call | solution.py:93
  61.8 3.8 %collective-permute-done.12.arrived = bf16[384,512]{1,0:T(8,128)(2,1)S(1)} collective-permute-done((bf16[384,512]{1,0:T(8,128)(2,1)S(1)}, bf16[384,512]{1,0:T(8,128)(2,1)S(1)}, u32[]{:S(2)}, u32[]{:S(2)}) %collective-permute-start.12) | collective-permute-done | bytes 393248 | tf_op jit(solution)/shard_map/ppermute | solution.py:25
  65.6 0.4 collective-permute-start.13
  66.1 0.4 fusion
  66.5 0.1 pad_maximum_fusion
  66.6 0.9 collective-permute-done.8.refs_0_
  67.5 0.2 key_sum.1.refs_3_
  67.7 0.8 collective-permute-start.9
  68.5 2.9 %collective-permute-done.13.refs_0_ = bf16[192,512]{1,0:T(8,128)(2,1)S(1)} collective-permute-done((bf16[192,512]{1,0:T(8,128)(2,1)S(1)}, bf16[192,512]{1,0:T(8,128)(2,1)S(1)}, u32[]{:S(2)}, u32[]{:S(2)}) %collective-permute-start.13) | collective-permute-done | bytes 196640 | tf_op jit(solution)/shard_map/ppermute | solution.py:25
  71.4 1.8 %collective-permute-start.14 = (bf16[192,512]{1,0:T(8,128)(2,1)S(1)}, bf16[192,512]{1,0:T(8,128)(2,1)S(1)}, u32[]{:S(2)}, u32[]{:S(2)}) collective-permute-start(bf16[192,512]{1,0:T(8,128)(2,1)S(1)} %value_sum.1.refs_3_), channel_id=1, source_target_pairs={{0,1},{1,2},{2,3},{3,4},{4,5},{5,6},{6,7},{7,0},{8,9},{9,10},{10,1... | collective-permute-start | bytes 589832 | tf_op jit(solution)/shard_map/ppermute | solution.py:25
  73.2 2.4 %collective-permute-start.11 = (bf16[192,512]{1,0:T(8,128)(2,1)S(1)}, bf16[192,512]{1,0:T(8,128)(2,1)S(1)}, u32[]{:S(2)}, u32[]{:S(2)}) collective-permute-start(bf16[192,512]{1,0:T(8,128)(2,1)S(1)} %key_sum.1.refs_3_), channel_id=1, source_target_pairs={{0,2},{1,3},{2,4},{3,5},{4,6},{5,7},{6,0},{7,1},{8,10},{9,11},{10,... | collective-permute-start | bytes 589832 | tf_op jit(solution)/shard_map/ppermute | solution.py:25
  75.6 4.5 %collective-permute-done.9.refs_2_ = bf16[192,512]{1,0:T(8,128)(2,1)S(1)} collective-permute-done((bf16[192,512]{1,0:T(8,128)(2,1)S(1)}, bf16[192,512]{1,0:T(8,128)(2,1)S(1)}, u32[]{:S(2)}, u32[]{:S(2)}) %collective-permute-start.9) | collective-permute-done | bytes 196640 | tf_op jit(solution)/shard_map/ppermute | solution.py:25
  80.1 4.2 %collective-permute-done.14.refs_2_ = bf16[192,512]{1,0:T(8,128)(2,1)S(1)} collective-permute-done((bf16[192,512]{1,0:T(8,128)(2,1)S(1)}, bf16[192,512]{1,0:T(8,128)(2,1)S(1)}, u32[]{:S(2)}, u32[]{:S(2)}) %collective-permute-start.14) | collective-permute-done | bytes 196640 | tf_op jit(solution)/shard_map/ppermute | solution.py:25
  84.4 5.3 %collective-permute-done.10.refs_0_ = bf16[192,512]{1,0:T(8,128)(2,1)S(1)} collective-permute-done((bf16[192,512]{1,0:T(8,128)(2,1)S(1)}, bf16[192,512]{1,0:T(8,128)(2,1)S(1)}, u32[]{:S(2)}, u32[]{:S(2)}) %collective-permute-start.10) | collective-permute-done | bytes 196640 | tf_op jit(solution)/shard_map/ppermute | solution.py:25
  89.7 6.6 %scores.1 = (bf16[2,4,768,384]{3,2,1,0:T(8,128)(2,1)S(1)}, f32[2,4,96,128]{3,2,1,0:T(8,128)S(1)}, f32[2,32,96]{2,1,0:T(8,128)}) custom-call(bf16[1,2,96,4096]{3,2,1,0:T(8,128)(2,1)S(1)} %copy-done.1, bf16[192,512]{1,0:T(8,128)(2,1)S(1)} %collective-permute-done.10.refs_0_, bf16[192,512]{1,0:T(8,128)(2,1)S(1)} %collective-permute-done.11.refs_1_, ...), custom_call_target="tpu_custom_call" | custom-call | flops 603979776 | bytes 8388608 | tf_op jit(solution)/shard_map/scores/pallas_call | solution.py:186
  96.3 2.5 %mixed_values.1 = bf16[1,2,96,4096]{3,2,1,0:T(8,128)(2,1)} custom-call(bf16[2,4,768,384]{3,2,1,0:T(8,128)(2,1)S(1)} %get-tuple-element.24.weights, f32[2,4,96,128]{3,2,1,0:T(8,128)S(1)} %get-tuple-element.25.sums, bf16[192,512]{1,0:T(8,128)(2,1)S(1)} %collective-permute-done.15.refs_0_, bf16[192,512]{1,0:T(8,128)(2,1)S(1)} %collective-permute-done.16.refs_1_, ...), custom_call_target="tpu_custom_call" | custom-call | flops 603979776 | bytes 8388608 | tf_op jit(solution)/shard_map/mixed_values/pallas_call | solution.py:230
  (43 shorter events, 1.1 us)
Async XLA Ops:
  0.6 6.6 %copy-start = (bf16[1,2,96,4096]{3,2,1,0:T(8,128)(2,1)S(1)}, bf16[1,2,96,4096]{3,2,1,0:T(8,128)(2,1)}, u32[]{:S(2)}) copy-start(bf16[1,2,96,4096]{3,2,1,0:T(8,128)(2,1)} %param.5) | copy-start | bytes 4718596
  0.6 6.5 %collective-permute-start = (bf16[1,4096]{1,0:T(2,128)(2,1)}, bf16[1,4096]{1,0:T(2,128)(2,1)S(1)}, u32[]{:S(2)}, u32[]{:S(2)}) collective-permute-start(bf16[1,4096]{1,0:T(2,128)(2,1)} %param.6), channel_id=1, source_target_pairs={{0,24},{8,0},{16,8},{24,16},{1,25},{9,1},{17,9},{25,17},{2,26},{10... | collective-permute-start | bytes 24584 | tf_op jit(solution)/shard_map/ppermute | solution.py:25
  3.1 9.1 %copy-start.4 = (s32[2,16]{1,0:T(2,128)S(1)}, s32[2,16]{1,0:T(2,128)}, u32[]{:S(2)}) copy-start(s32[2,16]{1,0:T(2,128)} %param.9) | copy-start | bytes 388
  4.4 25.7 %collective-permute-start.3 = (bf16[512,512]{1,0:T(8,128)(2,1)S(1)}, bf16[512,512]{1,0:T(8,128)(2,1)S(1)}, u32[]{:S(2)}, u32[]{:S(2)}) collective-permute-start(bf16[512,512]{1,0:T(8,128)(2,1)S(1)} %get-tuple-element.31.refs_2_), channel_id=1, source_target_pairs={{0,4},{1,5},{2,6},{3,7},{4,0},{5,1},{6,2},{7,3},{8,12},{9,13},{10,... | collective-permute-start | bytes 1572872 | tf_op jit(solution)/shard_map/ppermute | solution.py:25
  9.3 20.8 %collective-permute-start.4 = (bf16[192,1024]{1,0:T(8,128)(2,1)}, bf16[192,1024]{1,0:T(8,128)(2,1)S(1)}, u32[]{:S(2)}, u32[]{:S(2)}) collective-permute-start(bf16[192,1024]{1,0:T(8,128)(2,1)} %get-tuple-element.18), channel_id=1, source_target_pairs={{0,9},{1,8},{2,11},{3,10},{4,13},{5,12},{6,15},{7,14},{8,17},{9,16... | collective-permute-start | bytes 1179656 | tf_op jit(solution)/shard_map/ppermute | solution.py:268
  9.7 20.4 %collective-permute-start.5 = (bf16[192,1024]{1,0:T(8,128)(2,1)}, bf16[192,1024]{1,0:T(8,128)(2,1)S(1)}, u32[]{:S(2)}, u32[]{:S(2)}) collective-permute-start(bf16[192,1024]{1,0:T(8,128)(2,1)} %get-tuple-element.19), channel_id=1, source_target_pairs={{0,11},{1,10},{2,9},{3,8},{4,15},{5,14},{6,13},{7,12},{8,19},{9,18... | collective-permute-start | bytes 1179656 | tf_op jit(solution)/shard_map/ppermute | solution.py:268
  30.0 24.9 %collective-permute-start.6 = (bf16[512,512]{1,0:T(8,128)(2,1)S(1)}, bf16[512,512]{1,0:T(8,128)(2,1)S(1)}, u32[]{:S(2)}, u32[]{:S(2)}) collective-permute-start(bf16[512,512]{1,0:T(8,128)(2,1)S(1)} %get-tuple-element.20.refs_2_), channel_id=1, source_target_pairs={{0,4},{1,5},{2,6},{3,7},{4,0},{5,1},{6,2},{7,3},{8,12},{9,13},{10,... | collective-permute-start | bytes 1572872 | tf_op jit(solution)/shard_map/ppermute | solution.py:25
  31.5 0.7 copy-start.2
  32.2 24.3 %collective-permute-start.7 = (bf16[384,512]{1,0:T(8,128)(2,1)}, bf16[384,512]{1,0:T(8,128)(2,1)S(1)}, u32[]{:S(2)}, u32[]{:S(2)}) collective-permute-start(bf16[384,512]{1,0:T(8,128)(2,1)} %products.6), channel_id=1, source_target_pairs={{0,1},{1,0},{2,3},{3,2},{4,5},{5,4},{6,7},{7,6},{8,9},{9,8},{10,11... | collective-permute-start | bytes 1179656 | tf_op jit(solution)/shard_map/ppermute | solution.py:25
  36.3 21.9 %collective-permute-start.1 = (bf16[192,1024]{1,0:T(8,128)(2,1)}, bf16[192,1024]{1,0:T(8,128)(2,1)}, u32[]{:S(2)}, u32[]{:S(2)}) collective-permute-start(bf16[192,1024]{1,0:T(8,128)(2,1)} %get-tuple-element.16), channel_id=1, source_target_pairs={{0,8},{1,9},{2,10},{3,11},{4,12},{5,13},{6,14},{7,15},{8,16},{9,17... | collective-permute-start | bytes 1179656 | tf_op jit(solution)/shard_map/ppermute | solution.py:268
  36.3 21.9 %collective-permute-start.2 = (bf16[192,1024]{1,0:T(8,128)(2,1)S(1)}, bf16[192,1024]{1,0:T(8,128)(2,1)}, u32[]{:S(2)}, u32[]{:S(2)}) collective-permute-start(bf16[192,1024]{1,0:T(8,128)(2,1)S(1)} %get-tuple-element.17), channel_id=1, source_target_pairs={{0,10},{1,11},{2,8},{3,9},{4,14},{5,15},{6,12},{7,13},{8,18},{9,19... | collective-permute-start | bytes 1179656 | tf_op jit(solution)/shard_map/ppermute | solution.py:268
  54.9 1.0 %copy-start.3 = (bf16[192,1024]{1,0:T(8,128)(2,1)S(1)}, bf16[192,1024]{1,0:T(8,128)(2,1)}, u32[]{:S(2)}) copy-start(bf16[192,1024]{1,0:T(8,128)(2,1)} %copy-done.2) | copy-start | bytes 1179652
  56.5 9.1 %collective-permute-start.12 = (bf16[384,512]{1,0:T(8,128)(2,1)S(1)}, bf16[384,512]{1,0:T(8,128)(2,1)S(1)}, u32[]{:S(2)}, u32[]{:S(2)}) collective-permute-start(bf16[384,512]{1,0:T(8,128)(2,1)S(1)} %products.5), channel_id=1, source_target_pairs={{0,1},{1,0},{2,3},{3,2},{4,5},{5,4},{6,7},{7,6},{8,9},{9,8},{10,11... | collective-permute-start | bytes 1179656 | tf_op jit(solution)/shard_map/ppermute | solution.py:25
  60.0 7.5 %collective-permute-start.8 = (bf16[192,512]{1,0:T(8,128)(2,1)S(1)}, bf16[192,512]{1,0:T(8,128)(2,1)S(1)}, u32[]{:S(2)}, u32[]{:S(2)}) collective-permute-start(bf16[192,512]{1,0:T(8,128)(2,1)S(1)} %get-tuple-element.23), channel_id=1, source_target_pairs={{0,2},{1,3},{2,0},{3,1},{4,6},{5,7},{6,4},{7,5},{8,10},{9,11},{10,... | collective-permute-start | bytes 589832 | tf_op jit(solution)/shard_map/ppermute | solution.py:25
  65.6 24.1 %copy-start.1 = (bf16[1,2,96,4096]{3,2,1,0:T(8,128)(2,1)S(1)}, bf16[1,2,96,4096]{3,2,1,0:T(8,128)(2,1)}, u32[]{:S(2)}) copy-start(bf16[1,2,96,4096]{3,2,1,0:T(8,128)(2,1)} %q_ref.1) | copy-start | bytes 4718596
  65.6 5.7 %collective-permute-start.13 = (bf16[192,512]{1,0:T(8,128)(2,1)S(1)}, bf16[192,512]{1,0:T(8,128)(2,1)S(1)}, u32[]{:S(2)}, u32[]{:S(2)}) collective-permute-start(bf16[192,512]{1,0:T(8,128)(2,1)S(1)} %get-tuple-element.28), channel_id=1, source_target_pairs={{0,2},{1,3},{2,0},{3,1},{4,6},{5,7},{6,4},{7,5},{8,10},{9,11},{10,... | collective-permute-start | bytes 589832 | tf_op jit(solution)/shard_map/ppermute | solution.py:25
  67.7 12.4 %collective-permute-start.9 = (bf16[192,512]{1,0:T(8,128)(2,1)S(1)}, bf16[192,512]{1,0:T(8,128)(2,1)S(1)}, u32[]{:S(2)}, u32[]{:S(2)}) collective-permute-start(bf16[192,512]{1,0:T(8,128)(2,1)S(1)} %key_sum.1.refs_3_), channel_id=1, source_target_pairs={{0,1},{1,2},{2,3},{3,4},{4,5},{5,6},{6,7},{7,0},{8,9},{9,10},{10,1... | collective-permute-start | bytes 589832 | tf_op jit(solution)/shard_map/ppermute | solution.py:25
  71.4 12.9 %collective-permute-start.14 = (bf16[192,512]{1,0:T(8,128)(2,1)S(1)}, bf16[192,512]{1,0:T(8,128)(2,1)S(1)}, u32[]{:S(2)}, u32[]{:S(2)}) collective-permute-start(bf16[192,512]{1,0:T(8,128)(2,1)S(1)} %value_sum.1.refs_3_), channel_id=1, source_target_pairs={{0,1},{1,2},{2,3},{3,4},{4,5},{5,6},{6,7},{7,0},{8,9},{9,10},{10,1... | collective-permute-start | bytes 589832 | tf_op jit(solution)/shard_map/ppermute | solution.py:25
  73.2 11.2 %collective-permute-start.11 = (bf16[192,512]{1,0:T(8,128)(2,1)S(1)}, bf16[192,512]{1,0:T(8,128)(2,1)S(1)}, u32[]{:S(2)}, u32[]{:S(2)}) collective-permute-start(bf16[192,512]{1,0:T(8,128)(2,1)S(1)} %key_sum.1.refs_3_), channel_id=1, source_target_pairs={{0,2},{1,3},{2,4},{3,5},{4,6},{5,7},{6,0},{7,1},{8,10},{9,11},{10,... | collective-permute-start | bytes 589832 | tf_op jit(solution)/shard_map/ppermute | solution.py:25
  80.1 9.6 %collective-permute-start.10 = (bf16[192,512]{1,0:T(8,128)(2,1)S(1)}, bf16[192,512]{1,0:T(8,128)(2,1)S(1)}, u32[]{:S(2)}, u32[]{:S(2)}) collective-permute-start(bf16[192,512]{1,0:T(8,128)(2,1)S(1)} %collective-permute-done.9.refs_2_), channel_id=1, source_target_pairs={{0,2},{1,3},{2,4},{3,5},{4,6},{5,7},{6,0},{7,1},{8,10},{9,11},{10,... | collective-permute-start | bytes 589832 | tf_op jit(solution)/shard_map/ppermute | solution.py:25
  80.1 16.2 %collective-permute-start.16 = (bf16[192,512]{1,0:T(8,128)(2,1)S(1)}, bf16[192,512]{1,0:T(8,128)(2,1)S(1)}, u32[]{:S(2)}, u32[]{:S(2)}) collective-permute-start(bf16[192,512]{1,0:T(8,128)(2,1)S(1)} %value_sum.1.refs_3_), channel_id=1, source_target_pairs={{0,2},{1,3},{2,4},{3,5},{4,6},{5,7},{6,0},{7,1},{8,10},{9,11},{10,... | collective-permute-start | bytes 589832 | tf_op jit(solution)/shard_map/ppermute | solution.py:25
  84.3 12.0 %collective-permute-start.15 = (bf16[192,512]{1,0:T(8,128)(2,1)S(1)}, bf16[192,512]{1,0:T(8,128)(2,1)S(1)}, u32[]{:S(2)}, u32[]{:S(2)}) collective-permute-start(bf16[192,512]{1,0:T(8,128)(2,1)S(1)} %collective-permute-done.14.refs_2_), channel_id=1, source_target_pairs={{0,2},{1,3},{2,4},{3,5},{4,6},{5,7},{6,0},{7,1},{8,10},{9,11},{10,... | collective-permute-start | bytes 589832 | tf_op jit(solution)/shard_map/ppermute | solution.py:25

commit v10 on v9

--- a/solution.py
+++ b/solution.py
@@ -73,8 +73,9 @@
 
 def product_kernel(blocks, *refs):
     xs, shards, out = refs[:blocks], refs[blocks:-1], refs[-1]
-    rows, shard_rows = xs[0].shape[0], shards[0].shape[0]
-    for i, x in enumerate(xs):
+    shard_rows = shards[0].shape[0]
+    first = 0
+    for x in xs:
         total = 0.0
         for j, shard in enumerate(shards):
             total = total + jnp.dot(
@@ -82,17 +83,17 @@
                 shard[...],
                 preferred_element_type=jnp.float32,
             )
-        out[i * rows : (i + 1) * rows, :] = total.astype(out.dtype)
+        out[first : first + x.shape[0], :] = total.astype(out.dtype)
+        first += x.shape[0]
 
 
 def products(xs, shards, dtype):
-    rows, part = xs[0].shape
+    rows, part = sum(x.shape[0] for x in xs), xs[0].shape[1]
     width = shards[0].shape[1]
-    blocks = len(xs)
-    size = 8 * blocks * rows * part
-    return pl.pallas_call(
-        lambda *refs: product_kernel(blocks, *refs),
-        out_shape=jax.ShapeDtypeStruct((blocks * rows, width), dtype),
+    size = 8 * rows * part
+    return pl.pallas_call(
+        lambda *refs: product_kernel(len(xs), *refs),
+        out_shape=jax.ShapeDtypeStruct((rows, width), dtype),
         compiler_params=params(24),
         cost_estimate=cost(size * width, size),
         name="products",
@@ -150,9 +151,12 @@
     )(*tables, own, *parts)
 
 
-def score_kernel(q_ref, *refs):
+def score_kernel(odd_ref, q_ref, *refs):
     key_refs, (row_pos, col_pos, weights, sums, log_sums) = refs[:WINDOW], refs[WINDOW:]
-    keys = jnp.concatenate([ref[...] for ref in key_refs], axis=0)
+    beside, two_back, before, own = [ref[...] for ref in key_refs]
+    odd = odd_ref[0] == 1
+    one_back, three_back = jnp.where(odd, before, beside), jnp.where(odd, beside, before)
+    keys = jnp.concatenate([three_back, two_back, one_back, own], axis=0)
     tok_rows = q_ref.shape[2]
     visible = col_pos[0] <= row_pos[0]
     lane = lax.broadcasted_iota(jnp.int32, (tok_rows, LANES), 1)
@@ -180,13 +184,14 @@
     return [pl.BlockSpec((tok_rows, HD), lambda m, k: (m, k))] * WINDOW
 
 
-def scored(queries, window, row_pos, col_pos):
+def scored(odd, queries, window, row_pos, col_pos):
     _, micro_count, tok_rows, _ = queries.shape
     keys = WINDOW * tok_rows
     return pl.pallas_call(
         score_kernel,
         grid=(micro_count, KVH),
         in_specs=[
+            pl.BlockSpec(memory_space=pltpu.SMEM),
             pl.BlockSpec((1, 1, tok_rows, GROUP * HD), lambda m, k: (0, m, 0, k)),
             *window_specs(tok_rows),
             pl.BlockSpec((1, tok_rows, 1), lambda m, k: (m, 0, 0)),
@@ -205,7 +210,7 @@
         compiler_params=params(24),
         cost_estimate=cost(2 * micro_count * QH * tok_rows * keys * HD, 8 * 2**20),
         name="scores",
-    )(queries, *window, row_pos, col_pos)
+    )(odd, queries, *window, row_pos, col_pos)
 
 
 def mix_kernel(weights, sums, *refs):
@@ -254,6 +259,7 @@
     _, micro_count, tok_rows, _ = handoff.shape
 
     next_gain = moved(norm_gain, "section", lambda i: i - 1).astype(jnp.float32)
+    odd = own_index % 2
     quad_order = (own_quad - jnp.arange(quads, dtype=jnp.int32)) % quads * QUAD
     flips = jnp.arange(QUAD, dtype=jnp.int32)
     cut_starts = (quad_order[None, :] + (own_place ^ flips)[:, None]) * shard_rows
@@ -267,8 +273,6 @@
         ]
         return lax.ppermute(part, ("section", "ctx"), route)
 
-    arrived = [to_next_section(cuts[flip], flip) for flip in range(QUAD)]
-
     def same_place(part):
         return [part] + [
             moved(part, "ctx", lambda i, j=j: i + QUAD * j) for j in range(1, quads)
@@ -278,6 +282,14 @@
     late_part, _ = lax.optimization_barrier((weight[:, kv_width:], key_shards[-1]))
     value_shards = same_place(late_part)
 
+    late_cut, _ = lax.optimization_barrier((cuts[2], key_shards[-1]))
+    first_cuts = [to_next_section(cuts[flip], flip) for flip in (1, 3)]
+    held_cuts = [
+        to_next_section(cuts[0], 0),
+        to_next_section(late_cut[:tok_rows], 2),
+        to_next_section(late_cut[tok_rows:], 2),
+    ]
+
     def over_y(part):
         return moved(part, "ctx", lambda i: i ^ 1)
 
@@ -285,15 +297,18 @@
         return moved(part, "ctx", lambda i: i ^ 2)
 
     def for_others(shards):
-        return products([arrived[1], arrived[3]], shards, jnp.bfloat16)
+        return products(first_cuts, shards, jnp.bfloat16)
 
     def held_here(shards):
-        return products([arrived[0], arrived[2]], shards, jnp.float32)
-
-    def near_blocks(block):
-        return [moved(block, "ctx", lambda i, d=d: i + d) for d in (1, 2)]
-
-    def window_of(block, one_back, two_back):
+        return products(held_cuts, shards, jnp.float32)
+
+    def key_window_of(block, two_back):
+        beside = over_y(two_back)
+        onward = jnp.where(odd == 1, two_back, block)
+        return [beside, two_back, moved(onward, "ctx", lambda i: i + 1), block]
+
+    def value_window_of(block):
+        one_back, two_back = [moved(block, "ctx", lambda i, d=d: i + d) for d in (1, 2)]
         return [moved(one_back, "ctx", lambda i: i + 2), two_back, one_back, block]
 
     span_len = tok_rows // 2
@@ -314,23 +329,24 @@
     sine_part = jnp.concatenate([-sine_part, sine_part], axis=1)
 
     key_y = over_y(for_others(key_shards))
-    key_held = held_here(key_shards)
-    value_products, key_y = lax.optimization_barrier((for_others(value_shards), key_y))
-    own_keys, onward_keys = half_sum(key_held, key_y)
+    own_keys, onward_keys = half_sum(held_here(key_shards), key_y)
     key_z = over_z(onward_keys)
-    value_y = over_y(value_products)
-    value_held = held_here(value_shards)
+    value_shards, _ = lax.optimization_barrier((value_shards, onward_keys))
     key_block = block_sum(key_sum_kernel, "key_sum", own_keys, [key_z], cosine, sine_part)
-    key_near = near_blocks(key_block)
-    own_values, onward_values = half_sum(value_held, value_y)
+    key_two_back = moved(key_block, "ctx", lambda i: i + 2)
+    value_y = over_y(for_others(value_shards))
+    value_y, _ = lax.optimization_barrier((value_y, key_two_back))
+    own_values, onward_values = half_sum(held_here(value_shards), value_y)
     value_z = over_z(onward_values)
-    key_window = window_of(key_block, *key_near)
     weights, sums, log_sums = scored(
-        queries, key_window, own_pos[:, :, None], col_pos[:, None, :]
+        odd.astype(jnp.int32).reshape(1),
+        queries,
+        key_window_of(key_block, key_two_back),
+        own_pos[:, :, None],
+        col_pos[:, None, :],
     )
     value_block = block_sum(value_sum_kernel, "value_sum", own_values, [value_z])
-    value_window = window_of(value_block, *near_blocks(value_block))
-    out = mixed_values(weights, sums, value_window)
+    out = mixed_values(weights, sums, value_window_of(value_block))
     return (out, log_sums[None])
 
 

time: 101 us -> 102 us (level); the launches traced: 98.8 us -> 102 us
  starting transfers between devices: 22 us -> 24.7 us
  waiting for transfers between devices: 54.8 us -> 52.9 us
  Pallas kernels: 16.8 us -> 18.1 us
    ppermute x13, waiting for transfers between devices: 54.7 us -> 42.2 us  [moved(): lax.ppermute(block, axis, [(i, target(i) % size) for i in range(size)])]
    ppermute x4 -> x5, waiting for transfers between devices: 0.01 us -> 10.8 us  [to_next_section(): return lax.ppermute(part, ('section', 'ctx'), route)]
    ppermute x13, starting transfers between devices: 16.3 us -> 18.2 us  [moved(): lax.ppermute(block, axis, [(i, target(i) % size) for i in range(size)])]
    pallas_call x4, Pallas kernels: 5.32 us -> 6.56 us  [products(): pl.pallas_call(lambda *refs: product_kernel(len(xs), *refs), out_shape=ja...]
    ppermute x4 -> x5, starting transfers between devices: 5.76 us -> 6.5 us  [to_next_section(): return lax.ppermute(part, ('section', 'ctx'), route)]
  transfers between devices with their start and end apart: 17 -> 18, of which waited for: 8 -> 10; matrix products, arithmetic and copies ran while one was open for 3% -> 3% of each run, Pallas kernels for 15% -> 15%
where the time goes in v10:
time: 102 us
  waiting for transfers between devices  52.9 us (52%)
  starting transfers between devices  24.7 us (24%)
  Pallas kernels  18.1 us (18%)
  local copies, waits for them, and re-layouts  4.12 us (4%)
    ppermute x13, waiting for transfers between devices, moved(): lax.ppermute(block, axis, [(i, target(i) % size) for i in range(size)])  42.2 us
    ppermute x13, starting transfers between devices, moved(): lax.ppermute(block, axis, [(i, target(i) % size) for i in range(size)])  18.2 us
    ppermute x5, waiting for transfers between devices, to_next_section(): return lax.ppermute(part, ('section', 'ctx'), route)  10.8 us
    pallas_call x1, Pallas kernels, scored(): pl.pallas_call(score_kernel, grid=(micro_count, KVH), in_specs=[pl.BlockS...  6.65 us
    pallas_call x4, Pallas kernels, products(): pl.pallas_call(lambda *refs: product_kernel(len(xs), *refs), out_shape=ja...  6.56 us
    ppermute x5, starting transfers between devices, to_next_section(): return lax.ppermute(part, ('section', 'ctx'), route)  6.5 us
    pallas_call x1, Pallas kernels, mixed_values(): pl.pallas_call(mix_kernel, grid=(micro_count,), in_specs=[pl.BlockSpec((1...  2.46 us
    pallas_call x1, Pallas kernels, normed_cuts(): pl.pallas_call(norm_kernel, grid=(micro_count,), in_specs=[pl.BlockSpec(m...  2.07 us
  transfers between devices with their start and end apart: 18, of which 10 were waited for; matrix products, arithmetic and copies ran while one was open for 3% of the time, Pallas kernels for 15%

profile of v10, /device:TPU:0, one launch (start us, length us, event | category | flops | bytes accessed | tf_op | source)
XLA Modules:
  0.0 101.5 jit_solution(1129630817920006877)
XLA Ops:
  0.7 2.4 %collective-permute-start = (bf16[1,4096]{1,0:T(2,128)(2,1)}, bf16[1,4096]{1,0:T(2,128)(2,1)S(1)}, u32[]{:S(2)}, u32[]{:S(2)}) collective-permute-start(bf16[1,4096]{1,0:T(2,128)(2,1)} %param.6), channel_id=1, source_target_pairs={{0,24},{8,0},{16,8},{24,16},{1,25},{9,1},{17,9},{25,17},{2,26},{10... | collective-permute-start | bytes 24584 | tf_op jit(solution)/shard_map/ppermute | solution.py:25
  3.1 1.3 %fusion.4 = (bf16[512,512]{1,0:T(8,128)(2,1)S(1)}, bf16[512,512]{1,0:T(8,128)(2,1)S(1)}) fusion(bf16[512,1024]{1,0:T(8,128)(2,1)} %bitcast.7), kind=kLoop, calls=%fused_computation.21 | loop fusion | bytes 2097152 | tf_op jit(solution)/shard_map/slice | solution.py:282
  4.3 2.7 %collective-permute-start.2 = (bf16[512,512]{1,0:T(8,128)(2,1)S(1)}, bf16[512,512]{1,0:T(8,128)(2,1)S(1)}, u32[]{:S(2)}, u32[]{:S(2)}) collective-permute-start(bf16[512,512]{1,0:T(8,128)(2,1)S(1)} %get-tuple-element.35.refs_3_.refs_2_), channel_id=1, source_target_pairs={{0,4},{1,5},{2,6},{3,7},{4,0},{5,1},{6,2},{7,3},{8,12},{9,13},{10,... | collective-permute-start | bytes 1572872 | tf_op jit(solution)/shard_map/ppermute | solution.py:25
  7.4 2.1 %norm_cuts.1 = (bf16[192,1024]{1,0:T(8,128)(2,1)S(1)}, bf16[192,1024]{1,0:T(8,128)(2,1)}, bf16[192,1024]{1,0:T(8,128)(2,1)S(1)}, bf16[192,1024]{1,0:T(8,128)(2,1)}) custom-call(s32[4,2]{1,0:T(4,128)S(1)} %add_multiply_fusion.starts_ref, bf16[2,96,4096]{2,1,0:T(8,128)(2,1)S(1)} %bitcast.6, f32[1,4096]{1,0:T(1,128)S(1)} %convert_element_type.16.gain_ref), custom_call_target="tpu_custom_call" | custom-call | flops 4718592 | bytes 3145728 | tf_op jit(solution)/shard_map/norm_cuts/pallas_call | solution.py:58
  9.5 0.8 copy-done.6
  10.6 2.5 %collective-permute-start.6 = (bf16[192,1024]{1,0:T(8,128)(2,1)}, bf16[192,1024]{1,0:T(8,128)(2,1)}, u32[]{:S(2)}, u32[]{:S(2)}) collective-permute-start(bf16[192,1024]{1,0:T(8,128)(2,1)} %get-tuple-element.22), channel_id=1, source_target_pairs={{0,11},{1,10},{2,9},{3,8},{4,15},{5,14},{6,13},{7,12},{8,19},{9,18... | collective-permute-start | bytes 1179656 | tf_op jit(solution)/shard_map/ppermute | solution.py:274
  13.4 16.6 %collective-permute-done.2.refs_4_.refs_3_ = bf16[512,512]{1,0:T(8,128)(2,1)S(1)} collective-permute-done((bf16[512,512]{1,0:T(8,128)(2,1)S(1)}, bf16[512,512]{1,0:T(8,128)(2,1)S(1)}, u32[]{:S(2)}, u32[]{:S(2)}) %collective-permute-start.2) | collective-permute-done | bytes 524320 | tf_op jit(solution)/shard_map/ppermute | solution.py:25
  30.0 0.8 fusion.5
  30.8 3.5 %collective-permute-start.4 = (bf16[96,1024]{1,0:T(8,128)(2,1)}, bf16[96,1024]{1,0:T(8,128)(2,1)}, u32[]{:S(2)}, u32[]{:S(2)}) collective-permute-start(bf16[96,1024]{1,0:T(8,128)(2,1)} %get-tuple-element.36), channel_id=1, source_target_pairs={{0,10},{1,11},{2,8},{3,9},{4,14},{5,15},{6,12},{7,13},{8,18},{9,19... | collective-permute-start | bytes 589832 | tf_op jit(solution)/shard_map/ppermute | solution.py:274
  34.3 1.6 %products.5 = bf16[384,512]{1,0:T(8,128)(2,1)S(1)} custom-call(bf16[192,1024]{1,0:T(8,128)(2,1)S(1)} %collective-permute-done.5.refs_0_, bf16[192,1024]{1,0:T(8,128)(2,1)} %collective-permute-done.6.refs_1_, bf16[512,512]{1,0:T(8,128)(2,1)S(1)} %get-tuple-element.35.refs_3_.refs_2_, bf16[512,512]{1,0:T(8,128)(2,1)S(1)} %collective-permute-done.2.refs_4_.refs_3_), custom_call_target="tpu_custom_call" | custom-call | flops 1610612736 | bytes 3145728 | tf_op jit(solution)/shard_map/products/pallas_call | solution.py:94
  35.9 0.8 copy-done.4
  36.7 1.5 %collective-permute-start.7 = (bf16[384,512]{1,0:T(8,128)(2,1)S(1)}, bf16[384,512]{1,0:T(8,128)(2,1)S(1)}, u32[]{:S(2)}, u32[]{:S(2)}) collective-permute-start(bf16[384,512]{1,0:T(8,128)(2,1)S(1)} %products.5), channel_id=1, source_target_pairs={{0,1},{1,0},{2,3},{3,2},{4,5},{5,4},{6,7},{7,6},{8,9},{9,8},{10,11... | collective-permute-start | bytes 1179656 | tf_op jit(solution)/shard_map/ppermute | solution.py:25
  38.4 8.4 %collective-permute-done.4.refs_2_ = bf16[96,1024]{1,0:T(8,128)(2,1)} collective-permute-done((bf16[96,1024]{1,0:T(8,128)(2,1)}, bf16[96,1024]{1,0:T(8,128)(2,1)}, u32[]{:S(2)}, u32[]{:S(2)}) %collective-permute-start.4) | collective-permute-done | bytes 196640 | tf_op jit(solution)/shard_map/ppermute | solution.py:274
  46.8 2.4 %collective-permute-done.3.refs_1_ = bf16[96,1024]{1,0:T(8,128)(2,1)} collective-permute-done((bf16[96,1024]{1,0:T(8,128)(2,1)}, bf16[96,1024]{1,0:T(8,128)(2,1)}, u32[]{:S(2)}, u32[]{:S(2)}) %collective-permute-start.3) | collective-permute-done | bytes 196640 | tf_op jit(solution)/shard_map/ppermute | solution.py:274
  49.2 1.7 %products.4.held = f32[384,512]{1,0:T(8,128)S(1)} custom-call(bf16[192,1024]{1,0:T(8,128)(2,1)S(1)} %collective-permute-done.1.refs_0_, bf16[96,1024]{1,0:T(8,128)(2,1)} %collective-permute-done.3.refs_1_, bf16[96,1024]{1,0:T(8,128)(2,1)} %collective-permute-done.4.refs_2_, bf16[512,512]{1,0:T(8,128)(2,1)S(1)} %get-tuple-element.35.refs_3_.refs_2_, ...), custom_call_target="tpu_custom_call" | custom-call | flops 1610612736 | bytes 3145728 | tf_op jit(solution)/shard_map/products/pallas_call | solution.py:94
  51.0 3.1 %collective-permute-start.8 = (bf16[192,512]{1,0:T(8,128)(2,1)S(1)}, bf16[192,512]{1,0:T(8,128)(2,1)S(1)}, u32[]{:S(2)}, u32[]{:S(2)}) collective-permute-start(bf16[192,512]{1,0:T(8,128)(2,1)S(1)} %get-tuple-element.24), channel_id=1, source_target_pairs={{0,2},{1,3},{2,0},{3,1},{4,6},{5,7},{6,4},{7,5},{8,10},{9,11},{10,... | collective-permute-start | bytes 589832 | tf_op jit(solution)/shard_map/ppermute | solution.py:25
  54.1 0.9 collective-permute-done.12.refs_4_.refs_3_
  55.0 1.6 %products.7 = bf16[384,512]{1,0:T(8,128)(2,1)S(1)} custom-call(bf16[192,1024]{1,0:T(8,128)(2,1)S(1)} %copy-done.5, bf16[192,1024]{1,0:T(8,128)(2,1)} %collective-permute-done.6.refs_1_, bf16[512,512]{1,0:T(8,128)(2,1)S(1)} %get-tuple-element.28.refs_3_.refs_2_, bf16[512,512]{1,0:T(8,128)(2,1)S(1)} %collective-permute-done.12.refs_4_.refs_3_), custom_call_target="tpu_custom_call" | custom-call | flops 1610612736 | bytes 3145728 | tf_op jit(solution)/shard_map/products/pallas_call | solution.py:94
  56.6 1.7 %collective-permute-start.13 = (bf16[384,512]{1,0:T(8,128)(2,1)S(1)}, bf16[384,512]{1,0:T(8,128)(2,1)S(1)}, u32[]{:S(2)}, u32[]{:S(2)}) collective-permute-start(bf16[384,512]{1,0:T(8,128)(2,1)S(1)} %products.7), channel_id=1, source_target_pairs={{0,1},{1,0},{2,3},{3,2},{4,5},{5,4},{6,7},{7,6},{8,9},{9,8},{10,11... | collective-permute-start | bytes 1179656 | tf_op jit(solution)/shard_map/ppermute | solution.py:25
  58.3 0.4 fusion
  59.4 1.3 %collective-permute-start.9 = (bf16[192,512]{1,0:T(8,128)(2,1)S(1)}, bf16[192,512]{1,0:T(8,128)(2,1)S(1)}, u32[]{:S(2)}, u32[]{:S(2)}) collective-permute-start(bf16[192,512]{1,0:T(8,128)(2,1)S(1)} %key_sum.1.refs_3_), channel_id=1, source_target_pairs={{0,2},{1,3},{2,4},{3,5},{4,6},{5,7},{6,0},{7,1},{8,10},{9,11},{10,... | collective-permute-start | bytes 589832 | tf_op jit(solution)/shard_map/ppermute | solution.py:25
  60.7 1.7 %products.6.held = f32[384,512]{1,0:T(8,128)S(1)} custom-call(bf16[192,1024]{1,0:T(8,128)(2,1)S(1)} %copy-done.3, bf16[96,1024]{1,0:T(8,128)(2,1)} %collective-permute-done.3.refs_1_, bf16[96,1024]{1,0:T(8,128)(2,1)} %collective-permute-done.4.refs_2_, bf16[512,512]{1,0:T(8,128)(2,1)S(1)} %get-tuple-element.28.refs_3_.refs_2_, ...), custom_call_target="tpu_custom_call" | custom-call | flops 1610612736 | bytes 3145728 | tf_op jit(solution)/shard_map/products/pallas_call | solution.py:94
  62.4 6.7 %collective-permute-done.9.refs_1_ = bf16[192,512]{1,0:T(8,128)(2,1)S(1)} collective-permute-done((bf16[192,512]{1,0:T(8,128)(2,1)S(1)}, bf16[192,512]{1,0:T(8,128)(2,1)S(1)}, u32[]{:S(2)}, u32[]{:S(2)}) %collective-permute-start.9) | collective-permute-done | bytes 196640 | tf_op jit(solution)/shard_map/ppermute | solution.py:25
  69.2 6.9 %collective-permute-done.14.refs_0_ = bf16[192,512]{1,0:T(8,128)(2,1)S(1)} collective-permute-done((bf16[192,512]{1,0:T(8,128)(2,1)S(1)}, bf16[192,512]{1,0:T(8,128)(2,1)S(1)}, u32[]{:S(2)}, u32[]{:S(2)}) %collective-permute-start.14) | collective-permute-done | bytes 196640 | tf_op jit(solution)/shard_map/ppermute | solution.py:25
  76.2 1.5 %collective-permute-start.15 = (bf16[192,512]{1,0:T(8,128)(2,1)S(1)}, bf16[192,512]{1,0:T(8,128)(2,1)S(1)}, u32[]{:S(2)}, u32[]{:S(2)}) collective-permute-start(bf16[192,512]{1,0:T(8,128)(2,1)S(1)} %value_sum.1.refs_3_), channel_id=1, source_target_pairs={{0,1},{1,2},{2,3},{3,4},{4,5},{5,6},{6,7},{7,0},{8,9},{9,10},{10,1... | collective-permute-start | bytes 589832 | tf_op jit(solution)/shard_map/ppermute | solution.py:25
  78.1 1.5 %collective-permute-start.10 = (bf16[192,512]{1,0:T(8,128)(2,1)S(1)}, bf16[192,512]{1,0:T(8,128)(2,1)S(1)}, u32[]{:S(2)}, u32[]{:S(2)}) collective-permute-start(bf16[192,512]{1,0:T(8,128)(2,1)S(1)} %collective-permute-done.9.refs_1_), channel_id=1, source_target_pairs={{0,1},{1,0},{2,3},{3,2},{4,5},{5,4},{6,7},{7,6},{8,9},{9,8},{10,11... | collective-permute-start | bytes 589832 | tf_op jit(solution)/shard_map/ppermute | solution.py:25
  79.6 2.1 %collective-permute-start.17 = (bf16[192,512]{1,0:T(8,128)(2,1)S(1)}, bf16[192,512]{1,0:T(8,128)(2,1)S(1)}, u32[]{:S(2)}, u32[]{:S(2)}) collective-permute-start(bf16[192,512]{1,0:T(8,128)(2,1)S(1)} %value_sum.1.refs_3_), channel_id=1, source_target_pairs={{0,2},{1,3},{2,4},{3,5},{4,6},{5,7},{6,0},{7,1},{8,10},{9,11},{10,... | collective-permute-start | bytes 589832 | tf_op jit(solution)/shard_map/ppermute | solution.py:25
  81.6 5.3 %collective-permute-done.15.refs_2_ = bf16[192,512]{1,0:T(8,128)(2,1)S(1)} collective-permute-done((bf16[192,512]{1,0:T(8,128)(2,1)S(1)}, bf16[192,512]{1,0:T(8,128)(2,1)S(1)}, u32[]{:S(2)}, u32[]{:S(2)}) %collective-permute-start.15) | collective-permute-done | bytes 196640 | tf_op jit(solution)/shard_map/ppermute | solution.py:25
  87.0 4.0 %collective-permute-done.11.refs_2_ = bf16[192,512]{1,0:T(8,128)(2,1)S(1)} collective-permute-done((bf16[192,512]{1,0:T(8,128)(2,1)S(1)}, bf16[192,512]{1,0:T(8,128)(2,1)S(1)}, u32[]{:S(2)}, u32[]{:S(2)}) %collective-permute-start.11) | collective-permute-done | bytes 196640 | tf_op jit(solution)/shard_map/ppermute | solution.py:25
  91.0 1.3 %collective-permute-done.10.refs_0_ = bf16[192,512]{1,0:T(8,128)(2,1)S(1)} collective-permute-done((bf16[192,512]{1,0:T(8,128)(2,1)S(1)}, bf16[192,512]{1,0:T(8,128)(2,1)S(1)}, u32[]{:S(2)}, u32[]{:S(2)}) %collective-permute-start.10) | collective-permute-done | bytes 196640 | tf_op jit(solution)/shard_map/ppermute | solution.py:25
  92.4 6.6 %scores.1 = (bf16[2,4,768,384]{3,2,1,0:T(8,128)(2,1)S(1)}, f32[2,4,96,128]{3,2,1,0:T(8,128)S(1)}, f32[2,32,96]{2,1,0:T(8,128)}) custom-call(s32[1]{0:T(128)} %bitcast.odd_ref, bf16[1,2,96,4096]{3,2,1,0:T(8,128)(2,1)S(1)} %copy-done.1, bf16[192,512]{1,0:T(8,128)(2,1)S(1)} %collective-permute-done.10.refs_0_, ...), custom_call_target="tpu_custom_call" | custom-call | flops 603979776 | bytes 8388608 | tf_op jit(solution)/shard_map/scores/pallas_call | solution.py:190
  99.0 2.5 %mixed_values.1 = bf16[1,2,96,4096]{3,2,1,0:T(8,128)(2,1)} custom-call(bf16[2,4,768,384]{3,2,1,0:T(8,128)(2,1)S(1)} %get-tuple-element.25.weights, f32[2,4,96,128]{3,2,1,0:T(8,128)S(1)} %get-tuple-element.26.sums, bf16[192,512]{1,0:T(8,128)(2,1)S(1)} %collective-permute-done.16.refs_0_, bf16[192,512]{1,0:T(8,128)(2,1)S(1)} %collective-permute-done.17.refs_1_, ...), custom_call_target="tpu_custom_call" | custom-call | flops 603979776 | bytes 8388608 | tf_op jit(solution)/shard_map/mixed_values/pallas_call | solution.py:235
  (53 shorter events, 2.6 us)
Async XLA Ops:
  0.6 6.5 %copy-start.7 = (s32[2,16]{1,0:T(2,128)S(1)}, s32[2,16]{1,0:T(2,128)}, u32[]{:S(2)}) copy-start(s32[2,16]{1,0:T(2,128)} %param.9) | copy-start | bytes 388
  0.6 6.7 %copy-start = (bf16[1,2,96,4096]{3,2,1,0:T(8,128)(2,1)S(1)}, bf16[1,2,96,4096]{3,2,1,0:T(8,128)(2,1)}, u32[]{:S(2)}) copy-start(bf16[1,2,96,4096]{3,2,1,0:T(8,128)(2,1)} %param.5) | copy-start | bytes 4718596
  0.7 6.7 %collective-permute-start = (bf16[1,4096]{1,0:T(2,128)(2,1)}, bf16[1,4096]{1,0:T(2,128)(2,1)S(1)}, u32[]{:S(2)}, u32[]{:S(2)}) collective-permute-start(bf16[1,4096]{1,0:T(2,128)(2,1)} %param.6), channel_id=1, source_target_pairs={{0,24},{8,0},{16,8},{24,16},{1,25},{9,1},{17,9},{25,17},{2,26},{10... | collective-permute-start | bytes 24584 | tf_op jit(solution)/shard_map/ppermute | solution.py:25
  4.3 25.7 %collective-permute-start.2 = (bf16[512,512]{1,0:T(8,128)(2,1)S(1)}, bf16[512,512]{1,0:T(8,128)(2,1)S(1)}, u32[]{:S(2)}, u32[]{:S(2)}) collective-permute-start(bf16[512,512]{1,0:T(8,128)(2,1)S(1)} %get-tuple-element.35.refs_3_.refs_2_), channel_id=1, source_target_pairs={{0,4},{1,5},{2,6},{3,7},{4,0},{5,1},{6,2},{7,3},{8,12},{9,13},{10,... | collective-permute-start | bytes 1572872 | tf_op jit(solution)/shard_map/ppermute | solution.py:25
  9.5 0.8 copy-start.6
  10.2 24.1 %collective-permute-start.5 = (bf16[192,1024]{1,0:T(8,128)(2,1)}, bf16[192,1024]{1,0:T(8,128)(2,1)S(1)}, u32[]{:S(2)}, u32[]{:S(2)}) collective-permute-start(bf16[192,1024]{1,0:T(8,128)(2,1)} %get-tuple-element.21), channel_id=1, source_target_pairs={{0,9},{1,8},{2,11},{3,10},{4,13},{5,12},{6,15},{7,14},{8,17},{9,16... | collective-permute-start | bytes 1179656 | tf_op jit(solution)/shard_map/ppermute | solution.py:274
  10.6 23.7 %collective-permute-start.6 = (bf16[192,1024]{1,0:T(8,128)(2,1)}, bf16[192,1024]{1,0:T(8,128)(2,1)}, u32[]{:S(2)}, u32[]{:S(2)}) collective-permute-start(bf16[192,1024]{1,0:T(8,128)(2,1)} %get-tuple-element.22), channel_id=1, source_target_pairs={{0,11},{1,10},{2,9},{3,8},{4,15},{5,14},{6,13},{7,12},{8,19},{9,18... | collective-permute-start | bytes 1179656 | tf_op jit(solution)/shard_map/ppermute | solution.py:274
  13.3 25.1 %collective-permute-start.1 = (bf16[192,1024]{1,0:T(8,128)(2,1)}, bf16[192,1024]{1,0:T(8,128)(2,1)S(1)}, u32[]{:S(2)}, u32[]{:S(2)}) collective-permute-start(bf16[192,1024]{1,0:T(8,128)(2,1)} %copy-done.6), channel_id=1, source_target_pairs={{0,8},{1,9},{2,10},{3,11},{4,12},{5,13},{6,14},{7,15},{8,16},{9,17... | collective-permute-start | bytes 1179656 | tf_op jit(solution)/shard_map/ppermute | solution.py:274
  30.0 25.0 %collective-permute-start.12 = (bf16[512,512]{1,0:T(8,128)(2,1)S(1)}, bf16[512,512]{1,0:T(8,128)(2,1)S(1)}, u32[]{:S(2)}, u32[]{:S(2)}) collective-permute-start(bf16[512,512]{1,0:T(8,128)(2,1)S(1)} %get-tuple-element.28.refs_3_.refs_2_), channel_id=1, source_target_pairs={{0,4},{1,5},{2,6},{3,7},{4,0},{5,1},{6,2},{7,3},{8,12},{9,13},{10,... | collective-permute-start | bytes 1572872 | tf_op jit(solution)/shard_map/ppermute | solution.py:25
  30.8 16.0 %collective-permute-start.4 = (bf16[96,1024]{1,0:T(8,128)(2,1)}, bf16[96,1024]{1,0:T(8,128)(2,1)}, u32[]{:S(2)}, u32[]{:S(2)}) collective-permute-start(bf16[96,1024]{1,0:T(8,128)(2,1)} %get-tuple-element.36), channel_id=1, source_target_pairs={{0,10},{1,11},{2,8},{3,9},{4,14},{5,15},{6,12},{7,13},{8,18},{9,19... | collective-permute-start | bytes 589832 | tf_op jit(solution)/shard_map/ppermute | solution.py:274
  34.3 14.9 %collective-permute-start.3 = (bf16[96,1024]{1,0:T(8,128)(2,1)}, bf16[96,1024]{1,0:T(8,128)(2,1)}, u32[]{:S(2)}, u32[]{:S(2)}) collective-permute-start(bf16[96,1024]{1,0:T(8,128)(2,1)} %get-tuple-element.37), channel_id=1, source_target_pairs={{0,10},{1,11},{2,8},{3,9},{4,14},{5,15},{6,12},{7,13},{8,18},{9,19... | collective-permute-start | bytes 589832 | tf_op jit(solution)/shard_map/ppermute | solution.py:274
  35.9 0.8 copy-start.4
  36.7 14.2 %collective-permute-start.7 = (bf16[384,512]{1,0:T(8,128)(2,1)S(1)}, bf16[384,512]{1,0:T(8,128)(2,1)S(1)}, u32[]{:S(2)}, u32[]{:S(2)}) collective-permute-start(bf16[384,512]{1,0:T(8,128)(2,1)S(1)} %products.5), channel_id=1, source_target_pairs={{0,1},{1,0},{2,3},{3,2},{4,5},{5,4},{6,7},{7,6},{8,9},{9,8},{10,11... | collective-permute-start | bytes 1179656 | tf_op jit(solution)/shard_map/ppermute | solution.py:25
  38.4 16.6 %copy-start.5 = (bf16[192,1024]{1,0:T(8,128)(2,1)S(1)}, bf16[192,1024]{1,0:T(8,128)(2,1)}, u32[]{:S(2)}) copy-start(bf16[192,1024]{1,0:T(8,128)(2,1)} %copy-done.4) | copy-start | bytes 1179652
  38.4 12.5 %copy-start.2 = (bf16[192,1024]{1,0:T(8,128)(2,1)}, bf16[192,1024]{1,0:T(8,128)(2,1)S(1)}, u32[]{:S(2)}) copy-start(bf16[192,1024]{1,0:T(8,128)(2,1)S(1)} %collective-permute-done.1.refs_0_) | copy-start | bytes 1179652
  51.0 8.2 %collective-permute-start.8 = (bf16[192,512]{1,0:T(8,128)(2,1)S(1)}, bf16[192,512]{1,0:T(8,128)(2,1)S(1)}, u32[]{:S(2)}, u32[]{:S(2)}) collective-permute-start(bf16[192,512]{1,0:T(8,128)(2,1)S(1)} %get-tuple-element.24), channel_id=1, source_target_pairs={{0,2},{1,3},{2,0},{3,1},{4,6},{5,7},{6,4},{7,5},{8,10},{9,11},{10,... | collective-permute-start | bytes 589832 | tf_op jit(solution)/shard_map/ppermute | solution.py:25
  56.6 4.1 %copy-start.3 = (bf16[192,1024]{1,0:T(8,128)(2,1)S(1)}, bf16[192,1024]{1,0:T(8,128)(2,1)}, u32[]{:S(2)}) copy-start(bf16[192,1024]{1,0:T(8,128)(2,1)} %copy-done.2) | copy-start | bytes 1179652
  56.6 12.5 %collective-permute-start.13 = (bf16[384,512]{1,0:T(8,128)(2,1)S(1)}, bf16[384,512]{1,0:T(8,128)(2,1)S(1)}, u32[]{:S(2)}, u32[]{:S(2)}) collective-permute-start(bf16[384,512]{1,0:T(8,128)(2,1)S(1)} %products.7), channel_id=1, source_target_pairs={{0,1},{1,0},{2,3},{3,2},{4,5},{5,4},{6,7},{7,6},{8,9},{9,8},{10,11... | collective-permute-start | bytes 1179656 | tf_op jit(solution)/shard_map/ppermute | solution.py:25
  59.4 9.7 %collective-permute-start.9 = (bf16[192,512]{1,0:T(8,128)(2,1)S(1)}, bf16[192,512]{1,0:T(8,128)(2,1)S(1)}, u32[]{:S(2)}, u32[]{:S(2)}) collective-permute-start(bf16[192,512]{1,0:T(8,128)(2,1)S(1)} %key_sum.1.refs_3_), channel_id=1, source_target_pairs={{0,2},{1,3},{2,4},{3,5},{4,6},{5,7},{6,0},{7,1},{8,10},{9,11},{10,... | collective-permute-start | bytes 589832 | tf_op jit(solution)/shard_map/ppermute | solution.py:25
  62.4 30.0 %copy-start.1 = (bf16[1,2,96,4096]{3,2,1,0:T(8,128)(2,1)S(1)}, bf16[1,2,96,4096]{3,2,1,0:T(8,128)(2,1)}, u32[]{:S(2)}) copy-start(bf16[1,2,96,4096]{3,2,1,0:T(8,128)(2,1)} %q_ref.1) | copy-start | bytes 4718596
  69.1 7.0 %collective-permute-start.14 = (bf16[192,512]{1,0:T(8,128)(2,1)S(1)}, bf16[192,512]{1,0:T(8,128)(2,1)S(1)}, u32[]{:S(2)}, u32[]{:S(2)}) collective-permute-start(bf16[192,512]{1,0:T(8,128)(2,1)S(1)} %get-tuple-element.32), channel_id=1, source_target_pairs={{0,2},{1,3},{2,0},{3,1},{4,6},{5,7},{6,4},{7,5},{8,10},{9,11},{10,... | collective-permute-start | bytes 589832 | tf_op jit(solution)/shard_map/ppermute | solution.py:25
  76.2 10.7 %collective-permute-start.15 = (bf16[192,512]{1,0:T(8,128)(2,1)S(1)}, bf16[192,512]{1,0:T(8,128)(2,1)S(1)}, u32[]{:S(2)}, u32[]{:S(2)}) collective-permute-start(bf16[192,512]{1,0:T(8,128)(2,1)S(1)} %value_sum.1.refs_3_), channel_id=1, source_target_pairs={{0,1},{1,2},{2,3},{3,4},{4,5},{5,6},{6,7},{7,0},{8,9},{9,10},{10,1... | collective-permute-start | bytes 589832 | tf_op jit(solution)/shard_map/ppermute | solution.py:25
  77.8 13.3 %collective-permute-start.11 = (bf16[192,512]{1,0:T(8,128)(2,1)S(1)}, bf16[192,512]{1,0:T(8,128)(2,1)S(1)}, u32[]{:S(2)}, u32[]{:S(2)}) collective-permute-start(bf16[192,512]{1,0:T(8,128)(2,1)S(1)} %broadcast_select_fusion), channel_id=1, source_target_pairs={{0,1},{1,2},{2,3},{3,4},{4,5},{5,6},{6,7},{7,0},{8,9},{9,10},{10,1... | collective-permute-start | bytes 589832 | tf_op jit(solution)/shard_map/ppermute | solution.py:25
  78.1 14.3 %collective-permute-start.10 = (bf16[192,512]{1,0:T(8,128)(2,1)S(1)}, bf16[192,512]{1,0:T(8,128)(2,1)S(1)}, u32[]{:S(2)}, u32[]{:S(2)}) collective-permute-start(bf16[192,512]{1,0:T(8,128)(2,1)S(1)} %collective-permute-done.9.refs_1_), channel_id=1, source_target_pairs={{0,1},{1,0},{2,3},{3,2},{4,5},{5,4},{6,7},{7,6},{8,9},{9,8},{10,11... | collective-permute-start | bytes 589832 | tf_op jit(solution)/shard_map/ppermute | solution.py:25
  79.6 19.5 %collective-permute-start.17 = (bf16[192,512]{1,0:T(8,128)(2,1)S(1)}, bf16[192,512]{1,0:T(8,128)(2,1)S(1)}, u32[]{:S(2)}, u32[]{:S(2)}) collective-permute-start(bf16[192,512]{1,0:T(8,128)(2,1)S(1)} %value_sum.1.refs_3_), channel_id=1, source_target_pairs={{0,2},{1,3},{2,4},{3,5},{4,6},{5,7},{6,0},{7,1},{8,10},{9,11},{10,... | collective-permute-start | bytes 589832 | tf_op jit(solution)/shard_map/ppermute | solution.py:25
  86.9 12.2 %collective-permute-start.16 = (bf16[192,512]{1,0:T(8,128)(2,1)S(1)}, bf16[192,512]{1,0:T(8,128)(2,1)S(1)}, u32[]{:S(2)}, u32[]{:S(2)}) collective-permute-start(bf16[192,512]{1,0:T(8,128)(2,1)S(1)} %collective-permute-done.15.refs_2_), channel_id=1, source_target_pairs={{0,2},{1,3},{2,4},{3,5},{4,6},{5,7},{6,0},{7,1},{8,10},{9,11},{10,... | collective-permute-start | bytes 589832 | tf_op jit(solution)/shard_map/ppermute | solution.py:25

commit v11 on v10

--- a/solution.py
+++ b/solution.py
@@ -71,29 +71,34 @@
     )(starts, activations, gain)
 
 
-def product_kernel(blocks, *refs):
-    xs, shards, out = refs[:blocks], refs[blocks:-1], refs[-1]
+def product_kernel(counts, *refs):
+    blocks = sum(counts)
+    xs, shards, outs = list(refs[:blocks]), refs[blocks : -len(counts)], refs[-len(counts) :]
     shard_rows = shards[0].shape[0]
-    first = 0
-    for x in xs:
-        total = 0.0
-        for j, shard in enumerate(shards):
-            total = total + jnp.dot(
-                x[:, j * shard_rows : (j + 1) * shard_rows],
-                shard[...],
-                preferred_element_type=jnp.float32,
-            )
-        out[first : first + x.shape[0], :] = total.astype(out.dtype)
-        first += x.shape[0]
-
-
-def products(xs, shards, dtype):
-    rows, part = sum(x.shape[0] for x in xs), xs[0].shape[1]
+    for count, out in zip(counts, outs):
+        first = 0
+        for _ in range(count):
+            x = xs.pop(0)
+            total = 0.0
+            for j, shard in enumerate(shards):
+                total = total + jnp.dot(
+                    x[:, j * shard_rows : (j + 1) * shard_rows],
+                    shard[...],
+                    preferred_element_type=jnp.float32,
+                )
+            out[first : first + x.shape[0], :] = total.astype(out.dtype)
+            first += x.shape[0]
+
+
+def products(groups, shards, dtype):
+    counts = [len(group) for group in groups]
+    heights = [sum(x.shape[0] for x in group) for group in groups]
+    xs = [x for group in groups for x in group]
     width = shards[0].shape[1]
-    size = 8 * rows * part
-    return pl.pallas_call(
-        lambda *refs: product_kernel(len(xs), *refs),
-        out_shape=jax.ShapeDtypeStruct((rows, width), dtype),
+    size = 8 * sum(heights) * xs[0].shape[1]
+    return pl.pallas_call(
+        lambda *refs: product_kernel(counts, *refs),
+        out_shape=[jax.ShapeDtypeStruct((height, width), dtype) for height in heights],
         compiler_params=params(24),
         cost_estimate=cost(size * width, size),
         name="products",
@@ -296,19 +301,14 @@
     def over_z(part):
         return moved(part, "ctx", lambda i: i ^ 2)
 
-    def for_others(shards):
-        return products(first_cuts, shards, jnp.bfloat16)
-
-    def held_here(shards):
-        return products(held_cuts, shards, jnp.float32)
-
     def key_window_of(block, two_back):
         beside = over_y(two_back)
         onward = jnp.where(odd == 1, two_back, block)
         return [beside, two_back, moved(onward, "ctx", lambda i: i + 1), block]
 
-    def value_window_of(block):
+    def value_window_of(block, weights):
         one_back, two_back = [moved(block, "ctx", lambda i, d=d: i + d) for d in (1, 2)]
+        one_back, _ = lax.optimization_barrier((one_back, weights))
         return [moved(one_back, "ctx", lambda i: i + 2), two_back, one_back, block]
 
     span_len = tok_rows // 2
@@ -328,16 +328,24 @@
     cosine = jnp.concatenate([cosine, cosine], axis=1)
     sine_part = jnp.concatenate([-sine_part, sine_part], axis=1)
 
-    key_y = over_y(for_others(key_shards))
-    own_keys, onward_keys = half_sum(held_here(key_shards), key_y)
+    (key_products,) = products([first_cuts], key_shards, jnp.bfloat16)
+    key_y = over_y(key_products)
+    (key_held,) = products([held_cuts], key_shards, jnp.float32)
+    own_keys, onward_keys = half_sum(key_held, key_y)
     key_z = over_z(onward_keys)
     value_shards, _ = lax.optimization_barrier((value_shards, onward_keys))
+    value_products = products(
+        [first_cuts[:1], held_cuts[1:], first_cuts[1:]], value_shards, jnp.bfloat16
+    )
+    key_z, value_products = lax.optimization_barrier((key_z, value_products))
     key_block = block_sum(key_sum_kernel, "key_sum", own_keys, [key_z], cosine, sine_part)
     key_two_back = moved(key_block, "ctx", lambda i: i + 2)
-    value_y = over_y(for_others(value_shards))
-    value_y, _ = lax.optimization_barrier((value_y, key_two_back))
-    own_values, onward_values = half_sum(held_here(value_shards), value_y)
-    value_z = over_z(onward_values)
+    value_parts = [
+        moved(part, "ctx", lambda i, flip=flip: i ^ flip)
+        for flip, part in enumerate(value_products, start=1)
+    ]
+    (own_values,) = products([held_cuts[:1]], value_shards, jnp.float32)
+    value_parts, _ = lax.optimization_barrier((value_parts, key_two_back))
     weights, sums, log_sums = scored(
         odd.astype(jnp.int32).reshape(1),
         queries,
@@ -345,8 +353,8 @@
         own_pos[:, :, None],
         col_pos[:, None, :],
     )
-    value_block = block_sum(value_sum_kernel, "value_sum", own_values, [value_z])
-    out = mixed_values(weights, sums, value_window_of(value_block))
+    value_block = block_sum(value_sum_kernel, "value_sum", own_values, value_parts)
+    out = mixed_values(weights, sums, value_window_of(value_block, weights))
     return (out, log_sums[None])
 
 

time: 102 us -> 105 us (1.029)
  waiting for transfers between devices: 52.9 us -> 57.2 us
  Pallas kernels: 18.1 us -> 17 us
    ppermute x13 -> x14, waiting for transfers between devices: 42.2 us -> 45.7 us  [moved(): lax.ppermute(block, axis, [(i, target(i) % size) for i in range(size)])]
    pallas_call x4, Pallas kernels: 6.56 us -> 5.48 us  [products(): pl.pallas_call(lambda *refs: product_kernel(counts, *refs), out_shape=[ja...]
    ppermute x13 -> x14, starting transfers between devices: 18.2 us -> 18.3 us  [moved(): lax.ppermute(block, axis, [(i, target(i) % size) for i in range(size)])]
  transfers between devices with their start and end apart: 18 -> 19, of which waited for: 10 -> 10; matrix products, arithmetic and copies ran while one was open for 3% -> 3% of each run, Pallas kernels for 15% -> 14%
where the time goes in v11:
time: 105 us
  waiting for transfers between devices  57.2 us (54%)
  starting transfers between devices  24.9 us (24%)
  Pallas kernels  17 us (16%)
  local copies, waits for them, and re-layouts  3.59 us (3%)
  other arithmetic  1.51 us (1%)
    ppermute x14, waiting for transfers between devices, moved(): lax.ppermute(block, axis, [(i, target(i) % size) for i in range(size)])  45.7 us
    ppermute x14, starting transfers between devices, moved(): lax.ppermute(block, axis, [(i, target(i) % size) for i in range(size)])  18.3 us
    ppermute x5, waiting for transfers between devices, to_next_section(): return lax.ppermute(part, ('section', 'ctx'), route)  11.5 us
    pallas_call x1, Pallas kernels, scored(): pl.pallas_call(score_kernel, grid=(micro_count, KVH), in_specs=[pl.BlockS...  6.65 us
    ppermute x5, starting transfers between devices, to_next_section(): return lax.ppermute(part, ('section', 'ctx'), route)  6.64 us
    pallas_call x4, Pallas kernels, products(): pl.pallas_call(lambda *refs: product_kernel(counts, *refs), out_shape=[ja...  5.48 us
    pallas_call x1, Pallas kernels, mixed_values(): pl.pallas_call(mix_kernel, grid=(micro_count,), in_specs=[pl.BlockSpec((1...  2.44 us
  transfers between devices with their start and end apart: 19, of which 10 were waited for; matrix products, arithmetic and copies ran while one was open for 3% of the time, Pallas kernels for 14%

profile of v11, /device:TPU:0, one launch (start us, length us, event | category | flops | bytes accessed | tf_op | source)
XLA Modules:
  0.0 105.1 jit_solution(10576718954362436696)
XLA Ops:
  0.7 2.4 %collective-permute-start = (bf16[1,4096]{1,0:T(2,128)(2,1)}, bf16[1,4096]{1,0:T(2,128)(2,1)S(1)}, u32[]{:S(2)}, u32[]{:S(2)}) collective-permute-start(bf16[1,4096]{1,0:T(2,128)(2,1)} %param.6), channel_id=1, source_target_pairs={{0,24},{8,0},{16,8},{24,16},{1,25},{9,1},{17,9},{25,17},{2,26},{10... | collective-permute-start | bytes 24584 | tf_op jit(solution)/shard_map/ppermute | solution.py:25
  3.1 1.3 %fusion.4 = (bf16[512,512]{1,0:T(8,128)(2,1)S(1)}, bf16[512,512]{1,0:T(8,128)(2,1)S(1)}) fusion(bf16[512,1024]{1,0:T(8,128)(2,1)} %bitcast.7), kind=kLoop, calls=%fused_computation.21 | loop fusion | bytes 2097152 | tf_op jit(solution)/shard_map/slice | solution.py:287
  4.3 2.7 %collective-permute-start.2 = (bf16[512,512]{1,0:T(8,128)(2,1)S(1)}, bf16[512,512]{1,0:T(8,128)(2,1)S(1)}, u32[]{:S(2)}, u32[]{:S(2)}) collective-permute-start(bf16[512,512]{1,0:T(8,128)(2,1)S(1)} %get-tuple-element.51.refs_3_.refs_2_), channel_id=1, source_target_pairs={{0,4},{1,5},{2,6},{3,7},{4,0},{5,1},{6,2},{7,3},{8,12},{9,13},{10,... | collective-permute-start | bytes 1572872 | tf_op jit(solution)/shard_map/ppermute | solution.py:25
  7.6 2.1 %norm_cuts.1 = (bf16[192,1024]{1,0:T(8,128)(2,1)S(1)}, bf16[192,1024]{1,0:T(8,128)(2,1)}, bf16[192,1024]{1,0:T(8,128)(2,1)S(1)}, bf16[192,1024]{1,0:T(8,128)(2,1)}) custom-call(s32[4,2]{1,0:T(4,128)S(1)} %add_multiply_fusion.starts_ref, bf16[2,96,4096]{2,1,0:T(8,128)(2,1)S(1)} %bitcast.6, f32[1,4096]{1,0:T(1,128)S(1)} %convert_element_type.16.gain_ref), custom_call_target="tpu_custom_call" | custom-call | flops 4718592 | bytes 3145728 | tf_op jit(solution)/shard_map/norm_cuts/pallas_call | solution.py:58
  9.6 0.8 copy-done.8
  10.4 0.4 collective-permute-start.5
  10.8 2.5 %collective-permute-start.6 = (bf16[192,1024]{1,0:T(8,128)(2,1)}, bf16[192,1024]{1,0:T(8,128)(2,1)}, u32[]{:S(2)}, u32[]{:S(2)}) collective-permute-start(bf16[192,1024]{1,0:T(8,128)(2,1)} %get-tuple-element.30), channel_id=1, source_target_pairs={{0,11},{1,10},{2,9},{3,8},{4,15},{5,14},{6,13},{7,12},{8,19},{9,18... | collective-permute-start | bytes 1179656 | tf_op jit(solution)/shard_map/ppermute | solution.py:279
  13.6 16.4 %collective-permute-done.2.refs_4_.refs_3_ = bf16[512,512]{1,0:T(8,128)(2,1)S(1)} collective-permute-done((bf16[512,512]{1,0:T(8,128)(2,1)S(1)}, bf16[512,512]{1,0:T(8,128)(2,1)S(1)}, u32[]{:S(2)}, u32[]{:S(2)}) %collective-permute-start.2) | collective-permute-done | bytes 524320 | tf_op jit(solution)/shard_map/ppermute | solution.py:25
  30.0 3.5 %collective-permute-start.4 = (bf16[96,1024]{1,0:T(8,128)(2,1)S(1)}, bf16[96,1024]{1,0:T(8,128)(2,1)S(1)}, u32[]{:S(2)}, u32[]{:S(2)}) collective-permute-start(bf16[96,1024]{1,0:T(8,128)(2,1)S(1)} %get-tuple-element.52), channel_id=1, source_target_pairs={{0,10},{1,11},{2,8},{3,9},{4,14},{5,15},{6,12},{7,13},{8,18},{9,19... | collective-permute-start | bytes 589832 | tf_op jit(solution)/shard_map/ppermute | solution.py:279
  33.7 1.6 %products.5 = bf16[384,512]{1,0:T(8,128)(2,1)S(1)} custom-call(bf16[192,1024]{1,0:T(8,128)(2,1)S(1)} %collective-permute-done.5.refs_0_, bf16[192,1024]{1,0:T(8,128)(2,1)} %collective-permute-done.6.refs_1_.refs_3_, bf16[512,512]{1,0:T(8,128)(2,1)S(1)} %get-tuple-element.51.refs_3_.refs_2_, bf16[512,512]{1,0:T(8,128)(2,1)S(1)} %collective-permute-done.2.refs_4_.refs_3_), custom_call_target="tpu_custom_call" | custom-call | flops 1610612736 | bytes 3145728 | tf_op jit(solution)/shard_map/products/pallas_call | solution.py:99
  35.3 1.6 %collective-permute-start.7 = (bf16[384,512]{1,0:T(8,128)(2,1)S(1)}, bf16[384,512]{1,0:T(8,128)(2,1)S(1)}, u32[]{:S(2)}, u32[]{:S(2)}) collective-permute-start(bf16[384,512]{1,0:T(8,128)(2,1)S(1)} %products.5), channel_id=1, source_target_pairs={{0,1},{1,0},{2,3},{3,2},{4,5},{5,4},{6,7},{7,6},{8,9},{9,8},{10,11... | collective-permute-start | bytes 1179656 | tf_op jit(solution)/shard_map/ppermute | solution.py:25
  36.9 0.4 fusion
  37.5 9.1 %collective-permute-done.4.refs_2_ = bf16[96,1024]{1,0:T(8,128)(2,1)S(1)} collective-permute-done((bf16[96,1024]{1,0:T(8,128)(2,1)S(1)}, bf16[96,1024]{1,0:T(8,128)(2,1)S(1)}, u32[]{:S(2)}, u32[]{:S(2)}) %collective-permute-start.4) | collective-permute-done | bytes 196640 | tf_op jit(solution)/shard_map/ppermute | solution.py:279
  46.7 2.4 %collective-permute-done.3.refs_1_ = bf16[96,1024]{1,0:T(8,128)(2,1)S(1)} collective-permute-done((bf16[96,1024]{1,0:T(8,128)(2,1)S(1)}, bf16[96,1024]{1,0:T(8,128)(2,1)S(1)}, u32[]{:S(2)}, u32[]{:S(2)}) %collective-permute-start.3) | collective-permute-done | bytes 196640 | tf_op jit(solution)/shard_map/ppermute | solution.py:279
  49.1 0.7 products.4.held
  49.8 3.1 %collective-permute-start.8 = (bf16[192,512]{1,0:T(8,128)(2,1)S(1)}, bf16[192,512]{1,0:T(8,128)(2,1)S(1)}, u32[]{:S(2)}, u32[]{:S(2)}) collective-permute-start(bf16[192,512]{1,0:T(8,128)(2,1)S(1)} %get-tuple-element.32), channel_id=1, source_target_pairs={{0,2},{1,3},{2,0},{3,1},{4,6},{5,7},{6,4},{7,5},{8,10},{9,11},{10,... | collective-permute-start | bytes 589832 | tf_op jit(solution)/shard_map/ppermute | solution.py:25
  52.9 2.1 %collective-permute-done.9.refs_5_.refs_2_ = bf16[512,512]{1,0:T(8,128)(2,1)S(1)} collective-permute-done((bf16[512,512]{1,0:T(8,128)(2,1)S(1)}, bf16[512,512]{1,0:T(8,128)(2,1)S(1)}, u32[]{:S(2)}, u32[]{:S(2)}) %collective-permute-start.9) | collective-permute-done | bytes 524320 | tf_op jit(solution)/shard_map/ppermute | solution.py:25
  55.1 2.8 %products.6 = (bf16[192,512]{1,0:T(8,128)(2,1)}, bf16[192,512]{1,0:T(8,128)(2,1)}, bf16[192,512]{1,0:T(8,128)(2,1)}) custom-call(bf16[192,1024]{1,0:T(8,128)(2,1)S(1)} %copy-done.7, bf16[96,1024]{1,0:T(8,128)(2,1)S(1)} %collective-permute-done.3.refs_1_, bf16[96,1024]{1,0:T(8,128)(2,1)S(1)} %collective-permute-done.4.refs_2_, ...), custom_call_target="tpu_custom_call" | custom-call | flops 2415919104 | bytes 4718592 | tf_op jit(solution)/shard_map/products/pallas_call | solution.py:99
  57.8 1.3 %collective-permute-done.8.refs_0_ = bf16[192,512]{1,0:T(8,128)(2,1)S(1)} collective-permute-done((bf16[192,512]{1,0:T(8,128)(2,1)S(1)}, bf16[192,512]{1,0:T(8,128)(2,1)S(1)}, u32[]{:S(2)}, u32[]{:S(2)}) %collective-permute-start.8) | collective-permute-done | bytes 196640 | tf_op jit(solution)/shard_map/ppermute | solution.py:25
  59.6 1.6 %collective-permute-start.13 = (bf16[192,512]{1,0:T(8,128)(2,1)}, bf16[192,512]{1,0:T(8,128)(2,1)S(1)}, u32[]{:S(2)}, u32[]{:S(2)}) collective-permute-start(bf16[192,512]{1,0:T(8,128)(2,1)} %get-tuple-element.42), channel_id=1, source_target_pairs={{0,1},{1,0},{2,3},{3,2},{4,5},{5,4},{6,7},{7,6},{8,9},{9,8},{10,11... | collective-permute-start | bytes 589832 | tf_op jit(solution)/shard_map/ppermute | solution.py:25
  61.2 3.7 %collective-permute-start.14 = (bf16[192,512]{1,0:T(8,128)(2,1)}, bf16[192,512]{1,0:T(8,128)(2,1)S(1)}, u32[]{:S(2)}, u32[]{:S(2)}) collective-permute-start(bf16[192,512]{1,0:T(8,128)(2,1)} %get-tuple-element.43), channel_id=1, source_target_pairs={{0,2},{1,3},{2,0},{3,1},{4,6},{5,7},{6,4},{7,5},{8,10},{9,11},{10,... | collective-permute-start | bytes 589832 | tf_op jit(solution)/shard_map/ppermute | solution.py:25
  64.8 4.1 %collective-permute-done.10.refs_1_ = bf16[192,512]{1,0:T(8,128)(2,1)S(1)} collective-permute-done((bf16[192,512]{1,0:T(8,128)(2,1)S(1)}, bf16[192,512]{1,0:T(8,128)(2,1)S(1)}, u32[]{:S(2)}, u32[]{:S(2)}) %collective-permute-start.10) | collective-permute-done | bytes 196640 | tf_op jit(solution)/shard_map/ppermute | solution.py:25
  69.0 0.7 broadcast_select_fusion
  69.7 1.6 %collective-permute-start.12 = (bf16[192,512]{1,0:T(8,128)(2,1)}, bf16[192,512]{1,0:T(8,128)(2,1)S(1)}, u32[]{:S(2)}, u32[]{:S(2)}) collective-permute-start(bf16[192,512]{1,0:T(8,128)(2,1)} %broadcast_select_fusion), channel_id=1, source_target_pairs={{0,1},{1,2},{2,3},{3,4},{4,5},{5,6},{6,7},{7,0},{8,9},{9,10},{10,1... | collective-permute-start | bytes 589832 | tf_op jit(solution)/shard_map/ppermute | solution.py:25
  71.3 1.0 copy-done.5
  72.7 4.1 %collective-permute-done.15.refs_2_ = bf16[192,512]{1,0:T(8,128)(2,1)S(1)} collective-permute-done((bf16[192,512]{1,0:T(8,128)(2,1)}, bf16[192,512]{1,0:T(8,128)(2,1)S(1)}, u32[]{:S(2)}, u32[]{:S(2)}) %collective-permute-start.15) | collective-permute-done | bytes 196640 | tf_op jit(solution)/shard_map/ppermute | solution.py:25
  76.9 1.3 %collective-permute-start.16 = (bf16[192,512]{1,0:T(8,128)(2,1)S(1)}, bf16[192,512]{1,0:T(8,128)(2,1)S(1)}, u32[]{:S(2)}, u32[]{:S(2)}) collective-permute-start(bf16[192,512]{1,0:T(8,128)(2,1)S(1)} %value_sum.1.refs_3_), channel_id=1, source_target_pairs={{0,1},{1,2},{2,3},{3,4},{4,5},{5,6},{6,7},{7,0},{8,9},{9,10},{10,1... | collective-permute-start | bytes 589832 | tf_op jit(solution)/shard_map/ppermute | solution.py:25
  78.4 5.9 %collective-permute-done.12.refs_2_ = bf16[192,512]{1,0:T(8,128)(2,1)S(1)} collective-permute-done((bf16[192,512]{1,0:T(8,128)(2,1)}, bf16[192,512]{1,0:T(8,128)(2,1)S(1)}, u32[]{:S(2)}, u32[]{:S(2)}) %collective-permute-start.12) | collective-permute-done | bytes 196640 | tf_op jit(solution)/shard_map/ppermute | solution.py:25
  84.3 4.2 %collective-permute-done.11.refs_0_ = bf16[192,512]{1,0:T(8,128)(2,1)S(1)} collective-permute-done((bf16[192,512]{1,0:T(8,128)(2,1)S(1)}, bf16[192,512]{1,0:T(8,128)(2,1)S(1)}, u32[]{:S(2)}, u32[]{:S(2)}) %collective-permute-start.11) | collective-permute-done | bytes 196640 | tf_op jit(solution)/shard_map/ppermute | solution.py:25
  88.5 6.6 %scores.1 = (bf16[2,4,768,384]{3,2,1,0:T(8,128)(2,1)S(1)}, f32[2,4,96,128]{3,2,1,0:T(8,128)S(1)}, f32[2,32,96]{2,1,0:T(8,128)}) custom-call(s32[1]{0:T(128)} %bitcast.odd_ref, bf16[1,2,96,4096]{3,2,1,0:T(8,128)(2,1)S(1)} %copy-done.1, bf16[192,512]{1,0:T(8,128)(2,1)S(1)} %collective-permute-done.11.refs_0_, ...), custom_call_target="tpu_custom_call" | custom-call | flops 603979776 | bytes 8388608 | tf_op jit(solution)/shard_map/scores/pallas_call | solution.py:195
  95.2 7.5 %collective-permute-done.17.refs_0_ = bf16[192,512]{1,0:T(8,128)(2,1)S(1)} collective-permute-done((bf16[192,512]{1,0:T(8,128)(2,1)S(1)}, bf16[192,512]{1,0:T(8,128)(2,1)S(1)}, u32[]{:S(2)}, u32[]{:S(2)}) %collective-permute-start.17) | collective-permute-done | bytes 196640 | tf_op jit(solution)/shard_map/ppermute | solution.py:25
  102.6 2.4 %mixed_values.1 = bf16[1,2,96,4096]{3,2,1,0:T(8,128)(2,1)} custom-call(bf16[2,4,768,384]{3,2,1,0:T(8,128)(2,1)S(1)} %get-tuple-element.40.weights, f32[2,4,96,128]{3,2,1,0:T(8,128)S(1)} %get-tuple-element.41.sums, bf16[192,512]{1,0:T(8,128)(2,1)S(1)} %collective-permute-done.17.refs_0_, bf16[192,512]{1,0:T(8,128)(2,1)S(1)} %collective-permute-done.18.refs_1_, ...), custom_call_target="tpu_custom_call" | custom-call | flops 603979776 | bytes 8388608 | tf_op jit(solution)/shard_map/mixed_values/pallas_call | solution.py:240
  (58 shorter events, 2.2 us)
Async XLA Ops:
  0.6 6.4 %copy-start.9 = (s32[2,16]{1,0:T(2,128)S(1)}, s32[2,16]{1,0:T(2,128)}, u32[]{:S(2)}) copy-start(s32[2,16]{1,0:T(2,128)} %param.9) | copy-start | bytes 388
  0.6 6.9 %copy-start = (bf16[1,2,96,4096]{3,2,1,0:T(8,128)(2,1)S(1)}, bf16[1,2,96,4096]{3,2,1,0:T(8,128)(2,1)}, u32[]{:S(2)}) copy-start(bf16[1,2,96,4096]{3,2,1,0:T(8,128)(2,1)} %param.5) | copy-start | bytes 4718596
  0.7 6.9 %collective-permute-start = (bf16[1,4096]{1,0:T(2,128)(2,1)}, bf16[1,4096]{1,0:T(2,128)(2,1)S(1)}, u32[]{:S(2)}, u32[]{:S(2)}) collective-permute-start(bf16[1,4096]{1,0:T(2,128)(2,1)} %param.6), channel_id=1, source_target_pairs={{0,24},{8,0},{16,8},{24,16},{1,25},{9,1},{17,9},{25,17},{2,26},{10... | collective-permute-start | bytes 24584 | tf_op jit(solution)/shard_map/ppermute | solution.py:25
  4.3 25.7 %collective-permute-start.2 = (bf16[512,512]{1,0:T(8,128)(2,1)S(1)}, bf16[512,512]{1,0:T(8,128)(2,1)S(1)}, u32[]{:S(2)}, u32[]{:S(2)}) collective-permute-start(bf16[512,512]{1,0:T(8,128)(2,1)S(1)} %get-tuple-element.51.refs_3_.refs_2_), channel_id=1, source_target_pairs={{0,4},{1,5},{2,6},{3,7},{4,0},{5,1},{6,2},{7,3},{8,12},{9,13},{10,... | collective-permute-start | bytes 1572872 | tf_op jit(solution)/shard_map/ppermute | solution.py:25
  9.6 0.8 copy-start.8
  10.4 23.2 %collective-permute-start.5 = (bf16[192,1024]{1,0:T(8,128)(2,1)}, bf16[192,1024]{1,0:T(8,128)(2,1)S(1)}, u32[]{:S(2)}, u32[]{:S(2)}) collective-permute-start(bf16[192,1024]{1,0:T(8,128)(2,1)} %get-tuple-element.29), channel_id=1, source_target_pairs={{0,9},{1,8},{2,11},{3,10},{4,13},{5,12},{6,15},{7,14},{8,17},{9,16... | collective-permute-start | bytes 1179656 | tf_op jit(solution)/shard_map/ppermute | solution.py:279
  10.8 22.8 %collective-permute-start.6 = (bf16[192,1024]{1,0:T(8,128)(2,1)}, bf16[192,1024]{1,0:T(8,128)(2,1)}, u32[]{:S(2)}, u32[]{:S(2)}) collective-permute-start(bf16[192,1024]{1,0:T(8,128)(2,1)} %get-tuple-element.30), channel_id=1, source_target_pairs={{0,11},{1,10},{2,9},{3,8},{4,15},{5,14},{6,13},{7,12},{8,19},{9,18... | collective-permute-start | bytes 1179656 | tf_op jit(solution)/shard_map/ppermute | solution.py:279
  13.5 24.0 %collective-permute-start.1 = (bf16[192,1024]{1,0:T(8,128)(2,1)}, bf16[192,1024]{1,0:T(8,128)(2,1)S(1)}, u32[]{:S(2)}, u32[]{:S(2)}) collective-permute-start(bf16[192,1024]{1,0:T(8,128)(2,1)} %copy-done.8), channel_id=1, source_target_pairs={{0,8},{1,9},{2,10},{3,11},{4,12},{5,13},{6,14},{7,15},{8,16},{9,17... | collective-permute-start | bytes 1179656 | tf_op jit(solution)/shard_map/ppermute | solution.py:279
  30.0 25.1 %collective-permute-start.9 = (bf16[512,512]{1,0:T(8,128)(2,1)S(1)}, bf16[512,512]{1,0:T(8,128)(2,1)S(1)}, u32[]{:S(2)}, u32[]{:S(2)}) collective-permute-start(bf16[512,512]{1,0:T(8,128)(2,1)S(1)} %get-tuple-element.34.refs_4_.refs_1_), channel_id=1, source_target_pairs={{0,4},{1,5},{2,6},{3,7},{4,0},{5,1},{6,2},{7,3},{8,12},{9,13},{10,... | collective-permute-start | bytes 1572872 | tf_op jit(solution)/shard_map/ppermute | solution.py:25
  30.0 16.6 %collective-permute-start.4 = (bf16[96,1024]{1,0:T(8,128)(2,1)S(1)}, bf16[96,1024]{1,0:T(8,128)(2,1)S(1)}, u32[]{:S(2)}, u32[]{:S(2)}) collective-permute-start(bf16[96,1024]{1,0:T(8,128)(2,1)S(1)} %get-tuple-element.52), channel_id=1, source_target_pairs={{0,10},{1,11},{2,8},{3,9},{4,14},{5,15},{6,12},{7,13},{8,18},{9,19... | collective-permute-start | bytes 589832 | tf_op jit(solution)/shard_map/ppermute | solution.py:279
  33.6 1.7 %copy-start.6 = (bf16[192,1024]{1,0:T(8,128)(2,1)}, bf16[192,1024]{1,0:T(8,128)(2,1)S(1)}, u32[]{:S(2)}) copy-start(bf16[192,1024]{1,0:T(8,128)(2,1)S(1)} %collective-permute-done.5.refs_0_) | copy-start | bytes 1179652
  33.6 15.5 %collective-permute-start.3 = (bf16[96,1024]{1,0:T(8,128)(2,1)S(1)}, bf16[96,1024]{1,0:T(8,128)(2,1)S(1)}, u32[]{:S(2)}, u32[]{:S(2)}) collective-permute-start(bf16[96,1024]{1,0:T(8,128)(2,1)S(1)} %get-tuple-element.53), channel_id=1, source_target_pairs={{0,10},{1,11},{2,8},{3,9},{4,14},{5,15},{6,12},{7,13},{8,18},{9,19... | collective-permute-start | bytes 589832 | tf_op jit(solution)/shard_map/ppermute | solution.py:279
  35.3 14.4 %collective-permute-start.7 = (bf16[384,512]{1,0:T(8,128)(2,1)S(1)}, bf16[384,512]{1,0:T(8,128)(2,1)S(1)}, u32[]{:S(2)}, u32[]{:S(2)}) collective-permute-start(bf16[384,512]{1,0:T(8,128)(2,1)S(1)} %products.5), channel_id=1, source_target_pairs={{0,1},{1,0},{2,3},{3,2},{4,5},{5,4},{6,7},{7,6},{8,9},{9,8},{10,11... | collective-permute-start | bytes 1179656 | tf_op jit(solution)/shard_map/ppermute | solution.py:25
  37.5 17.6 %copy-start.7 = (bf16[192,1024]{1,0:T(8,128)(2,1)S(1)}, bf16[192,1024]{1,0:T(8,128)(2,1)}, u32[]{:S(2)}) copy-start(bf16[192,1024]{1,0:T(8,128)(2,1)} %copy-done.6) | copy-start | bytes 1179652
  37.5 12.2 %copy-start.4 = (bf16[192,1024]{1,0:T(8,128)(2,1)}, bf16[192,1024]{1,0:T(8,128)(2,1)S(1)}, u32[]{:S(2)}) copy-start(bf16[192,1024]{1,0:T(8,128)(2,1)S(1)} %collective-permute-done.1.refs_0_) | copy-start | bytes 1179652
  49.8 9.3 %collective-permute-start.8 = (bf16[192,512]{1,0:T(8,128)(2,1)S(1)}, bf16[192,512]{1,0:T(8,128)(2,1)S(1)}, u32[]{:S(2)}, u32[]{:S(2)}) collective-permute-start(bf16[192,512]{1,0:T(8,128)(2,1)S(1)} %get-tuple-element.32), channel_id=1, source_target_pairs={{0,2},{1,3},{2,0},{3,1},{4,6},{5,7},{6,4},{7,5},{8,10},{9,11},{10,... | collective-permute-start | bytes 589832 | tf_op jit(solution)/shard_map/ppermute | solution.py:25
  55.1 2.8 %copy-start.2 = (bf16[512,512]{1,0:T(8,128)(2,1)}, bf16[512,512]{1,0:T(8,128)(2,1)S(1)}, u32[]{:S(2)}) copy-start(bf16[512,512]{1,0:T(8,128)(2,1)S(1)} %collective-permute-done.9.refs_5_.refs_2_) | copy-start | bytes 1572868
  59.2 12.1 %copy-start.3 = (bf16[512,512]{1,0:T(8,128)(2,1)S(1)}, bf16[512,512]{1,0:T(8,128)(2,1)}, u32[]{:S(2)}) copy-start(bf16[512,512]{1,0:T(8,128)(2,1)} %copy-done.2) | copy-start | bytes 1572868
  59.4 9.6 %collective-permute-start.10 = (bf16[192,512]{1,0:T(8,128)(2,1)S(1)}, bf16[192,512]{1,0:T(8,128)(2,1)S(1)}, u32[]{:S(2)}, u32[]{:S(2)}) collective-permute-start(bf16[192,512]{1,0:T(8,128)(2,1)S(1)} %key_sum.1.refs_3_), channel_id=1, source_target_pairs={{0,2},{1,3},{2,4},{3,5},{4,6},{5,7},{6,0},{7,1},{8,10},{9,11},{10,... | collective-permute-start | bytes 589832 | tf_op jit(solution)/shard_map/ppermute | solution.py:25
  59.6 13.2 %collective-permute-start.13 = (bf16[192,512]{1,0:T(8,128)(2,1)}, bf16[192,512]{1,0:T(8,128)(2,1)S(1)}, u32[]{:S(2)}, u32[]{:S(2)}) collective-permute-start(bf16[192,512]{1,0:T(8,128)(2,1)} %get-tuple-element.42), channel_id=1, source_target_pairs={{0,1},{1,0},{2,3},{3,2},{4,5},{5,4},{6,7},{7,6},{8,9},{9,8},{10,11... | collective-permute-start | bytes 589832 | tf_op jit(solution)/shard_map/ppermute | solution.py:25
  61.2 11.5 %collective-permute-start.14 = (bf16[192,512]{1,0:T(8,128)(2,1)}, bf16[192,512]{1,0:T(8,128)(2,1)S(1)}, u32[]{:S(2)}, u32[]{:S(2)}) collective-permute-start(bf16[192,512]{1,0:T(8,128)(2,1)} %get-tuple-element.43), channel_id=1, source_target_pairs={{0,2},{1,3},{2,0},{3,1},{4,6},{5,7},{6,4},{7,5},{8,10},{9,11},{10,... | collective-permute-start | bytes 589832 | tf_op jit(solution)/shard_map/ppermute | solution.py:25
  64.8 12.0 %collective-permute-start.15 = (bf16[192,512]{1,0:T(8,128)(2,1)}, bf16[192,512]{1,0:T(8,128)(2,1)S(1)}, u32[]{:S(2)}, u32[]{:S(2)}) collective-permute-start(bf16[192,512]{1,0:T(8,128)(2,1)} %get-tuple-element.44), channel_id=1, source_target_pairs={{0,3},{1,2},{2,1},{3,0},{4,7},{5,6},{6,5},{7,4},{8,11},{9,10},{10,... | collective-permute-start | bytes 589832 | tf_op jit(solution)/shard_map/ppermute | solution.py:25
  69.7 18.9 %copy-start.1 = (bf16[1,2,96,4096]{3,2,1,0:T(8,128)(2,1)S(1)}, bf16[1,2,96,4096]{3,2,1,0:T(8,128)(2,1)}, u32[]{:S(2)}) copy-start(bf16[1,2,96,4096]{3,2,1,0:T(8,128)(2,1)} %q_ref.1) | copy-start | bytes 4718596
  69.7 14.7 %collective-permute-start.12 = (bf16[192,512]{1,0:T(8,128)(2,1)}, bf16[192,512]{1,0:T(8,128)(2,1)S(1)}, u32[]{:S(2)}, u32[]{:S(2)}) collective-permute-start(bf16[192,512]{1,0:T(8,128)(2,1)} %broadcast_select_fusion), channel_id=1, source_target_pairs={{0,1},{1,2},{2,3},{3,4},{4,5},{5,6},{6,7},{7,0},{8,9},{9,10},{10,1... | collective-permute-start | bytes 589832 | tf_op jit(solution)/shard_map/ppermute | solution.py:25
  71.3 17.2 %collective-permute-start.11 = (bf16[192,512]{1,0:T(8,128)(2,1)S(1)}, bf16[192,512]{1,0:T(8,128)(2,1)S(1)}, u32[]{:S(2)}, u32[]{:S(2)}) collective-permute-start(bf16[192,512]{1,0:T(8,128)(2,1)S(1)} %collective-permute-done.10.refs_1_), channel_id=1, source_target_pairs={{0,1},{1,0},{2,3},{3,2},{4,5},{5,4},{6,7},{7,6},{8,9},{9,8},{10,11... | collective-permute-start | bytes 589832 | tf_op jit(solution)/shard_map/ppermute | solution.py:25
  71.3 1.0 copy-start.5
  76.9 18.3 %collective-permute-start.16 = (bf16[192,512]{1,0:T(8,128)(2,1)S(1)}, bf16[192,512]{1,0:T(8,128)(2,1)S(1)}, u32[]{:S(2)}, u32[]{:S(2)}) collective-permute-start(bf16[192,512]{1,0:T(8,128)(2,1)S(1)} %value_sum.1.refs_3_), channel_id=1, source_target_pairs={{0,1},{1,2},{2,3},{3,4},{4,5},{5,6},{6,7},{7,0},{8,9},{9,10},{10,1... | collective-permute-start | bytes 589832 | tf_op jit(solution)/shard_map/ppermute | solution.py:25
  78.3 16.9 %collective-permute-start.18 = (bf16[192,512]{1,0:T(8,128)(2,1)S(1)}, bf16[192,512]{1,0:T(8,128)(2,1)S(1)}, u32[]{:S(2)}, u32[]{:S(2)}) collective-permute-start(bf16[192,512]{1,0:T(8,128)(2,1)S(1)} %value_sum.1.refs_3_), channel_id=1, source_target_pairs={{0,2},{1,3},{2,4},{3,5},{4,6},{5,7},{6,0},{7,1},{8,10},{9,11},{10,... | collective-permute-start | bytes 589832 | tf_op jit(solution)/shard_map/ppermute | solution.py:25
  95.2 7.5 %collective-permute-start.17 = (bf16[192,512]{1,0:T(8,128)(2,1)S(1)}, bf16[192,512]{1,0:T(8,128)(2,1)S(1)}, u32[]{:S(2)}, u32[]{:S(2)}) collective-permute-start(bf16[192,512]{1,0:T(8,128)(2,1)S(1)} %collective-permute-done.16.refs_2_), channel_id=1, source_target_pairs={{0,2},{1,3},{2,4},{3,5},{4,6},{5,7},{6,0},{7,1},{8,10},{9,11},{10,... | collective-permute-start | bytes 589832 | tf_op jit(solution)/shard_map/ppermute | solution.py:25

commit v12 on v11

--- a/solution.py
+++ b/solution.py
@@ -158,61 +158,63 @@
 
 def score_kernel(odd_ref, q_ref, *refs):
     key_refs, (row_pos, col_pos, weights, sums, log_sums) = refs[:WINDOW], refs[WINDOW:]
-    beside, two_back, before, own = [ref[...] for ref in key_refs]
+    beside, two_back, before, own = key_refs
     odd = odd_ref[0] == 1
-    one_back, three_back = jnp.where(odd, before, beside), jnp.where(odd, beside, before)
-    keys = jnp.concatenate([three_back, two_back, one_back, own], axis=0)
     tok_rows = q_ref.shape[2]
     visible = col_pos[0] <= row_pos[0]
     lane = lax.broadcasted_iota(jnp.int32, (tok_rows, LANES), 1)
-    all_sums = jnp.ones((tok_rows, LANES), jnp.float32)
-    all_max = jnp.zeros((tok_rows, LANES), jnp.float32)
-    for h in range(GROUP):
-        dots = lax.dot_general(
-            q_ref[0, 0, :, h * HD : (h + 1) * HD],
-            keys,
-            (((1,), (1,)), ((), ())),
-            preferred_element_type=jnp.float32,
-        )
-        dots = jnp.where(visible, dots, -jnp.inf)
-        row_max = jnp.max(dots, axis=-1, keepdims=True)
-        exps = jnp.exp2((dots - row_max) * (SCALE * LOG2_E))
-        running = jnp.sum(exps, axis=-1, keepdims=True)
-        weights[0, 0, h * tok_rows : (h + 1) * tok_rows, :] = exps.astype(jnp.bfloat16)
-        all_sums = jnp.where(lane == h, running, all_sums)
-        all_max = jnp.where(lane == h, row_max, all_max)
-    sums[0, 0] = all_sums
-    log_sums[0] = jnp.transpose(all_max * SCALE + jnp.log(all_sums))[:GROUP]
-
-
-def window_specs(tok_rows):
-    return [pl.BlockSpec((tok_rows, HD), lambda m, k: (m, k))] * WINDOW
+    for k in range(KVH):
+        cols = slice(k * HD, (k + 1) * HD)
+        one_back = jnp.where(odd, before[:, cols], beside[:, cols])
+        three_back = jnp.where(odd, beside[:, cols], before[:, cols])
+        keys = jnp.concatenate([three_back, two_back[:, cols], one_back, own[:, cols]], axis=0)
+        all_sums = jnp.ones((tok_rows, LANES), jnp.float32)
+        all_max = jnp.zeros((tok_rows, LANES), jnp.float32)
+        for h in range(GROUP):
+            head = k * GROUP + h
+            dots = lax.dot_general(
+                q_ref[0, 0, :, head * HD : (head + 1) * HD],
+                keys,
+                (((1,), (1,)), ((), ())),
+                preferred_element_type=jnp.float32,
+            )
+            dots = jnp.where(visible, dots, -jnp.inf)
+            row_max = jnp.max(dots, axis=-1, keepdims=True)
+            exps = jnp.exp2((dots - row_max) * (SCALE * LOG2_E))
+            running = jnp.sum(exps, axis=-1, keepdims=True)
+            weights[0, k, h * tok_rows : (h + 1) * tok_rows, :] = exps.astype(jnp.bfloat16)
+            all_sums = jnp.where(lane == h, running, all_sums)
+            all_max = jnp.where(lane == h, row_max, all_max)
+        sums[0, k] = all_sums
+        log_sums[0, k * GROUP : (k + 1) * GROUP, :] = jnp.transpose(
+            all_max * SCALE + jnp.log(all_sums)
+        )[:GROUP]
 
 
 def scored(odd, queries, window, row_pos, col_pos):
-    _, micro_count, tok_rows, _ = queries.shape
+    _, micro_count, tok_rows, width = queries.shape
     keys = WINDOW * tok_rows
     return pl.pallas_call(
         score_kernel,
-        grid=(micro_count, KVH),
+        grid=(micro_count,),
         in_specs=[
             pl.BlockSpec(memory_space=pltpu.SMEM),
-            pl.BlockSpec((1, 1, tok_rows, GROUP * HD), lambda m, k: (0, m, 0, k)),
-            *window_specs(tok_rows),
-            pl.BlockSpec((1, tok_rows, 1), lambda m, k: (m, 0, 0)),
-            pl.BlockSpec((1, 1, keys), lambda m, k: (m, 0, 0)),
+            pl.BlockSpec((1, 1, tok_rows, width), lambda m: (0, m, 0, 0)),
+            *[pl.BlockSpec((tok_rows, KVH * HD), lambda m: (m, 0))] * WINDOW,
+            pl.BlockSpec((1, tok_rows, 1), lambda m: (m, 0, 0)),
+            pl.BlockSpec((1, 1, keys), lambda m: (m, 0, 0)),
         ],
         out_specs=[
-            pl.BlockSpec((1, 1, GROUP * tok_rows, keys), lambda m, k: (m, k, 0, 0)),
-            pl.BlockSpec((1, 1, tok_rows, LANES), lambda m, k: (m, k, 0, 0)),
-            pl.BlockSpec((1, GROUP, tok_rows), lambda m, k: (m, k, 0)),
+            pl.BlockSpec((1, KVH, GROUP * tok_rows, keys), lambda m: (m, 0, 0, 0)),
+            pl.BlockSpec((1, KVH, tok_rows, LANES), lambda m: (m, 0, 0, 0)),
+            pl.BlockSpec((1, QH, tok_rows), lambda m: (m, 0, 0)),
         ],
         out_shape=[
             jax.ShapeDtypeStruct((micro_count, KVH, GROUP * tok_rows, keys), jnp.bfloat16),
             jax.ShapeDtypeStruct((micro_count, KVH, tok_rows, LANES), jnp.float32),
             jax.ShapeDtypeStruct((micro_count, QH, tok_rows), jnp.float32),
         ],
-        compiler_params=params(24),
+        compiler_params=params(32),
         cost_estimate=cost(2 * micro_count * QH * tok_rows * keys * HD, 8 * 2**20),
         name="scores",
     )(odd, queries, *window, row_pos, col_pos)
@@ -306,9 +308,8 @@
         onward = jnp.where(odd == 1, two_back, block)
         return [beside, two_back, moved(onward, "ctx", lambda i: i + 1), block]
 
-    def value_window_of(block, weights):
+    def value_window_of(block):
         one_back, two_back = [moved(block, "ctx", lambda i, d=d: i + d) for d in (1, 2)]
-        one_back, _ = lax.optimization_barrier((one_back, weights))
         return [moved(one_back, "ctx", lambda i: i + 2), two_back, one_back, block]
 
     span_len = tok_rows // 2
@@ -354,7 +355,7 @@
         col_pos[:, None, :],
     )
     value_block = block_sum(value_sum_kernel, "value_sum", own_values, value_parts)
-    out = mixed_values(weights, sums, value_window_of(value_block, weights))
+    out = mixed_values(weights, sums, value_window_of(value_block))
     return (out, log_sums[None])
 
 

time: 105 us -> 101 us (0.962)
  Pallas kernels: 17 us -> 14.7 us
  waiting for transfers between devices: 57.2 us -> 55.4 us
  starting transfers between devices: 24.9 us -> 26 us
    pallas_call x1, Pallas kernels: 6.65 us -> 4.75 us  [scored(): pl.pallas_call(score_kernel, grid=(micro_count,), in_specs=[pl.BlockSpec(...]
    ppermute x14, waiting for transfers between devices: 45.7 us -> 43.8 us  [moved(): lax.ppermute(block, axis, [(i, target(i) % size) for i in range(size)])]
    ppermute x14, starting transfers between devices: 18.3 us -> 19.4 us  [moved(): lax.ppermute(block, axis, [(i, target(i) % size) for i in range(size)])]
  transfers between devices with their start and end apart: 19 -> 19, of which waited for: 10 -> 11; matrix products, arithmetic and copies ran while one was open for 3% -> 3% of each run, Pallas kernels for 14% -> 12%
where the time goes in v12:
time: 101 us; the launch traced here: 100 us
  waiting for transfers between devices  55.4 us (55%)
  starting transfers between devices  26 us (26%)
  Pallas kernels  14.7 us (15%)
  local copies, waits for them, and re-layouts  2.59 us (3%)
    ppermute x14, waiting for transfers between devices, moved(): lax.ppermute(block, axis, [(i, target(i) % size) for i in range(size)])  43.8 us
    ppermute x14, starting transfers between devices, moved(): lax.ppermute(block, axis, [(i, target(i) % size) for i in range(size)])  19.4 us
    ppermute x5, waiting for transfers between devices, to_next_section(): return lax.ppermute(part, ('section', 'ctx'), route)  11.6 us
    ppermute x5, starting transfers between devices, to_next_section(): return lax.ppermute(part, ('section', 'ctx'), route)  6.64 us
    pallas_call x4, Pallas kernels, products(): pl.pallas_call(lambda *refs: product_kernel(counts, *refs), out_shape=[ja...  5.1 us
    pallas_call x1, Pallas kernels, scored(): pl.pallas_call(score_kernel, grid=(micro_count,), in_specs=[pl.BlockSpec(...  4.75 us
    pallas_call x1, Pallas kernels, mixed_values(): pl.pallas_call(mix_kernel, grid=(micro_count,), in_specs=[pl.BlockSpec((1...  2.5 us
    pallas_call x1, Pallas kernels, normed_cuts(): pl.pallas_call(norm_kernel, grid=(micro_count,), in_specs=[pl.BlockSpec(m...  2.08 us
  transfers between devices with their start and end apart: 19, of which 11 were waited for; matrix products, arithmetic and copies ran while one was open for 3% of the time, Pallas kernels for 12%

profile of v12, /device:TPU:0, one launch (start us, length us, event | category | flops | bytes accessed | tf_op | source)
XLA Modules:
  0.0 100.4 jit_solution(2278223061382882648)
XLA Ops:
  0.7 2.4 %collective-permute-start = (bf16[1,4096]{1,0:T(2,128)(2,1)}, bf16[1,4096]{1,0:T(2,128)(2,1)S(1)}, u32[]{:S(2)}, u32[]{:S(2)}) collective-permute-start(bf16[1,4096]{1,0:T(2,128)(2,1)} %param.6), channel_id=1, source_target_pairs={{0,24},{8,0},{16,8},{24,16},{1,25},{9,1},{17,9},{25,17},{2,26},{10... | collective-permute-start | bytes 24584 | tf_op jit(solution)/shard_map/ppermute | solution.py:25
  3.1 1.3 %fusion.4 = (bf16[512,512]{1,0:T(8,128)(2,1)S(1)}, bf16[512,512]{1,0:T(8,128)(2,1)S(1)}) fusion(bf16[512,1024]{1,0:T(8,128)(2,1)} %bitcast.7), kind=kLoop, calls=%fused_computation.21 | loop fusion | bytes 2097152 | tf_op jit(solution)/shard_map/slice | solution.py:289
  4.3 2.7 %collective-permute-start.2 = (bf16[512,512]{1,0:T(8,128)(2,1)S(1)}, bf16[512,512]{1,0:T(8,128)(2,1)S(1)}, u32[]{:S(2)}, u32[]{:S(2)}) collective-permute-start(bf16[512,512]{1,0:T(8,128)(2,1)S(1)} %get-tuple-element.49.refs_3_.refs_2_), channel_id=1, source_target_pairs={{0,4},{1,5},{2,6},{3,7},{4,0},{5,1},{6,2},{7,3},{8,12},{9,13},{10,... | collective-permute-start | bytes 1572872 | tf_op jit(solution)/shard_map/ppermute | solution.py:25
  7.6 2.1 %norm_cuts.1 = (bf16[192,1024]{1,0:T(8,128)(2,1)S(1)}, bf16[192,1024]{1,0:T(8,128)(2,1)}, bf16[192,1024]{1,0:T(8,128)(2,1)S(1)}, bf16[192,1024]{1,0:T(8,128)(2,1)}) custom-call(s32[4,2]{1,0:T(4,128)S(1)} %add_multiply_fusion.starts_ref, bf16[2,96,4096]{2,1,0:T(8,128)(2,1)S(1)} %bitcast.6, f32[1,4096]{1,0:T(1,128)S(1)} %convert_element_type.16.gain_ref), custom_call_target="tpu_custom_call" | custom-call | flops 4718592 | bytes 3145728 | tf_op jit(solution)/shard_map/norm_cuts/pallas_call | solution.py:58
  9.7 0.8 copy-done.4
  10.4 0.4 collective-permute-start.5
  10.8 2.5 %collective-permute-start.6 = (bf16[192,1024]{1,0:T(8,128)(2,1)}, bf16[192,1024]{1,0:T(8,128)(2,1)}, u32[]{:S(2)}, u32[]{:S(2)}) collective-permute-start(bf16[192,1024]{1,0:T(8,128)(2,1)} %get-tuple-element.29), channel_id=1, source_target_pairs={{0,11},{1,10},{2,9},{3,8},{4,15},{5,14},{6,13},{7,12},{8,19},{9,18... | collective-permute-start | bytes 1179656 | tf_op jit(solution)/shard_map/ppermute | solution.py:281
  13.6 16.4 %collective-permute-done.2.refs_4_.refs_3_ = bf16[512,512]{1,0:T(8,128)(2,1)S(1)} collective-permute-done((bf16[512,512]{1,0:T(8,128)(2,1)S(1)}, bf16[512,512]{1,0:T(8,128)(2,1)S(1)}, u32[]{:S(2)}, u32[]{:S(2)}) %collective-permute-start.2) | collective-permute-done | bytes 524320 | tf_op jit(solution)/shard_map/ppermute | solution.py:25
  30.0 3.5 %collective-permute-start.4 = (bf16[96,1024]{1,0:T(8,128)(2,1)S(1)}, bf16[96,1024]{1,0:T(8,128)(2,1)S(1)}, u32[]{:S(2)}, u32[]{:S(2)}) collective-permute-start(bf16[96,1024]{1,0:T(8,128)(2,1)S(1)} %get-tuple-element.50), channel_id=1, source_target_pairs={{0,10},{1,11},{2,8},{3,9},{4,14},{5,15},{6,12},{7,13},{8,18},{9,19... | collective-permute-start | bytes 589832 | tf_op jit(solution)/shard_map/ppermute | solution.py:281
  33.7 1.6 %products.5 = bf16[384,512]{1,0:T(8,128)(2,1)S(1)} custom-call(bf16[192,1024]{1,0:T(8,128)(2,1)S(1)} %collective-permute-done.5.refs_0_, bf16[192,1024]{1,0:T(8,128)(2,1)} %collective-permute-done.6.refs_1_.refs_3_, bf16[512,512]{1,0:T(8,128)(2,1)S(1)} %get-tuple-element.49.refs_3_.refs_2_, bf16[512,512]{1,0:T(8,128)(2,1)S(1)} %collective-permute-done.2.refs_4_.refs_3_), custom_call_target="tpu_custom_call" | custom-call | flops 1610612736 | bytes 3145728 | tf_op jit(solution)/shard_map/products/pallas_call | solution.py:99
  35.3 1.6 %collective-permute-start.7 = (bf16[384,512]{1,0:T(8,128)(2,1)S(1)}, bf16[384,512]{1,0:T(8,128)(2,1)S(1)}, u32[]{:S(2)}, u32[]{:S(2)}) collective-permute-start(bf16[384,512]{1,0:T(8,128)(2,1)S(1)} %products.5), channel_id=1, source_target_pairs={{0,1},{1,0},{2,3},{3,2},{4,5},{5,4},{6,7},{7,6},{8,9},{9,8},{10,11... | collective-permute-start | bytes 1179656 | tf_op jit(solution)/shard_map/ppermute | solution.py:25
  36.9 0.4 fusion
  37.5 9.1 %collective-permute-done.4.refs_2_ = bf16[96,1024]{1,0:T(8,128)(2,1)S(1)} collective-permute-done((bf16[96,1024]{1,0:T(8,128)(2,1)S(1)}, bf16[96,1024]{1,0:T(8,128)(2,1)S(1)}, u32[]{:S(2)}, u32[]{:S(2)}) %collective-permute-start.4) | collective-permute-done | bytes 196640 | tf_op jit(solution)/shard_map/ppermute | solution.py:281
  46.6 2.4 %collective-permute-done.3.refs_1_ = bf16[96,1024]{1,0:T(8,128)(2,1)S(1)} collective-permute-done((bf16[96,1024]{1,0:T(8,128)(2,1)S(1)}, bf16[96,1024]{1,0:T(8,128)(2,1)S(1)}, u32[]{:S(2)}, u32[]{:S(2)}) %collective-permute-start.3) | collective-permute-done | bytes 196640 | tf_op jit(solution)/shard_map/ppermute | solution.py:281
  49.1 0.7 products.4.held
  49.8 3.1 %collective-permute-start.8 = (bf16[192,512]{1,0:T(8,128)(2,1)S(1)}, bf16[192,512]{1,0:T(8,128)(2,1)S(1)}, u32[]{:S(2)}, u32[]{:S(2)}) collective-permute-start(bf16[192,512]{1,0:T(8,128)(2,1)S(1)} %get-tuple-element.31), channel_id=1, source_target_pairs={{0,2},{1,3},{2,0},{3,1},{4,6},{5,7},{6,4},{7,5},{8,10},{9,11},{10,... | collective-permute-start | bytes 589832 | tf_op jit(solution)/shard_map/ppermute | solution.py:25
  52.9 2.1 %collective-permute-done.9.refs_5_.refs_2_ = bf16[512,512]{1,0:T(8,128)(2,1)S(1)} collective-permute-done((bf16[512,512]{1,0:T(8,128)(2,1)S(1)}, bf16[512,512]{1,0:T(8,128)(2,1)S(1)}, u32[]{:S(2)}, u32[]{:S(2)}) %collective-permute-start.9) | collective-permute-done | bytes 524320 | tf_op jit(solution)/shard_map/ppermute | solution.py:25
  55.1 2.4 %products.6 = (bf16[192,512]{1,0:T(8,128)(2,1)}, bf16[192,512]{1,0:T(8,128)(2,1)S(1)}, bf16[192,512]{1,0:T(8,128)(2,1)S(1)}) custom-call(bf16[192,1024]{1,0:T(8,128)(2,1)S(1)} %copy-done.3, bf16[96,1024]{1,0:T(8,128)(2,1)S(1)} %collective-permute-done.3.refs_1_, bf16[96,1024]{1,0:T(8,128)(2,1)S(1)} %collective-permute-done.4.refs_2_, ...), custom_call_target="tpu_custom_call" | custom-call | flops 2415919104 | bytes 4718592 | tf_op jit(solution)/shard_map/products/pallas_call | solution.py:99
  57.4 1.7 %collective-permute-done.8.refs_0_ = bf16[192,512]{1,0:T(8,128)(2,1)S(1)} collective-permute-done((bf16[192,512]{1,0:T(8,128)(2,1)S(1)}, bf16[192,512]{1,0:T(8,128)(2,1)S(1)}, u32[]{:S(2)}, u32[]{:S(2)}) %collective-permute-start.8) | collective-permute-done | bytes 196640 | tf_op jit(solution)/shard_map/ppermute | solution.py:25
  59.5 1.6 %collective-permute-start.13 = (bf16[192,512]{1,0:T(8,128)(2,1)}, bf16[192,512]{1,0:T(8,128)(2,1)S(1)}, u32[]{:S(2)}, u32[]{:S(2)}) collective-permute-start(bf16[192,512]{1,0:T(8,128)(2,1)} %get-tuple-element.41), channel_id=1, source_target_pairs={{0,1},{1,0},{2,3},{3,2},{4,5},{5,4},{6,7},{7,6},{8,9},{9,8},{10,11... | collective-permute-start | bytes 589832 | tf_op jit(solution)/shard_map/ppermute | solution.py:25
  61.2 3.7 %collective-permute-start.14 = (bf16[192,512]{1,0:T(8,128)(2,1)S(1)}, bf16[192,512]{1,0:T(8,128)(2,1)S(1)}, u32[]{:S(2)}, u32[]{:S(2)}) collective-permute-start(bf16[192,512]{1,0:T(8,128)(2,1)S(1)} %get-tuple-element.42), channel_id=1, source_target_pairs={{0,2},{1,3},{2,0},{3,1},{4,6},{5,7},{6,4},{7,5},{8,10},{9,11},{10,... | collective-permute-start | bytes 589832 | tf_op jit(solution)/shard_map/ppermute | solution.py:25
  64.8 0.4 products.7.own
  65.2 3.7 %collective-permute-done.10.refs_1_ = bf16[192,512]{1,0:T(8,128)(2,1)S(1)} collective-permute-done((bf16[192,512]{1,0:T(8,128)(2,1)S(1)}, bf16[192,512]{1,0:T(8,128)(2,1)S(1)}, u32[]{:S(2)}, u32[]{:S(2)}) %collective-permute-start.10) | collective-permute-done | bytes 196640 | tf_op jit(solution)/shard_map/ppermute | solution.py:25
  69.0 3.4 %collective-permute-done.14.refs_1_ = bf16[192,512]{1,0:T(8,128)(2,1)S(1)} collective-permute-done((bf16[192,512]{1,0:T(8,128)(2,1)S(1)}, bf16[192,512]{1,0:T(8,128)(2,1)S(1)}, u32[]{:S(2)}, u32[]{:S(2)}) %collective-permute-start.14) | collective-permute-done | bytes 196640 | tf_op jit(solution)/shard_map/ppermute | solution.py:25
  72.3 4.1 %collective-permute-done.15.refs_2_ = bf16[192,512]{1,0:T(8,128)(2,1)S(1)} collective-permute-done((bf16[192,512]{1,0:T(8,128)(2,1)S(1)}, bf16[192,512]{1,0:T(8,128)(2,1)S(1)}, u32[]{:S(2)}, u32[]{:S(2)}) %collective-permute-start.15) | collective-permute-done | bytes 196640 | tf_op jit(solution)/shard_map/ppermute | solution.py:25
  76.6 1.5 %collective-permute-start.16 = (bf16[192,512]{1,0:T(8,128)(2,1)S(1)}, bf16[192,512]{1,0:T(8,128)(2,1)S(1)}, u32[]{:S(2)}, u32[]{:S(2)}) collective-permute-start(bf16[192,512]{1,0:T(8,128)(2,1)S(1)} %value_sum.1.refs_3_), channel_id=1, source_target_pairs={{0,1},{1,2},{2,3},{3,4},{4,5},{5,6},{6,7},{7,0},{8,9},{9,10},{10,1... | collective-permute-start | bytes 589832 | tf_op jit(solution)/shard_map/ppermute | solution.py:25
  78.3 2.5 %collective-permute-start.18 = (bf16[192,512]{1,0:T(8,128)(2,1)S(1)}, bf16[192,512]{1,0:T(8,128)(2,1)S(1)}, u32[]{:S(2)}, u32[]{:S(2)}) collective-permute-start(bf16[192,512]{1,0:T(8,128)(2,1)S(1)} %value_sum.1.refs_3_), channel_id=1, source_target_pairs={{0,2},{1,3},{2,4},{3,5},{4,6},{5,7},{6,0},{7,1},{8,10},{9,11},{10,... | collective-permute-start | bytes 589832 | tf_op jit(solution)/shard_map/ppermute | solution.py:25
  80.7 6.3 %collective-permute-done.16.refs_2_ = bf16[192,512]{1,0:T(8,128)(2,1)S(1)} collective-permute-done((bf16[192,512]{1,0:T(8,128)(2,1)S(1)}, bf16[192,512]{1,0:T(8,128)(2,1)S(1)}, u32[]{:S(2)}, u32[]{:S(2)}) %collective-permute-start.16) | collective-permute-done | bytes 196640 | tf_op jit(solution)/shard_map/ppermute | solution.py:25
  87.1 4.0 %collective-permute-done.12.refs_2_ = bf16[192,512]{1,0:T(8,128)(2,1)S(1)} collective-permute-done((bf16[192,512]{1,0:T(8,128)(2,1)S(1)}, bf16[192,512]{1,0:T(8,128)(2,1)S(1)}, u32[]{:S(2)}, u32[]{:S(2)}) %collective-permute-start.12) | collective-permute-done | bytes 196640 | tf_op jit(solution)/shard_map/ppermute | solution.py:25
  91.1 2.0 %collective-permute-done.11.refs_0_ = bf16[192,512]{1,0:T(8,128)(2,1)S(1)} collective-permute-done((bf16[192,512]{1,0:T(8,128)(2,1)S(1)}, bf16[192,512]{1,0:T(8,128)(2,1)S(1)}, u32[]{:S(2)}, u32[]{:S(2)}) %collective-permute-start.11) | collective-permute-done | bytes 196640 | tf_op jit(solution)/shard_map/ppermute | solution.py:25
  93.2 4.7 %scores.1 = (bf16[2,4,768,384]{3,2,1,0:T(8,128)(2,1)S(1)}, f32[2,4,96,128]{3,2,1,0:T(8,128)S(1)}, f32[2,32,96]{2,1,0:T(8,128)}) custom-call(s32[1]{0:T(128)} %bitcast.odd_ref, bf16[1,2,96,4096]{3,2,1,0:T(8,128)(2,1)S(1)} %copy-done.1, bf16[192,512]{1,0:T(8,128)(2,1)S(1)} %collective-permute-done.11.refs_0_, ...), custom_call_target="tpu_custom_call" | custom-call | flops 603979776 | bytes 8388608 | tf_op jit(solution)/shard_map/scores/pallas_call | solution.py:197
  97.9 2.5 %mixed_values.1 = bf16[1,2,96,4096]{3,2,1,0:T(8,128)(2,1)} custom-call(bf16[2,4,768,384]{3,2,1,0:T(8,128)(2,1)S(1)} %get-tuple-element.39.weights, f32[2,4,96,128]{3,2,1,0:T(8,128)S(1)} %get-tuple-element.40.sums, bf16[192,512]{1,0:T(8,128)(2,1)S(1)} %collective-permute-done.17.refs_0_, bf16[192,512]{1,0:T(8,128)(2,1)S(1)} %collective-permute-done.18.refs_1_, ...), custom_call_target="tpu_custom_call" | custom-call | flops 603979776 | bytes 8388608 | tf_op jit(solution)/shard_map/mixed_values/pallas_call | solution.py:242
  (50 shorter events, 1.9 us)
Async XLA Ops:
  0.6 6.4 %copy-start.5 = (s32[2,16]{1,0:T(2,128)S(1)}, s32[2,16]{1,0:T(2,128)}, u32[]{:S(2)}) copy-start(s32[2,16]{1,0:T(2,128)} %param.9) | copy-start | bytes 388
  0.6 6.9 %copy-start = (bf16[1,2,96,4096]{3,2,1,0:T(8,128)(2,1)S(1)}, bf16[1,2,96,4096]{3,2,1,0:T(8,128)(2,1)}, u32[]{:S(2)}) copy-start(bf16[1,2,96,4096]{3,2,1,0:T(8,128)(2,1)} %param.5) | copy-start | bytes 4718596
  0.7 6.9 %collective-permute-start = (bf16[1,4096]{1,0:T(2,128)(2,1)}, bf16[1,4096]{1,0:T(2,128)(2,1)S(1)}, u32[]{:S(2)}, u32[]{:S(2)}) collective-permute-start(bf16[1,4096]{1,0:T(2,128)(2,1)} %param.6), channel_id=1, source_target_pairs={{0,24},{8,0},{16,8},{24,16},{1,25},{9,1},{17,9},{25,17},{2,26},{10... | collective-permute-start | bytes 24584 | tf_op jit(solution)/shard_map/ppermute | solution.py:25
  4.3 25.7 %collective-permute-start.2 = (bf16[512,512]{1,0:T(8,128)(2,1)S(1)}, bf16[512,512]{1,0:T(8,128)(2,1)S(1)}, u32[]{:S(2)}, u32[]{:S(2)}) collective-permute-start(bf16[512,512]{1,0:T(8,128)(2,1)S(1)} %get-tuple-element.49.refs_3_.refs_2_), channel_id=1, source_target_pairs={{0,4},{1,5},{2,6},{3,7},{4,0},{5,1},{6,2},{7,3},{8,12},{9,13},{10,... | collective-permute-start | bytes 1572872 | tf_op jit(solution)/shard_map/ppermute | solution.py:25
  9.7 0.8 copy-start.4
  10.4 23.2 %collective-permute-start.5 = (bf16[192,1024]{1,0:T(8,128)(2,1)}, bf16[192,1024]{1,0:T(8,128)(2,1)S(1)}, u32[]{:S(2)}, u32[]{:S(2)}) collective-permute-start(bf16[192,1024]{1,0:T(8,128)(2,1)} %get-tuple-element.28), channel_id=1, source_target_pairs={{0,9},{1,8},{2,11},{3,10},{4,13},{5,12},{6,15},{7,14},{8,17},{9,16... | collective-permute-start | bytes 1179656 | tf_op jit(solution)/shard_map/ppermute | solution.py:281
  10.8 22.8 %collective-permute-start.6 = (bf16[192,1024]{1,0:T(8,128)(2,1)}, bf16[192,1024]{1,0:T(8,128)(2,1)}, u32[]{:S(2)}, u32[]{:S(2)}) collective-permute-start(bf16[192,1024]{1,0:T(8,128)(2,1)} %get-tuple-element.29), channel_id=1, source_target_pairs={{0,11},{1,10},{2,9},{3,8},{4,15},{5,14},{6,13},{7,12},{8,19},{9,18... | collective-permute-start | bytes 1179656 | tf_op jit(solution)/shard_map/ppermute | solution.py:281
  13.5 24.0 %collective-permute-start.1 = (bf16[192,1024]{1,0:T(8,128)(2,1)}, bf16[192,1024]{1,0:T(8,128)(2,1)S(1)}, u32[]{:S(2)}, u32[]{:S(2)}) collective-permute-start(bf16[192,1024]{1,0:T(8,128)(2,1)} %copy-done.4), channel_id=1, source_target_pairs={{0,8},{1,9},{2,10},{3,11},{4,12},{5,13},{6,14},{7,15},{8,16},{9,17... | collective-permute-start | bytes 1179656 | tf_op jit(solution)/shard_map/ppermute | solution.py:281
  30.0 25.1 %collective-permute-start.9 = (bf16[512,512]{1,0:T(8,128)(2,1)S(1)}, bf16[512,512]{1,0:T(8,128)(2,1)S(1)}, u32[]{:S(2)}, u32[]{:S(2)}) collective-permute-start(bf16[512,512]{1,0:T(8,128)(2,1)S(1)} %get-tuple-element.33.refs_4_.refs_1_), channel_id=1, source_target_pairs={{0,4},{1,5},{2,6},{3,7},{4,0},{5,1},{6,2},{7,3},{8,12},{9,13},{10,... | collective-permute-start | bytes 1572872 | tf_op jit(solution)/shard_map/ppermute | solution.py:25
  30.0 16.6 %collective-permute-start.4 = (bf16[96,1024]{1,0:T(8,128)(2,1)S(1)}, bf16[96,1024]{1,0:T(8,128)(2,1)S(1)}, u32[]{:S(2)}, u32[]{:S(2)}) collective-permute-start(bf16[96,1024]{1,0:T(8,128)(2,1)S(1)} %get-tuple-element.50), channel_id=1, source_target_pairs={{0,10},{1,11},{2,8},{3,9},{4,14},{5,15},{6,12},{7,13},{8,18},{9,19... | collective-permute-start | bytes 589832 | tf_op jit(solution)/shard_map/ppermute | solution.py:281
  33.6 1.7 %copy-start.2 = (bf16[192,1024]{1,0:T(8,128)(2,1)}, bf16[192,1024]{1,0:T(8,128)(2,1)S(1)}, u32[]{:S(2)}) copy-start(bf16[192,1024]{1,0:T(8,128)(2,1)S(1)} %collective-permute-done.5.refs_0_) | copy-start | bytes 1179652
  33.6 15.5 %collective-permute-start.3 = (bf16[96,1024]{1,0:T(8,128)(2,1)S(1)}, bf16[96,1024]{1,0:T(8,128)(2,1)S(1)}, u32[]{:S(2)}, u32[]{:S(2)}) collective-permute-start(bf16[96,1024]{1,0:T(8,128)(2,1)S(1)} %get-tuple-element.51), channel_id=1, source_target_pairs={{0,10},{1,11},{2,8},{3,9},{4,14},{5,15},{6,12},{7,13},{8,18},{9,19... | collective-permute-start | bytes 589832 | tf_op jit(solution)/shard_map/ppermute | solution.py:281
  35.3 14.4 %collective-permute-start.7 = (bf16[384,512]{1,0:T(8,128)(2,1)S(1)}, bf16[384,512]{1,0:T(8,128)(2,1)S(1)}, u32[]{:S(2)}, u32[]{:S(2)}) collective-permute-start(bf16[384,512]{1,0:T(8,128)(2,1)S(1)} %products.5), channel_id=1, source_target_pairs={{0,1},{1,0},{2,3},{3,2},{4,5},{5,4},{6,7},{7,6},{8,9},{9,8},{10,11... | collective-permute-start | bytes 1179656 | tf_op jit(solution)/shard_map/ppermute | solution.py:25
  37.5 17.6 %copy-start.3 = (bf16[192,1024]{1,0:T(8,128)(2,1)S(1)}, bf16[192,1024]{1,0:T(8,128)(2,1)}, u32[]{:S(2)}) copy-start(bf16[192,1024]{1,0:T(8,128)(2,1)} %copy-done.2) | copy-start | bytes 1179652
  49.8 9.3 %collective-permute-start.8 = (bf16[192,512]{1,0:T(8,128)(2,1)S(1)}, bf16[192,512]{1,0:T(8,128)(2,1)S(1)}, u32[]{:S(2)}, u32[]{:S(2)}) collective-permute-start(bf16[192,512]{1,0:T(8,128)(2,1)S(1)} %get-tuple-element.31), channel_id=1, source_target_pairs={{0,2},{1,3},{2,0},{3,1},{4,6},{5,7},{6,4},{7,5},{8,10},{9,11},{10,... | collective-permute-start | bytes 589832 | tf_op jit(solution)/shard_map/ppermute | solution.py:25
  59.3 9.6 %collective-permute-start.10 = (bf16[192,512]{1,0:T(8,128)(2,1)S(1)}, bf16[192,512]{1,0:T(8,128)(2,1)S(1)}, u32[]{:S(2)}, u32[]{:S(2)}) collective-permute-start(bf16[192,512]{1,0:T(8,128)(2,1)S(1)} %key_sum.1.refs_3_), channel_id=1, source_target_pairs={{0,2},{1,3},{2,4},{3,5},{4,6},{5,7},{6,0},{7,1},{8,10},{9,11},{10,... | collective-permute-start | bytes 589832 | tf_op jit(solution)/shard_map/ppermute | solution.py:25
  59.5 9.4 %collective-permute-start.13 = (bf16[192,512]{1,0:T(8,128)(2,1)}, bf16[192,512]{1,0:T(8,128)(2,1)S(1)}, u32[]{:S(2)}, u32[]{:S(2)}) collective-permute-start(bf16[192,512]{1,0:T(8,128)(2,1)} %get-tuple-element.41), channel_id=1, source_target_pairs={{0,1},{1,0},{2,3},{3,2},{4,5},{5,4},{6,7},{7,6},{8,9},{9,8},{10,11... | collective-permute-start | bytes 589832 | tf_op jit(solution)/shard_map/ppermute | solution.py:25
  61.2 11.2 %collective-permute-start.14 = (bf16[192,512]{1,0:T(8,128)(2,1)S(1)}, bf16[192,512]{1,0:T(8,128)(2,1)S(1)}, u32[]{:S(2)}, u32[]{:S(2)}) collective-permute-start(bf16[192,512]{1,0:T(8,128)(2,1)S(1)} %get-tuple-element.42), channel_id=1, source_target_pairs={{0,2},{1,3},{2,0},{3,1},{4,6},{5,7},{6,4},{7,5},{8,10},{9,11},{10,... | collective-permute-start | bytes 589832 | tf_op jit(solution)/shard_map/ppermute | solution.py:25
  64.8 11.6 %collective-permute-start.15 = (bf16[192,512]{1,0:T(8,128)(2,1)S(1)}, bf16[192,512]{1,0:T(8,128)(2,1)S(1)}, u32[]{:S(2)}, u32[]{:S(2)}) collective-permute-start(bf16[192,512]{1,0:T(8,128)(2,1)S(1)} %get-tuple-element.43), channel_id=1, source_target_pairs={{0,3},{1,2},{2,1},{3,0},{4,7},{5,6},{6,5},{7,4},{8,11},{9,10},{10,... | collective-permute-start | bytes 589832 | tf_op jit(solution)/shard_map/ppermute | solution.py:25
  65.2 28.0 %copy-start.1 = (bf16[1,2,96,4096]{3,2,1,0:T(8,128)(2,1)S(1)}, bf16[1,2,96,4096]{3,2,1,0:T(8,128)(2,1)}, u32[]{:S(2)}) copy-start(bf16[1,2,96,4096]{3,2,1,0:T(8,128)(2,1)} %q_ref.1) | copy-start | bytes 4718596
  76.6 10.4 %collective-permute-start.16 = (bf16[192,512]{1,0:T(8,128)(2,1)S(1)}, bf16[192,512]{1,0:T(8,128)(2,1)S(1)}, u32[]{:S(2)}, u32[]{:S(2)}) collective-permute-start(bf16[192,512]{1,0:T(8,128)(2,1)S(1)} %value_sum.1.refs_3_), channel_id=1, source_target_pairs={{0,1},{1,2},{2,3},{3,4},{4,5},{5,6},{6,7},{7,0},{8,9},{9,10},{10,1... | collective-permute-start | bytes 589832 | tf_op jit(solution)/shard_map/ppermute | solution.py:25
  78.1 13.1 %collective-permute-start.12 = (bf16[192,512]{1,0:T(8,128)(2,1)S(1)}, bf16[192,512]{1,0:T(8,128)(2,1)S(1)}, u32[]{:S(2)}, u32[]{:S(2)}) collective-permute-start(bf16[192,512]{1,0:T(8,128)(2,1)S(1)} %broadcast_select_fusion), channel_id=1, source_target_pairs={{0,1},{1,2},{2,3},{3,4},{4,5},{5,6},{6,7},{7,0},{8,9},{9,10},{10,1... | collective-permute-start | bytes 589832 | tf_op jit(solution)/shard_map/ppermute | solution.py:25
  78.2 15.0 %collective-permute-start.11 = (bf16[192,512]{1,0:T(8,128)(2,1)S(1)}, bf16[192,512]{1,0:T(8,128)(2,1)S(1)}, u32[]{:S(2)}, u32[]{:S(2)}) collective-permute-start(bf16[192,512]{1,0:T(8,128)(2,1)S(1)} %collective-permute-done.10.refs_1_), channel_id=1, source_target_pairs={{0,1},{1,0},{2,3},{3,2},{4,5},{5,4},{6,7},{7,6},{8,9},{9,8},{10,11... | collective-permute-start | bytes 589832 | tf_op jit(solution)/shard_map/ppermute | solution.py:25
  78.3 19.7 %collective-permute-start.18 = (bf16[192,512]{1,0:T(8,128)(2,1)S(1)}, bf16[192,512]{1,0:T(8,128)(2,1)S(1)}, u32[]{:S(2)}, u32[]{:S(2)}) collective-permute-start(bf16[192,512]{1,0:T(8,128)(2,1)S(1)} %value_sum.1.refs_3_), channel_id=1, source_target_pairs={{0,2},{1,3},{2,4},{3,5},{4,6},{5,7},{6,0},{7,1},{8,10},{9,11},{10,... | collective-permute-start | bytes 589832 | tf_op jit(solution)/shard_map/ppermute | solution.py:25
  87.0 10.9 %collective-permute-start.17 = (bf16[192,512]{1,0:T(8,128)(2,1)S(1)}, bf16[192,512]{1,0:T(8,128)(2,1)S(1)}, u32[]{:S(2)}, u32[]{:S(2)}) collective-permute-start(bf16[192,512]{1,0:T(8,128)(2,1)S(1)} %collective-permute-done.16.refs_2_), channel_id=1, source_target_pairs={{0,2},{1,3},{2,4},{3,5},{4,6},{5,7},{6,0},{7,1},{8,10},{9,11},{10,... | collective-permute-start | bytes 589832 | tf_op jit(solution)/shard_map/ppermute | solution.py:25

commit v13 on v12

--- a/solution.py
+++ b/solution.py
@@ -338,7 +338,6 @@
     value_products = products(
         [first_cuts[:1], held_cuts[1:], first_cuts[1:]], value_shards, jnp.bfloat16
     )
-    key_z, value_products = lax.optimization_barrier((key_z, value_products))
     key_block = block_sum(key_sum_kernel, "key_sum", own_keys, [key_z], cosine, sine_part)
     key_two_back = moved(key_block, "ctx", lambda i: i + 2)
     value_parts = [

time: 101 us -> 97.6 us (0.966)
  starting transfers between devices: 26 us -> 22.2 us
    ppermute x14, starting transfers between devices: 19.4 us -> 15.5 us  [moved(): lax.ppermute(block, axis, [(i, target(i) % size) for i in range(size)])]
where the time goes in v13:
time: 97.6 us; the launch traced here: 97.4 us
  waiting for transfers between devices  56.2 us (58%)
  starting transfers between devices  22.2 us (23%)
  Pallas kernels  14.7 us (15%)
  local copies, waits for them, and re-layouts  2.59 us (3%)
    ppermute x14, waiting for transfers between devices, moved(): lax.ppermute(block, axis, [(i, target(i) % size) for i in range(size)])  44.7 us
    ppermute x14, starting transfers between devices, moved(): lax.ppermute(block, axis, [(i, target(i) % size) for i in range(size)])  15.5 us
    ppermute x5, waiting for transfers between devices, to_next_section(): return lax.ppermute(part, ('section', 'ctx'), route)  11.6 us
    ppermute x5, starting transfers between devices, to_next_section(): return lax.ppermute(part, ('section', 'ctx'), route)  6.64 us
    pallas_call x4, Pallas kernels, products(): pl.pallas_call(lambda *refs: product_kernel(counts, *refs), out_shape=[ja...  5.09 us
    pallas_call x1, Pallas kernels, scored(): pl.pallas_call(score_kernel, grid=(micro_count,), in_specs=[pl.BlockSpec(...  4.75 us
    pallas_call x1, Pallas kernels, mixed_values(): pl.pallas_call(mix_kernel, grid=(micro_count,), in_specs=[pl.BlockSpec((1...  2.5 us
    pallas_call x1, Pallas kernels, normed_cuts(): pl.pallas_call(norm_kernel, grid=(micro_count,), in_specs=[pl.BlockSpec(m...  2.08 us
  transfers between devices with their start and end apart: 19, of which 11 were waited for; matrix products, arithmetic and copies ran while one was open for 3% of the time, Pallas kernels for 12%

profile of v13, /device:TPU:0, one launch (start us, length us, event | category | flops | bytes accessed | tf_op | source)
XLA Modules:
  0.0 97.4 jit_solution(18254789800655731223)
XLA Ops:
  0.7 2.4 %collective-permute-start = (bf16[1,4096]{1,0:T(2,128)(2,1)}, bf16[1,4096]{1,0:T(2,128)(2,1)S(1)}, u32[]{:S(2)}, u32[]{:S(2)}) collective-permute-start(bf16[1,4096]{1,0:T(2,128)(2,1)} %param.6), channel_id=1, source_target_pairs={{0,24},{8,0},{16,8},{24,16},{1,25},{9,1},{17,9},{25,17},{2,26},{10... | collective-permute-start | bytes 24584 | tf_op jit(solution)/shard_map/ppermute | solution.py:25
  3.1 1.3 %fusion.4 = (bf16[512,512]{1,0:T(8,128)(2,1)S(1)}, bf16[512,512]{1,0:T(8,128)(2,1)S(1)}) fusion(bf16[512,1024]{1,0:T(8,128)(2,1)} %bitcast.7), kind=kLoop, calls=%fused_computation.21 | loop fusion | bytes 2097152 | tf_op jit(solution)/shard_map/slice | solution.py:289
  4.3 2.7 %collective-permute-start.2 = (bf16[512,512]{1,0:T(8,128)(2,1)S(1)}, bf16[512,512]{1,0:T(8,128)(2,1)S(1)}, u32[]{:S(2)}, u32[]{:S(2)}) collective-permute-start(bf16[512,512]{1,0:T(8,128)(2,1)S(1)} %get-tuple-element.41.refs_3_.refs_2_), channel_id=1, source_target_pairs={{0,4},{1,5},{2,6},{3,7},{4,0},{5,1},{6,2},{7,3},{8,12},{9,13},{10,... | collective-permute-start | bytes 1572872 | tf_op jit(solution)/shard_map/ppermute | solution.py:25
  7.6 2.1 %norm_cuts.1 = (bf16[192,1024]{1,0:T(8,128)(2,1)S(1)}, bf16[192,1024]{1,0:T(8,128)(2,1)}, bf16[192,1024]{1,0:T(8,128)(2,1)S(1)}, bf16[192,1024]{1,0:T(8,128)(2,1)}) custom-call(s32[4,2]{1,0:T(4,128)S(1)} %add_multiply_fusion.starts_ref, bf16[2,96,4096]{2,1,0:T(8,128)(2,1)S(1)} %bitcast.6, f32[1,4096]{1,0:T(1,128)S(1)} %convert_element_type.16.gain_ref), custom_call_target="tpu_custom_call" | custom-call | flops 4718592 | bytes 3145728 | tf_op jit(solution)/shard_map/norm_cuts/pallas_call | solution.py:58
  9.7 0.8 copy-done.4
  10.4 0.4 collective-permute-start.5
  10.8 2.5 %collective-permute-start.6 = (bf16[192,1024]{1,0:T(8,128)(2,1)}, bf16[192,1024]{1,0:T(8,128)(2,1)}, u32[]{:S(2)}, u32[]{:S(2)}) collective-permute-start(bf16[192,1024]{1,0:T(8,128)(2,1)} %get-tuple-element.25), channel_id=1, source_target_pairs={{0,11},{1,10},{2,9},{3,8},{4,15},{5,14},{6,13},{7,12},{8,19},{9,18... | collective-permute-start | bytes 1179656 | tf_op jit(solution)/shard_map/ppermute | solution.py:281
  13.6 16.4 %collective-permute-done.2.refs_4_.refs_3_ = bf16[512,512]{1,0:T(8,128)(2,1)S(1)} collective-permute-done((bf16[512,512]{1,0:T(8,128)(2,1)S(1)}, bf16[512,512]{1,0:T(8,128)(2,1)S(1)}, u32[]{:S(2)}, u32[]{:S(2)}) %collective-permute-start.2) | collective-permute-done | bytes 524320 | tf_op jit(solution)/shard_map/ppermute | solution.py:25
  30.0 3.5 %collective-permute-start.4 = (bf16[96,1024]{1,0:T(8,128)(2,1)S(1)}, bf16[96,1024]{1,0:T(8,128)(2,1)S(1)}, u32[]{:S(2)}, u32[]{:S(2)}) collective-permute-start(bf16[96,1024]{1,0:T(8,128)(2,1)S(1)} %get-tuple-element.42), channel_id=1, source_target_pairs={{0,10},{1,11},{2,8},{3,9},{4,14},{5,15},{6,12},{7,13},{8,18},{9,19... | collective-permute-start | bytes 589832 | tf_op jit(solution)/shard_map/ppermute | solution.py:281
  33.7 1.6 %products.5 = bf16[384,512]{1,0:T(8,128)(2,1)S(1)} custom-call(bf16[192,1024]{1,0:T(8,128)(2,1)S(1)} %collective-permute-done.5.refs_0_, bf16[192,1024]{1,0:T(8,128)(2,1)} %collective-permute-done.6.refs_1_.refs_3_, bf16[512,512]{1,0:T(8,128)(2,1)S(1)} %get-tuple-element.41.refs_3_.refs_2_, bf16[512,512]{1,0:T(8,128)(2,1)S(1)} %collective-permute-done.2.refs_4_.refs_3_), custom_call_target="tpu_custom_call" | custom-call | flops 1610612736 | bytes 3145728 | tf_op jit(solution)/shard_map/products/pallas_call | solution.py:99
  35.3 1.6 %collective-permute-start.7 = (bf16[384,512]{1,0:T(8,128)(2,1)S(1)}, bf16[384,512]{1,0:T(8,128)(2,1)S(1)}, u32[]{:S(2)}, u32[]{:S(2)}) collective-permute-start(bf16[384,512]{1,0:T(8,128)(2,1)S(1)} %products.5), channel_id=1, source_target_pairs={{0,1},{1,0},{2,3},{3,2},{4,5},{5,4},{6,7},{7,6},{8,9},{9,8},{10,11... | collective-permute-start | bytes 1179656 | tf_op jit(solution)/shard_map/ppermute | solution.py:25
  36.9 0.4 fusion
  37.5 9.1 %collective-permute-done.4.refs_2_ = bf16[96,1024]{1,0:T(8,128)(2,1)S(1)} collective-permute-done((bf16[96,1024]{1,0:T(8,128)(2,1)S(1)}, bf16[96,1024]{1,0:T(8,128)(2,1)S(1)}, u32[]{:S(2)}, u32[]{:S(2)}) %collective-permute-start.4) | collective-permute-done | bytes 196640 | tf_op jit(solution)/shard_map/ppermute | solution.py:281
  46.6 2.4 %collective-permute-done.3.refs_1_ = bf16[96,1024]{1,0:T(8,128)(2,1)S(1)} collective-permute-done((bf16[96,1024]{1,0:T(8,128)(2,1)S(1)}, bf16[96,1024]{1,0:T(8,128)(2,1)S(1)}, u32[]{:S(2)}, u32[]{:S(2)}) %collective-permute-start.3) | collective-permute-done | bytes 196640 | tf_op jit(solution)/shard_map/ppermute | solution.py:281
  49.1 0.7 products.4.held
  49.8 3.1 %collective-permute-start.8 = (bf16[192,512]{1,0:T(8,128)(2,1)S(1)}, bf16[192,512]{1,0:T(8,128)(2,1)S(1)}, u32[]{:S(2)}, u32[]{:S(2)}) collective-permute-start(bf16[192,512]{1,0:T(8,128)(2,1)S(1)} %get-tuple-element.27), channel_id=1, source_target_pairs={{0,2},{1,3},{2,0},{3,1},{4,6},{5,7},{6,4},{7,5},{8,10},{9,11},{10,... | collective-permute-start | bytes 589832 | tf_op jit(solution)/shard_map/ppermute | solution.py:25
  52.9 2.1 %collective-permute-done.12.refs_2_.refs_5_ = bf16[512,512]{1,0:T(8,128)(2,1)S(1)} collective-permute-done((bf16[512,512]{1,0:T(8,128)(2,1)S(1)}, bf16[512,512]{1,0:T(8,128)(2,1)S(1)}, u32[]{:S(2)}, u32[]{:S(2)}) %collective-permute-start.12) | collective-permute-done | bytes 524320 | tf_op jit(solution)/shard_map/ppermute | solution.py:25
  55.1 2.4 %products.7 = (bf16[192,512]{1,0:T(8,128)(2,1)}, bf16[192,512]{1,0:T(8,128)(2,1)S(1)}, bf16[192,512]{1,0:T(8,128)(2,1)S(1)}) custom-call(bf16[192,1024]{1,0:T(8,128)(2,1)S(1)} %copy-done.3, bf16[96,1024]{1,0:T(8,128)(2,1)S(1)} %collective-permute-done.3.refs_1_, bf16[96,1024]{1,0:T(8,128)(2,1)S(1)} %collective-permute-done.4.refs_2_, ...), custom_call_target="tpu_custom_call" | custom-call | flops 2415919104 | bytes 4718592 | tf_op jit(solution)/shard_map/products/pallas_call | solution.py:99
  57.4 1.6 %collective-permute-start.13 = (bf16[192,512]{1,0:T(8,128)(2,1)}, bf16[192,512]{1,0:T(8,128)(2,1)S(1)}, u32[]{:S(2)}, u32[]{:S(2)}) collective-permute-start(bf16[192,512]{1,0:T(8,128)(2,1)} %get-tuple-element.33), channel_id=1, source_target_pairs={{0,1},{1,0},{2,3},{3,2},{4,5},{5,4},{6,7},{7,6},{8,9},{9,8},{10,11... | collective-permute-start | bytes 589832 | tf_op jit(solution)/shard_map/ppermute | solution.py:25
  59.1 1.9 %collective-permute-start.15 = (bf16[192,512]{1,0:T(8,128)(2,1)S(1)}, bf16[192,512]{1,0:T(8,128)(2,1)S(1)}, u32[]{:S(2)}, u32[]{:S(2)}) collective-permute-start(bf16[192,512]{1,0:T(8,128)(2,1)S(1)} %get-tuple-element.35), channel_id=1, source_target_pairs={{0,3},{1,2},{2,1},{3,0},{4,7},{5,6},{6,5},{7,4},{8,11},{9,10},{10,... | collective-permute-start | bytes 589832 | tf_op jit(solution)/shard_map/ppermute | solution.py:25
  61.3 0.4 products.6.own
  61.7 3.0 %collective-permute-done.13.refs_0_ = bf16[192,512]{1,0:T(8,128)(2,1)S(1)} collective-permute-done((bf16[192,512]{1,0:T(8,128)(2,1)}, bf16[192,512]{1,0:T(8,128)(2,1)S(1)}, u32[]{:S(2)}, u32[]{:S(2)}) %collective-permute-start.13) | collective-permute-done | bytes 196640 | tf_op jit(solution)/shard_map/ppermute | solution.py:25
  64.7 1.1 %collective-permute-done.14.refs_1_ = bf16[192,512]{1,0:T(8,128)(2,1)S(1)} collective-permute-done((bf16[192,512]{1,0:T(8,128)(2,1)S(1)}, bf16[192,512]{1,0:T(8,128)(2,1)S(1)}, u32[]{:S(2)}, u32[]{:S(2)}) %collective-permute-start.14) | collective-permute-done | bytes 196640 | tf_op jit(solution)/shard_map/ppermute | solution.py:25
  65.8 2.9 %collective-permute-done.15.refs_2_ = bf16[192,512]{1,0:T(8,128)(2,1)S(1)} collective-permute-done((bf16[192,512]{1,0:T(8,128)(2,1)S(1)}, bf16[192,512]{1,0:T(8,128)(2,1)S(1)}, u32[]{:S(2)}, u32[]{:S(2)}) %collective-permute-start.15) | collective-permute-done | bytes 196640 | tf_op jit(solution)/shard_map/ppermute | solution.py:25
  68.7 5.9 %collective-permute-done.9.refs_1_ = bf16[192,512]{1,0:T(8,128)(2,1)S(1)} collective-permute-done((bf16[192,512]{1,0:T(8,128)(2,1)S(1)}, bf16[192,512]{1,0:T(8,128)(2,1)S(1)}, u32[]{:S(2)}, u32[]{:S(2)}) %collective-permute-start.9) | collective-permute-done | bytes 196640 | tf_op jit(solution)/shard_map/ppermute | solution.py:25
  74.7 1.6 %collective-permute-start.16 = (bf16[192,512]{1,0:T(8,128)(2,1)S(1)}, bf16[192,512]{1,0:T(8,128)(2,1)S(1)}, u32[]{:S(2)}, u32[]{:S(2)}) collective-permute-start(bf16[192,512]{1,0:T(8,128)(2,1)S(1)} %value_sum.1.refs_3_), channel_id=1, source_target_pairs={{0,1},{1,2},{2,3},{3,4},{4,5},{5,6},{6,7},{7,0},{8,9},{9,10},{10,1... | collective-permute-start | bytes 589832 | tf_op jit(solution)/shard_map/ppermute | solution.py:25
  76.4 0.3 collective-permute-start.18
  76.7 8.6 %collective-permute-done.16.refs_2_ = bf16[192,512]{1,0:T(8,128)(2,1)S(1)} collective-permute-done((bf16[192,512]{1,0:T(8,128)(2,1)S(1)}, bf16[192,512]{1,0:T(8,128)(2,1)S(1)}, u32[]{:S(2)}, u32[]{:S(2)}) %collective-permute-start.16) | collective-permute-done | bytes 196640 | tf_op jit(solution)/shard_map/ppermute | solution.py:25
  85.5 4.0 %collective-permute-done.11.refs_2_ = bf16[192,512]{1,0:T(8,128)(2,1)S(1)} collective-permute-done((bf16[192,512]{1,0:T(8,128)(2,1)S(1)}, bf16[192,512]{1,0:T(8,128)(2,1)S(1)}, u32[]{:S(2)}, u32[]{:S(2)}) %collective-permute-start.11) | collective-permute-done | bytes 196640 | tf_op jit(solution)/shard_map/ppermute | solution.py:25
  89.5 0.6 collective-permute-done.10.refs_0_
  90.1 4.7 %scores.1 = (bf16[2,4,768,384]{3,2,1,0:T(8,128)(2,1)S(1)}, f32[2,4,96,128]{3,2,1,0:T(8,128)S(1)}, f32[2,32,96]{2,1,0:T(8,128)}) custom-call(s32[1]{0:T(128)} %bitcast.odd_ref, bf16[1,2,96,4096]{3,2,1,0:T(8,128)(2,1)S(1)} %copy-done.1, bf16[192,512]{1,0:T(8,128)(2,1)S(1)} %collective-permute-done.10.refs_0_, ...), custom_call_target="tpu_custom_call" | custom-call | flops 603979776 | bytes 8388608 | tf_op jit(solution)/shard_map/scores/pallas_call | solution.py:197
  94.9 2.5 %mixed_values.1 = bf16[1,2,96,4096]{3,2,1,0:T(8,128)(2,1)} custom-call(bf16[2,4,768,384]{3,2,1,0:T(8,128)(2,1)S(1)} %get-tuple-element.28.weights, f32[2,4,96,128]{3,2,1,0:T(8,128)S(1)} %get-tuple-element.29.sums, bf16[192,512]{1,0:T(8,128)(2,1)S(1)} %collective-permute-done.17.refs_0_, bf16[192,512]{1,0:T(8,128)(2,1)S(1)} %collective-permute-done.18.refs_1_, ...), custom_call_target="tpu_custom_call" | custom-call | flops 603979776 | bytes 8388608 | tf_op jit(solution)/shard_map/mixed_values/pallas_call | solution.py:242
  (50 shorter events, 1.9 us)
Async XLA Ops:
  0.6 6.4 %copy-start.5 = (s32[2,16]{1,0:T(2,128)S(1)}, s32[2,16]{1,0:T(2,128)}, u32[]{:S(2)}) copy-start(s32[2,16]{1,0:T(2,128)} %param.9) | copy-start | bytes 388
  0.6 6.9 %copy-start = (bf16[1,2,96,4096]{3,2,1,0:T(8,128)(2,1)S(1)}, bf16[1,2,96,4096]{3,2,1,0:T(8,128)(2,1)}, u32[]{:S(2)}) copy-start(bf16[1,2,96,4096]{3,2,1,0:T(8,128)(2,1)} %param.5) | copy-start | bytes 4718596
  0.7 6.9 %collective-permute-start = (bf16[1,4096]{1,0:T(2,128)(2,1)}, bf16[1,4096]{1,0:T(2,128)(2,1)S(1)}, u32[]{:S(2)}, u32[]{:S(2)}) collective-permute-start(bf16[1,4096]{1,0:T(2,128)(2,1)} %param.6), channel_id=1, source_target_pairs={{0,24},{8,0},{16,8},{24,16},{1,25},{9,1},{17,9},{25,17},{2,26},{10... | collective-permute-start | bytes 24584 | tf_op jit(solution)/shard_map/ppermute | solution.py:25
  4.3 25.7 %collective-permute-start.2 = (bf16[512,512]{1,0:T(8,128)(2,1)S(1)}, bf16[512,512]{1,0:T(8,128)(2,1)S(1)}, u32[]{:S(2)}, u32[]{:S(2)}) collective-permute-start(bf16[512,512]{1,0:T(8,128)(2,1)S(1)} %get-tuple-element.41.refs_3_.refs_2_), channel_id=1, source_target_pairs={{0,4},{1,5},{2,6},{3,7},{4,0},{5,1},{6,2},{7,3},{8,12},{9,13},{10,... | collective-permute-start | bytes 1572872 | tf_op jit(solution)/shard_map/ppermute | solution.py:25
  9.7 0.8 copy-start.4
  10.4 23.2 %collective-permute-start.5 = (bf16[192,1024]{1,0:T(8,128)(2,1)}, bf16[192,1024]{1,0:T(8,128)(2,1)S(1)}, u32[]{:S(2)}, u32[]{:S(2)}) collective-permute-start(bf16[192,1024]{1,0:T(8,128)(2,1)} %get-tuple-element.24), channel_id=1, source_target_pairs={{0,9},{1,8},{2,11},{3,10},{4,13},{5,12},{6,15},{7,14},{8,17},{9,16... | collective-permute-start | bytes 1179656 | tf_op jit(solution)/shard_map/ppermute | solution.py:281
  10.8 22.8 %collective-permute-start.6 = (bf16[192,1024]{1,0:T(8,128)(2,1)}, bf16[192,1024]{1,0:T(8,128)(2,1)}, u32[]{:S(2)}, u32[]{:S(2)}) collective-permute-start(bf16[192,1024]{1,0:T(8,128)(2,1)} %get-tuple-element.25), channel_id=1, source_target_pairs={{0,11},{1,10},{2,9},{3,8},{4,15},{5,14},{6,13},{7,12},{8,19},{9,18... | collective-permute-start | bytes 1179656 | tf_op jit(solution)/shard_map/ppermute | solution.py:281
  13.5 24.0 %collective-permute-start.1 = (bf16[192,1024]{1,0:T(8,128)(2,1)}, bf16[192,1024]{1,0:T(8,128)(2,1)S(1)}, u32[]{:S(2)}, u32[]{:S(2)}) collective-permute-start(bf16[192,1024]{1,0:T(8,128)(2,1)} %copy-done.4), channel_id=1, source_target_pairs={{0,8},{1,9},{2,10},{3,11},{4,12},{5,13},{6,14},{7,15},{8,16},{9,17... | collective-permute-start | bytes 1179656 | tf_op jit(solution)/shard_map/ppermute | solution.py:281
  30.0 25.1 %collective-permute-start.12 = (bf16[512,512]{1,0:T(8,128)(2,1)S(1)}, bf16[512,512]{1,0:T(8,128)(2,1)S(1)}, u32[]{:S(2)}, u32[]{:S(2)}) collective-permute-start(bf16[512,512]{1,0:T(8,128)(2,1)S(1)} %get-tuple-element.31.refs_1_.refs_4_), channel_id=1, source_target_pairs={{0,4},{1,5},{2,6},{3,7},{4,0},{5,1},{6,2},{7,3},{8,12},{9,13},{10,... | collective-permute-start | bytes 1572872 | tf_op jit(solution)/shard_map/ppermute | solution.py:25
  30.0 16.6 %collective-permute-start.4 = (bf16[96,1024]{1,0:T(8,128)(2,1)S(1)}, bf16[96,1024]{1,0:T(8,128)(2,1)S(1)}, u32[]{:S(2)}, u32[]{:S(2)}) collective-permute-start(bf16[96,1024]{1,0:T(8,128)(2,1)S(1)} %get-tuple-element.42), channel_id=1, source_target_pairs={{0,10},{1,11},{2,8},{3,9},{4,14},{5,15},{6,12},{7,13},{8,18},{9,19... | collective-permute-start | bytes 589832 | tf_op jit(solution)/shard_map/ppermute | solution.py:281
  33.6 1.7 %copy-start.2 = (bf16[192,1024]{1,0:T(8,128)(2,1)}, bf16[192,1024]{1,0:T(8,128)(2,1)S(1)}, u32[]{:S(2)}) copy-start(bf16[192,1024]{1,0:T(8,128)(2,1)S(1)} %collective-permute-done.5.refs_0_) | copy-start | bytes 1179652
  33.6 15.5 %collective-permute-start.3 = (bf16[96,1024]{1,0:T(8,128)(2,1)S(1)}, bf16[96,1024]{1,0:T(8,128)(2,1)S(1)}, u32[]{:S(2)}, u32[]{:S(2)}) collective-permute-start(bf16[96,1024]{1,0:T(8,128)(2,1)S(1)} %get-tuple-element.43), channel_id=1, source_target_pairs={{0,10},{1,11},{2,8},{3,9},{4,14},{5,15},{6,12},{7,13},{8,18},{9,19... | collective-permute-start | bytes 589832 | tf_op jit(solution)/shard_map/ppermute | solution.py:281
  35.3 14.4 %collective-permute-start.7 = (bf16[384,512]{1,0:T(8,128)(2,1)S(1)}, bf16[384,512]{1,0:T(8,128)(2,1)S(1)}, u32[]{:S(2)}, u32[]{:S(2)}) collective-permute-start(bf16[384,512]{1,0:T(8,128)(2,1)S(1)} %products.5), channel_id=1, source_target_pairs={{0,1},{1,0},{2,3},{3,2},{4,5},{5,4},{6,7},{7,6},{8,9},{9,8},{10,11... | collective-permute-start | bytes 1179656 | tf_op jit(solution)/shard_map/ppermute | solution.py:25
  37.5 17.6 %copy-start.3 = (bf16[192,1024]{1,0:T(8,128)(2,1)S(1)}, bf16[192,1024]{1,0:T(8,128)(2,1)}, u32[]{:S(2)}) copy-start(bf16[192,1024]{1,0:T(8,128)(2,1)} %copy-done.2) | copy-start | bytes 1179652
  49.8 11.1 %collective-permute-start.8 = (bf16[192,512]{1,0:T(8,128)(2,1)S(1)}, bf16[192,512]{1,0:T(8,128)(2,1)S(1)}, u32[]{:S(2)}, u32[]{:S(2)}) collective-permute-start(bf16[192,512]{1,0:T(8,128)(2,1)S(1)} %get-tuple-element.27), channel_id=1, source_target_pairs={{0,2},{1,3},{2,0},{3,1},{4,6},{5,7},{6,4},{7,5},{8,10},{9,11},{10,... | collective-permute-start | bytes 589832 | tf_op jit(solution)/shard_map/ppermute | solution.py:25
  57.4 7.2 %collective-permute-start.13 = (bf16[192,512]{1,0:T(8,128)(2,1)}, bf16[192,512]{1,0:T(8,128)(2,1)S(1)}, u32[]{:S(2)}, u32[]{:S(2)}) collective-permute-start(bf16[192,512]{1,0:T(8,128)(2,1)} %get-tuple-element.33), channel_id=1, source_target_pairs={{0,1},{1,0},{2,3},{3,2},{4,5},{5,4},{6,7},{7,6},{8,9},{9,8},{10,11... | collective-permute-start | bytes 589832 | tf_op jit(solution)/shard_map/ppermute | solution.py:25
  59.1 6.7 %collective-permute-start.14 = (bf16[192,512]{1,0:T(8,128)(2,1)S(1)}, bf16[192,512]{1,0:T(8,128)(2,1)S(1)}, u32[]{:S(2)}, u32[]{:S(2)}) collective-permute-start(bf16[192,512]{1,0:T(8,128)(2,1)S(1)} %get-tuple-element.34), channel_id=1, source_target_pairs={{0,2},{1,3},{2,0},{3,1},{4,6},{5,7},{6,4},{7,5},{8,10},{9,11},{10,... | collective-permute-start | bytes 589832 | tf_op jit(solution)/shard_map/ppermute | solution.py:25
  59.1 9.6 %collective-permute-start.15 = (bf16[192,512]{1,0:T(8,128)(2,1)S(1)}, bf16[192,512]{1,0:T(8,128)(2,1)S(1)}, u32[]{:S(2)}, u32[]{:S(2)}) collective-permute-start(bf16[192,512]{1,0:T(8,128)(2,1)S(1)} %get-tuple-element.35), channel_id=1, source_target_pairs={{0,3},{1,2},{2,1},{3,0},{4,7},{5,6},{6,5},{7,4},{8,11},{9,10},{10,... | collective-permute-start | bytes 589832 | tf_op jit(solution)/shard_map/ppermute | solution.py:25
  61.1 13.5 %collective-permute-start.9 = (bf16[192,512]{1,0:T(8,128)(2,1)S(1)}, bf16[192,512]{1,0:T(8,128)(2,1)S(1)}, u32[]{:S(2)}, u32[]{:S(2)}) collective-permute-start(bf16[192,512]{1,0:T(8,128)(2,1)S(1)} %key_sum.1.refs_3_), channel_id=1, source_target_pairs={{0,2},{1,3},{2,4},{3,5},{4,6},{5,7},{6,0},{7,1},{8,10},{9,11},{10,... | collective-permute-start | bytes 589832 | tf_op jit(solution)/shard_map/ppermute | solution.py:25
  61.7 28.4 %copy-start.1 = (bf16[1,2,96,4096]{3,2,1,0:T(8,128)(2,1)S(1)}, bf16[1,2,96,4096]{3,2,1,0:T(8,128)(2,1)}, u32[]{:S(2)}) copy-start(bf16[1,2,96,4096]{3,2,1,0:T(8,128)(2,1)} %q_ref.1) | copy-start | bytes 4718596
  74.7 10.7 %collective-permute-start.16 = (bf16[192,512]{1,0:T(8,128)(2,1)S(1)}, bf16[192,512]{1,0:T(8,128)(2,1)S(1)}, u32[]{:S(2)}, u32[]{:S(2)}) collective-permute-start(bf16[192,512]{1,0:T(8,128)(2,1)S(1)} %value_sum.1.refs_3_), channel_id=1, source_target_pairs={{0,1},{1,2},{2,3},{3,4},{4,5},{5,6},{6,7},{7,0},{8,9},{9,10},{10,1... | collective-permute-start | bytes 589832 | tf_op jit(solution)/shard_map/ppermute | solution.py:25
  76.3 13.2 %collective-permute-start.11 = (bf16[192,512]{1,0:T(8,128)(2,1)S(1)}, bf16[192,512]{1,0:T(8,128)(2,1)S(1)}, u32[]{:S(2)}, u32[]{:S(2)}) collective-permute-start(bf16[192,512]{1,0:T(8,128)(2,1)S(1)} %broadcast_select_fusion), channel_id=1, source_target_pairs={{0,1},{1,2},{2,3},{3,4},{4,5},{5,6},{6,7},{7,0},{8,9},{9,10},{10,1... | collective-permute-start | bytes 589832 | tf_op jit(solution)/shard_map/ppermute | solution.py:25
  76.3 13.8 %collective-permute-start.10 = (bf16[192,512]{1,0:T(8,128)(2,1)S(1)}, bf16[192,512]{1,0:T(8,128)(2,1)S(1)}, u32[]{:S(2)}, u32[]{:S(2)}) collective-permute-start(bf16[192,512]{1,0:T(8,128)(2,1)S(1)} %collective-permute-done.9.refs_1_), channel_id=1, source_target_pairs={{0,1},{1,0},{2,3},{3,2},{4,5},{5,4},{6,7},{7,6},{8,9},{9,8},{10,11... | collective-permute-start | bytes 589832 | tf_op jit(solution)/shard_map/ppermute | solution.py:25
  76.4 18.5 %collective-permute-start.18 = (bf16[192,512]{1,0:T(8,128)(2,1)S(1)}, bf16[192,512]{1,0:T(8,128)(2,1)S(1)}, u32[]{:S(2)}, u32[]{:S(2)}) collective-permute-start(bf16[192,512]{1,0:T(8,128)(2,1)S(1)} %value_sum.1.refs_3_), channel_id=1, source_target_pairs={{0,2},{1,3},{2,4},{3,5},{4,6},{5,7},{6,0},{7,1},{8,10},{9,11},{10,... | collective-permute-start | bytes 589832 | tf_op jit(solution)/shard_map/ppermute | solution.py:25
  85.4 9.5 %collective-permute-start.17 = (bf16[192,512]{1,0:T(8,128)(2,1)S(1)}, bf16[192,512]{1,0:T(8,128)(2,1)S(1)}, u32[]{:S(2)}, u32[]{:S(2)}) collective-permute-start(bf16[192,512]{1,0:T(8,128)(2,1)S(1)} %collective-permute-done.16.refs_2_), channel_id=1, source_target_pairs={{0,2},{1,3},{2,4},{3,5},{4,6},{5,7},{6,0},{7,1},{8,10},{9,11},{10,... | collective-permute-start | bytes 589832 | tf_op jit(solution)/shard_map/ppermute | solution.py:25

commit v14 on v13

--- a/solution.py
+++ b/solution.py
@@ -345,7 +345,6 @@
         for flip, part in enumerate(value_products, start=1)
     ]
     (own_values,) = products([held_cuts[:1]], value_shards, jnp.float32)
-    value_parts, _ = lax.optimization_barrier((value_parts, key_two_back))
     weights, sums, log_sums = scored(
         odd.astype(jnp.int32).reshape(1),
         queries,

time: 97.6 us -> 95.6 us (0.980)
  waiting for transfers between devices: 56.2 us -> 52.6 us
  starting transfers between devices: 22.2 us -> 23.9 us
    ppermute x14, waiting for transfers between devices: 44.7 us -> 41 us  [moved(): lax.ppermute(block, axis, [(i, target(i) % size) for i in range(size)])]
    ppermute x14, starting transfers between devices: 15.5 us -> 17.2 us  [moved(): lax.ppermute(block, axis, [(i, target(i) % size) for i in range(size)])]
  transfers between devices with their start and end apart: 19 -> 19, of which waited for: 11 -> 11; matrix products, arithmetic and copies ran while one was open for 3% -> 3% of each run, Pallas kernels for 12% -> 13%
where the time goes in v14:
time: 95.6 us; the launch traced here: 95.4 us
  waiting for transfers between devices  52.6 us (55%)
  starting transfers between devices  23.9 us (25%)
  Pallas kernels  14.7 us (15%)
  local copies, waits for them, and re-layouts  2.59 us (3%)
    ppermute x14, waiting for transfers between devices, moved(): lax.ppermute(block, axis, [(i, target(i) % size) for i in range(size)])  41 us
    ppermute x14, starting transfers between devices, moved(): lax.ppermute(block, axis, [(i, target(i) % size) for i in range(size)])  17.2 us
    ppermute x5, waiting for transfers between devices, to_next_section(): return lax.ppermute(part, ('section', 'ctx'), route)  11.6 us
    ppermute x5, starting transfers between devices, to_next_section(): return lax.ppermute(part, ('section', 'ctx'), route)  6.64 us
    pallas_call x4, Pallas kernels, products(): pl.pallas_call(lambda *refs: product_kernel(counts, *refs), out_shape=[ja...  5.09 us
    pallas_call x1, Pallas kernels, scored(): pl.pallas_call(score_kernel, grid=(micro_count,), in_specs=[pl.BlockSpec(...  4.75 us
    pallas_call x1, Pallas kernels, mixed_values(): pl.pallas_call(mix_kernel, grid=(micro_count,), in_specs=[pl.BlockSpec((1...  2.5 us
    pallas_call x1, Pallas kernels, normed_cuts(): pl.pallas_call(norm_kernel, grid=(micro_count,), in_specs=[pl.BlockSpec(m...  2.08 us
  transfers between devices with their start and end apart: 19, of which 11 were waited for; matrix products, arithmetic and copies ran while one was open for 3% of the time, Pallas kernels for 13%

profile of v14, /device:TPU:0, one launch (start us, length us, event | category | flops | bytes accessed | tf_op | source)
XLA Modules:
  0.0 95.4 jit_solution(17421728654697783177)
XLA Ops:
  0.7 2.4 %collective-permute-start = (bf16[1,4096]{1,0:T(2,128)(2,1)}, bf16[1,4096]{1,0:T(2,128)(2,1)S(1)}, u32[]{:S(2)}, u32[]{:S(2)}) collective-permute-start(bf16[1,4096]{1,0:T(2,128)(2,1)} %param.6), channel_id=1, source_target_pairs={{0,24},{8,0},{16,8},{24,16},{1,25},{9,1},{17,9},{25,17},{2,26},{10... | collective-permute-start | bytes 24584 | tf_op jit(solution)/shard_map/ppermute | solution.py:25
  3.1 1.3 %fusion.4 = (bf16[512,512]{1,0:T(8,128)(2,1)S(1)}, bf16[512,512]{1,0:T(8,128)(2,1)S(1)}) fusion(bf16[512,1024]{1,0:T(8,128)(2,1)} %bitcast.7), kind=kLoop, calls=%fused_computation.21 | loop fusion | bytes 2097152 | tf_op jit(solution)/shard_map/slice | solution.py:289
  4.3 2.7 %collective-permute-start.2 = (bf16[512,512]{1,0:T(8,128)(2,1)S(1)}, bf16[512,512]{1,0:T(8,128)(2,1)S(1)}, u32[]{:S(2)}, u32[]{:S(2)}) collective-permute-start(bf16[512,512]{1,0:T(8,128)(2,1)S(1)} %get-tuple-element.35.refs_3_.refs_2_), channel_id=1, source_target_pairs={{0,4},{1,5},{2,6},{3,7},{4,0},{5,1},{6,2},{7,3},{8,12},{9,13},{10,... | collective-permute-start | bytes 1572872 | tf_op jit(solution)/shard_map/ppermute | solution.py:25
  7.6 2.1 %norm_cuts.1 = (bf16[192,1024]{1,0:T(8,128)(2,1)S(1)}, bf16[192,1024]{1,0:T(8,128)(2,1)}, bf16[192,1024]{1,0:T(8,128)(2,1)S(1)}, bf16[192,1024]{1,0:T(8,128)(2,1)}) custom-call(s32[4,2]{1,0:T(4,128)S(1)} %add_multiply_fusion.starts_ref, bf16[2,96,4096]{2,1,0:T(8,128)(2,1)S(1)} %bitcast.6, f32[1,4096]{1,0:T(1,128)S(1)} %convert_element_type.16.gain_ref), custom_call_target="tpu_custom_call" | custom-call | flops 4718592 | bytes 3145728 | tf_op jit(solution)/shard_map/norm_cuts/pallas_call | solution.py:58
  9.7 0.8 copy-done.4
  10.4 0.4 collective-permute-start.5
  10.8 2.5 %collective-permute-start.6 = (bf16[192,1024]{1,0:T(8,128)(2,1)}, bf16[192,1024]{1,0:T(8,128)(2,1)}, u32[]{:S(2)}, u32[]{:S(2)}) collective-permute-start(bf16[192,1024]{1,0:T(8,128)(2,1)} %get-tuple-element.22), channel_id=1, source_target_pairs={{0,11},{1,10},{2,9},{3,8},{4,15},{5,14},{6,13},{7,12},{8,19},{9,18... | collective-permute-start | bytes 1179656 | tf_op jit(solution)/shard_map/ppermute | solution.py:281
  13.6 16.4 %collective-permute-done.2.refs_4_.refs_3_ = bf16[512,512]{1,0:T(8,128)(2,1)S(1)} collective-permute-done((bf16[512,512]{1,0:T(8,128)(2,1)S(1)}, bf16[512,512]{1,0:T(8,128)(2,1)S(1)}, u32[]{:S(2)}, u32[]{:S(2)}) %collective-permute-start.2) | collective-permute-done | bytes 524320 | tf_op jit(solution)/shard_map/ppermute | solution.py:25
  30.0 3.5 %collective-permute-start.4 = (bf16[96,1024]{1,0:T(8,128)(2,1)S(1)}, bf16[96,1024]{1,0:T(8,128)(2,1)S(1)}, u32[]{:S(2)}, u32[]{:S(2)}) collective-permute-start(bf16[96,1024]{1,0:T(8,128)(2,1)S(1)} %get-tuple-element.36), channel_id=1, source_target_pairs={{0,10},{1,11},{2,8},{3,9},{4,14},{5,15},{6,12},{7,13},{8,18},{9,19... | collective-permute-start | bytes 589832 | tf_op jit(solution)/shard_map/ppermute | solution.py:281
  33.7 1.6 %products.5 = bf16[384,512]{1,0:T(8,128)(2,1)S(1)} custom-call(bf16[192,1024]{1,0:T(8,128)(2,1)S(1)} %collective-permute-done.5.refs_0_, bf16[192,1024]{1,0:T(8,128)(2,1)} %collective-permute-done.6.refs_1_.refs_3_, bf16[512,512]{1,0:T(8,128)(2,1)S(1)} %get-tuple-element.35.refs_3_.refs_2_, bf16[512,512]{1,0:T(8,128)(2,1)S(1)} %collective-permute-done.2.refs_4_.refs_3_), custom_call_target="tpu_custom_call" | custom-call | flops 1610612736 | bytes 3145728 | tf_op jit(solution)/shard_map/products/pallas_call | solution.py:99
  35.3 1.6 %collective-permute-start.7 = (bf16[384,512]{1,0:T(8,128)(2,1)S(1)}, bf16[384,512]{1,0:T(8,128)(2,1)S(1)}, u32[]{:S(2)}, u32[]{:S(2)}) collective-permute-start(bf16[384,512]{1,0:T(8,128)(2,1)S(1)} %products.5), channel_id=1, source_target_pairs={{0,1},{1,0},{2,3},{3,2},{4,5},{5,4},{6,7},{7,6},{8,9},{9,8},{10,11... | collective-permute-start | bytes 1179656 | tf_op jit(solution)/shard_map/ppermute | solution.py:25
  36.9 0.4 fusion
  37.5 9.1 %collective-permute-done.4.refs_2_ = bf16[96,1024]{1,0:T(8,128)(2,1)S(1)} collective-permute-done((bf16[96,1024]{1,0:T(8,128)(2,1)S(1)}, bf16[96,1024]{1,0:T(8,128)(2,1)S(1)}, u32[]{:S(2)}, u32[]{:S(2)}) %collective-permute-start.4) | collective-permute-done | bytes 196640 | tf_op jit(solution)/shard_map/ppermute | solution.py:281
  46.6 2.4 %collective-permute-done.3.refs_1_ = bf16[96,1024]{1,0:T(8,128)(2,1)S(1)} collective-permute-done((bf16[96,1024]{1,0:T(8,128)(2,1)S(1)}, bf16[96,1024]{1,0:T(8,128)(2,1)S(1)}, u32[]{:S(2)}, u32[]{:S(2)}) %collective-permute-start.3) | collective-permute-done | bytes 196640 | tf_op jit(solution)/shard_map/ppermute | solution.py:281
  49.1 0.7 products.4.held
  49.8 3.1 %collective-permute-start.8 = (bf16[192,512]{1,0:T(8,128)(2,1)S(1)}, bf16[192,512]{1,0:T(8,128)(2,1)S(1)}, u32[]{:S(2)}, u32[]{:S(2)}) collective-permute-start(bf16[192,512]{1,0:T(8,128)(2,1)S(1)} %get-tuple-element.24), channel_id=1, source_target_pairs={{0,2},{1,3},{2,0},{3,1},{4,6},{5,7},{6,4},{7,5},{8,10},{9,11},{10,... | collective-permute-start | bytes 589832 | tf_op jit(solution)/shard_map/ppermute | solution.py:25
  52.9 2.1 %collective-permute-done.12.refs_2_.refs_5_ = bf16[512,512]{1,0:T(8,128)(2,1)S(1)} collective-permute-done((bf16[512,512]{1,0:T(8,128)(2,1)S(1)}, bf16[512,512]{1,0:T(8,128)(2,1)S(1)}, u32[]{:S(2)}, u32[]{:S(2)}) %collective-permute-start.12) | collective-permute-done | bytes 524320 | tf_op jit(solution)/shard_map/ppermute | solution.py:25
  55.1 2.4 %products.7 = (bf16[192,512]{1,0:T(8,128)(2,1)}, bf16[192,512]{1,0:T(8,128)(2,1)S(1)}, bf16[192,512]{1,0:T(8,128)(2,1)S(1)}) custom-call(bf16[192,1024]{1,0:T(8,128)(2,1)S(1)} %copy-done.3, bf16[96,1024]{1,0:T(8,128)(2,1)S(1)} %collective-permute-done.3.refs_1_, bf16[96,1024]{1,0:T(8,128)(2,1)S(1)} %collective-permute-done.4.refs_2_, ...), custom_call_target="tpu_custom_call" | custom-call | flops 2415919104 | bytes 4718592 | tf_op jit(solution)/shard_map/products/pallas_call | solution.py:99
  57.4 1.6 %collective-permute-start.13 = (bf16[192,512]{1,0:T(8,128)(2,1)}, bf16[192,512]{1,0:T(8,128)(2,1)S(1)}, u32[]{:S(2)}, u32[]{:S(2)}) collective-permute-start(bf16[192,512]{1,0:T(8,128)(2,1)} %get-tuple-element.30), channel_id=1, source_target_pairs={{0,1},{1,0},{2,3},{3,2},{4,5},{5,4},{6,7},{7,6},{8,9},{9,8},{10,11... | collective-permute-start | bytes 589832 | tf_op jit(solution)/shard_map/ppermute | solution.py:25
  59.1 1.9 %collective-permute-start.15 = (bf16[192,512]{1,0:T(8,128)(2,1)S(1)}, bf16[192,512]{1,0:T(8,128)(2,1)S(1)}, u32[]{:S(2)}, u32[]{:S(2)}) collective-permute-start(bf16[192,512]{1,0:T(8,128)(2,1)S(1)} %get-tuple-element.32), channel_id=1, source_target_pairs={{0,3},{1,2},{2,1},{3,0},{4,7},{5,6},{6,5},{7,4},{8,11},{9,10},{10,... | collective-permute-start | bytes 589832 | tf_op jit(solution)/shard_map/ppermute | solution.py:25
  61.3 0.4 products.6.own
  61.7 3.0 %collective-permute-done.13.refs_0_ = bf16[192,512]{1,0:T(8,128)(2,1)S(1)} collective-permute-done((bf16[192,512]{1,0:T(8,128)(2,1)}, bf16[192,512]{1,0:T(8,128)(2,1)S(1)}, u32[]{:S(2)}, u32[]{:S(2)}) %collective-permute-start.13) | collective-permute-done | bytes 196640 | tf_op jit(solution)/shard_map/ppermute | solution.py:25
  64.7 1.1 %collective-permute-done.14.refs_1_ = bf16[192,512]{1,0:T(8,128)(2,1)S(1)} collective-permute-done((bf16[192,512]{1,0:T(8,128)(2,1)S(1)}, bf16[192,512]{1,0:T(8,128)(2,1)S(1)}, u32[]{:S(2)}, u32[]{:S(2)}) %collective-permute-start.14) | collective-permute-done | bytes 196640 | tf_op jit(solution)/shard_map/ppermute | solution.py:25
  65.8 2.9 %collective-permute-done.15.refs_2_ = bf16[192,512]{1,0:T(8,128)(2,1)S(1)} collective-permute-done((bf16[192,512]{1,0:T(8,128)(2,1)S(1)}, bf16[192,512]{1,0:T(8,128)(2,1)S(1)}, u32[]{:S(2)}, u32[]{:S(2)}) %collective-permute-start.15) | collective-permute-done | bytes 196640 | tf_op jit(solution)/shard_map/ppermute | solution.py:25
  68.8 0.7 collective-permute-start.16
  69.5 5.1 %collective-permute-done.9.refs_1_ = bf16[192,512]{1,0:T(8,128)(2,1)S(1)} collective-permute-done((bf16[192,512]{1,0:T(8,128)(2,1)S(1)}, bf16[192,512]{1,0:T(8,128)(2,1)S(1)}, u32[]{:S(2)}, u32[]{:S(2)}) %collective-permute-start.9) | collective-permute-done | bytes 196640 | tf_op jit(solution)/shard_map/ppermute | solution.py:25
  74.6 2.9 %collective-permute-start.11 = (bf16[192,512]{1,0:T(8,128)(2,1)S(1)}, bf16[192,512]{1,0:T(8,128)(2,1)S(1)}, u32[]{:S(2)}, u32[]{:S(2)}) collective-permute-start(bf16[192,512]{1,0:T(8,128)(2,1)S(1)} %broadcast_select_fusion), channel_id=1, source_target_pairs={{0,1},{1,2},{2,3},{3,4},{4,5},{5,6},{6,7},{7,0},{8,9},{9,10},{10,1... | collective-permute-start | bytes 589832 | tf_op jit(solution)/shard_map/ppermute | solution.py:25
  77.6 3.0 %collective-permute-done.16.refs_2_ = bf16[192,512]{1,0:T(8,128)(2,1)S(1)} collective-permute-done((bf16[192,512]{1,0:T(8,128)(2,1)S(1)}, bf16[192,512]{1,0:T(8,128)(2,1)S(1)}, u32[]{:S(2)}, u32[]{:S(2)}) %collective-permute-start.16) | collective-permute-done | bytes 196640 | tf_op jit(solution)/shard_map/ppermute | solution.py:25
  80.7 4.5 %collective-permute-done.11.refs_2_ = bf16[192,512]{1,0:T(8,128)(2,1)S(1)} collective-permute-done((bf16[192,512]{1,0:T(8,128)(2,1)S(1)}, bf16[192,512]{1,0:T(8,128)(2,1)S(1)}, u32[]{:S(2)}, u32[]{:S(2)}) %collective-permute-start.11) | collective-permute-done | bytes 196640 | tf_op jit(solution)/shard_map/ppermute | solution.py:25
  85.2 2.9 %collective-permute-done.10.refs_0_ = bf16[192,512]{1,0:T(8,128)(2,1)S(1)} collective-permute-done((bf16[192,512]{1,0:T(8,128)(2,1)S(1)}, bf16[192,512]{1,0:T(8,128)(2,1)S(1)}, u32[]{:S(2)}, u32[]{:S(2)}) %collective-permute-start.10) | collective-permute-done | bytes 196640 | tf_op jit(solution)/shard_map/ppermute | solution.py:25
  88.2 4.7 %scores.1 = (bf16[2,4,768,384]{3,2,1,0:T(8,128)(2,1)S(1)}, f32[2,4,96,128]{3,2,1,0:T(8,128)S(1)}, f32[2,32,96]{2,1,0:T(8,128)}) custom-call(s32[1]{0:T(128)} %bitcast.odd_ref, bf16[1,2,96,4096]{3,2,1,0:T(8,128)(2,1)S(1)} %copy-done.1, bf16[192,512]{1,0:T(8,128)(2,1)S(1)} %collective-permute-done.10.refs_0_, ...), custom_call_target="tpu_custom_call" | custom-call | flops 603979776 | bytes 8388608 | tf_op jit(solution)/shard_map/scores/pallas_call | solution.py:197
  92.9 2.5 %mixed_values.1 = bf16[1,2,96,4096]{3,2,1,0:T(8,128)(2,1)} custom-call(bf16[2,4,768,384]{3,2,1,0:T(8,128)(2,1)S(1)} %get-tuple-element.25.weights, f32[2,4,96,128]{3,2,1,0:T(8,128)S(1)} %get-tuple-element.26.sums, bf16[192,512]{1,0:T(8,128)(2,1)S(1)} %collective-permute-done.17.refs_0_, bf16[192,512]{1,0:T(8,128)(2,1)S(1)} %collective-permute-done.18.refs_1_, ...), custom_call_target="tpu_custom_call" | custom-call | flops 603979776 | bytes 8388608 | tf_op jit(solution)/shard_map/mixed_values/pallas_call | solution.py:242
  (50 shorter events, 1.8 us)
Async XLA Ops:
  0.6 6.4 %copy-start.5 = (s32[2,16]{1,0:T(2,128)S(1)}, s32[2,16]{1,0:T(2,128)}, u32[]{:S(2)}) copy-start(s32[2,16]{1,0:T(2,128)} %param.9) | copy-start | bytes 388
  0.6 6.9 %copy-start = (bf16[1,2,96,4096]{3,2,1,0:T(8,128)(2,1)S(1)}, bf16[1,2,96,4096]{3,2,1,0:T(8,128)(2,1)}, u32[]{:S(2)}) copy-start(bf16[1,2,96,4096]{3,2,1,0:T(8,128)(2,1)} %param.5) | copy-start | bytes 4718596
  0.7 6.9 %collective-permute-start = (bf16[1,4096]{1,0:T(2,128)(2,1)}, bf16[1,4096]{1,0:T(2,128)(2,1)S(1)}, u32[]{:S(2)}, u32[]{:S(2)}) collective-permute-start(bf16[1,4096]{1,0:T(2,128)(2,1)} %param.6), channel_id=1, source_target_pairs={{0,24},{8,0},{16,8},{24,16},{1,25},{9,1},{17,9},{25,17},{2,26},{10... | collective-permute-start | bytes 24584 | tf_op jit(solution)/shard_map/ppermute | solution.py:25
  4.3 25.7 %collective-permute-start.2 = (bf16[512,512]{1,0:T(8,128)(2,1)S(1)}, bf16[512,512]{1,0:T(8,128)(2,1)S(1)}, u32[]{:S(2)}, u32[]{:S(2)}) collective-permute-start(bf16[512,512]{1,0:T(8,128)(2,1)S(1)} %get-tuple-element.35.refs_3_.refs_2_), channel_id=1, source_target_pairs={{0,4},{1,5},{2,6},{3,7},{4,0},{5,1},{6,2},{7,3},{8,12},{9,13},{10,... | collective-permute-start | bytes 1572872 | tf_op jit(solution)/shard_map/ppermute | solution.py:25
  9.7 0.8 copy-start.4
  10.4 23.2 %collective-permute-start.5 = (bf16[192,1024]{1,0:T(8,128)(2,1)}, bf16[192,1024]{1,0:T(8,128)(2,1)S(1)}, u32[]{:S(2)}, u32[]{:S(2)}) collective-permute-start(bf16[192,1024]{1,0:T(8,128)(2,1)} %get-tuple-element.21), channel_id=1, source_target_pairs={{0,9},{1,8},{2,11},{3,10},{4,13},{5,12},{6,15},{7,14},{8,17},{9,16... | collective-permute-start | bytes 1179656 | tf_op jit(solution)/shard_map/ppermute | solution.py:281
  10.8 22.8 %collective-permute-start.6 = (bf16[192,1024]{1,0:T(8,128)(2,1)}, bf16[192,1024]{1,0:T(8,128)(2,1)}, u32[]{:S(2)}, u32[]{:S(2)}) collective-permute-start(bf16[192,1024]{1,0:T(8,128)(2,1)} %get-tuple-element.22), channel_id=1, source_target_pairs={{0,11},{1,10},{2,9},{3,8},{4,15},{5,14},{6,13},{7,12},{8,19},{9,18... | collective-permute-start | bytes 1179656 | tf_op jit(solution)/shard_map/ppermute | solution.py:281
  13.5 24.0 %collective-permute-start.1 = (bf16[192,1024]{1,0:T(8,128)(2,1)}, bf16[192,1024]{1,0:T(8,128)(2,1)S(1)}, u32[]{:S(2)}, u32[]{:S(2)}) collective-permute-start(bf16[192,1024]{1,0:T(8,128)(2,1)} %copy-done.4), channel_id=1, source_target_pairs={{0,8},{1,9},{2,10},{3,11},{4,12},{5,13},{6,14},{7,15},{8,16},{9,17... | collective-permute-start | bytes 1179656 | tf_op jit(solution)/shard_map/ppermute | solution.py:281
  30.0 25.1 %collective-permute-start.12 = (bf16[512,512]{1,0:T(8,128)(2,1)S(1)}, bf16[512,512]{1,0:T(8,128)(2,1)S(1)}, u32[]{:S(2)}, u32[]{:S(2)}) collective-permute-start(bf16[512,512]{1,0:T(8,128)(2,1)S(1)} %get-tuple-element.28.refs_1_.refs_4_), channel_id=1, source_target_pairs={{0,4},{1,5},{2,6},{3,7},{4,0},{5,1},{6,2},{7,3},{8,12},{9,13},{10,... | collective-permute-start | bytes 1572872 | tf_op jit(solution)/shard_map/ppermute | solution.py:25
  30.0 16.6 %collective-permute-start.4 = (bf16[96,1024]{1,0:T(8,128)(2,1)S(1)}, bf16[96,1024]{1,0:T(8,128)(2,1)S(1)}, u32[]{:S(2)}, u32[]{:S(2)}) collective-permute-start(bf16[96,1024]{1,0:T(8,128)(2,1)S(1)} %get-tuple-element.36), channel_id=1, source_target_pairs={{0,10},{1,11},{2,8},{3,9},{4,14},{5,15},{6,12},{7,13},{8,18},{9,19... | collective-permute-start | bytes 589832 | tf_op jit(solution)/shard_map/ppermute | solution.py:281
  33.6 1.7 %copy-start.2 = (bf16[192,1024]{1,0:T(8,128)(2,1)}, bf16[192,1024]{1,0:T(8,128)(2,1)S(1)}, u32[]{:S(2)}) copy-start(bf16[192,1024]{1,0:T(8,128)(2,1)S(1)} %collective-permute-done.5.refs_0_) | copy-start | bytes 1179652
  33.6 15.5 %collective-permute-start.3 = (bf16[96,1024]{1,0:T(8,128)(2,1)S(1)}, bf16[96,1024]{1,0:T(8,128)(2,1)S(1)}, u32[]{:S(2)}, u32[]{:S(2)}) collective-permute-start(bf16[96,1024]{1,0:T(8,128)(2,1)S(1)} %get-tuple-element.37), channel_id=1, source_target_pairs={{0,10},{1,11},{2,8},{3,9},{4,14},{5,15},{6,12},{7,13},{8,18},{9,19... | collective-permute-start | bytes 589832 | tf_op jit(solution)/shard_map/ppermute | solution.py:281
  35.3 14.4 %collective-permute-start.7 = (bf16[384,512]{1,0:T(8,128)(2,1)S(1)}, bf16[384,512]{1,0:T(8,128)(2,1)S(1)}, u32[]{:S(2)}, u32[]{:S(2)}) collective-permute-start(bf16[384,512]{1,0:T(8,128)(2,1)S(1)} %products.5), channel_id=1, source_target_pairs={{0,1},{1,0},{2,3},{3,2},{4,5},{5,4},{6,7},{7,6},{8,9},{9,8},{10,11... | collective-permute-start | bytes 1179656 | tf_op jit(solution)/shard_map/ppermute | solution.py:25
  37.5 17.6 %copy-start.3 = (bf16[192,1024]{1,0:T(8,128)(2,1)S(1)}, bf16[192,1024]{1,0:T(8,128)(2,1)}, u32[]{:S(2)}) copy-start(bf16[192,1024]{1,0:T(8,128)(2,1)} %copy-done.2) | copy-start | bytes 1179652
  49.8 11.1 %collective-permute-start.8 = (bf16[192,512]{1,0:T(8,128)(2,1)S(1)}, bf16[192,512]{1,0:T(8,128)(2,1)S(1)}, u32[]{:S(2)}, u32[]{:S(2)}) collective-permute-start(bf16[192,512]{1,0:T(8,128)(2,1)S(1)} %get-tuple-element.24), channel_id=1, source_target_pairs={{0,2},{1,3},{2,0},{3,1},{4,6},{5,7},{6,4},{7,5},{8,10},{9,11},{10,... | collective-permute-start | bytes 589832 | tf_op jit(solution)/shard_map/ppermute | solution.py:25
  57.4 7.2 %collective-permute-start.13 = (bf16[192,512]{1,0:T(8,128)(2,1)}, bf16[192,512]{1,0:T(8,128)(2,1)S(1)}, u32[]{:S(2)}, u32[]{:S(2)}) collective-permute-start(bf16[192,512]{1,0:T(8,128)(2,1)} %get-tuple-element.30), channel_id=1, source_target_pairs={{0,1},{1,0},{2,3},{3,2},{4,5},{5,4},{6,7},{7,6},{8,9},{9,8},{10,11... | collective-permute-start | bytes 589832 | tf_op jit(solution)/shard_map/ppermute | solution.py:25
  59.1 6.7 %collective-permute-start.14 = (bf16[192,512]{1,0:T(8,128)(2,1)S(1)}, bf16[192,512]{1,0:T(8,128)(2,1)S(1)}, u32[]{:S(2)}, u32[]{:S(2)}) collective-permute-start(bf16[192,512]{1,0:T(8,128)(2,1)S(1)} %get-tuple-element.31), channel_id=1, source_target_pairs={{0,2},{1,3},{2,0},{3,1},{4,6},{5,7},{6,4},{7,5},{8,10},{9,11},{10,... | collective-permute-start | bytes 589832 | tf_op jit(solution)/shard_map/ppermute | solution.py:25
  59.1 9.6 %collective-permute-start.15 = (bf16[192,512]{1,0:T(8,128)(2,1)S(1)}, bf16[192,512]{1,0:T(8,128)(2,1)S(1)}, u32[]{:S(2)}, u32[]{:S(2)}) collective-permute-start(bf16[192,512]{1,0:T(8,128)(2,1)S(1)} %get-tuple-element.32), channel_id=1, source_target_pairs={{0,3},{1,2},{2,1},{3,0},{4,7},{5,6},{6,5},{7,4},{8,11},{9,10},{10,... | collective-permute-start | bytes 589832 | tf_op jit(solution)/shard_map/ppermute | solution.py:25
  61.1 13.5 %collective-permute-start.9 = (bf16[192,512]{1,0:T(8,128)(2,1)S(1)}, bf16[192,512]{1,0:T(8,128)(2,1)S(1)}, u32[]{:S(2)}, u32[]{:S(2)}) collective-permute-start(bf16[192,512]{1,0:T(8,128)(2,1)S(1)} %key_sum.1.refs_3_), channel_id=1, source_target_pairs={{0,2},{1,3},{2,4},{3,5},{4,6},{5,7},{6,0},{7,1},{8,10},{9,11},{10,... | collective-permute-start | bytes 589832 | tf_op jit(solution)/shard_map/ppermute | solution.py:25
  61.7 26.5 %copy-start.1 = (bf16[1,2,96,4096]{3,2,1,0:T(8,128)(2,1)S(1)}, bf16[1,2,96,4096]{3,2,1,0:T(8,128)(2,1)}, u32[]{:S(2)}) copy-start(bf16[1,2,96,4096]{3,2,1,0:T(8,128)(2,1)} %q_ref.1) | copy-start | bytes 4718596
  68.8 11.8 %collective-permute-start.16 = (bf16[192,512]{1,0:T(8,128)(2,1)S(1)}, bf16[192,512]{1,0:T(8,128)(2,1)S(1)}, u32[]{:S(2)}, u32[]{:S(2)}) collective-permute-start(bf16[192,512]{1,0:T(8,128)(2,1)S(1)} %value_sum.1.refs_3_), channel_id=1, source_target_pairs={{0,1},{1,2},{2,3},{3,4},{4,5},{5,6},{6,7},{7,0},{8,9},{9,10},{10,1... | collective-permute-start | bytes 589832 | tf_op jit(solution)/shard_map/ppermute | solution.py:25
  74.6 10.6 %collective-permute-start.11 = (bf16[192,512]{1,0:T(8,128)(2,1)S(1)}, bf16[192,512]{1,0:T(8,128)(2,1)S(1)}, u32[]{:S(2)}, u32[]{:S(2)}) collective-permute-start(bf16[192,512]{1,0:T(8,128)(2,1)S(1)} %broadcast_select_fusion), channel_id=1, source_target_pairs={{0,1},{1,2},{2,3},{3,4},{4,5},{5,6},{6,7},{7,0},{8,9},{9,10},{10,1... | collective-permute-start | bytes 589832 | tf_op jit(solution)/shard_map/ppermute | solution.py:25
  77.5 10.7 %collective-permute-start.10 = (bf16[192,512]{1,0:T(8,128)(2,1)S(1)}, bf16[192,512]{1,0:T(8,128)(2,1)S(1)}, u32[]{:S(2)}, u32[]{:S(2)}) collective-permute-start(bf16[192,512]{1,0:T(8,128)(2,1)S(1)} %collective-permute-done.9.refs_1_), channel_id=1, source_target_pairs={{0,1},{1,0},{2,3},{3,2},{4,5},{5,4},{6,7},{7,6},{8,9},{9,8},{10,11... | collective-permute-start | bytes 589832 | tf_op jit(solution)/shard_map/ppermute | solution.py:25
  77.6 15.3 %collective-permute-start.18 = (bf16[192,512]{1,0:T(8,128)(2,1)S(1)}, bf16[192,512]{1,0:T(8,128)(2,1)S(1)}, u32[]{:S(2)}, u32[]{:S(2)}) collective-permute-start(bf16[192,512]{1,0:T(8,128)(2,1)S(1)} %value_sum.1.refs_3_), channel_id=1, source_target_pairs={{0,2},{1,3},{2,4},{3,5},{4,6},{5,7},{6,0},{7,1},{8,10},{9,11},{10,... | collective-permute-start | bytes 589832 | tf_op jit(solution)/shard_map/ppermute | solution.py:25
  80.6 12.4 %collective-permute-start.17 = (bf16[192,512]{1,0:T(8,128)(2,1)S(1)}, bf16[192,512]{1,0:T(8,128)(2,1)S(1)}, u32[]{:S(2)}, u32[]{:S(2)}) collective-permute-start(bf16[192,512]{1,0:T(8,128)(2,1)S(1)} %collective-permute-done.16.refs_2_), channel_id=1, source_target_pairs={{0,2},{1,3},{2,4},{3,5},{4,6},{5,7},{6,0},{7,1},{8,10},{9,11},{10,... | collective-permute-start | bytes 589832 | tf_op jit(solution)/shard_map/ppermute | solution.py:25

commit v15 on v14

--- a/solution.py
+++ b/solution.py
@@ -336,13 +336,13 @@
     key_z = over_z(onward_keys)
     value_shards, _ = lax.optimization_barrier((value_shards, onward_keys))
     value_products = products(
-        [first_cuts[:1], held_cuts[1:], first_cuts[1:]], value_shards, jnp.bfloat16
+        [held_cuts[1:], first_cuts[1:], first_cuts[:1]], value_shards, jnp.bfloat16
     )
     key_block = block_sum(key_sum_kernel, "key_sum", own_keys, [key_z], cosine, sine_part)
     key_two_back = moved(key_block, "ctx", lambda i: i + 2)
     value_parts = [
         moved(part, "ctx", lambda i, flip=flip: i ^ flip)
-        for flip, part in enumerate(value_products, start=1)
+        for flip, part in zip((2, 3, 1), value_products)
     ]
     (own_values,) = products([held_cuts[:1]], value_shards, jnp.float32)
     weights, sums, log_sums = scored(

time: 95.6 us -> 95.6 us (level)
  no operation moved by 1% of the time
where the time goes in v15:
time: 95.6 us; the launch traced here: 95.4 us
  waiting for transfers between devices  53 us (55%)
  starting transfers between devices  23.6 us (25%)
  Pallas kernels  14.6 us (15%)
  local copies, waits for them, and re-layouts  2.59 us (3%)
    ppermute x14, waiting for transfers between devices, moved(): lax.ppermute(block, axis, [(i, target(i) % size) for i in range(size)])  41.4 us
    ppermute x14, starting transfers between devices, moved(): lax.ppermute(block, axis, [(i, target(i) % size) for i in range(size)])  16.9 us
    ppermute x5, waiting for transfers between devices, to_next_section(): return lax.ppermute(part, ('section', 'ctx'), route)  11.6 us
    ppermute x5, starting transfers between devices, to_next_section(): return lax.ppermute(part, ('section', 'ctx'), route)  6.64 us
    pallas_call x4, Pallas kernels, products(): pl.pallas_call(lambda *refs: product_kernel(counts, *refs), out_shape=[ja...  4.98 us
    pallas_call x1, Pallas kernels, scored(): pl.pallas_call(score_kernel, grid=(micro_count,), in_specs=[pl.BlockSpec(...  4.75 us
    pallas_call x1, Pallas kernels, mixed_values(): pl.pallas_call(mix_kernel, grid=(micro_count,), in_specs=[pl.BlockSpec((1...  2.5 us
    pallas_call x1, Pallas kernels, normed_cuts(): pl.pallas_call(norm_kernel, grid=(micro_count,), in_specs=[pl.BlockSpec(m...  2.08 us
  transfers between devices with their start and end apart: 19, of which 11 were waited for; matrix products, arithmetic and copies ran while one was open for 3% of the time, Pallas kernels for 13%

profile of v15, /device:TPU:0, one launch (start us, length us, event | category | flops | bytes accessed | tf_op | source)
XLA Modules:
  0.0 95.4 jit_solution(7055122281175949745)
XLA Ops:
  0.7 2.4 %collective-permute-start = (bf16[1,4096]{1,0:T(2,128)(2,1)}, bf16[1,4096]{1,0:T(2,128)(2,1)S(1)}, u32[]{:S(2)}, u32[]{:S(2)}) collective-permute-start(bf16[1,4096]{1,0:T(2,128)(2,1)} %param.6), channel_id=1, source_target_pairs={{0,24},{8,0},{16,8},{24,16},{1,25},{9,1},{17,9},{25,17},{2,26},{10... | collective-permute-start | bytes 24584 | tf_op jit(solution)/shard_map/ppermute | solution.py:25
  3.1 1.3 %fusion.4 = (bf16[512,512]{1,0:T(8,128)(2,1)S(1)}, bf16[512,512]{1,0:T(8,128)(2,1)S(1)}) fusion(bf16[512,1024]{1,0:T(8,128)(2,1)} %bitcast.7), kind=kLoop, calls=%fused_computation.21 | loop fusion | bytes 2097152 | tf_op jit(solution)/shard_map/slice | solution.py:289
  4.3 2.7 %collective-permute-start.2 = (bf16[512,512]{1,0:T(8,128)(2,1)S(1)}, bf16[512,512]{1,0:T(8,128)(2,1)S(1)}, u32[]{:S(2)}, u32[]{:S(2)}) collective-permute-start(bf16[512,512]{1,0:T(8,128)(2,1)S(1)} %get-tuple-element.35.refs_3_.refs_2_), channel_id=1, source_target_pairs={{0,4},{1,5},{2,6},{3,7},{4,0},{5,1},{6,2},{7,3},{8,12},{9,13},{10,... | collective-permute-start | bytes 1572872 | tf_op jit(solution)/shard_map/ppermute | solution.py:25
  7.6 2.1 %norm_cuts.1 = (bf16[192,1024]{1,0:T(8,128)(2,1)S(1)}, bf16[192,1024]{1,0:T(8,128)(2,1)}, bf16[192,1024]{1,0:T(8,128)(2,1)S(1)}, bf16[192,1024]{1,0:T(8,128)(2,1)}) custom-call(s32[4,2]{1,0:T(4,128)S(1)} %add_multiply_fusion.starts_ref, bf16[2,96,4096]{2,1,0:T(8,128)(2,1)S(1)} %bitcast.6, f32[1,4096]{1,0:T(1,128)S(1)} %convert_element_type.16.gain_ref), custom_call_target="tpu_custom_call" | custom-call | flops 4718592 | bytes 3145728 | tf_op jit(solution)/shard_map/norm_cuts/pallas_call | solution.py:58
  9.7 0.8 copy-done.4
  10.4 0.4 collective-permute-start.5
  10.8 2.5 %collective-permute-start.6 = (bf16[192,1024]{1,0:T(8,128)(2,1)}, bf16[192,1024]{1,0:T(8,128)(2,1)}, u32[]{:S(2)}, u32[]{:S(2)}) collective-permute-start(bf16[192,1024]{1,0:T(8,128)(2,1)} %get-tuple-element.22), channel_id=1, source_target_pairs={{0,11},{1,10},{2,9},{3,8},{4,15},{5,14},{6,13},{7,12},{8,19},{9,18... | collective-permute-start | bytes 1179656 | tf_op jit(solution)/shard_map/ppermute | solution.py:281
  13.6 16.4 %collective-permute-done.2.refs_4_.refs_3_ = bf16[512,512]{1,0:T(8,128)(2,1)S(1)} collective-permute-done((bf16[512,512]{1,0:T(8,128)(2,1)S(1)}, bf16[512,512]{1,0:T(8,128)(2,1)S(1)}, u32[]{:S(2)}, u32[]{:S(2)}) %collective-permute-start.2) | collective-permute-done | bytes 524320 | tf_op jit(solution)/shard_map/ppermute | solution.py:25
  30.0 3.5 %collective-permute-start.4 = (bf16[96,1024]{1,0:T(8,128)(2,1)S(1)}, bf16[96,1024]{1,0:T(8,128)(2,1)S(1)}, u32[]{:S(2)}, u32[]{:S(2)}) collective-permute-start(bf16[96,1024]{1,0:T(8,128)(2,1)S(1)} %get-tuple-element.36), channel_id=1, source_target_pairs={{0,10},{1,11},{2,8},{3,9},{4,14},{5,15},{6,12},{7,13},{8,18},{9,19... | collective-permute-start | bytes 589832 | tf_op jit(solution)/shard_map/ppermute | solution.py:281
  33.7 1.6 %products.5 = bf16[384,512]{1,0:T(8,128)(2,1)S(1)} custom-call(bf16[192,1024]{1,0:T(8,128)(2,1)S(1)} %collective-permute-done.5.refs_0_.refs_3_, bf16[192,1024]{1,0:T(8,128)(2,1)} %collective-permute-done.6.refs_1_.refs_2_, bf16[512,512]{1,0:T(8,128)(2,1)S(1)} %get-tuple-element.35.refs_3_.refs_2_, bf16[512,512]{1,0:T(8,128)(2,1)S(1)} %collective-permute-done.2.refs_4_.refs_3_), custom_call_target="tpu_custom_call" | custom-call | flops 1610612736 | bytes 3145728 | tf_op jit(solution)/shard_map/products/pallas_call | solution.py:99
  35.3 1.6 %collective-permute-start.7 = (bf16[384,512]{1,0:T(8,128)(2,1)S(1)}, bf16[384,512]{1,0:T(8,128)(2,1)S(1)}, u32[]{:S(2)}, u32[]{:S(2)}) collective-permute-start(bf16[384,512]{1,0:T(8,128)(2,1)S(1)} %products.5), channel_id=1, source_target_pairs={{0,1},{1,0},{2,3},{3,2},{4,5},{5,4},{6,7},{7,6},{8,9},{9,8},{10,11... | collective-permute-start | bytes 1179656 | tf_op jit(solution)/shard_map/ppermute | solution.py:25
  36.9 0.4 fusion
  37.5 9.1 %collective-permute-done.4.refs_2_.refs_1_ = bf16[96,1024]{1,0:T(8,128)(2,1)S(1)} collective-permute-done((bf16[96,1024]{1,0:T(8,128)(2,1)S(1)}, bf16[96,1024]{1,0:T(8,128)(2,1)S(1)}, u32[]{:S(2)}, u32[]{:S(2)}) %collective-permute-start.4) | collective-permute-done | bytes 196640 | tf_op jit(solution)/shard_map/ppermute | solution.py:281
  46.6 2.4 %collective-permute-done.3.refs_1_.refs_0_ = bf16[96,1024]{1,0:T(8,128)(2,1)S(1)} collective-permute-done((bf16[96,1024]{1,0:T(8,128)(2,1)S(1)}, bf16[96,1024]{1,0:T(8,128)(2,1)S(1)}, u32[]{:S(2)}, u32[]{:S(2)}) %collective-permute-start.3) | collective-permute-done | bytes 196640 | tf_op jit(solution)/shard_map/ppermute | solution.py:281
  49.1 0.7 products.4.held
  49.8 3.1 %collective-permute-start.8 = (bf16[192,512]{1,0:T(8,128)(2,1)S(1)}, bf16[192,512]{1,0:T(8,128)(2,1)S(1)}, u32[]{:S(2)}, u32[]{:S(2)}) collective-permute-start(bf16[192,512]{1,0:T(8,128)(2,1)S(1)} %get-tuple-element.24), channel_id=1, source_target_pairs={{0,2},{1,3},{2,0},{3,1},{4,6},{5,7},{6,4},{7,5},{8,10},{9,11},{10,... | collective-permute-start | bytes 589832 | tf_op jit(solution)/shard_map/ppermute | solution.py:25
  52.9 2.1 %collective-permute-done.12.refs_2_.refs_5_ = bf16[512,512]{1,0:T(8,128)(2,1)S(1)} collective-permute-done((bf16[512,512]{1,0:T(8,128)(2,1)S(1)}, bf16[512,512]{1,0:T(8,128)(2,1)S(1)}, u32[]{:S(2)}, u32[]{:S(2)}) %collective-permute-start.12) | collective-permute-done | bytes 524320 | tf_op jit(solution)/shard_map/ppermute | solution.py:25
  55.1 2.3 %products.7 = (bf16[192,512]{1,0:T(8,128)(2,1)}, bf16[192,512]{1,0:T(8,128)(2,1)S(1)}, bf16[192,512]{1,0:T(8,128)(2,1)S(1)}) custom-call(bf16[96,1024]{1,0:T(8,128)(2,1)S(1)} %collective-permute-done.3.refs_1_.refs_0_, bf16[96,1024]{1,0:T(8,128)(2,1)S(1)} %collective-permute-done.4.refs_2_.refs_1_, bf16[192,1024]{1,0:T(8,128)(2,1)} %collective-permute-done.6.refs_1_.refs_2_, ...), custom_call_target="tpu_custom_call" | custom-call | flops 2415919104 | bytes 4718592 | tf_op jit(solution)/shard_map/products/pallas_call | solution.py:99
  57.3 3.1 %collective-permute-start.14 = (bf16[192,512]{1,0:T(8,128)(2,1)S(1)}, bf16[192,512]{1,0:T(8,128)(2,1)S(1)}, u32[]{:S(2)}, u32[]{:S(2)}) collective-permute-start(bf16[192,512]{1,0:T(8,128)(2,1)S(1)} %get-tuple-element.31), channel_id=1, source_target_pairs={{0,3},{1,2},{2,1},{3,0},{4,7},{5,6},{6,5},{7,4},{8,11},{9,10},{10,... | collective-permute-start | bytes 589832 | tf_op jit(solution)/shard_map/ppermute | solution.py:25
  60.4 0.4 collective-permute-start.15
  61.2 0.4 products.6.own
  61.6 3.8 %collective-permute-done.13.refs_0_ = bf16[192,512]{1,0:T(8,128)(2,1)S(1)} collective-permute-done((bf16[192,512]{1,0:T(8,128)(2,1)}, bf16[192,512]{1,0:T(8,128)(2,1)S(1)}, u32[]{:S(2)}, u32[]{:S(2)}) %collective-permute-start.13) | collective-permute-done | bytes 196640 | tf_op jit(solution)/shard_map/ppermute | solution.py:25
  65.4 3.4 %collective-permute-done.14.refs_1_ = bf16[192,512]{1,0:T(8,128)(2,1)S(1)} collective-permute-done((bf16[192,512]{1,0:T(8,128)(2,1)S(1)}, bf16[192,512]{1,0:T(8,128)(2,1)S(1)}, u32[]{:S(2)}, u32[]{:S(2)}) %collective-permute-start.14) | collective-permute-done | bytes 196640 | tf_op jit(solution)/shard_map/ppermute | solution.py:25
  68.8 0.8 collective-permute-done.15.refs_2_
  69.6 0.5 collective-permute-start.16
  70.1 4.5 %collective-permute-done.9.refs_1_ = bf16[192,512]{1,0:T(8,128)(2,1)S(1)} collective-permute-done((bf16[192,512]{1,0:T(8,128)(2,1)S(1)}, bf16[192,512]{1,0:T(8,128)(2,1)S(1)}, u32[]{:S(2)}, u32[]{:S(2)}) %collective-permute-start.9) | collective-permute-done | bytes 196640 | tf_op jit(solution)/shard_map/ppermute | solution.py:25
  74.6 2.9 %collective-permute-start.11 = (bf16[192,512]{1,0:T(8,128)(2,1)S(1)}, bf16[192,512]{1,0:T(8,128)(2,1)S(1)}, u32[]{:S(2)}, u32[]{:S(2)}) collective-permute-start(bf16[192,512]{1,0:T(8,128)(2,1)S(1)} %broadcast_select_fusion), channel_id=1, source_target_pairs={{0,1},{1,2},{2,3},{3,4},{4,5},{5,6},{6,7},{7,0},{8,9},{9,10},{10,1... | collective-permute-start | bytes 589832 | tf_op jit(solution)/shard_map/ppermute | solution.py:25
  77.6 3.2 %collective-permute-done.16.refs_2_ = bf16[192,512]{1,0:T(8,128)(2,1)S(1)} collective-permute-done((bf16[192,512]{1,0:T(8,128)(2,1)S(1)}, bf16[192,512]{1,0:T(8,128)(2,1)S(1)}, u32[]{:S(2)}, u32[]{:S(2)}) %collective-permute-start.16) | collective-permute-done | bytes 196640 | tf_op jit(solution)/shard_map/ppermute | solution.py:25
  80.9 4.3 %collective-permute-done.11.refs_2_ = bf16[192,512]{1,0:T(8,128)(2,1)S(1)} collective-permute-done((bf16[192,512]{1,0:T(8,128)(2,1)S(1)}, bf16[192,512]{1,0:T(8,128)(2,1)S(1)}, u32[]{:S(2)}, u32[]{:S(2)}) %collective-permute-start.11) | collective-permute-done | bytes 196640 | tf_op jit(solution)/shard_map/ppermute | solution.py:25
  85.2 2.9 %collective-permute-done.10.refs_0_ = bf16[192,512]{1,0:T(8,128)(2,1)S(1)} collective-permute-done((bf16[192,512]{1,0:T(8,128)(2,1)S(1)}, bf16[192,512]{1,0:T(8,128)(2,1)S(1)}, u32[]{:S(2)}, u32[]{:S(2)}) %collective-permute-start.10) | collective-permute-done | bytes 196640 | tf_op jit(solution)/shard_map/ppermute | solution.py:25
  88.2 4.7 %scores.1 = (bf16[2,4,768,384]{3,2,1,0:T(8,128)(2,1)S(1)}, f32[2,4,96,128]{3,2,1,0:T(8,128)S(1)}, f32[2,32,96]{2,1,0:T(8,128)}) custom-call(s32[1]{0:T(128)} %bitcast.odd_ref, bf16[1,2,96,4096]{3,2,1,0:T(8,128)(2,1)S(1)} %copy-done.1, bf16[192,512]{1,0:T(8,128)(2,1)S(1)} %collective-permute-done.10.refs_0_, ...), custom_call_target="tpu_custom_call" | custom-call | flops 603979776 | bytes 8388608 | tf_op jit(solution)/shard_map/scores/pallas_call | solution.py:197
  92.9 2.5 %mixed_values.1 = bf16[1,2,96,4096]{3,2,1,0:T(8,128)(2,1)} custom-call(bf16[2,4,768,384]{3,2,1,0:T(8,128)(2,1)S(1)} %get-tuple-element.25.weights, f32[2,4,96,128]{3,2,1,0:T(8,128)S(1)} %get-tuple-element.26.sums, bf16[192,512]{1,0:T(8,128)(2,1)S(1)} %collective-permute-done.17.refs_0_, bf16[192,512]{1,0:T(8,128)(2,1)S(1)} %collective-permute-done.18.refs_1_, ...), custom_call_target="tpu_custom_call" | custom-call | flops 603979776 | bytes 8388608 | tf_op jit(solution)/shard_map/mixed_values/pallas_call | solution.py:242
  (50 shorter events, 1.8 us)
Async XLA Ops:
  0.6 6.4 %copy-start.5 = (s32[2,16]{1,0:T(2,128)S(1)}, s32[2,16]{1,0:T(2,128)}, u32[]{:S(2)}) copy-start(s32[2,16]{1,0:T(2,128)} %param.9) | copy-start | bytes 388
  0.6 6.9 %copy-start = (bf16[1,2,96,4096]{3,2,1,0:T(8,128)(2,1)S(1)}, bf16[1,2,96,4096]{3,2,1,0:T(8,128)(2,1)}, u32[]{:S(2)}) copy-start(bf16[1,2,96,4096]{3,2,1,0:T(8,128)(2,1)} %param.5) | copy-start | bytes 4718596
  0.7 6.9 %collective-permute-start = (bf16[1,4096]{1,0:T(2,128)(2,1)}, bf16[1,4096]{1,0:T(2,128)(2,1)S(1)}, u32[]{:S(2)}, u32[]{:S(2)}) collective-permute-start(bf16[1,4096]{1,0:T(2,128)(2,1)} %param.6), channel_id=1, source_target_pairs={{0,24},{8,0},{16,8},{24,16},{1,25},{9,1},{17,9},{25,17},{2,26},{10... | collective-permute-start | bytes 24584 | tf_op jit(solution)/shard_map/ppermute | solution.py:25
  4.3 25.7 %collective-permute-start.2 = (bf16[512,512]{1,0:T(8,128)(2,1)S(1)}, bf16[512,512]{1,0:T(8,128)(2,1)S(1)}, u32[]{:S(2)}, u32[]{:S(2)}) collective-permute-start(bf16[512,512]{1,0:T(8,128)(2,1)S(1)} %get-tuple-element.35.refs_3_.refs_2_), channel_id=1, source_target_pairs={{0,4},{1,5},{2,6},{3,7},{4,0},{5,1},{6,2},{7,3},{8,12},{9,13},{10,... | collective-permute-start | bytes 1572872 | tf_op jit(solution)/shard_map/ppermute | solution.py:25
  9.7 0.8 copy-start.4
  10.4 23.2 %collective-permute-start.5 = (bf16[192,1024]{1,0:T(8,128)(2,1)}, bf16[192,1024]{1,0:T(8,128)(2,1)S(1)}, u32[]{:S(2)}, u32[]{:S(2)}) collective-permute-start(bf16[192,1024]{1,0:T(8,128)(2,1)} %get-tuple-element.21), channel_id=1, source_target_pairs={{0,9},{1,8},{2,11},{3,10},{4,13},{5,12},{6,15},{7,14},{8,17},{9,16... | collective-permute-start | bytes 1179656 | tf_op jit(solution)/shard_map/ppermute | solution.py:281
  10.8 22.8 %collective-permute-start.6 = (bf16[192,1024]{1,0:T(8,128)(2,1)}, bf16[192,1024]{1,0:T(8,128)(2,1)}, u32[]{:S(2)}, u32[]{:S(2)}) collective-permute-start(bf16[192,1024]{1,0:T(8,128)(2,1)} %get-tuple-element.22), channel_id=1, source_target_pairs={{0,11},{1,10},{2,9},{3,8},{4,15},{5,14},{6,13},{7,12},{8,19},{9,18... | collective-permute-start | bytes 1179656 | tf_op jit(solution)/shard_map/ppermute | solution.py:281
  13.5 24.0 %collective-permute-start.1 = (bf16[192,1024]{1,0:T(8,128)(2,1)}, bf16[192,1024]{1,0:T(8,128)(2,1)S(1)}, u32[]{:S(2)}, u32[]{:S(2)}) collective-permute-start(bf16[192,1024]{1,0:T(8,128)(2,1)} %copy-done.4), channel_id=1, source_target_pairs={{0,8},{1,9},{2,10},{3,11},{4,12},{5,13},{6,14},{7,15},{8,16},{9,17... | collective-permute-start | bytes 1179656 | tf_op jit(solution)/shard_map/ppermute | solution.py:281
  30.0 25.1 %collective-permute-start.12 = (bf16[512,512]{1,0:T(8,128)(2,1)S(1)}, bf16[512,512]{1,0:T(8,128)(2,1)S(1)}, u32[]{:S(2)}, u32[]{:S(2)}) collective-permute-start(bf16[512,512]{1,0:T(8,128)(2,1)S(1)} %get-tuple-element.28.refs_1_.refs_4_), channel_id=1, source_target_pairs={{0,4},{1,5},{2,6},{3,7},{4,0},{5,1},{6,2},{7,3},{8,12},{9,13},{10,... | collective-permute-start | bytes 1572872 | tf_op jit(solution)/shard_map/ppermute | solution.py:25
  30.0 16.6 %collective-permute-start.4 = (bf16[96,1024]{1,0:T(8,128)(2,1)S(1)}, bf16[96,1024]{1,0:T(8,128)(2,1)S(1)}, u32[]{:S(2)}, u32[]{:S(2)}) collective-permute-start(bf16[96,1024]{1,0:T(8,128)(2,1)S(1)} %get-tuple-element.36), channel_id=1, source_target_pairs={{0,10},{1,11},{2,8},{3,9},{4,14},{5,15},{6,12},{7,13},{8,18},{9,19... | collective-permute-start | bytes 589832 | tf_op jit(solution)/shard_map/ppermute | solution.py:281
  33.6 1.7 %copy-start.2 = (bf16[192,1024]{1,0:T(8,128)(2,1)}, bf16[192,1024]{1,0:T(8,128)(2,1)S(1)}, u32[]{:S(2)}) copy-start(bf16[192,1024]{1,0:T(8,128)(2,1)S(1)} %collective-permute-done.5.refs_0_.refs_3_) | copy-start | bytes 1179652
  33.6 15.5 %collective-permute-start.3 = (bf16[96,1024]{1,0:T(8,128)(2,1)S(1)}, bf16[96,1024]{1,0:T(8,128)(2,1)S(1)}, u32[]{:S(2)}, u32[]{:S(2)}) collective-permute-start(bf16[96,1024]{1,0:T(8,128)(2,1)S(1)} %get-tuple-element.37), channel_id=1, source_target_pairs={{0,10},{1,11},{2,8},{3,9},{4,14},{5,15},{6,12},{7,13},{8,18},{9,19... | collective-permute-start | bytes 589832 | tf_op jit(solution)/shard_map/ppermute | solution.py:281
  35.3 14.4 %collective-permute-start.7 = (bf16[384,512]{1,0:T(8,128)(2,1)S(1)}, bf16[384,512]{1,0:T(8,128)(2,1)S(1)}, u32[]{:S(2)}, u32[]{:S(2)}) collective-permute-start(bf16[384,512]{1,0:T(8,128)(2,1)S(1)} %products.5), channel_id=1, source_target_pairs={{0,1},{1,0},{2,3},{3,2},{4,5},{5,4},{6,7},{7,6},{8,9},{9,8},{10,11... | collective-permute-start | bytes 1179656 | tf_op jit(solution)/shard_map/ppermute | solution.py:25
  37.5 17.6 %copy-start.3 = (bf16[192,1024]{1,0:T(8,128)(2,1)S(1)}, bf16[192,1024]{1,0:T(8,128)(2,1)}, u32[]{:S(2)}) copy-start(bf16[192,1024]{1,0:T(8,128)(2,1)} %copy-done.2) | copy-start | bytes 1179652
  49.8 11.0 %collective-permute-start.8 = (bf16[192,512]{1,0:T(8,128)(2,1)S(1)}, bf16[192,512]{1,0:T(8,128)(2,1)S(1)}, u32[]{:S(2)}, u32[]{:S(2)}) collective-permute-start(bf16[192,512]{1,0:T(8,128)(2,1)S(1)} %get-tuple-element.24), channel_id=1, source_target_pairs={{0,2},{1,3},{2,0},{3,1},{4,6},{5,7},{6,4},{7,5},{8,10},{9,11},{10,... | collective-permute-start | bytes 589832 | tf_op jit(solution)/shard_map/ppermute | solution.py:25
  57.3 8.0 %collective-permute-start.13 = (bf16[192,512]{1,0:T(8,128)(2,1)}, bf16[192,512]{1,0:T(8,128)(2,1)S(1)}, u32[]{:S(2)}, u32[]{:S(2)}) collective-permute-start(bf16[192,512]{1,0:T(8,128)(2,1)} %get-tuple-element.30), channel_id=1, source_target_pairs={{0,2},{1,3},{2,0},{3,1},{4,6},{5,7},{6,4},{7,5},{8,10},{9,11},{10,... | collective-permute-start | bytes 589832 | tf_op jit(solution)/shard_map/ppermute | solution.py:25
  57.3 11.4 %collective-permute-start.14 = (bf16[192,512]{1,0:T(8,128)(2,1)S(1)}, bf16[192,512]{1,0:T(8,128)(2,1)S(1)}, u32[]{:S(2)}, u32[]{:S(2)}) collective-permute-start(bf16[192,512]{1,0:T(8,128)(2,1)S(1)} %get-tuple-element.31), channel_id=1, source_target_pairs={{0,3},{1,2},{2,1},{3,0},{4,7},{5,6},{6,5},{7,4},{8,11},{9,10},{10,... | collective-permute-start | bytes 589832 | tf_op jit(solution)/shard_map/ppermute | solution.py:25
  60.4 9.1 %collective-permute-start.15 = (bf16[192,512]{1,0:T(8,128)(2,1)S(1)}, bf16[192,512]{1,0:T(8,128)(2,1)S(1)}, u32[]{:S(2)}, u32[]{:S(2)}) collective-permute-start(bf16[192,512]{1,0:T(8,128)(2,1)S(1)} %get-tuple-element.32), channel_id=1, source_target_pairs={{0,1},{1,0},{2,3},{3,2},{4,5},{5,4},{6,7},{7,6},{8,9},{9,8},{10,11... | collective-permute-start | bytes 589832 | tf_op jit(solution)/shard_map/ppermute | solution.py:25
  61.0 13.6 %collective-permute-start.9 = (bf16[192,512]{1,0:T(8,128)(2,1)S(1)}, bf16[192,512]{1,0:T(8,128)(2,1)S(1)}, u32[]{:S(2)}, u32[]{:S(2)}) collective-permute-start(bf16[192,512]{1,0:T(8,128)(2,1)S(1)} %key_sum.1.refs_3_), channel_id=1, source_target_pairs={{0,2},{1,3},{2,4},{3,5},{4,6},{5,7},{6,0},{7,1},{8,10},{9,11},{10,... | collective-permute-start | bytes 589832 | tf_op jit(solution)/shard_map/ppermute | solution.py:25
  61.6 26.6 %copy-start.1 = (bf16[1,2,96,4096]{3,2,1,0:T(8,128)(2,1)S(1)}, bf16[1,2,96,4096]{3,2,1,0:T(8,128)(2,1)}, u32[]{:S(2)}) copy-start(bf16[1,2,96,4096]{3,2,1,0:T(8,128)(2,1)} %q_ref.1) | copy-start | bytes 4718596
  69.6 11.2 %collective-permute-start.16 = (bf16[192,512]{1,0:T(8,128)(2,1)S(1)}, bf16[192,512]{1,0:T(8,128)(2,1)S(1)}, u32[]{:S(2)}, u32[]{:S(2)}) collective-permute-start(bf16[192,512]{1,0:T(8,128)(2,1)S(1)} %value_sum.1.refs_3_), channel_id=1, source_target_pairs={{0,1},{1,2},{2,3},{3,4},{4,5},{5,6},{6,7},{7,0},{8,9},{9,10},{10,1... | collective-permute-start | bytes 589832 | tf_op jit(solution)/shard_map/ppermute | solution.py:25
  74.6 10.6 %collective-permute-start.11 = (bf16[192,512]{1,0:T(8,128)(2,1)S(1)}, bf16[192,512]{1,0:T(8,128)(2,1)S(1)}, u32[]{:S(2)}, u32[]{:S(2)}) collective-permute-start(bf16[192,512]{1,0:T(8,128)(2,1)S(1)} %broadcast_select_fusion), channel_id=1, source_target_pairs={{0,1},{1,2},{2,3},{3,4},{4,5},{5,6},{6,7},{7,0},{8,9},{9,10},{10,1... | collective-permute-start | bytes 589832 | tf_op jit(solution)/shard_map/ppermute | solution.py:25
  77.5 10.7 %collective-permute-start.10 = (bf16[192,512]{1,0:T(8,128)(2,1)S(1)}, bf16[192,512]{1,0:T(8,128)(2,1)S(1)}, u32[]{:S(2)}, u32[]{:S(2)}) collective-permute-start(bf16[192,512]{1,0:T(8,128)(2,1)S(1)} %collective-permute-done.9.refs_1_), channel_id=1, source_target_pairs={{0,1},{1,0},{2,3},{3,2},{4,5},{5,4},{6,7},{7,6},{8,9},{9,8},{10,11... | collective-permute-start | bytes 589832 | tf_op jit(solution)/shard_map/ppermute | solution.py:25
  77.6 15.3 %collective-permute-start.18 = (bf16[192,512]{1,0:T(8,128)(2,1)S(1)}, bf16[192,512]{1,0:T(8,128)(2,1)S(1)}, u32[]{:S(2)}, u32[]{:S(2)}) collective-permute-start(bf16[192,512]{1,0:T(8,128)(2,1)S(1)} %value_sum.1.refs_3_), channel_id=1, source_target_pairs={{0,2},{1,3},{2,4},{3,5},{4,6},{5,7},{6,0},{7,1},{8,10},{9,11},{10,... | collective-permute-start | bytes 589832 | tf_op jit(solution)/shard_map/ppermute | solution.py:25
  80.8 12.1 %collective-permute-start.17 = (bf16[192,512]{1,0:T(8,128)(2,1)S(1)}, bf16[192,512]{1,0:T(8,128)(2,1)S(1)}, u32[]{:S(2)}, u32[]{:S(2)}) collective-permute-start(bf16[192,512]{1,0:T(8,128)(2,1)S(1)} %collective-permute-done.16.refs_2_), channel_id=1, source_target_pairs={{0,2},{1,3},{2,4},{3,5},{4,6},{5,7},{6,0},{7,1},{8,10},{9,11},{10,... | collective-permute-start | bytes 589832 | tf_op jit(solution)/shard_map/ppermute | solution.py:25

commit v16 on v15

--- a/solution.py
+++ b/solution.py
@@ -335,11 +335,10 @@
     own_keys, onward_keys = half_sum(key_held, key_y)
     key_z = over_z(onward_keys)
     value_shards, _ = lax.optimization_barrier((value_shards, onward_keys))
-    value_products = products(
-        [held_cuts[1:], first_cuts[1:], first_cuts[:1]], value_shards, jnp.bfloat16
-    )
+    value_products = products([held_cuts[1:], first_cuts[1:]], value_shards, jnp.bfloat16)
     key_block = block_sum(key_sum_kernel, "key_sum", own_keys, [key_z], cosine, sine_part)
     key_two_back = moved(key_block, "ctx", lambda i: i + 2)
+    value_products += products([first_cuts[:1]], value_shards, jnp.bfloat16)
     value_parts = [
         moved(part, "ctx", lambda i, flip=flip: i ^ flip)
         for flip, part in zip((2, 3, 1), value_products)

time: 95.6 us -> 95.5 us (level)
  waiting for transfers between devices: 53 us -> 54 us
    pallas_call x4 -> x5, Pallas kernels: 4.98 us -> 4.05 us  [products(): pl.pallas_call(lambda *refs: product_kernel(counts, *refs), out_shape=[ja...]
  transfers between devices with their start and end apart: 19 -> 19, of which waited for: 11 -> 11; matrix products, arithmetic and copies ran while one was open for 3% -> 3% of each run, Pallas kernels for 13% -> 12%
where the time goes in v16:
time: 95.5 us; the launch traced here: 95.3 us
  waiting for transfers between devices  54 us (57%)
  starting transfers between devices  23.1 us (24%)
  Pallas kernels  13.7 us (14%)
  local copies, waits for them, and re-layouts  2.81 us (3%)
    ppermute x14, waiting for transfers between devices, moved(): lax.ppermute(block, axis, [(i, target(i) % size) for i in range(size)])  41.6 us
    ppermute x14, starting transfers between devices, moved(): lax.ppermute(block, axis, [(i, target(i) % size) for i in range(size)])  16.6 us
    ppermute x5, waiting for transfers between devices, to_next_section(): return lax.ppermute(part, ('section', 'ctx'), route)  12.5 us
    ppermute x5, starting transfers between devices, to_next_section(): return lax.ppermute(part, ('section', 'ctx'), route)  6.53 us
    pallas_call x1, Pallas kernels, scored(): pl.pallas_call(score_kernel, grid=(micro_count,), in_specs=[pl.BlockSpec(...  4.74 us
    pallas_call x5, Pallas kernels, products(): pl.pallas_call(lambda *refs: product_kernel(counts, *refs), out_shape=[ja...  4.05 us
    pallas_call x1, Pallas kernels, mixed_values(): pl.pallas_call(mix_kernel, grid=(micro_count,), in_specs=[pl.BlockSpec((1...  2.5 us
    pallas_call x1, Pallas kernels, normed_cuts(): pl.pallas_call(norm_kernel, grid=(micro_count,), in_specs=[pl.BlockSpec(m...  2.07 us
  transfers between devices with their start and end apart: 19, of which 11 were waited for; matrix products, arithmetic and copies ran while one was open for 3% of the time, Pallas kernels for 12%

profile of v16, /device:TPU:0, one launch (start us, length us, event | category | flops | bytes accessed | tf_op | source)
XLA Modules:
  0.0 95.3 jit_solution(15680980754809810560)
XLA Ops:
  0.7 2.4 %collective-permute-start = (bf16[1,4096]{1,0:T(2,128)(2,1)}, bf16[1,4096]{1,0:T(2,128)(2,1)S(1)}, u32[]{:S(2)}, u32[]{:S(2)}) collective-permute-start(bf16[1,4096]{1,0:T(2,128)(2,1)} %param.6), channel_id=1, source_target_pairs={{0,24},{8,0},{16,8},{24,16},{1,25},{9,1},{17,9},{25,17},{2,26},{10... | collective-permute-start | bytes 24584 | tf_op jit(solution)/shard_map/ppermute | solution.py:25
  3.1 1.3 %fusion.4 = (bf16[512,512]{1,0:T(8,128)(2,1)S(1)}, bf16[512,512]{1,0:T(8,128)(2,1)S(1)}) fusion(bf16[512,1024]{1,0:T(8,128)(2,1)} %bitcast.7), kind=kLoop, calls=%fused_computation.21 | loop fusion | bytes 2097152 | tf_op jit(solution)/shard_map/slice | solution.py:289
  4.3 2.7 %collective-permute-start.2 = (bf16[512,512]{1,0:T(8,128)(2,1)S(1)}, bf16[512,512]{1,0:T(8,128)(2,1)S(1)}, u32[]{:S(2)}, u32[]{:S(2)}) collective-permute-start(bf16[512,512]{1,0:T(8,128)(2,1)S(1)} %get-tuple-element.33.refs_3_.refs_2_), channel_id=1, source_target_pairs={{0,4},{1,5},{2,6},{3,7},{4,0},{5,1},{6,2},{7,3},{8,12},{9,13},{10,... | collective-permute-start | bytes 1572872 | tf_op jit(solution)/shard_map/ppermute | solution.py:25
  7.6 2.1 %norm_cuts.1 = (bf16[192,1024]{1,0:T(8,128)(2,1)S(1)}, bf16[192,1024]{1,0:T(8,128)(2,1)}, bf16[192,1024]{1,0:T(8,128)(2,1)S(1)}, bf16[192,1024]{1,0:T(8,128)(2,1)}) custom-call(s32[4,2]{1,0:T(4,128)S(1)} %add_multiply_fusion.starts_ref, bf16[2,96,4096]{2,1,0:T(8,128)(2,1)S(1)} %bitcast.6, f32[1,4096]{1,0:T(1,128)S(1)} %convert_element_type.16.gain_ref), custom_call_target="tpu_custom_call" | custom-call | flops 4718592 | bytes 3145728 | tf_op jit(solution)/shard_map/norm_cuts/pallas_call | solution.py:58
  9.7 0.7 copy-done.8
  10.4 0.4 collective-permute-start.5
  10.8 2.5 %collective-permute-start.6 = (bf16[192,1024]{1,0:T(8,128)(2,1)}, bf16[192,1024]{1,0:T(8,128)(2,1)S(1)}, u32[]{:S(2)}, u32[]{:S(2)}) collective-permute-start(bf16[192,1024]{1,0:T(8,128)(2,1)} %get-tuple-element.21), channel_id=1, source_target_pairs={{0,11},{1,10},{2,9},{3,8},{4,15},{5,14},{6,13},{7,12},{8,19},{9,18... | collective-permute-start | bytes 1179656 | tf_op jit(solution)/shard_map/ppermute | solution.py:281
  13.6 16.4 %collective-permute-done.2.refs_4_.refs_3_ = bf16[512,512]{1,0:T(8,128)(2,1)S(1)} collective-permute-done((bf16[512,512]{1,0:T(8,128)(2,1)S(1)}, bf16[512,512]{1,0:T(8,128)(2,1)S(1)}, u32[]{:S(2)}, u32[]{:S(2)}) %collective-permute-start.2) | collective-permute-done | bytes 524320 | tf_op jit(solution)/shard_map/ppermute | solution.py:25
  30.0 3.4 %collective-permute-start.4 = (bf16[96,1024]{1,0:T(8,128)(2,1)S(1)}, bf16[96,1024]{1,0:T(8,128)(2,1)S(1)}, u32[]{:S(2)}, u32[]{:S(2)}) collective-permute-start(bf16[96,1024]{1,0:T(8,128)(2,1)S(1)} %get-tuple-element.34), channel_id=1, source_target_pairs={{0,10},{1,11},{2,8},{3,9},{4,14},{5,15},{6,12},{7,13},{8,18},{9,19... | collective-permute-start | bytes 589832 | tf_op jit(solution)/shard_map/ppermute | solution.py:281
  33.6 0.6 products.6
  34.4 1.5 %collective-permute-start.7 = (bf16[384,512]{1,0:T(8,128)(2,1)S(1)}, bf16[384,512]{1,0:T(8,128)(2,1)S(1)}, u32[]{:S(2)}, u32[]{:S(2)}) collective-permute-start(bf16[384,512]{1,0:T(8,128)(2,1)S(1)} %products.6), channel_id=1, source_target_pairs={{0,1},{1,0},{2,3},{3,2},{4,5},{5,4},{6,7},{7,6},{8,9},{9,8},{10,11... | collective-permute-start | bytes 1179656 | tf_op jit(solution)/shard_map/ppermute | solution.py:25
  35.9 0.4 fusion
  36.5 10.2 %collective-permute-done.4.refs_2_.refs_1_ = bf16[96,1024]{1,0:T(8,128)(2,1)S(1)} collective-permute-done((bf16[96,1024]{1,0:T(8,128)(2,1)S(1)}, bf16[96,1024]{1,0:T(8,128)(2,1)S(1)}, u32[]{:S(2)}, u32[]{:S(2)}) %collective-permute-start.4) | collective-permute-done | bytes 196640 | tf_op jit(solution)/shard_map/ppermute | solution.py:281
  46.7 2.3 %collective-permute-done.3.refs_1_.refs_0_ = bf16[96,1024]{1,0:T(8,128)(2,1)S(1)} collective-permute-done((bf16[96,1024]{1,0:T(8,128)(2,1)S(1)}, bf16[96,1024]{1,0:T(8,128)(2,1)S(1)}, u32[]{:S(2)}, u32[]{:S(2)}) %collective-permute-start.3) | collective-permute-done | bytes 196640 | tf_op jit(solution)/shard_map/ppermute | solution.py:281
  48.9 0.7 products.5.held
  49.8 3.0 %collective-permute-start.8 = (bf16[192,512]{1,0:T(8,128)(2,1)S(1)}, bf16[192,512]{1,0:T(8,128)(2,1)S(1)}, u32[]{:S(2)}, u32[]{:S(2)}) collective-permute-start(bf16[192,512]{1,0:T(8,128)(2,1)S(1)} %get-tuple-element.23), channel_id=1, source_target_pairs={{0,2},{1,3},{2,0},{3,1},{4,6},{5,7},{6,4},{7,5},{8,10},{9,11},{10,... | collective-permute-start | bytes 589832 | tf_op jit(solution)/shard_map/ppermute | solution.py:25
  52.7 2.2 %collective-permute-done.12.refs_2_.refs_4_ = bf16[512,512]{1,0:T(8,128)(2,1)S(1)} collective-permute-done((bf16[512,512]{1,0:T(8,128)(2,1)S(1)}, bf16[512,512]{1,0:T(8,128)(2,1)S(1)}, u32[]{:S(2)}, u32[]{:S(2)}) %collective-permute-start.12) | collective-permute-done | bytes 524320 | tf_op jit(solution)/shard_map/ppermute | solution.py:25
  55.0 1.4 %products.8 = (bf16[192,512]{1,0:T(8,128)(2,1)}, bf16[192,512]{1,0:T(8,128)(2,1)}) custom-call(bf16[96,1024]{1,0:T(8,128)(2,1)S(1)} %collective-permute-done.3.refs_1_.refs_0_, bf16[96,1024]{1,0:T(8,128)(2,1)S(1)} %collective-permute-done.4.refs_2_.refs_1_, bf16[192,1024]{1,0:T(8,128)(2,1)S(1)} %copy-done.7, ...), custom_call_target="tpu_custom_call" | custom-call | flops 1610612736 | bytes 3145728 | tf_op jit(solution)/shard_map/products/pallas_call | solution.py:99
  56.3 3.1 %collective-permute-start.14 = (bf16[192,512]{1,0:T(8,128)(2,1)}, bf16[192,512]{1,0:T(8,128)(2,1)S(1)}, u32[]{:S(2)}, u32[]{:S(2)}) collective-permute-start(bf16[192,512]{1,0:T(8,128)(2,1)} %get-tuple-element.30), channel_id=1, source_target_pairs={{0,3},{1,2},{2,1},{3,0},{4,7},{5,6},{6,5},{7,4},{8,11},{9,10},{10,... | collective-permute-start | bytes 589832 | tf_op jit(solution)/shard_map/ppermute | solution.py:25
  59.4 1.0 %products.9 = bf16[192,512]{1,0:T(8,128)(2,1)} custom-call(bf16[192,1024]{1,0:T(8,128)(2,1)S(1)} %copy-done.5, bf16[512,512]{1,0:T(8,128)(2,1)S(1)} %get-tuple-element.27.refs_1_.refs_3_, bf16[512,512]{1,0:T(8,128)(2,1)S(1)} %collective-permute-done.12.refs_2_.refs_4_), custom_call_target="tpu_custom_call" | custom-call | flops 805306368 | bytes 1572864 | tf_op jit(solution)/shard_map/products/pallas_call | solution.py:99
  60.5 0.4 collective-permute-start.15
  61.6 2.7 %collective-permute-done.13.refs_0_ = bf16[192,512]{1,0:T(8,128)(2,1)S(1)} collective-permute-done((bf16[192,512]{1,0:T(8,128)(2,1)}, bf16[192,512]{1,0:T(8,128)(2,1)S(1)}, u32[]{:S(2)}, u32[]{:S(2)}) %collective-permute-start.13) | collective-permute-done | bytes 196640 | tf_op jit(solution)/shard_map/ppermute | solution.py:25
  64.4 4.3 %collective-permute-done.14.refs_1_ = bf16[192,512]{1,0:T(8,128)(2,1)S(1)} collective-permute-done((bf16[192,512]{1,0:T(8,128)(2,1)}, bf16[192,512]{1,0:T(8,128)(2,1)S(1)}, u32[]{:S(2)}, u32[]{:S(2)}) %collective-permute-start.14) | collective-permute-done | bytes 196640 | tf_op jit(solution)/shard_map/ppermute | solution.py:25
  68.7 1.4 %collective-permute-done.15.refs_2_ = bf16[192,512]{1,0:T(8,128)(2,1)S(1)} collective-permute-done((bf16[192,512]{1,0:T(8,128)(2,1)}, bf16[192,512]{1,0:T(8,128)(2,1)S(1)}, u32[]{:S(2)}, u32[]{:S(2)}) %collective-permute-start.15) | collective-permute-done | bytes 196640 | tf_op jit(solution)/shard_map/ppermute | solution.py:25
  70.1 0.5 collective-permute-start.16
  70.6 3.9 %collective-permute-done.9.refs_1_ = bf16[192,512]{1,0:T(8,128)(2,1)S(1)} collective-permute-done((bf16[192,512]{1,0:T(8,128)(2,1)S(1)}, bf16[192,512]{1,0:T(8,128)(2,1)S(1)}, u32[]{:S(2)}, u32[]{:S(2)}) %collective-permute-start.9) | collective-permute-done | bytes 196640 | tf_op jit(solution)/shard_map/ppermute | solution.py:25
  74.5 2.8 %collective-permute-start.11 = (bf16[192,512]{1,0:T(8,128)(2,1)S(1)}, bf16[192,512]{1,0:T(8,128)(2,1)S(1)}, u32[]{:S(2)}, u32[]{:S(2)}) collective-permute-start(bf16[192,512]{1,0:T(8,128)(2,1)S(1)} %broadcast_select_fusion), channel_id=1, source_target_pairs={{0,1},{1,2},{2,3},{3,4},{4,5},{5,6},{6,7},{7,0},{8,9},{9,10},{10,1... | collective-permute-start | bytes 589832 | tf_op jit(solution)/shard_map/ppermute | solution.py:25
  77.4 3.2 %collective-permute-done.16.refs_2_ = bf16[192,512]{1,0:T(8,128)(2,1)S(1)} collective-permute-done((bf16[192,512]{1,0:T(8,128)(2,1)S(1)}, bf16[192,512]{1,0:T(8,128)(2,1)S(1)}, u32[]{:S(2)}, u32[]{:S(2)}) %collective-permute-start.16) | collective-permute-done | bytes 196640 | tf_op jit(solution)/shard_map/ppermute | solution.py:25
  80.7 4.5 %collective-permute-done.11.refs_2_ = bf16[192,512]{1,0:T(8,128)(2,1)S(1)} collective-permute-done((bf16[192,512]{1,0:T(8,128)(2,1)S(1)}, bf16[192,512]{1,0:T(8,128)(2,1)S(1)}, u32[]{:S(2)}, u32[]{:S(2)}) %collective-permute-start.11) | collective-permute-done | bytes 196640 | tf_op jit(solution)/shard_map/ppermute | solution.py:25
  85.2 2.9 %collective-permute-done.10.refs_0_ = bf16[192,512]{1,0:T(8,128)(2,1)S(1)} collective-permute-done((bf16[192,512]{1,0:T(8,128)(2,1)S(1)}, bf16[192,512]{1,0:T(8,128)(2,1)S(1)}, u32[]{:S(2)}, u32[]{:S(2)}) %collective-permute-start.10) | collective-permute-done | bytes 196640 | tf_op jit(solution)/shard_map/ppermute | solution.py:25
  88.1 4.7 %scores.1 = (bf16[2,4,768,384]{3,2,1,0:T(8,128)(2,1)S(1)}, f32[2,4,96,128]{3,2,1,0:T(8,128)S(1)}, f32[2,32,96]{2,1,0:T(8,128)}) custom-call(s32[1]{0:T(128)} %bitcast.odd_ref, bf16[1,2,96,4096]{3,2,1,0:T(8,128)(2,1)S(1)} %copy-done.1, bf16[192,512]{1,0:T(8,128)(2,1)S(1)} %collective-permute-done.10.refs_0_, ...), custom_call_target="tpu_custom_call" | custom-call | flops 603979776 | bytes 8388608 | tf_op jit(solution)/shard_map/scores/pallas_call | solution.py:197
  92.8 2.5 %mixed_values.1 = bf16[1,2,96,4096]{3,2,1,0:T(8,128)(2,1)} custom-call(bf16[2,4,768,384]{3,2,1,0:T(8,128)(2,1)S(1)} %get-tuple-element.24.weights, f32[2,4,96,128]{3,2,1,0:T(8,128)S(1)} %get-tuple-element.25.sums, bf16[192,512]{1,0:T(8,128)(2,1)S(1)} %collective-permute-done.17.refs_0_, bf16[192,512]{1,0:T(8,128)(2,1)S(1)} %collective-permute-done.18.refs_1_, ...), custom_call_target="tpu_custom_call" | custom-call | flops 603979776 | bytes 8388608 | tf_op jit(solution)/shard_map/mixed_values/pallas_call | solution.py:242
  (59 shorter events, 2.4 us)
Async XLA Ops:
  0.6 6.4 %copy-start.9 = (s32[2,16]{1,0:T(2,128)S(1)}, s32[2,16]{1,0:T(2,128)}, u32[]{:S(2)}) copy-start(s32[2,16]{1,0:T(2,128)} %param.9) | copy-start | bytes 388
  0.6 6.9 %copy-start = (bf16[1,2,96,4096]{3,2,1,0:T(8,128)(2,1)S(1)}, bf16[1,2,96,4096]{3,2,1,0:T(8,128)(2,1)}, u32[]{:S(2)}) copy-start(bf16[1,2,96,4096]{3,2,1,0:T(8,128)(2,1)} %param.5) | copy-start | bytes 4718596
  0.7 6.9 %collective-permute-start = (bf16[1,4096]{1,0:T(2,128)(2,1)}, bf16[1,4096]{1,0:T(2,128)(2,1)S(1)}, u32[]{:S(2)}, u32[]{:S(2)}) collective-permute-start(bf16[1,4096]{1,0:T(2,128)(2,1)} %param.6), channel_id=1, source_target_pairs={{0,24},{8,0},{16,8},{24,16},{1,25},{9,1},{17,9},{25,17},{2,26},{10... | collective-permute-start | bytes 24584 | tf_op jit(solution)/shard_map/ppermute | solution.py:25
  4.3 25.7 %collective-permute-start.2 = (bf16[512,512]{1,0:T(8,128)(2,1)S(1)}, bf16[512,512]{1,0:T(8,128)(2,1)S(1)}, u32[]{:S(2)}, u32[]{:S(2)}) collective-permute-start(bf16[512,512]{1,0:T(8,128)(2,1)S(1)} %get-tuple-element.33.refs_3_.refs_2_), channel_id=1, source_target_pairs={{0,4},{1,5},{2,6},{3,7},{4,0},{5,1},{6,2},{7,3},{8,12},{9,13},{10,... | collective-permute-start | bytes 1572872 | tf_op jit(solution)/shard_map/ppermute | solution.py:25
  9.7 0.7 copy-start.8
  10.4 23.1 %collective-permute-start.5 = (bf16[192,1024]{1,0:T(8,128)(2,1)}, bf16[192,1024]{1,0:T(8,128)(2,1)S(1)}, u32[]{:S(2)}, u32[]{:S(2)}) collective-permute-start(bf16[192,1024]{1,0:T(8,128)(2,1)} %get-tuple-element.20), channel_id=1, source_target_pairs={{0,9},{1,8},{2,11},{3,10},{4,13},{5,12},{6,15},{7,14},{8,17},{9,16... | collective-permute-start | bytes 1179656 | tf_op jit(solution)/shard_map/ppermute | solution.py:281
  10.8 22.8 %collective-permute-start.6 = (bf16[192,1024]{1,0:T(8,128)(2,1)}, bf16[192,1024]{1,0:T(8,128)(2,1)S(1)}, u32[]{:S(2)}, u32[]{:S(2)}) collective-permute-start(bf16[192,1024]{1,0:T(8,128)(2,1)} %get-tuple-element.21), channel_id=1, source_target_pairs={{0,11},{1,10},{2,9},{3,8},{4,15},{5,14},{6,13},{7,12},{8,19},{9,18... | collective-permute-start | bytes 1179656 | tf_op jit(solution)/shard_map/ppermute | solution.py:281
  13.5 23.0 %collective-permute-start.1 = (bf16[192,1024]{1,0:T(8,128)(2,1)}, bf16[192,1024]{1,0:T(8,128)(2,1)S(1)}, u32[]{:S(2)}, u32[]{:S(2)}) collective-permute-start(bf16[192,1024]{1,0:T(8,128)(2,1)} %copy-done.8), channel_id=1, source_target_pairs={{0,8},{1,9},{2,10},{3,11},{4,12},{5,13},{6,14},{7,15},{8,16},{9,17... | collective-permute-start | bytes 1179656 | tf_op jit(solution)/shard_map/ppermute | solution.py:281
  30.0 24.9 %collective-permute-start.12 = (bf16[512,512]{1,0:T(8,128)(2,1)S(1)}, bf16[512,512]{1,0:T(8,128)(2,1)S(1)}, u32[]{:S(2)}, u32[]{:S(2)}) collective-permute-start(bf16[512,512]{1,0:T(8,128)(2,1)S(1)} %get-tuple-element.27.refs_1_.refs_3_), channel_id=1, source_target_pairs={{0,4},{1,5},{2,6},{3,7},{4,0},{5,1},{6,2},{7,3},{8,12},{9,13},{10,... | collective-permute-start | bytes 1572872 | tf_op jit(solution)/shard_map/ppermute | solution.py:25
  30.0 16.6 %collective-permute-start.4 = (bf16[96,1024]{1,0:T(8,128)(2,1)S(1)}, bf16[96,1024]{1,0:T(8,128)(2,1)S(1)}, u32[]{:S(2)}, u32[]{:S(2)}) collective-permute-start(bf16[96,1024]{1,0:T(8,128)(2,1)S(1)} %get-tuple-element.34), channel_id=1, source_target_pairs={{0,10},{1,11},{2,8},{3,9},{4,14},{5,15},{6,12},{7,13},{8,18},{9,19... | collective-permute-start | bytes 589832 | tf_op jit(solution)/shard_map/ppermute | solution.py:281
  33.5 0.7 copy-start.4
  33.5 15.5 %collective-permute-start.3 = (bf16[96,1024]{1,0:T(8,128)(2,1)S(1)}, bf16[96,1024]{1,0:T(8,128)(2,1)S(1)}, u32[]{:S(2)}, u32[]{:S(2)}) collective-permute-start(bf16[96,1024]{1,0:T(8,128)(2,1)S(1)} %get-tuple-element.35), channel_id=1, source_target_pairs={{0,10},{1,11},{2,8},{3,9},{4,14},{5,15},{6,12},{7,13},{8,18},{9,19... | collective-permute-start | bytes 589832 | tf_op jit(solution)/shard_map/ppermute | solution.py:281
  33.6 0.8 copy-start.6
  34.4 15.3 %collective-permute-start.7 = (bf16[384,512]{1,0:T(8,128)(2,1)S(1)}, bf16[384,512]{1,0:T(8,128)(2,1)S(1)}, u32[]{:S(2)}, u32[]{:S(2)}) collective-permute-start(bf16[384,512]{1,0:T(8,128)(2,1)S(1)} %products.6), channel_id=1, source_target_pairs={{0,1},{1,0},{2,3},{3,2},{4,5},{5,4},{6,7},{7,6},{8,9},{9,8},{10,11... | collective-permute-start | bytes 1179656 | tf_op jit(solution)/shard_map/ppermute | solution.py:25
  36.5 18.5 %copy-start.7 = (bf16[192,1024]{1,0:T(8,128)(2,1)S(1)}, bf16[192,1024]{1,0:T(8,128)(2,1)}, u32[]{:S(2)}) copy-start(bf16[192,1024]{1,0:T(8,128)(2,1)} %copy-done.6) | copy-start | bytes 1179652
  36.5 13.2 %copy-start.2 = (bf16[192,1024]{1,0:T(8,128)(2,1)}, bf16[192,1024]{1,0:T(8,128)(2,1)S(1)}, u32[]{:S(2)}) copy-start(bf16[192,1024]{1,0:T(8,128)(2,1)S(1)} %collective-permute-done.1.refs_0_) | copy-start | bytes 1179652
  49.7 9.7 %copy-start.5 = (bf16[192,1024]{1,0:T(8,128)(2,1)S(1)}, bf16[192,1024]{1,0:T(8,128)(2,1)}, u32[]{:S(2)}) copy-start(bf16[192,1024]{1,0:T(8,128)(2,1)} %copy-done.4) | copy-start | bytes 1179652
  49.8 11.1 %collective-permute-start.8 = (bf16[192,512]{1,0:T(8,128)(2,1)S(1)}, bf16[192,512]{1,0:T(8,128)(2,1)S(1)}, u32[]{:S(2)}, u32[]{:S(2)}) collective-permute-start(bf16[192,512]{1,0:T(8,128)(2,1)S(1)} %get-tuple-element.23), channel_id=1, source_target_pairs={{0,2},{1,3},{2,0},{3,1},{4,6},{5,7},{6,4},{7,5},{8,10},{9,11},{10,... | collective-permute-start | bytes 589832 | tf_op jit(solution)/shard_map/ppermute | solution.py:25
  56.3 8.0 %collective-permute-start.13 = (bf16[192,512]{1,0:T(8,128)(2,1)}, bf16[192,512]{1,0:T(8,128)(2,1)S(1)}, u32[]{:S(2)}, u32[]{:S(2)}) collective-permute-start(bf16[192,512]{1,0:T(8,128)(2,1)} %get-tuple-element.29), channel_id=1, source_target_pairs={{0,2},{1,3},{2,0},{3,1},{4,6},{5,7},{6,4},{7,5},{8,10},{9,11},{10,... | collective-permute-start | bytes 589832 | tf_op jit(solution)/shard_map/ppermute | solution.py:25
  56.3 4.9 %copy-start.3 = (bf16[192,1024]{1,0:T(8,128)(2,1)S(1)}, bf16[192,1024]{1,0:T(8,128)(2,1)}, u32[]{:S(2)}) copy-start(bf16[192,1024]{1,0:T(8,128)(2,1)} %copy-done.2) | copy-start | bytes 1179652
  56.3 12.3 %collective-permute-start.14 = (bf16[192,512]{1,0:T(8,128)(2,1)}, bf16[192,512]{1,0:T(8,128)(2,1)S(1)}, u32[]{:S(2)}, u32[]{:S(2)}) collective-permute-start(bf16[192,512]{1,0:T(8,128)(2,1)} %get-tuple-element.30), channel_id=1, source_target_pairs={{0,3},{1,2},{2,1},{3,0},{4,7},{5,6},{6,5},{7,4},{8,11},{9,10},{10,... | collective-permute-start | bytes 589832 | tf_op jit(solution)/shard_map/ppermute | solution.py:25
  60.5 9.6 %collective-permute-start.15 = (bf16[192,512]{1,0:T(8,128)(2,1)}, bf16[192,512]{1,0:T(8,128)(2,1)S(1)}, u32[]{:S(2)}, u32[]{:S(2)}) collective-permute-start(bf16[192,512]{1,0:T(8,128)(2,1)} %products.9), channel_id=1, source_target_pairs={{0,1},{1,0},{2,3},{3,2},{4,5},{5,4},{6,7},{7,6},{8,9},{9,8},{10,11... | collective-permute-start | bytes 589832 | tf_op jit(solution)/shard_map/ppermute | solution.py:25
  61.0 13.5 %collective-permute-start.9 = (bf16[192,512]{1,0:T(8,128)(2,1)S(1)}, bf16[192,512]{1,0:T(8,128)(2,1)S(1)}, u32[]{:S(2)}, u32[]{:S(2)}) collective-permute-start(bf16[192,512]{1,0:T(8,128)(2,1)S(1)} %key_sum.1.refs_3_), channel_id=1, source_target_pairs={{0,2},{1,3},{2,4},{3,5},{4,6},{5,7},{6,0},{7,1},{8,10},{9,11},{10,... | collective-permute-start | bytes 589832 | tf_op jit(solution)/shard_map/ppermute | solution.py:25
  61.6 26.5 %copy-start.1 = (bf16[1,2,96,4096]{3,2,1,0:T(8,128)(2,1)S(1)}, bf16[1,2,96,4096]{3,2,1,0:T(8,128)(2,1)}, u32[]{:S(2)}) copy-start(bf16[1,2,96,4096]{3,2,1,0:T(8,128)(2,1)} %q_ref.1) | copy-start | bytes 4718596
  70.1 10.4 %collective-permute-start.16 = (bf16[192,512]{1,0:T(8,128)(2,1)S(1)}, bf16[192,512]{1,0:T(8,128)(2,1)S(1)}, u32[]{:S(2)}, u32[]{:S(2)}) collective-permute-start(bf16[192,512]{1,0:T(8,128)(2,1)S(1)} %value_sum.1.refs_3_), channel_id=1, source_target_pairs={{0,1},{1,2},{2,3},{3,4},{4,5},{5,6},{6,7},{7,0},{8,9},{9,10},{10,1... | collective-permute-start | bytes 589832 | tf_op jit(solution)/shard_map/ppermute | solution.py:25
  74.5 10.6 %collective-permute-start.11 = (bf16[192,512]{1,0:T(8,128)(2,1)S(1)}, bf16[192,512]{1,0:T(8,128)(2,1)S(1)}, u32[]{:S(2)}, u32[]{:S(2)}) collective-permute-start(bf16[192,512]{1,0:T(8,128)(2,1)S(1)} %broadcast_select_fusion), channel_id=1, source_target_pairs={{0,1},{1,2},{2,3},{3,4},{4,5},{5,6},{6,7},{7,0},{8,9},{9,10},{10,1... | collective-permute-start | bytes 589832 | tf_op jit(solution)/shard_map/ppermute | solution.py:25
  77.3 10.8 %collective-permute-start.10 = (bf16[192,512]{1,0:T(8,128)(2,1)S(1)}, bf16[192,512]{1,0:T(8,128)(2,1)S(1)}, u32[]{:S(2)}, u32[]{:S(2)}) collective-permute-start(bf16[192,512]{1,0:T(8,128)(2,1)S(1)} %collective-permute-done.9.refs_1_), channel_id=1, source_target_pairs={{0,1},{1,0},{2,3},{3,2},{4,5},{5,4},{6,7},{7,6},{8,9},{9,8},{10,11... | collective-permute-start | bytes 589832 | tf_op jit(solution)/shard_map/ppermute | solution.py:25
  77.4 15.5 %collective-permute-start.18 = (bf16[192,512]{1,0:T(8,128)(2,1)S(1)}, bf16[192,512]{1,0:T(8,128)(2,1)S(1)}, u32[]{:S(2)}, u32[]{:S(2)}) collective-permute-start(bf16[192,512]{1,0:T(8,128)(2,1)S(1)} %value_sum.1.refs_3_), channel_id=1, source_target_pairs={{0,2},{1,3},{2,4},{3,5},{4,6},{5,7},{6,0},{7,1},{8,10},{9,11},{10,... | collective-permute-start | bytes 589832 | tf_op jit(solution)/shard_map/ppermute | solution.py:25
  80.6 12.3 %collective-permute-start.17 = (bf16[192,512]{1,0:T(8,128)(2,1)S(1)}, bf16[192,512]{1,0:T(8,128)(2,1)S(1)}, u32[]{:S(2)}, u32[]{:S(2)}) collective-permute-start(bf16[192,512]{1,0:T(8,128)(2,1)S(1)} %collective-permute-done.16.refs_2_), channel_id=1, source_target_pairs={{0,2},{1,3},{2,4},{3,5},{4,6},{5,7},{6,0},{7,1},{8,10},{9,11},{10,... | collective-permute-start | bytes 589832 | tf_op jit(solution)/shard_map/ppermute | solution.py:25

commit v17 on v16

--- a/solution.py
+++ b/solution.py
@@ -338,7 +338,8 @@
     value_products = products([held_cuts[1:], first_cuts[1:]], value_shards, jnp.bfloat16)
     key_block = block_sum(key_sum_kernel, "key_sum", own_keys, [key_z], cosine, sine_part)
     key_two_back = moved(key_block, "ctx", lambda i: i + 2)
-    value_products += products([first_cuts[:1]], value_shards, jnp.bfloat16)
+    last_shards, _ = lax.optimization_barrier((value_shards, key_block))
+    value_products += products([first_cuts[:1]], last_shards, jnp.bfloat16)
     value_parts = [
         moved(part, "ctx", lambda i, flip=flip: i ^ flip)
         for flip, part in zip((2, 3, 1), value_products)

time: 95.5 us -> 103 us (1.079)
  waiting for transfers between devices: 54 us -> 58.5 us
  Pallas kernels: 13.7 us -> 15.1 us
  starting transfers between devices: 23.1 us -> 24.5 us
    ppermute x5, waiting for transfers between devices: 12.5 us -> 20 us  [to_next_section(): return lax.ppermute(part, ('section', 'ctx'), route)]
    ppermute x14, waiting for transfers between devices: 41.6 us -> 38.5 us  [moved(): lax.ppermute(block, axis, [(i, target(i) % size) for i in range(size)])]
    pallas_call x5, Pallas kernels: 4.05 us -> 5.43 us  [products(): pl.pallas_call(lambda *refs: product_kernel(counts, *refs), out_shape=[ja...]
  transfers between devices with their start and end apart: 19 -> 19, of which waited for: 11 -> 12; matrix products, arithmetic and copies ran while one was open for 3% -> 3% of each run, Pallas kernels for 12% -> 12%
where the time goes in v17:
time: 103 us
  waiting for transfers between devices  58.5 us (57%)
  starting transfers between devices  24.5 us (24%)
  Pallas kernels  15.1 us (15%)
  local copies, waits for them, and re-layouts  3.17 us (3%)
    ppermute x14, waiting for transfers between devices, moved(): lax.ppermute(block, axis, [(i, target(i) % size) for i in range(size)])  38.5 us
    ppermute x5, waiting for transfers between devices, to_next_section(): return lax.ppermute(part, ('section', 'ctx'), route)  20 us
    ppermute x14, starting transfers between devices, moved(): lax.ppermute(block, axis, [(i, target(i) % size) for i in range(size)])  17.3 us
    ppermute x5, starting transfers between devices, to_next_section(): return lax.ppermute(part, ('section', 'ctx'), route)  7.23 us
    pallas_call x5, Pallas kernels, products(): pl.pallas_call(lambda *refs: product_kernel(counts, *refs), out_shape=[ja...  5.43 us
    pallas_call x1, Pallas kernels, scored(): pl.pallas_call(score_kernel, grid=(micro_count,), in_specs=[pl.BlockSpec(...  4.74 us
    pallas_call x1, Pallas kernels, mixed_values(): pl.pallas_call(mix_kernel, grid=(micro_count,), in_specs=[pl.BlockSpec((1...  2.5 us
    pallas_call x1, Pallas kernels, normed_cuts(): pl.pallas_call(norm_kernel, grid=(micro_count,), in_specs=[pl.BlockSpec(m...  2.07 us
  transfers between devices with their start and end apart: 19, of which 12 were waited for; matrix products, arithmetic and copies ran while one was open for 3% of the time, Pallas kernels for 12%

profile of v17, /device:TPU:0, one launch (start us, length us, event | category | flops | bytes accessed | tf_op | source)
XLA Modules:
  0.0 102.9 jit_solution(2596034503123033017)
XLA Ops:
  0.7 2.4 %collective-permute-start = (bf16[1,4096]{1,0:T(2,128)(2,1)}, bf16[1,4096]{1,0:T(2,128)(2,1)S(1)}, u32[]{:S(2)}, u32[]{:S(2)}) collective-permute-start(bf16[1,4096]{1,0:T(2,128)(2,1)} %param.6), channel_id=1, source_target_pairs={{0,24},{8,0},{16,8},{24,16},{1,25},{9,1},{17,9},{25,17},{2,26},{10... | collective-permute-start | bytes 24584 | tf_op jit(solution)/shard_map/ppermute | solution.py:25
  3.1 1.3 %fusion.4 = (bf16[512,512]{1,0:T(8,128)(2,1)S(1)}, bf16[512,512]{1,0:T(8,128)(2,1)S(1)}) fusion(bf16[512,1024]{1,0:T(8,128)(2,1)} %bitcast.7), kind=kLoop, calls=%fused_computation.21 | loop fusion | bytes 2097152 | tf_op jit(solution)/shard_map/slice | solution.py:289
  4.3 2.7 %collective-permute-start.2 = (bf16[512,512]{1,0:T(8,128)(2,1)S(1)}, bf16[512,512]{1,0:T(8,128)(2,1)S(1)}, u32[]{:S(2)}, u32[]{:S(2)}) collective-permute-start(bf16[512,512]{1,0:T(8,128)(2,1)S(1)} %get-tuple-element.37.refs_3_.refs_2_), channel_id=1, source_target_pairs={{0,4},{1,5},{2,6},{3,7},{4,0},{5,1},{6,2},{7,3},{8,12},{9,13},{10,... | collective-permute-start | bytes 1572872 | tf_op jit(solution)/shard_map/ppermute | solution.py:25
  7.4 0.7 slice.24
  8.1 2.1 %norm_cuts.1 = (bf16[192,1024]{1,0:T(8,128)(2,1)S(1)}, bf16[192,1024]{1,0:T(8,128)(2,1)}, bf16[192,1024]{1,0:T(8,128)(2,1)S(1)}, bf16[192,1024]{1,0:T(8,128)(2,1)}) custom-call(s32[4,2]{1,0:T(4,128)S(1)} %add_multiply_fusion.starts_ref, bf16[2,96,4096]{2,1,0:T(8,128)(2,1)S(1)} %bitcast.6, f32[1,4096]{1,0:T(1,128)S(1)} %convert_element_type.16.gain_ref), custom_call_target="tpu_custom_call" | custom-call | flops 4718592 | bytes 3145728 | tf_op jit(solution)/shard_map/norm_cuts/pallas_call | solution.py:58
  10.1 0.8 copy-done.4
  11.3 2.5 %collective-permute-start.6 = (bf16[192,1024]{1,0:T(8,128)(2,1)}, bf16[192,1024]{1,0:T(8,128)(2,1)}, u32[]{:S(2)}, u32[]{:S(2)}) collective-permute-start(bf16[192,1024]{1,0:T(8,128)(2,1)} %get-tuple-element.23), channel_id=1, source_target_pairs={{0,11},{1,10},{2,9},{3,8},{4,15},{5,14},{6,13},{7,12},{8,19},{9,18... | collective-permute-start | bytes 1179656 | tf_op jit(solution)/shard_map/ppermute | solution.py:281
  14.2 15.8 %collective-permute-done.2.refs_4_.refs_3_ = bf16[512,512]{1,0:T(8,128)(2,1)S(1)} collective-permute-done((bf16[512,512]{1,0:T(8,128)(2,1)S(1)}, bf16[512,512]{1,0:T(8,128)(2,1)S(1)}, u32[]{:S(2)}, u32[]{:S(2)}) %collective-permute-start.2) | collective-permute-done | bytes 524320 | tf_op jit(solution)/shard_map/ppermute | solution.py:25
  30.0 3.6 %collective-permute-done.6.refs_1_.refs_2_ = bf16[192,1024]{1,0:T(8,128)(2,1)} collective-permute-done((bf16[192,1024]{1,0:T(8,128)(2,1)}, bf16[192,1024]{1,0:T(8,128)(2,1)}, u32[]{:S(2)}, u32[]{:S(2)}) %collective-permute-start.6) | collective-permute-done | bytes 393248 | tf_op jit(solution)/shard_map/ppermute | solution.py:281
  33.6 1.6 %products.6 = bf16[384,512]{1,0:T(8,128)(2,1)S(1)} custom-call(bf16[192,1024]{1,0:T(8,128)(2,1)S(1)} %collective-permute-done.5.refs_0_, bf16[192,1024]{1,0:T(8,128)(2,1)} %collective-permute-done.6.refs_1_.refs_2_, bf16[512,512]{1,0:T(8,128)(2,1)S(1)} %get-tuple-element.37.refs_3_.refs_2_, bf16[512,512]{1,0:T(8,128)(2,1)S(1)} %collective-permute-done.2.refs_4_.refs_3_), custom_call_target="tpu_custom_call" | custom-call | flops 1610612736 | bytes 3145728 | tf_op jit(solution)/shard_map/products/pallas_call | solution.py:99
  35.2 2.0 %collective-permute-start.7 = (bf16[384,512]{1,0:T(8,128)(2,1)S(1)}, bf16[384,512]{1,0:T(8,128)(2,1)S(1)}, u32[]{:S(2)}, u32[]{:S(2)}) collective-permute-start(bf16[384,512]{1,0:T(8,128)(2,1)S(1)} %products.6), channel_id=1, source_target_pairs={{0,1},{1,0},{2,3},{3,2},{4,5},{5,4},{6,7},{7,6},{8,9},{9,8},{10,11... | collective-permute-start | bytes 1179656 | tf_op jit(solution)/shard_map/ppermute | solution.py:25
  37.6 3.9 %collective-permute-start.3 = (bf16[96,1024]{1,0:T(8,128)(2,1)S(1)}, bf16[96,1024]{1,0:T(8,128)(2,1)S(1)}, u32[]{:S(2)}, u32[]{:S(2)}) collective-permute-start(bf16[96,1024]{1,0:T(8,128)(2,1)S(1)} %get-tuple-element.39), channel_id=1, source_target_pairs={{0,10},{1,11},{2,8},{3,9},{4,14},{5,15},{6,12},{7,13},{8,18},{9,19... | collective-permute-start | bytes 589832 | tf_op jit(solution)/shard_map/ppermute | solution.py:281
  41.4 0.4 fusion
  41.9 4.3 %collective-permute-done.4.refs_2_.refs_1_ = bf16[96,1024]{1,0:T(8,128)(2,1)S(1)} collective-permute-done((bf16[96,1024]{1,0:T(8,128)(2,1)S(1)}, bf16[96,1024]{1,0:T(8,128)(2,1)S(1)}, u32[]{:S(2)}, u32[]{:S(2)}) %collective-permute-start.4) | collective-permute-done | bytes 196640 | tf_op jit(solution)/shard_map/ppermute | solution.py:281
  46.2 12.0 %collective-permute-done.3.refs_1_.refs_0_ = bf16[96,1024]{1,0:T(8,128)(2,1)S(1)} collective-permute-done((bf16[96,1024]{1,0:T(8,128)(2,1)S(1)}, bf16[96,1024]{1,0:T(8,128)(2,1)S(1)}, u32[]{:S(2)}, u32[]{:S(2)}) %collective-permute-start.3) | collective-permute-done | bytes 196640 | tf_op jit(solution)/shard_map/ppermute | solution.py:281
  58.2 0.7 products.5.held
  59.5 1.7 %products.8 = (bf16[192,512]{1,0:T(8,128)(2,1)S(1)}, bf16[192,512]{1,0:T(8,128)(2,1)S(1)}) custom-call(bf16[96,1024]{1,0:T(8,128)(2,1)S(1)} %collective-permute-done.3.refs_1_.refs_0_, bf16[96,1024]{1,0:T(8,128)(2,1)S(1)} %collective-permute-done.4.refs_2_.refs_1_, bf16[192,1024]{1,0:T(8,128)(2,1)} %collective-permute-done.6.refs_1_.refs_2_, ...), custom_call_target="tpu_custom_call" | custom-call | flops 1610612736 | bytes 3145728 | tf_op jit(solution)/shard_map/products/pallas_call | solution.py:99
  61.2 1.9 %collective-permute-start.13 = (bf16[192,512]{1,0:T(8,128)(2,1)S(1)}, bf16[192,512]{1,0:T(8,128)(2,1)S(1)}, u32[]{:S(2)}, u32[]{:S(2)}) collective-permute-start(bf16[192,512]{1,0:T(8,128)(2,1)S(1)} %get-tuple-element.31), channel_id=1, source_target_pairs={{0,2},{1,3},{2,0},{3,1},{4,6},{5,7},{6,4},{7,5},{8,10},{9,11},{10,... | collective-permute-start | bytes 589832 | tf_op jit(solution)/shard_map/ppermute | solution.py:25
  63.1 1.7 %collective-permute-start.14 = (bf16[192,512]{1,0:T(8,128)(2,1)S(1)}, bf16[192,512]{1,0:T(8,128)(2,1)S(1)}, u32[]{:S(2)}, u32[]{:S(2)}) collective-permute-start(bf16[192,512]{1,0:T(8,128)(2,1)S(1)} %get-tuple-element.32), channel_id=1, source_target_pairs={{0,3},{1,2},{2,1},{3,0},{4,7},{5,6},{6,5},{7,4},{8,11},{9,10},{10,... | collective-permute-start | bytes 589832 | tf_op jit(solution)/shard_map/ppermute | solution.py:25
  64.8 2.0 %collective-permute-done.8.refs_0_ = bf16[192,512]{1,0:T(8,128)(2,1)S(1)} collective-permute-done((bf16[192,512]{1,0:T(8,128)(2,1)S(1)}, bf16[192,512]{1,0:T(8,128)(2,1)S(1)}, u32[]{:S(2)}, u32[]{:S(2)}) %collective-permute-start.8) | collective-permute-done | bytes 196640 | tf_op jit(solution)/shard_map/ppermute | solution.py:25
  67.0 1.1 %products.9 = bf16[192,512]{1,0:T(8,128)(2,1)} custom-call(bf16[192,1024]{1,0:T(8,128)(2,1)S(1)} %copy-done.3, bf16[512,512]{1,0:T(8,128)(2,1)S(1)} %get-tuple-element.33.refs_1_.refs_3_, bf16[512,512]{1,0:T(8,128)(2,1)S(1)} %collective-permute-done.12.refs_2_.refs_4_), custom_call_target="tpu_custom_call" | custom-call | flops 805306368 | bytes 1572864 | tf_op jit(solution)/shard_map/products/pallas_call | solution.py:99
  68.0 2.3 %collective-permute-start.9 = (bf16[192,512]{1,0:T(8,128)(2,1)S(1)}, bf16[192,512]{1,0:T(8,128)(2,1)S(1)}, u32[]{:S(2)}, u32[]{:S(2)}) collective-permute-start(bf16[192,512]{1,0:T(8,128)(2,1)S(1)} %key_sum.1.refs_3_), channel_id=1, source_target_pairs={{0,2},{1,3},{2,4},{3,5},{4,6},{5,7},{6,0},{7,1},{8,10},{9,11},{10,... | collective-permute-start | bytes 589832 | tf_op jit(solution)/shard_map/ppermute | solution.py:25
  71.0 3.9 %collective-permute-done.14.refs_1_ = bf16[192,512]{1,0:T(8,128)(2,1)S(1)} collective-permute-done((bf16[192,512]{1,0:T(8,128)(2,1)S(1)}, bf16[192,512]{1,0:T(8,128)(2,1)S(1)}, u32[]{:S(2)}, u32[]{:S(2)}) %collective-permute-start.14) | collective-permute-done | bytes 196640 | tf_op jit(solution)/shard_map/ppermute | solution.py:25
  74.9 3.7 %collective-permute-done.15.refs_2_ = bf16[192,512]{1,0:T(8,128)(2,1)S(1)} collective-permute-done((bf16[192,512]{1,0:T(8,128)(2,1)}, bf16[192,512]{1,0:T(8,128)(2,1)S(1)}, u32[]{:S(2)}, u32[]{:S(2)}) %collective-permute-start.15) | collective-permute-done | bytes 196640 | tf_op jit(solution)/shard_map/ppermute | solution.py:25
  78.7 1.3 %collective-permute-start.16 = (bf16[192,512]{1,0:T(8,128)(2,1)S(1)}, bf16[192,512]{1,0:T(8,128)(2,1)S(1)}, u32[]{:S(2)}, u32[]{:S(2)}) collective-permute-start(bf16[192,512]{1,0:T(8,128)(2,1)S(1)} %value_sum.1.refs_3_), channel_id=1, source_target_pairs={{0,1},{1,2},{2,3},{3,4},{4,5},{5,6},{6,7},{7,0},{8,9},{9,10},{10,1... | collective-permute-start | bytes 589832 | tf_op jit(solution)/shard_map/ppermute | solution.py:25
  80.1 1.6 %collective-permute-start.11 = (bf16[192,512]{1,0:T(8,128)(2,1)S(1)}, bf16[192,512]{1,0:T(8,128)(2,1)S(1)}, u32[]{:S(2)}, u32[]{:S(2)}) collective-permute-start(bf16[192,512]{1,0:T(8,128)(2,1)S(1)} %broadcast_select_fusion), channel_id=1, source_target_pairs={{0,1},{1,2},{2,3},{3,4},{4,5},{5,6},{6,7},{7,0},{8,9},{9,10},{10,1... | collective-permute-start | bytes 589832 | tf_op jit(solution)/shard_map/ppermute | solution.py:25
  81.7 0.8 collective-permute-start.10
  82.8 6.5 %collective-permute-done.16.refs_2_ = bf16[192,512]{1,0:T(8,128)(2,1)S(1)} collective-permute-done((bf16[192,512]{1,0:T(8,128)(2,1)S(1)}, bf16[192,512]{1,0:T(8,128)(2,1)S(1)}, u32[]{:S(2)}, u32[]{:S(2)}) %collective-permute-start.16) | collective-permute-done | bytes 196640 | tf_op jit(solution)/shard_map/ppermute | solution.py:25
  89.5 4.0 %collective-permute-done.11.refs_2_ = bf16[192,512]{1,0:T(8,128)(2,1)S(1)} collective-permute-done((bf16[192,512]{1,0:T(8,128)(2,1)S(1)}, bf16[192,512]{1,0:T(8,128)(2,1)S(1)}, u32[]{:S(2)}, u32[]{:S(2)}) %collective-permute-start.11) | collective-permute-done | bytes 196640 | tf_op jit(solution)/shard_map/ppermute | solution.py:25
  93.5 2.1 %collective-permute-done.10.refs_0_ = bf16[192,512]{1,0:T(8,128)(2,1)S(1)} collective-permute-done((bf16[192,512]{1,0:T(8,128)(2,1)S(1)}, bf16[192,512]{1,0:T(8,128)(2,1)S(1)}, u32[]{:S(2)}, u32[]{:S(2)}) %collective-permute-start.10) | collective-permute-done | bytes 196640 | tf_op jit(solution)/shard_map/ppermute | solution.py:25
  95.7 4.7 %scores.1 = (bf16[2,4,768,384]{3,2,1,0:T(8,128)(2,1)S(1)}, f32[2,4,96,128]{3,2,1,0:T(8,128)S(1)}, f32[2,32,96]{2,1,0:T(8,128)}) custom-call(s32[1]{0:T(128)} %bitcast.odd_ref, bf16[1,2,96,4096]{3,2,1,0:T(8,128)(2,1)S(1)} %copy-done.1, bf16[192,512]{1,0:T(8,128)(2,1)S(1)} %collective-permute-done.10.refs_0_, ...), custom_call_target="tpu_custom_call" | custom-call | flops 603979776 | bytes 8388608 | tf_op jit(solution)/shard_map/scores/pallas_call | solution.py:197
  100.4 2.5 %mixed_values.1 = bf16[1,2,96,4096]{3,2,1,0:T(8,128)(2,1)} custom-call(bf16[2,4,768,384]{3,2,1,0:T(8,128)(2,1)S(1)} %get-tuple-element.26.weights, f32[2,4,96,128]{3,2,1,0:T(8,128)S(1)} %get-tuple-element.27.sums, bf16[192,512]{1,0:T(8,128)(2,1)S(1)} %collective-permute-done.17.refs_0_, bf16[192,512]{1,0:T(8,128)(2,1)S(1)} %collective-permute-done.18.refs_1_, ...), custom_call_target="tpu_custom_call" | custom-call | flops 603979776 | bytes 8388608 | tf_op jit(solution)/shard_map/mixed_values/pallas_call | solution.py:242
  (53 shorter events, 3.5 us)
Async XLA Ops:
  0.6 6.4 %copy-start.6 = (s32[2,16]{1,0:T(2,128)S(1)}, s32[2,16]{1,0:T(2,128)}, u32[]{:S(2)}) copy-start(s32[2,16]{1,0:T(2,128)} %param.9) | copy-start | bytes 388
  0.6 7.4 %copy-start = (bf16[1,2,96,4096]{3,2,1,0:T(8,128)(2,1)S(1)}, bf16[1,2,96,4096]{3,2,1,0:T(8,128)(2,1)}, u32[]{:S(2)}) copy-start(bf16[1,2,96,4096]{3,2,1,0:T(8,128)(2,1)} %param.5) | copy-start | bytes 4718596
  0.7 7.4 %collective-permute-start = (bf16[1,4096]{1,0:T(2,128)(2,1)}, bf16[1,4096]{1,0:T(2,128)(2,1)S(1)}, u32[]{:S(2)}, u32[]{:S(2)}) collective-permute-start(bf16[1,4096]{1,0:T(2,128)(2,1)} %param.6), channel_id=1, source_target_pairs={{0,24},{8,0},{16,8},{24,16},{1,25},{9,1},{17,9},{25,17},{2,26},{10... | collective-permute-start | bytes 24584 | tf_op jit(solution)/shard_map/ppermute | solution.py:25
  4.3 25.7 %collective-permute-start.2 = (bf16[512,512]{1,0:T(8,128)(2,1)S(1)}, bf16[512,512]{1,0:T(8,128)(2,1)S(1)}, u32[]{:S(2)}, u32[]{:S(2)}) collective-permute-start(bf16[512,512]{1,0:T(8,128)(2,1)S(1)} %get-tuple-element.37.refs_3_.refs_2_), channel_id=1, source_target_pairs={{0,4},{1,5},{2,6},{3,7},{4,0},{5,1},{6,2},{7,3},{8,12},{9,13},{10,... | collective-permute-start | bytes 1572872 | tf_op jit(solution)/shard_map/ppermute | solution.py:25
  8.0 5.8 %copy-start.5 = (s32[2,288]{1,0:T(2,128)S(1)}, s32[2,288]{1,0:T(2,128)}, u32[]{:S(2)}) copy-start(s32[2,288]{1,0:T(2,128)} %slice.24) | copy-start | bytes 6916
  10.1 0.8 copy-start.4
  10.9 19.1 %collective-permute-start.5 = (bf16[192,1024]{1,0:T(8,128)(2,1)}, bf16[192,1024]{1,0:T(8,128)(2,1)S(1)}, u32[]{:S(2)}, u32[]{:S(2)}) collective-permute-start(bf16[192,1024]{1,0:T(8,128)(2,1)} %get-tuple-element.22), channel_id=1, source_target_pairs={{0,9},{1,8},{2,11},{3,10},{4,13},{5,12},{6,15},{7,14},{8,17},{9,16... | collective-permute-start | bytes 1179656 | tf_op jit(solution)/shard_map/ppermute | solution.py:281
  11.3 22.3 %collective-permute-start.6 = (bf16[192,1024]{1,0:T(8,128)(2,1)}, bf16[192,1024]{1,0:T(8,128)(2,1)}, u32[]{:S(2)}, u32[]{:S(2)}) collective-permute-start(bf16[192,1024]{1,0:T(8,128)(2,1)} %get-tuple-element.23), channel_id=1, source_target_pairs={{0,11},{1,10},{2,9},{3,8},{4,15},{5,14},{6,13},{7,12},{8,19},{9,18... | collective-permute-start | bytes 1179656 | tf_op jit(solution)/shard_map/ppermute | solution.py:281
  14.1 27.8 %collective-permute-start.1 = (bf16[192,1024]{1,0:T(8,128)(2,1)}, bf16[192,1024]{1,0:T(8,128)(2,1)S(1)}, u32[]{:S(2)}, u32[]{:S(2)}) collective-permute-start(bf16[192,1024]{1,0:T(8,128)(2,1)} %copy-done.4), channel_id=1, source_target_pairs={{0,8},{1,9},{2,10},{3,11},{4,12},{5,13},{6,14},{7,15},{8,16},{9,17... | collective-permute-start | bytes 1179656 | tf_op jit(solution)/shard_map/ppermute | solution.py:281
  30.0 29.4 %collective-permute-start.12 = (bf16[512,512]{1,0:T(8,128)(2,1)S(1)}, bf16[512,512]{1,0:T(8,128)(2,1)S(1)}, u32[]{:S(2)}, u32[]{:S(2)}) collective-permute-start(bf16[512,512]{1,0:T(8,128)(2,1)S(1)} %get-tuple-element.33.refs_1_.refs_3_), channel_id=1, source_target_pairs={{0,4},{1,5},{2,6},{3,7},{4,0},{5,1},{6,2},{7,3},{8,12},{9,13},{10,... | collective-permute-start | bytes 1572872 | tf_op jit(solution)/shard_map/ppermute | solution.py:25
  30.0 5.2 %copy-start.2 = (bf16[192,1024]{1,0:T(8,128)(2,1)}, bf16[192,1024]{1,0:T(8,128)(2,1)S(1)}, u32[]{:S(2)}) copy-start(bf16[192,1024]{1,0:T(8,128)(2,1)S(1)} %collective-permute-done.5.refs_0_) | copy-start | bytes 1179652
  35.2 23.7 %collective-permute-start.7 = (bf16[384,512]{1,0:T(8,128)(2,1)S(1)}, bf16[384,512]{1,0:T(8,128)(2,1)S(1)}, u32[]{:S(2)}, u32[]{:S(2)}) collective-permute-start(bf16[384,512]{1,0:T(8,128)(2,1)S(1)} %products.6), channel_id=1, source_target_pairs={{0,1},{1,0},{2,3},{3,2},{4,5},{5,4},{6,7},{7,6},{8,9},{9,8},{10,11... | collective-permute-start | bytes 1179656 | tf_op jit(solution)/shard_map/ppermute | solution.py:25
  37.2 9.0 %collective-permute-start.4 = (bf16[96,1024]{1,0:T(8,128)(2,1)S(1)}, bf16[96,1024]{1,0:T(8,128)(2,1)S(1)}, u32[]{:S(2)}, u32[]{:S(2)}) collective-permute-start(bf16[96,1024]{1,0:T(8,128)(2,1)S(1)} %get-tuple-element.38), channel_id=1, source_target_pairs={{0,10},{1,11},{2,8},{3,9},{4,14},{5,15},{6,12},{7,13},{8,18},{9,19... | collective-permute-start | bytes 589832 | tf_op jit(solution)/shard_map/ppermute | solution.py:281
  37.6 20.7 %collective-permute-start.3 = (bf16[96,1024]{1,0:T(8,128)(2,1)S(1)}, bf16[96,1024]{1,0:T(8,128)(2,1)S(1)}, u32[]{:S(2)}, u32[]{:S(2)}) collective-permute-start(bf16[96,1024]{1,0:T(8,128)(2,1)S(1)} %get-tuple-element.39), channel_id=1, source_target_pairs={{0,10},{1,11},{2,8},{3,9},{4,14},{5,15},{6,12},{7,13},{8,18},{9,19... | collective-permute-start | bytes 589832 | tf_op jit(solution)/shard_map/ppermute | solution.py:281
  59.0 7.8 %collective-permute-start.8 = (bf16[192,512]{1,0:T(8,128)(2,1)S(1)}, bf16[192,512]{1,0:T(8,128)(2,1)S(1)}, u32[]{:S(2)}, u32[]{:S(2)}) collective-permute-start(bf16[192,512]{1,0:T(8,128)(2,1)S(1)} %get-tuple-element.25), channel_id=1, source_target_pairs={{0,2},{1,3},{2,0},{3,1},{4,6},{5,7},{6,4},{7,5},{8,10},{9,11},{10,... | collective-permute-start | bytes 589832 | tf_op jit(solution)/shard_map/ppermute | solution.py:25
  59.4 7.5 %copy-start.3 = (bf16[192,1024]{1,0:T(8,128)(2,1)S(1)}, bf16[192,1024]{1,0:T(8,128)(2,1)}, u32[]{:S(2)}) copy-start(bf16[192,1024]{1,0:T(8,128)(2,1)} %copy-done.2) | copy-start | bytes 1179652
  61.2 9.8 %collective-permute-start.13 = (bf16[192,512]{1,0:T(8,128)(2,1)S(1)}, bf16[192,512]{1,0:T(8,128)(2,1)S(1)}, u32[]{:S(2)}, u32[]{:S(2)}) collective-permute-start(bf16[192,512]{1,0:T(8,128)(2,1)S(1)} %get-tuple-element.31), channel_id=1, source_target_pairs={{0,2},{1,3},{2,0},{3,1},{4,6},{5,7},{6,4},{7,5},{8,10},{9,11},{10,... | collective-permute-start | bytes 589832 | tf_op jit(solution)/shard_map/ppermute | solution.py:25
  63.1 11.8 %collective-permute-start.14 = (bf16[192,512]{1,0:T(8,128)(2,1)S(1)}, bf16[192,512]{1,0:T(8,128)(2,1)S(1)}, u32[]{:S(2)}, u32[]{:S(2)}) collective-permute-start(bf16[192,512]{1,0:T(8,128)(2,1)S(1)} %get-tuple-element.32), channel_id=1, source_target_pairs={{0,3},{1,2},{2,1},{3,0},{4,7},{5,6},{6,5},{7,4},{8,11},{9,10},{10,... | collective-permute-start | bytes 589832 | tf_op jit(solution)/shard_map/ppermute | solution.py:25
  68.0 10.6 %collective-permute-start.15 = (bf16[192,512]{1,0:T(8,128)(2,1)}, bf16[192,512]{1,0:T(8,128)(2,1)S(1)}, u32[]{:S(2)}, u32[]{:S(2)}) collective-permute-start(bf16[192,512]{1,0:T(8,128)(2,1)} %products.9), channel_id=1, source_target_pairs={{0,1},{1,0},{2,3},{3,2},{4,5},{5,4},{6,7},{7,6},{8,9},{9,8},{10,11... | collective-permute-start | bytes 589832 | tf_op jit(solution)/shard_map/ppermute | solution.py:25
  68.0 12.1 %collective-permute-start.9 = (bf16[192,512]{1,0:T(8,128)(2,1)S(1)}, bf16[192,512]{1,0:T(8,128)(2,1)S(1)}, u32[]{:S(2)}, u32[]{:S(2)}) collective-permute-start(bf16[192,512]{1,0:T(8,128)(2,1)S(1)} %key_sum.1.refs_3_), channel_id=1, source_target_pairs={{0,2},{1,3},{2,4},{3,5},{4,6},{5,7},{6,0},{7,1},{8,10},{9,11},{10,... | collective-permute-start | bytes 589832 | tf_op jit(solution)/shard_map/ppermute | solution.py:25
  70.7 25.0 %copy-start.1 = (bf16[1,2,96,4096]{3,2,1,0:T(8,128)(2,1)S(1)}, bf16[1,2,96,4096]{3,2,1,0:T(8,128)(2,1)}, u32[]{:S(2)}) copy-start(bf16[1,2,96,4096]{3,2,1,0:T(8,128)(2,1)} %q_ref.1) | copy-start | bytes 4718596
  78.7 10.7 %collective-permute-start.16 = (bf16[192,512]{1,0:T(8,128)(2,1)S(1)}, bf16[192,512]{1,0:T(8,128)(2,1)S(1)}, u32[]{:S(2)}, u32[]{:S(2)}) collective-permute-start(bf16[192,512]{1,0:T(8,128)(2,1)S(1)} %value_sum.1.refs_3_), channel_id=1, source_target_pairs={{0,1},{1,2},{2,3},{3,4},{4,5},{5,6},{6,7},{7,0},{8,9},{9,10},{10,1... | collective-permute-start | bytes 589832 | tf_op jit(solution)/shard_map/ppermute | solution.py:25
  80.1 13.4 %collective-permute-start.11 = (bf16[192,512]{1,0:T(8,128)(2,1)S(1)}, bf16[192,512]{1,0:T(8,128)(2,1)S(1)}, u32[]{:S(2)}, u32[]{:S(2)}) collective-permute-start(bf16[192,512]{1,0:T(8,128)(2,1)S(1)} %broadcast_select_fusion), channel_id=1, source_target_pairs={{0,1},{1,2},{2,3},{3,4},{4,5},{5,6},{6,7},{7,0},{8,9},{9,10},{10,1... | collective-permute-start | bytes 589832 | tf_op jit(solution)/shard_map/ppermute | solution.py:25
  81.7 13.9 %collective-permute-start.10 = (bf16[192,512]{1,0:T(8,128)(2,1)S(1)}, bf16[192,512]{1,0:T(8,128)(2,1)S(1)}, u32[]{:S(2)}, u32[]{:S(2)}) collective-permute-start(bf16[192,512]{1,0:T(8,128)(2,1)S(1)} %collective-permute-done.9.refs_1_), channel_id=1, source_target_pairs={{0,1},{1,0},{2,3},{3,2},{4,5},{5,4},{6,7},{7,6},{8,9},{9,8},{10,11... | collective-permute-start | bytes 589832 | tf_op jit(solution)/shard_map/ppermute | solution.py:25
  82.6 17.9 %collective-permute-start.18 = (bf16[192,512]{1,0:T(8,128)(2,1)S(1)}, bf16[192,512]{1,0:T(8,128)(2,1)S(1)}, u32[]{:S(2)}, u32[]{:S(2)}) collective-permute-start(bf16[192,512]{1,0:T(8,128)(2,1)S(1)} %value_sum.1.refs_3_), channel_id=1, source_target_pairs={{0,2},{1,3},{2,4},{3,5},{4,6},{5,7},{6,0},{7,1},{8,10},{9,11},{10,... | collective-permute-start | bytes 589832 | tf_op jit(solution)/shard_map/ppermute | solution.py:25
  89.4 11.0 %collective-permute-start.17 = (bf16[192,512]{1,0:T(8,128)(2,1)S(1)}, bf16[192,512]{1,0:T(8,128)(2,1)S(1)}, u32[]{:S(2)}, u32[]{:S(2)}) collective-permute-start(bf16[192,512]{1,0:T(8,128)(2,1)S(1)} %collective-permute-done.16.refs_2_), channel_id=1, source_target_pairs={{0,2},{1,3},{2,4},{3,5},{4,6},{5,7},{6,0},{7,1},{8,10},{9,11},{10,... | collective-permute-start | bytes 589832 | tf_op jit(solution)/shard_map/ppermute | solution.py:25
